TPU v7x, 32 devices: a whole 2x2x4 slice. The times are simulated.
32 devices in a mesh: space: 8 (over z, y), tm: 4 (over x, core).
Axes of the slice: x: 2, y: 2, z: 4, core: 2. Of those that a mesh axis runs over, the one named last changes fastest.
Arguments:
- snapshots: bfloat16 [256, 65536], P('tm', 'space'), may hold values from -75 to 75
- prior_basis: bfloat16 [256, 65536], P('tm', 'space'), may hold values from -75 to 75
- mass_factor: bfloat16 [7, 64, 65536], P(None, None, 'space'), may hold values from -1 to 3.2, as said below
- neighbours: int32 [1024, 7], P('space'), may hold values from 0 to 1023, as said below
Outputs:
- merged_basis: bfloat16 [64, 65536], P(None, ('space', 'tm'))
- merged_weighted: bfloat16 [64, 65536], P(None, ('space', 'tm'))
Inputs may be any that keep to these rules, and one draw needn't show every extreme that they name: `mass_factor`: factor entries; the diagonal of each block's own coupling lies in 1.5 to 3. neighbours[i, 0] = i; every entry lies within 8 blocks of i; in every draw some entries lie exactly 8 blocks below and above their block.
All inputs are finite; a program needn't handle non-finite values.
Results may differ from a plain program's by a relative error of at most 0.018.
Values may be sent and summed in bfloat16 or wider, within the bound.
No kernel may reach another device: no remote copies, remote signals or barrier semaphores. Data moves between devices by JAX's collectives and lax.ppermute only.
A program may use at most 128 MiB of HBM per device.

v0:
```python
import jax
import jax.numpy as jnp
from jax import lax
from jax.sharding import PartitionSpec as P

BLOCK_DOFS = 64
RANK = 64
NEIGHBOURS = 7
REACH = 8
SUBSPACE_STEPS = 3
LOCAL_BLOCKS = 128


def padded(block, sides, width):
    for axis, dim in sides:
        count = lax.axis_size(axis)
        forward = [(i, i + 1) for i in range(count - 1)]
        backward = [(target, source) for source, target in forward]
        low = lax.ppermute(
            lax.slice_in_dim(block, block.shape[dim] - width, None, axis=dim), axis, forward
        )
        high = lax.ppermute(lax.slice_in_dim(block, 0, width, axis=dim), axis, backward)
        block = jnp.concatenate([low, block, high], axis=dim)
    return block


def partner(block, axis, bit):
    count = lax.axis_size(axis)
    route = []
    for low in range(count):
        high = low | 1 << bit
        if high != low and high < count:
            route += [(low, high), (high, low)]
    return lax.ppermute(block, axis, route)


def weigh_rows(stacked, mass_factor, local_index):
    columns = stacked.shape[0]
    widened = padded(stacked, (("space", 1),), REACH * BLOCK_DOFS)
    blocks = widened.reshape(columns, -1, BLOCK_DOFS)
    picked = jnp.take(blocks, local_index, axis=1)
    factor = mass_factor.reshape(NEIGHBOURS, BLOCK_DOFS, -1, BLOCK_DOFS)
    result = jnp.einsum("cbkq,kqbr->cbr", picked, factor, preferred_element_type=jnp.float32)
    return result.reshape(columns, -1).astype(jnp.bfloat16)


def compress(gram_total):
    highest = lax.Precision.HIGHEST
    order_size = gram_total.shape[0]
    weights = jnp.eye(order_size, RANK, dtype=jnp.float32)
    for repeat in range(SUBSPACE_STEPS):
        product = jnp.dot(gram_total, weights, precision=highest)
        inner_gram = jnp.dot(
            product.T, jnp.dot(gram_total, product, precision=highest), precision=highest
        )
        scales = jnp.sqrt(jnp.diagonal(inner_gram))
        factor_lower = jnp.linalg.cholesky(inner_gram / (scales[:, None] * scales[None, :]))
        normed = product / scales[None, :]
        weights = lax.linalg.triangular_solve(
            factor_lower, normed, left_side=False, lower=True, transpose_a=True
        )
    product = jnp.dot(gram_total, weights, precision=highest)
    lengths = jnp.sqrt(jnp.sum(product * product, axis=0) + 1e-06)
    return (weights * lengths[None, :]).astype(jnp.bfloat16)


def coefficients_of(weighted):
    local_gram = jnp.dot(weighted, weighted.T, preferred_element_type=jnp.float32)
    return compress(lax.psum(local_gram, "space"))


def apply_coefficients(coefficients, stacked, weighted):
    basis = jnp.dot(coefficients.T, stacked, preferred_element_type=jnp.float32).astype(
        jnp.bfloat16
    )
    weighted_basis = jnp.dot(coefficients.T, weighted, preferred_element_type=jnp.float32).astype(
        jnp.bfloat16
    )
    return (basis, weighted_basis)


def ordered(upper_half, own_rows, partner_rows):
    lower_part = jnp.where(upper_half, partner_rows, own_rows)
    upper_part = jnp.where(upper_half, own_rows, partner_rows)
    return jnp.concatenate([lower_part, upper_part], axis=0)


def shards(snapshots, prior_basis, mass_factor, neighbours):
    local_index = neighbours - (lax.axis_index("space") * LOCAL_BLOCKS - REACH)
    stacked = jnp.concatenate([prior_basis, snapshots], axis=0)
    weighted = weigh_rows(stacked, mass_factor, local_index)
    basis, weighted_basis = apply_coefficients(coefficients_of(weighted), stacked, weighted)
    member = lax.axis_index("tm")
    for level_bit in range(lax.axis_size("tm").bit_length() - 1):
        upper_half = member // (1 << level_bit) % 2 == 1
        partner_weighted = partner(weighted_basis, "tm", level_bit)
        weighted = ordered(upper_half, weighted_basis, partner_weighted)
        coefficients = coefficients_of(weighted)
        partner_rows = partner(basis, "tm", level_bit)
        stacked = ordered(upper_half, basis, partner_rows)
        basis, weighted_basis = apply_coefficients(coefficients, stacked, weighted)
    share_width = basis.shape[1] // lax.axis_size("tm")
    basis_share = lax.dynamic_slice_in_dim(basis, member * share_width, share_width, 1)
    weighted_share = lax.dynamic_slice_in_dim(weighted_basis, member * share_width, share_width, 1)
    return (basis_share, weighted_share)


def solution(mesh):
    return jax.shard_map(
        shards,
        mesh=mesh,
        in_specs=(P("tm", "space"), P("tm", "space"), P(None, None, "space"), P("space", None)),
        out_specs=(P(None, ("space", "tm")), P(None, ("space", "tm"))),
        check_vma=False,
    )
```

profile of v0, /device:TPU:0, one launch (start us, length us, event | category | flops | bytes accessed | tf_op | source)
XLA Modules:
  0.0 492.5 jit_solution(6582942118367420781)
XLA Ops:
  7.2 2.1 copy.30
  12.5 4.9 collective-permute-start
  19.2 20.9 %reshape.97 = bf16[7,64,128,64]{3,2,1,0:T(8,128)(2,1)} reshape(bf16[7,64,8192]{2,1,0:T(8,128)(2,1)} %param.9) | data formatting | bytes 14680064 | tf_op jit(solution)/shard_map/reshape | solution.py:42
  40.1 6.7 %pad_maximum_fusion = bf16[128,9216]{0,1:T(8,128)(2,1)S(1)} fusion(bf16[128,512]{0,1:T(8,128)(2,1)S(1)} %collective-permute-done.1, bf16[64,8192]{0,1:T(8,128)(2,1)} %copy.31, bf16[64,8192]{0,1:T(8,128)(2,1)} %copy-done, bf16[128,512]{0,1:T(8,128)(2,1)S(1)} %collective-permute-done), kind=kLoop, calls=%fused_computation.21 | loop fusion | flops 9437184 | bytes 4718592 | tf_op jit(solution)/shard_map/concatenate | solution.py:23
  46.8 22.8 %gather_fusion = bf16[896,128,64]{1,2,0:T(8,128)(2,1)} fusion(bf16[128,144,64]{0,2,1:T(8,128)(2,1)S(1)} %bitcast.178, s32[1024]{0:T(1024)S(1)} %pad_clamp_fusion), kind=kCustom, calls=%fused_computation | custom fusion | bytes 29363712 | tf_op jit(solution)/shard_map/jit(_take)/gather | solution.py:41
  69.6 29.2 %bitcast_convert_fusion = bf16[128,128,64]{1,2,0:T(8,128)(2,1)S(1)} fusion(bf16[128,7,128,64]{2,3,1,0:T(8,128)(2,1)} %bitcast.179, pred[128,7]{1,0:T(8,128)(4,1)S(1)} %copy.29, bf16[7,64,128,64]{3,2,1,0:T(8,128)(2,1)} %reshape.97), kind=kOutput, calls=%fused_computation.20 | convolution fusion | flops 947912704 | bytes 24118144 | tf_op jit(solution)/shard_map/cbkq,kqbr->cbr/dot_general | solution.py:43
  100.3 70.9 %all-reduce.4.cloned.1.call-done = f32[128,128]{1,0:T(8,128)} async-done(((f32[128,128]{1,0:T(8,128)}), f32[128,128]{1,0:T(8,128)}) %all-reduce.4.cloned.1.call-update) | async-done | bytes 65552 | tf_op jit(solution)/shard_map/psum | solution.py:69
  174.8 5.8 %cholesky.149 = f32[64,64]{1,0:T(8,128)S(1)} custom-call(f32[64,64]{1,0:T(8,128)S(1)} %fusion.60), custom_call_target="Cholesky" | custom-call | tf_op jit(solution)/shard_map/jit(cholesky)/cholesky | solution.py:57
  182.0 4.9 custom-call.31
  190.7 5.8 %cholesky.160 = f32[64,64]{1,0:T(8,128)S(1)} custom-call(f32[64,64]{1,0:T(8,128)S(1)} %fusion.58), custom_call_target="Cholesky" | custom-call | tf_op jit(solution)/shard_map/jit(cholesky)/cholesky | solution.py:57
  197.8 4.9 custom-call.32
  204.9 5.8 %cholesky.171 = f32[64,64]{1,0:T(8,128)S(1)} custom-call(f32[64,64]{1,0:T(8,128)S(1)} %fusion.56), custom_call_target="Cholesky" | custom-call | tf_op jit(solution)/shard_map/jit(cholesky)/cholesky | solution.py:57
  212.0 4.9 custom-call.33
  218.6 2.6 collective-permute-done.2
  224.4 2.9 convolution_convert_fusion.1
  227.5 65.2 %all-reduce.6.cloned.1.call-done = f32[128,128]{1,0:T(8,128)} async-done(((f32[128,128]{1,0:T(8,128)}), f32[128,128]{1,0:T(8,128)}) %all-reduce.6.cloned.1.call-update) | async-done | bytes 65552 | tf_op jit(solution)/shard_map/psum | solution.py:69
  296.2 5.8 %cholesky.182 = f32[64,64]{1,0:T(8,128)S(1)} custom-call(f32[64,64]{1,0:T(8,128)S(1)} %fusion.54), custom_call_target="Cholesky" | custom-call | tf_op jit(solution)/shard_map/jit(cholesky)/cholesky | solution.py:57
  303.4 4.9 custom-call.34
  312.1 5.8 %cholesky.193 = f32[64,64]{1,0:T(8,128)S(1)} custom-call(f32[64,64]{1,0:T(8,128)S(1)} %fusion.52), custom_call_target="Cholesky" | custom-call | tf_op jit(solution)/shard_map/jit(cholesky)/cholesky | solution.py:57
  319.3 4.9 custom-call.35
  326.3 5.8 %cholesky.204 = f32[64,64]{1,0:T(8,128)S(1)} custom-call(f32[64,64]{1,0:T(8,128)S(1)} %fusion.50), custom_call_target="Cholesky" | custom-call | tf_op jit(solution)/shard_map/jit(cholesky)/cholesky | solution.py:57
  333.5 4.9 custom-call.36
  344.8 22.1 %collective-permute-done.3 = bf16[64,8192]{1,0:T(8,128)(2,1)S(1)} collective-permute-done((bf16[64,8192]{1,0:T(8,128)(2,1)S(1)}, bf16[64,8192]{1,0:T(8,128)(2,1)S(1)}, u32[]{:S(2)}, u32[]{:S(2)}) %collective-permute-start.3) | collective-permute-done | bytes 1048608 | tf_op jit(solution)/shard_map/ppermute | solution.py:34
  368.4 18.0 %collective-permute-done.5 = bf16[64,8192]{1,0:T(8,128)(2,1)} collective-permute-done((bf16[64,8192]{1,0:T(8,128)(2,1)S(1)}, bf16[64,8192]{1,0:T(8,128)(2,1)}, u32[]{:S(2)}, u32[]{:S(2)}) %collective-permute-start.5) | collective-permute-done | bytes 1048608 | tf_op jit(solution)/shard_map/ppermute | solution.py:34
  386.5 2.7 broadcast_select_fusion.5
  389.1 47.9 %all-reduce.8.cloned.1.call-done = f32[128,128]{1,0:T(8,128)} async-done(((f32[128,128]{1,0:T(8,128)}), f32[128,128]{1,0:T(8,128)}) %all-reduce.8.cloned.1.call-update) | async-done | bytes 65552 | tf_op jit(solution)/shard_map/psum | solution.py:69
  440.5 6.1 %cholesky.215 = f32[64,64]{1,0:T(8,128)S(1)} custom-call(f32[64,64]{1,0:T(8,128)S(1)} %fusion.48), custom_call_target="Cholesky" | custom-call | tf_op jit(solution)/shard_map/jit(cholesky)/cholesky | solution.py:57
  447.9 4.9 custom-call.37
  456.6 5.8 %cholesky.226 = f32[64,64]{1,0:T(8,128)S(1)} custom-call(f32[64,64]{1,0:T(8,128)S(1)} %fusion.46), custom_call_target="Cholesky" | custom-call | tf_op jit(solution)/shard_map/jit(cholesky)/cholesky | solution.py:57
  463.8 4.9 custom-call.38
  470.8 5.8 %cholesky.237 = f32[64,64]{1,0:T(8,128)S(1)} custom-call(f32[64,64]{1,0:T(8,128)S(1)} %fusion.44), custom_call_target="Cholesky" | custom-call | tf_op jit(solution)/shard_map/jit(cholesky)/cholesky | solution.py:57
  478.0 4.9 custom-call.39
  (181 shorter events, 61.6 us)
Async XLA Ops:
  7.2 2.2 copy-start.5
  7.2 164.1 %all-reduce.4.cloned.1.call-start = ((), (), s32[]{:S(2)}) async-start(), calls=%async_computation | async-start | bytes 131072 | tf_op jit(solution)/shard_map/psum | solution.py:69
  9.3 3.2 copy-start
  11.4 7.3 %copy-start.11 = (s32[128,7]{0,1:T(8,128)S(1)}, s32[128,7]{0,1:T(8,128)}, u32[]{:S(2)}) copy-start(s32[128,7]{0,1:T(8,128)} %param.10) | copy-start | bytes 10756
  12.5 27.6 %collective-permute-start = (bf16[128,512]{0,1:T(8,128)(2,1)S(1)}, bf16[128,512]{0,1:T(8,128)(2,1)S(1)}, u32[]{:S(2)}, u32[]{:S(2)}) collective-permute-start(bf16[128,512]{0,1:T(8,128)(2,1)S(1)} %get-tuple-element.6), channel_id=1, source_target_pairs={{0,4},{4,8},{8,12},{12,16},{16,20},{20,24},{24,28},{1,5},{5,9},{9,... | collective-permute-start | bytes 393224 | tf_op jit(solution)/shard_map/ppermute | solution.py:19
  17.4 22.7 %collective-permute-start.1 = (bf16[128,512]{0,1:T(8,128)(2,1)S(1)}, bf16[128,512]{0,1:T(8,128)(2,1)S(1)}, u32[]{:S(2)}, u32[]{:S(2)}) collective-permute-start(bf16[128,512]{0,1:T(8,128)(2,1)S(1)} %get-tuple-element.7), channel_id=1, source_target_pairs={{4,0},{8,4},{12,8},{16,12},{20,16},{24,20},{28,24},{5,1},{9,5},{13... | collective-permute-start | bytes 393224 | tf_op jit(solution)/shard_map/ppermute | solution.py:22
  100.3 192.4 %all-reduce.6.cloned.1.call-start = ((), (), s32[]{:S(2)}) async-start(), calls=%async_computation.1 | async-start | bytes 131072 | tf_op jit(solution)/shard_map/psum | solution.py:69
  171.2 31.8 %copy-start.4 = (f32[128,128]{1,0:T(8,128)S(1)}, f32[128,128]{1,0:T(8,128)}, u32[]{:S(2)}) copy-start(f32[128,128]{1,0:T(8,128)} %all-reduce.4.cloned.1.call-done) | copy-start | bytes 196612
  218.5 2.7 collective-permute-start.2
  221.4 1.0 copy-start.6
  221.4 1.4 copy-start.8
  221.4 3.0 copy-start.1
  224.1 212.9 %all-reduce.8.cloned.1.call-start = ((), (), s32[]{:S(2)}) async-start(), calls=%async_computation.2 | async-start | bytes 131072 | tf_op jit(solution)/shard_map/psum | solution.py:69
  227.3 111.7 %copy-start.7 = (bf16[64,8192]{1,0:T(8,128)(2,1)S(1)}, bf16[64,8192]{1,0:T(8,128)(2,1)}, u32[]{:S(2)}) copy-start(bf16[64,8192]{1,0:T(8,128)(2,1)} %copy-done.6) | copy-start | bytes 3145732
  227.3 115.0 %collective-permute-start.4 = (bf16[64,8192]{1,0:T(8,128)(2,1)S(1)}, bf16[64,8192]{1,0:T(8,128)(2,1)}, u32[]{:S(2)}, u32[]{:S(2)}) collective-permute-start(bf16[64,8192]{1,0:T(8,128)(2,1)S(1)} %convolution_convert_fusion.1), channel_id=1, source_target_pairs={{0,1},{1,0},{2,3},{3,2},{4,5},{5,4},{6,7},{7,6},{8,9},{9,8},{10,11... | collective-permute-start | bytes 3145736 | tf_op jit(solution)/shard_map/ppermute | solution.py:34
  292.7 31.8 %copy-start.2 = (f32[128,128]{1,0:T(8,128)S(1)}, f32[128,128]{1,0:T(8,128)}, u32[]{:S(2)}) copy-start(f32[128,128]{1,0:T(8,128)} %all-reduce.6.cloned.1.call-done) | copy-start | bytes 196612
  340.8 26.2 %collective-permute-start.3 = (bf16[64,8192]{1,0:T(8,128)(2,1)S(1)}, bf16[64,8192]{1,0:T(8,128)(2,1)S(1)}, u32[]{:S(2)}, u32[]{:S(2)}) collective-permute-start(bf16[64,8192]{1,0:T(8,128)(2,1)S(1)} %convolution_convert_fusion.2), channel_id=1, source_target_pairs={{0,2},{2,0},{1,3},{3,1},{4,6},{6,4},{5,7},{7,5},{8,10},{10,8},{9,1... | collective-permute-start | bytes 3145736 | tf_op jit(solution)/shard_map/ppermute | solution.py:34
  344.2 24.2 %copy-start.10 = (bf16[64,8192]{1,0:T(8,128)(2,1)}, bf16[64,8192]{1,0:T(8,128)(2,1)S(1)}, u32[]{:S(2)}) copy-start(bf16[64,8192]{1,0:T(8,128)(2,1)S(1)} %convolution_convert_fusion) | copy-start | bytes 3145732
  344.2 42.3 %collective-permute-start.5 = (bf16[64,8192]{1,0:T(8,128)(2,1)S(1)}, bf16[64,8192]{1,0:T(8,128)(2,1)}, u32[]{:S(2)}, u32[]{:S(2)}) collective-permute-start(bf16[64,8192]{1,0:T(8,128)(2,1)S(1)} %convolution_convert_fusion), channel_id=1, source_target_pairs={{0,2},{2,0},{1,3},{3,1},{4,6},{6,4},{5,7},{7,5},{8,10},{10,8},{9,1... | collective-permute-start | bytes 3145736 | tf_op jit(solution)/shard_map/ppermute | solution.py:34
  437.0 32.0 %copy-start.3 = (f32[128,128]{1,0:T(8,128)S(1)}, f32[128,128]{1,0:T(8,128)}, u32[]{:S(2)}) copy-start(f32[128,128]{1,0:T(8,128)} %all-reduce.8.cloned.1.call-done) | copy-start | bytes 196612
  482.9 1.2 copy-start.9
Sparse Core Ops, SparseCore 0:
  100.4 70.8 all-reduce.3
  224.2 68.4 all-reduce.5
  368.6 68.3 all-reduce.7
where the time goes:
time: 501 us; the launch traced here: 492 us
  waiting for transfers between devices  227 us (45%)
  other arithmetic  123 us (25%)
  matrix products  59.7 us (12%)
  local copies, waits for them, and re-layouts  59.3 us (12%)
  between operations  15.1 us (3%)
  starting transfers between devices  8.93 us (2%)
    psum x3, waiting for transfers between devices, coefficients_of(): return compress(lax.psum(local_gram, 'space'))  184 us
    another operation x27, other arithmetic, compress(): jnp.linalg.cholesky(inner_gram / (scales[:, None] * scales[None, :]))  58.9 us
    another operation x18, other arithmetic, compress(): lax.linalg.triangular_solve(factor_lower, normed, left_side=False, lower=...  49.9 us
    ppermute x4, waiting for transfers between devices, partner(): return lax.ppermute(block, axis, route)  42.8 us
    dot_general x1, matrix products, weigh_rows(): jnp.einsum('cbkq,kqbr->cbr', picked, factor, preferred_element_type=jnp.f...  29.2 us
    gather x1, local copies, waits for them, and re-layouts, weigh_rows(): picked = jnp.take(blocks, local_index, axis=1)  22.8 us
    reshape x1, local copies, waits for them, and re-layouts, weigh_rows(): factor = mass_factor.reshape(NEIGHBOURS, BLOCK_DOFS, -1, BLOCK_DOFS)  20.9 us
  transfers between devices with their start and end apart: 9, of which 6 were waited for; matrix products, arithmetic and copies ran while one was open for 16% of the time, Pallas kernels for 0%

commit v1 on v0

v1 whole, which is shorter than its diff:
```python
import functools
import jax
import jax.numpy as jnp
from jax import lax
from jax.experimental import pallas as pl
from jax.experimental.pallas import tpu as pltpu
from jax.sharding import PartitionSpec as P

BLOCK_DOFS = 64
RANK = 64
REACH = 8
SUBSPACE_STEPS = 3
PANEL = 8
TILE = 128
F32 = jnp.float32
BF16 = jnp.bfloat16
HIGHEST = lax.Precision.HIGHEST
NT = (((1,), (1,)), ((), ()))


def halo(block, axis, width):
    count = lax.axis_size(axis)
    forward = [(i, i + 1) for i in range(count - 1)]
    backward = [(target, source) for source, target in forward]
    low = lax.ppermute(block[:, block.shape[1] - width:], axis, forward)
    high = lax.ppermute(block[:, :width], axis, backward)
    return low, high


def total(block, axis):
    count = lax.axis_size(axis)
    if count & (count - 1):
        return lax.psum(block, axis)
    step = 1
    while step < count:
        block = block + lax.ppermute(block, axis, [(i, i ^ step) for i in range(count)])
        step *= 2
    return block


def partner(block, axis, bit):
    count = lax.axis_size(axis)
    route = []
    for low in range(count):
        high = low | 1 << bit
        if high != low and high < count:
            route += [(low, high), (high, low)]
    return lax.ppermute(block, axis, route)


def weigh_kernel(spots, prior_ref, snap_ref, low_ref, high_ref, factor_ref, weighted_ref, gram_ref, bank):
    step = pl.program_id(0)
    rows, width = prior_ref.shape
    edge = low_ref.shape[1]
    neighbours, block, chunk = factor_ref.shape
    columns = bank.shape[0]
    whole = width + 2 * edge

    @pl.when(step == 0)
    def _():
        bank[:, 0:edge] = low_ref[...]
        bank[:rows, edge:edge + width] = prior_ref[...]
        bank[rows:, edge:edge + width] = snap_ref[...]
        bank[:, edge + width:whole] = high_ref[...]
        bank[:, whole + TILE:2 * whole] = bank[:, block:whole - block]
        bank[:, whole:whole + TILE] = bank[:, 0:TILE]
        bank[:, whole + block:whole + TILE] = bank[:, 0:block]
        bank[:, 2 * whole:2 * whole + TILE] = bank[:, whole - TILE:whole]
        bank[:, 2 * whole:2 * whole + block] = bank[:, whole - block:whole]
        gram_ref[...] = jnp.zeros_like(gram_ref)

    lower = lax.broadcasted_iota(jnp.int32, (columns, TILE), 1) < block
    pieces = []
    for tile in range(chunk // TILE):
        results = []
        for side in range(2):
            row = step * (chunk // block) + tile * 2 + side
            parts = []
            for k in range(neighbours):
                spot = spots[row * neighbours + k]
                parts.append(bank[:, pl.ds(pl.multiple_of(spot * TILE, TILE), TILE)])
            joined = [jnp.where(lower, parts[k], parts[k + 1]) for k in range(0, neighbours - 1, 2)]
            if neighbours % 2:
                joined.append(parts[-1][:, :block])
            results.append(jnp.concatenate(joined, axis=1))
        left = jnp.concatenate(results, axis=0)
        right = factor_ref[:, :, tile * TILE:(tile + 1) * TILE].reshape(neighbours * block, TILE)
        product = jnp.dot(left, right, preferred_element_type=F32)
        pieces.append(jnp.where(lower, product[:columns], product[columns:]).astype(BF16))
    weighted = jnp.concatenate(pieces, axis=1)
    weighted_ref[...] = weighted
    gram_ref[...] += lax.dot_general(weighted, weighted, NT, preferred_element_type=F32)


def weigh(prior, snapshots, low, high, factor, neighbours):
    rows, width = prior.shape
    columns = 2 * rows
    count, block, _ = factor.shape
    edge = low.shape[1]
    whole = width + 2 * edge
    local = neighbours - (lax.axis_index("space") * (width // block) - edge // block)
    half, odd = local // 2, local % 2
    side = jnp.arange(count, dtype=jnp.int32)[None, :] % 2
    spots = half + jnp.where(side == 0, odd * (whole // TILE + 1), (1 - odd) * (whole // TILE))
    chunk = min(width, 1024)
    full = lambda i, s: (0, 0)
    return pl.pallas_call(
        weigh_kernel,
        out_shape=(
            jax.ShapeDtypeStruct((columns, width), BF16),
            jax.ShapeDtypeStruct((columns, columns), F32),
        ),
        grid_spec=pltpu.PrefetchScalarGridSpec(
            num_scalar_prefetch=1,
            grid=(width // chunk,),
            in_specs=[
                pl.BlockSpec((rows, width), full),
                pl.BlockSpec((rows, width), full),
                pl.BlockSpec((columns, edge), full),
                pl.BlockSpec((columns, edge), full),
                pl.BlockSpec((count, block, chunk), lambda i, s: (0, 0, i)),
            ],
            out_specs=(
                pl.BlockSpec((columns, chunk), lambda i, s: (0, i)),
                pl.BlockSpec((columns, columns), full),
            ),
            scratch_shapes=[pltpu.VMEM((columns, 2 * whole + TILE), BF16)],
        ),
        compiler_params=pltpu.CompilerParams(vmem_limit_bytes=40 * 1024 * 1024),
        name="weigh",
    )(spots.reshape(-1).astype(jnp.int32), prior, snapshots, low, high, factor)


def lanes_of(group, column):
    return jnp.broadcast_to(group[:, column:column + 1], (group.shape[0], TILE))


def row_of(group, row):
    return jnp.broadcast_to(group[row:row + 1, :], group.shape)


def eliminate(left, right, solved):
    groups = left.shape[0]
    sub = lax.broadcasted_iota(jnp.int32, (PANEL, TILE), 0)

    def panel(p, _):
        pivot, image = left[p], right[p]
        cols = [lanes_of(pivot, s) for s in range(PANEL)]
        d = [[row_of(cols[c], r) if r >= c else None for c in range(PANEL)] for r in range(PANEL)]
        rows_a = [row_of(pivot, r) for r in range(PANEL)]
        rows_n = [row_of(image, r) for r in range(PANEL)]
        inverse = []
        for s in range(PANEL):
            inverse.append(1.0 / d[s][s])
            for r in range(s + 1, PANEL):
                m = d[r][s] * inverse[s]
                for c in range(s + 1, r + 1):
                    d[r][c] = d[r][c] - m * d[c][s]
                rows_a[r] = rows_a[r] - m * rows_a[s]
                rows_n[r] = rows_n[r] - m * rows_n[s]
        for q in range(groups):
            fresh_a, fresh_n = left[q], right[q]
            work = [lanes_of(fresh_a, s) for s in range(PANEL)]
            for s in range(PANEL):
                factor = work[s] * inverse[s]
                for c in range(s + 1, PANEL):
                    work[c] = work[c] - factor * d[c][s]
                fresh_a = fresh_a - factor * rows_a[s]
                fresh_n = fresh_n - factor * rows_n[s]
            left[q] = pltpu.roll(fresh_a, TILE - PANEL, 1)
            right[q] = fresh_n
        merged = rows_n[0] * lax.rsqrt(d[0][0])
        for r in range(1, PANEL):
            merged = jnp.where(sub == r, rows_n[r] * lax.rsqrt(d[r][r]), merged)
        solved[p] = merged
        return 0

    lax.fori_loop(0, groups, panel, 0)


def compress_kernel(gram_ref, out_ref, left, right, solved):
    gram = gram_ref[...]

    product = gram[:RANK]
    for _ in range(SUBSPACE_STEPS):
        image = jnp.dot(product, gram, precision=HIGHEST, preferred_element_type=F32)
        scale = 1.0 / jnp.sqrt(jnp.sum(product * image, axis=1, keepdims=True))
        normed = product * scale
        image = jnp.concatenate([image * scale, jnp.zeros((TILE - RANK, TILE), F32)], axis=0)
        inner = lax.dot_general(normed, image, NT, precision=HIGHEST, preferred_element_type=F32)
        left[...] = inner.reshape(left.shape)
        right[...] = normed.reshape(right.shape)
        eliminate(left, right, solved)
        weights = solved[...].reshape(RANK, TILE)
        product = jnp.dot(weights, gram, precision=HIGHEST, preferred_element_type=F32)
    lengths = jnp.sqrt(jnp.sum(product * product, axis=1, keepdims=True) + 1e-06)
    out_ref[...] = (solved[...].reshape(RANK, TILE) * lengths).astype(BF16)


def compress(gram):
    order = gram.shape[0]
    return pl.pallas_call(
        compress_kernel,
        out_shape=jax.ShapeDtypeStruct((RANK, order), BF16),
        scratch_shapes=[pltpu.VMEM((RANK // PANEL, PANEL, TILE), F32)] * 3,
        compiler_params=pltpu.CompilerParams(vmem_limit_bytes=16 * 1024 * 1024),
        name="compress",
    )(gram)


def combine(coefficients, rows):
    return jnp.dot(coefficients, rows, preferred_element_type=F32).astype(BF16)


def ordered(upper_half, own_rows, partner_rows):
    lower_part = jnp.where(upper_half, partner_rows, own_rows)
    upper_part = jnp.where(upper_half, own_rows, partner_rows)
    return jnp.concatenate([lower_part, upper_part], axis=0)


def shards(snapshots, prior_basis, mass_factor, neighbours):
    stacked = jnp.concatenate([prior_basis, snapshots], axis=0)
    low, high = halo(stacked, "space", REACH * BLOCK_DOFS)
    weighted, gram = weigh(prior_basis, snapshots, low, high, mass_factor, neighbours)
    coefficients = compress(total(gram, "space"))
    basis, weighted_basis = combine(coefficients, stacked), combine(coefficients, weighted)
    member = lax.axis_index("tm")
    for level_bit in range(lax.axis_size("tm").bit_length() - 1):
        upper_half = member // (1 << level_bit) % 2 == 1
        weighted = ordered(upper_half, weighted_basis, partner(weighted_basis, "tm", level_bit))
        stacked = ordered(upper_half, basis, partner(basis, "tm", level_bit))
        gram = lax.dot_general(weighted, weighted, NT, preferred_element_type=F32)
        coefficients = compress(total(gram, "space"))
        basis, weighted_basis = combine(coefficients, stacked), combine(coefficients, weighted)
    share_width = basis.shape[1] // lax.axis_size("tm")
    basis_share = lax.dynamic_slice_in_dim(basis, member * share_width, share_width, 1)
    weighted_share = lax.dynamic_slice_in_dim(weighted_basis, member * share_width, share_width, 1)
    return (basis_share, weighted_share)


def solution(mesh):
    return jax.shard_map(
        shards,
        mesh=mesh,
        in_specs=(P("tm", "space"), P("tm", "space"), P(None, None, "space"), P("space", None)),
        out_specs=(P(None, ("space", "tm")), P(None, ("space", "tm"))),
        check_vma=False,
    )
```

time: 501 us -> 144 us (0.29); the launches traced: 492 us -> 144 us
  waiting for transfers between devices: 227 us -> 55.2 us
  other arithmetic: 123 us -> 3.49 us
  matrix products: 59.7 us -> 6.22 us
  local copies, waits for them, and re-layouts: 59.3 us -> 6.27 us
  Pallas kernels: 0 us -> 40.9 us
  starting transfers between devices: 8.93 us -> 30.8 us
  between operations: 15.1 us -> 0.9 us
    psum x3 -> x0, waiting for transfers between devices: 184 us -> none  [coefficients_of(): return compress(lax.psum(local_gram, 'space'))]
    another operation x45 -> x0, other arithmetic: 109 us -> none  [the longest x27 58.9 us: compress(): jnp.linalg.cholesky(inner_gram / (scales[:, None] * scales[None, :]))]
    dot_general x40 -> x8, matrix products: 57.3 us -> 6.22 us  [the longest x6 4.81 us: combine(): return jnp.dot(coefficients, rows, preferred_element_type=F32).astype(BF16)]
    pallas_call x0 -> x4, Pallas kernels: none -> 40.9 us  [the longest x3 31.4 us: compress(): pl.pallas_call(compress_kernel, out_shape=jax.ShapeDtypeStruct((RANK, ord...]
    gather x10 -> x0, local copies, waits for them, and re-layouts: 30.1 us -> none  [the longest x1 22.8 us: weigh_rows(): picked = jnp.take(blocks, local_index, axis=1)]
    ppermute x2 -> x11, waiting for transfers between devices: 0.01 us -> 23.7 us  [the longest x9 19.6 us: total(): lax.ppermute(block, axis, [(i, i ^ step) for i in range(count)])]
    ppermute x2 -> x11, starting transfers between devices: 6.17 us -> 28 us  [the longest x9 21.2 us: total(): lax.ppermute(block, axis, [(i, i ^ step) for i in range(count)])]
    reshape x1, local copies, waits for them, and re-layouts: 20.9 us -> 0.2 us  [weigh(): spots.reshape(-1).astype(jnp.int32)]
  transfers between devices with their start and end apart: 9 -> 15, of which waited for: 6 -> 13; matrix products, arithmetic and copies ran while one was open for 16% -> 5% of each run, Pallas kernels for 0% -> 7%
where the time goes in v1:
time: 144 us
  waiting for transfers between devices  55.2 us (38%)
  Pallas kernels  40.9 us (28%)
  starting transfers between devices  30.8 us (21%)
  local copies, waits for them, and re-layouts  6.27 us (4%)
  matrix products  6.22 us (4%)
  other arithmetic  3.49 us (2%)
    ppermute x4, waiting for transfers between devices, partner(): return lax.ppermute(block, axis, route)  31.5 us
    pallas_call x3, Pallas kernels, compress(): pl.pallas_call(compress_kernel, out_shape=jax.ShapeDtypeStruct((RANK, ord...  31.4 us
    ppermute x9, starting transfers between devices, total(): lax.ppermute(block, axis, [(i, i ^ step) for i in range(count)])  21.2 us
    ppermute x9, waiting for transfers between devices, total(): lax.ppermute(block, axis, [(i, i ^ step) for i in range(count)])  19.6 us
    pallas_call x1, Pallas kernels, weigh(): pl.pallas_call(weigh_kernel, out_shape=(jax.ShapeDtypeStruct((columns, wi...  9.5 us
    ppermute x1, starting transfers between devices, halo(): low = lax.ppermute(block[:, block.shape[1] - width:], axis, forward)  5.51 us
    unnamed x15, local copies, waits for them, and re-layouts  5.03 us
    dot_general x6, matrix products, combine(): return jnp.dot(coefficients, rows, preferred_element_type=F32).astype(BF16)  4.81 us
  transfers between devices with their start and end apart: 15, of which 13 were waited for; matrix products, arithmetic and copies ran while one was open for 5% of the time, Pallas kernels for 7%

profile of v1, /device:TPU:0, one launch (start us, length us, event | category | flops | bytes accessed | tf_op | source)
XLA Modules:
  0.0 143.7 jit_solution(16431870218330735578)
XLA Ops:
  0.7 1.4 %constant_dynamic-update-slice_fusion.1 = bf16[128,8192]{1,0:T(8,128)(2,1)S(1)} fusion(bf16[64,8192]{1,0:T(8,128)(2,1)} %prior_ref.1), kind=kLoop, calls=%fused_computation.27 | loop fusion | bytes 2097152
  2.4 1.3 collective-permute-start.1
  3.7 5.5 %collective-permute-start = (bf16[128,512]{1,0:T(8,128)(2,1)S(1)}, bf16[128,512]{1,0:T(8,128)(2,1)S(1)}, u32[]{:S(2)}, u32[]{:S(2)}) collective-permute-start(bf16[128,512]{1,0:T(8,128)(2,1)S(1)} %get-tuple-element.15), channel_id=1, source_target_pairs={{0,4},{4,8},{8,12},{12,16},{16,20},{20,24},{24,28},{1,5},{5,9},{9,... | collective-permute-start | bytes 393224 | tf_op jit(solution)/shard_map/ppermute | solution.py:25
  10.7 3.0 %collective-permute-done.low_ref = bf16[128,512]{1,0:T(8,128)(2,1)S(1)} collective-permute-done((bf16[128,512]{1,0:T(8,128)(2,1)S(1)}, bf16[128,512]{1,0:T(8,128)(2,1)S(1)}, u32[]{:S(2)}, u32[]{:S(2)}) %collective-permute-start) | collective-permute-done | bytes 131104 | tf_op jit(solution)/shard_map/ppermute | solution.py:25
  13.7 3.1 %copy-done = bf16[7,64,8192]{2,1,0:T(8,128)(2,1)S(1)} copy-done((bf16[7,64,8192]{2,1,0:T(8,128)(2,1)S(1)}, bf16[7,64,8192]{2,1,0:T(8,128)(2,1)}, u32[]{:S(2)}) %copy-start) | copy-done | bytes 7340056
  16.8 9.5 %weigh.1 = (bf16[128,8192]{1,0:T(8,128)(2,1)S(1)}, f32[128,128]{1,0:T(8,128)S(1)}) custom-call(s32[896]{0:T(1024)S(1)} %reshape.24.spots, bf16[64,8192]{1,0:T(8,128)(2,1)S(1)} %copy-done.1, bf16[64,8192]{1,0:T(8,128)(2,1)S(1)} %copy-done.2, bf16[128,512]{1,0:T(8,128)(2,1)S(1)} %collective-permute-done.low_ref, ...), custom_call_target="tpu_custom_call" | custom-call | tf_op jit(solution)/shard_map/weigh/pallas_call | solution.py:107
  26.3 2.6 %collective-permute-start.2 = (f32[128,128]{1,0:T(8,128)S(1)}, f32[128,128]{1,0:T(8,128)S(1)}, u32[]{:S(2)}, u32[]{:S(2)}) collective-permute-start(f32[128,128]{1,0:T(8,128)S(1)} %get-tuple-element.4), channel_id=1, source_target_pairs={{0,4},{4,0},{8,12},{12,8},{16,20},{20,16},{24,28},{28,24},{1,5},{5... | collective-permute-start | bytes 196616 | tf_op jit(solution)/shard_map/ppermute | solution.py:36
  28.9 2.3 %collective-permute-done.2 = f32[128,128]{1,0:T(8,128)S(1)} collective-permute-done((f32[128,128]{1,0:T(8,128)S(1)}, f32[128,128]{1,0:T(8,128)S(1)}, u32[]{:S(2)}, u32[]{:S(2)}) %collective-permute-start.2) | collective-permute-done | bytes 65568 | tf_op jit(solution)/shard_map/ppermute | solution.py:36
  31.2 2.3 %collective-permute-start.3 = (f32[128,128]{1,0:T(8,128)S(1)}, f32[128,128]{1,0:T(8,128)S(1)}, u32[]{:S(2)}, u32[]{:S(2)}) collective-permute-start(f32[128,128]{1,0:T(8,128)S(1)} %add.67), channel_id=1, source_target_pairs={{0,8},{4,12},{8,0},{12,4},{16,24},{20,28},{24,16},{28,20},{1,9},{5... | collective-permute-start | bytes 196616 | tf_op jit(solution)/shard_map/ppermute | solution.py:36
  33.5 2.2 %collective-permute-done.3 = f32[128,128]{1,0:T(8,128)S(1)} collective-permute-done((f32[128,128]{1,0:T(8,128)S(1)}, f32[128,128]{1,0:T(8,128)S(1)}, u32[]{:S(2)}, u32[]{:S(2)}) %collective-permute-start.3) | collective-permute-done | bytes 65568 | tf_op jit(solution)/shard_map/ppermute | solution.py:36
  35.8 3.4 %collective-permute-start.4 = (f32[128,128]{1,0:T(8,128)S(1)}, f32[128,128]{1,0:T(8,128)S(1)}, u32[]{:S(2)}, u32[]{:S(2)}) collective-permute-start(f32[128,128]{1,0:T(8,128)S(1)} %add.68), channel_id=1, source_target_pairs={{0,16},{4,20},{8,24},{12,28},{16,0},{20,4},{24,8},{28,12},{1,17},{... | collective-permute-start | bytes 196616 | tf_op jit(solution)/shard_map/ppermute | solution.py:36
  39.2 2.2 %collective-permute-done.4 = f32[128,128]{1,0:T(8,128)S(1)} collective-permute-done((f32[128,128]{1,0:T(8,128)S(1)}, f32[128,128]{1,0:T(8,128)S(1)}, u32[]{:S(2)}, u32[]{:S(2)}) %collective-permute-start.4) | collective-permute-done | bytes 65568 | tf_op jit(solution)/shard_map/ppermute | solution.py:36
  41.5 10.5 %compress.3 = bf16[64,128]{1,0:T(8,128)(2,1)S(1)} custom-call(f32[128,128]{1,0:T(8,128)S(1)} %add.69.gram_ref), custom_call_target="tpu_custom_call" | custom-call | tf_op jit(solution)/shard_map/compress/pallas_call | solution.py:202
  51.9 1.4 convolution_convert_fusion.3
  54.4 2.0 %collective-permute-done.5 = bf16[64,8192]{1,0:T(8,128)(2,1)} collective-permute-done((bf16[64,8192]{1,0:T(8,128)(2,1)}, bf16[64,8192]{1,0:T(8,128)(2,1)}, u32[]{:S(2)}, u32[]{:S(2)}) %collective-permute-start.5) | collective-permute-done | bytes 1048608 | tf_op jit(solution)/shard_map/ppermute | solution.py:48
  56.4 1.7 %broadcast_select_fusion.3 = (bf16[64,8192]{1,0:T(8,128)(2,1)S(1)}, bf16[64,8192]{1,0:T(8,128)(2,1)S(1)}) fusion(bf16[64,8192]{1,0:T(8,128)(2,1)} %collective-permute-done.5, bf16[64,8192]{1,0:T(8,128)(2,1)} %convolution_convert_fusion.3, pred[]{:T(512)S(6)} %eq.22), kind=kLoop, calls=%fused_computation.19 | loop fusion | flops 1048576 | bytes 4194305 | tf_op jit(solution)/shard_map/jit(_where)/select_n | solution.py:216
  60.3 3.0 %collective-permute-done.6 = f32[128,128]{1,0:T(8,128)S(1)} collective-permute-done((f32[128,128]{1,0:T(8,128)S(1)}, f32[128,128]{1,0:T(8,128)S(1)}, u32[]{:S(2)}, u32[]{:S(2)}) %collective-permute-start.6) | collective-permute-done | bytes 65568 | tf_op jit(solution)/shard_map/ppermute | solution.py:36
  63.3 2.1 %collective-permute-start.7 = (f32[128,128]{1,0:T(8,128)S(1)}, f32[128,128]{1,0:T(8,128)S(1)}, u32[]{:S(2)}, u32[]{:S(2)}) collective-permute-start(f32[128,128]{1,0:T(8,128)S(1)} %add.70), channel_id=1, source_target_pairs={{0,8},{4,12},{8,0},{12,4},{16,24},{20,28},{24,16},{28,20},{1,9},{5... | collective-permute-start | bytes 196616 | tf_op jit(solution)/shard_map/ppermute | solution.py:36
  65.4 2.3 %collective-permute-done.7 = f32[128,128]{1,0:T(8,128)S(1)} collective-permute-done((f32[128,128]{1,0:T(8,128)S(1)}, f32[128,128]{1,0:T(8,128)S(1)}, u32[]{:S(2)}, u32[]{:S(2)}) %collective-permute-start.7) | collective-permute-done | bytes 65568 | tf_op jit(solution)/shard_map/ppermute | solution.py:36
  67.7 3.1 %collective-permute-start.8 = (f32[128,128]{1,0:T(8,128)S(1)}, f32[128,128]{1,0:T(8,128)S(1)}, u32[]{:S(2)}, u32[]{:S(2)}) collective-permute-start(f32[128,128]{1,0:T(8,128)S(1)} %add.71), channel_id=1, source_target_pairs={{0,16},{4,20},{8,24},{12,28},{16,0},{20,4},{24,8},{28,12},{1,17},{... | collective-permute-start | bytes 196616 | tf_op jit(solution)/shard_map/ppermute | solution.py:36
  70.8 2.2 %collective-permute-done.8 = f32[128,128]{1,0:T(8,128)S(1)} collective-permute-done((f32[128,128]{1,0:T(8,128)S(1)}, f32[128,128]{1,0:T(8,128)S(1)}, u32[]{:S(2)}, u32[]{:S(2)}) %collective-permute-start.8) | collective-permute-done | bytes 65568 | tf_op jit(solution)/shard_map/ppermute | solution.py:36
  73.1 10.5 %compress.4 = bf16[64,128]{1,0:T(8,128)(2,1)S(1)} custom-call(f32[128,128]{1,0:T(8,128)S(1)} %add.72.gram_ref), custom_call_target="tpu_custom_call" | custom-call | tf_op jit(solution)/shard_map/compress/pallas_call | solution.py:202
  83.5 1.7 %convolution_convert_fusion.2 = bf16[64,8192]{1,0:T(8,128)(2,1)S(1)} fusion(bf16[64,128]{1,0:T(8,128)(2,1)S(1)} %compress.4, bf16[64,8192]{1,0:T(8,128)(2,1)} %copy-done.5, bf16[64,8192]{1,0:T(8,128)(2,1)S(1)} %get-tuple-element.12), kind=kOutput, calls=%fused_computation.2 | convolution fusion | flops 138936320 | bytes 3162112 | tf_op jit(solution)/shard_map/dot_general | solution.py:212
  85.2 1.6 %collective-permute-start.9 = (bf16[64,8192]{1,0:T(8,128)(2,1)S(1)}, bf16[64,8192]{1,0:T(8,128)(2,1)S(1)}, u32[]{:S(2)}, u32[]{:S(2)}) collective-permute-start(bf16[64,8192]{1,0:T(8,128)(2,1)S(1)} %convolution_convert_fusion.2), channel_id=1, source_target_pairs={{0,2},{2,0},{1,3},{3,1},{4,6},{6,4},{5,7},{7,5},{8,10},{10,8},{9,1... | collective-permute-start | bytes 3145736 | tf_op jit(solution)/shard_map/ppermute | solution.py:48
  87.9 23.4 %collective-permute-done.9 = bf16[64,8192]{1,0:T(8,128)(2,1)S(1)} collective-permute-done((bf16[64,8192]{1,0:T(8,128)(2,1)S(1)}, bf16[64,8192]{1,0:T(8,128)(2,1)S(1)}, u32[]{:S(2)}, u32[]{:S(2)}) %collective-permute-start.9) | collective-permute-done | bytes 1048608 | tf_op jit(solution)/shard_map/ppermute | solution.py:48
  113.4 3.1 %collective-permute-done.10 = f32[128,128]{1,0:T(8,128)S(1)} collective-permute-done((f32[128,128]{1,0:T(8,128)S(1)}, f32[128,128]{1,0:T(8,128)S(1)}, u32[]{:S(2)}, u32[]{:S(2)}) %collective-permute-start.10) | collective-permute-done | bytes 65568 | tf_op jit(solution)/shard_map/ppermute | solution.py:36
  116.6 2.1 %collective-permute-start.11 = (f32[128,128]{1,0:T(8,128)S(1)}, f32[128,128]{1,0:T(8,128)S(1)}, u32[]{:S(2)}, u32[]{:S(2)}) collective-permute-start(f32[128,128]{1,0:T(8,128)S(1)} %add.73), channel_id=1, source_target_pairs={{0,8},{4,12},{8,0},{12,4},{16,24},{20,28},{24,16},{28,20},{1,9},{5... | collective-permute-start | bytes 196616 | tf_op jit(solution)/shard_map/ppermute | solution.py:36
  118.7 2.2 %collective-permute-done.11 = f32[128,128]{1,0:T(8,128)S(1)} collective-permute-done((f32[128,128]{1,0:T(8,128)S(1)}, f32[128,128]{1,0:T(8,128)S(1)}, u32[]{:S(2)}, u32[]{:S(2)}) %collective-permute-start.11) | collective-permute-done | bytes 65568 | tf_op jit(solution)/shard_map/ppermute | solution.py:36
  120.9 3.1 %collective-permute-start.12 = (f32[128,128]{1,0:T(8,128)S(1)}, f32[128,128]{1,0:T(8,128)S(1)}, u32[]{:S(2)}, u32[]{:S(2)}) collective-permute-start(f32[128,128]{1,0:T(8,128)S(1)} %add.74), channel_id=1, source_target_pairs={{0,16},{4,20},{8,24},{12,28},{16,0},{20,4},{24,8},{28,12},{1,17},{... | collective-permute-start | bytes 196616 | tf_op jit(solution)/shard_map/ppermute | solution.py:36
  124.0 6.1 %collective-permute-done.14 = bf16[64,8192]{1,0:T(8,128)(2,1)} collective-permute-done((bf16[64,8192]{1,0:T(8,128)(2,1)S(1)}, bf16[64,8192]{1,0:T(8,128)(2,1)}, u32[]{:S(2)}, u32[]{:S(2)}) %collective-permute-start.14) | collective-permute-done | bytes 1048608 | tf_op jit(solution)/shard_map/ppermute | solution.py:48
  130.2 1.4 broadcast_select_fusion.5
  131.5 10.5 %compress.5 = bf16[64,128]{1,0:T(8,128)(2,1)S(1)} custom-call(f32[128,128]{1,0:T(8,128)S(1)} %add.75.gram_ref), custom_call_target="tpu_custom_call" | custom-call | tf_op jit(solution)/shard_map/compress/pallas_call | solution.py:202
  (45 shorter events, 10.1 us)
Async XLA Ops:
  0.6 13.1 %copy-start.1 = (bf16[64,8192]{1,0:T(8,128)(2,1)S(1)}, bf16[64,8192]{1,0:T(8,128)(2,1)}, u32[]{:S(2)}) copy-start(bf16[64,8192]{1,0:T(8,128)(2,1)} %prior_ref.1) | copy-start | bytes 3145732
  0.6 1.6 %copy-start.2 = (bf16[64,8192]{1,0:T(8,128)(2,1)S(1)}, bf16[64,8192]{1,0:T(8,128)(2,1)}, u32[]{:S(2)}) copy-start(bf16[64,8192]{1,0:T(8,128)(2,1)} %snap_ref.1) | copy-start | bytes 3145732
  0.6 8.6 %copy-start.6 = (s32[128,7]{0,1:T(8,128)S(1)}, s32[128,7]{0,1:T(8,128)}, u32[]{:S(2)}) copy-start(s32[128,7]{0,1:T(8,128)} %param.7) | copy-start | bytes 10756
  2.3 1.3 copy-start.3
  2.4 8.4 %collective-permute-start.1 = (bf16[128,512]{1,0:T(8,128)(2,1)S(1)}, bf16[128,512]{1,0:T(8,128)(2,1)S(1)}, u32[]{:S(2)}, u32[]{:S(2)}) collective-permute-start(bf16[128,512]{1,0:T(8,128)(2,1)S(1)} %get-tuple-element.14), channel_id=1, source_target_pairs={{4,0},{8,4},{12,8},{16,12},{20,16},{24,20},{28,24},{5,1},{9,5},{13... | collective-permute-start | bytes 393224 | tf_op jit(solution)/shard_map/ppermute | solution.py:26
  3.7 10.0 %collective-permute-start = (bf16[128,512]{1,0:T(8,128)(2,1)S(1)}, bf16[128,512]{1,0:T(8,128)(2,1)S(1)}, u32[]{:S(2)}, u32[]{:S(2)}) collective-permute-start(bf16[128,512]{1,0:T(8,128)(2,1)S(1)} %get-tuple-element.15), channel_id=1, source_target_pairs={{0,4},{4,8},{8,12},{12,16},{16,20},{20,24},{24,28},{1,5},{5,9},{9,... | collective-permute-start | bytes 393224 | tf_op jit(solution)/shard_map/ppermute | solution.py:25
  13.7 3.1 %copy-start = (bf16[7,64,8192]{2,1,0:T(8,128)(2,1)S(1)}, bf16[7,64,8192]{2,1,0:T(8,128)(2,1)}, u32[]{:S(2)}) copy-start(bf16[7,64,8192]{2,1,0:T(8,128)(2,1)} %factor_ref.1) | copy-start | bytes 22020100
  26.3 27.0 %copy-start.4 = (bf16[128,8192]{1,0:T(8,128)(2,1)S(1)}, bf16[128,8192]{1,0:T(8,128)(2,1)}, u32[]{:S(2)}) copy-start(bf16[128,8192]{1,0:T(8,128)(2,1)} %copy-done.3) | copy-start | bytes 6291460
  26.3 4.8 %collective-permute-start.2 = (f32[128,128]{1,0:T(8,128)S(1)}, f32[128,128]{1,0:T(8,128)S(1)}, u32[]{:S(2)}, u32[]{:S(2)}) collective-permute-start(f32[128,128]{1,0:T(8,128)S(1)} %get-tuple-element.4), channel_id=1, source_target_pairs={{0,4},{4,0},{8,12},{12,8},{16,20},{20,16},{24,28},{28,24},{1,5},{5... | collective-permute-start | bytes 196616 | tf_op jit(solution)/shard_map/ppermute | solution.py:36
  31.2 4.6 %collective-permute-start.3 = (f32[128,128]{1,0:T(8,128)S(1)}, f32[128,128]{1,0:T(8,128)S(1)}, u32[]{:S(2)}, u32[]{:S(2)}) collective-permute-start(f32[128,128]{1,0:T(8,128)S(1)} %add.67), channel_id=1, source_target_pairs={{0,8},{4,12},{8,0},{12,4},{16,24},{20,28},{24,16},{28,20},{1,9},{5... | collective-permute-start | bytes 196616 | tf_op jit(solution)/shard_map/ppermute | solution.py:36
  35.8 5.7 %collective-permute-start.4 = (f32[128,128]{1,0:T(8,128)S(1)}, f32[128,128]{1,0:T(8,128)S(1)}, u32[]{:S(2)}, u32[]{:S(2)}) collective-permute-start(f32[128,128]{1,0:T(8,128)S(1)} %add.68), channel_id=1, source_target_pairs={{0,16},{4,20},{8,24},{12,28},{16,0},{20,4},{24,8},{28,12},{1,17},{... | collective-permute-start | bytes 196616 | tf_op jit(solution)/shard_map/ppermute | solution.py:36
  53.4 3.0 %collective-permute-start.5 = (bf16[64,8192]{1,0:T(8,128)(2,1)}, bf16[64,8192]{1,0:T(8,128)(2,1)}, u32[]{:S(2)}, u32[]{:S(2)}) collective-permute-start(bf16[64,8192]{1,0:T(8,128)(2,1)} %convolution_convert_fusion.3), channel_id=1, source_target_pairs={{0,1},{1,0},{2,3},{3,2},{4,5},{5,4},{6,7},{7,6},{8,9},{9,8},{10,11... | collective-permute-start | bytes 3145736 | tf_op jit(solution)/shard_map/ppermute | solution.py:48
  53.8 33.0 %collective-permute-start.13 = (bf16[64,8192]{1,0:T(8,128)(2,1)S(1)}, bf16[64,8192]{1,0:T(8,128)(2,1)S(1)}, u32[]{:S(2)}, u32[]{:S(2)}) collective-permute-start(bf16[64,8192]{1,0:T(8,128)(2,1)S(1)} %convolution_convert_fusion.1), channel_id=1, source_target_pairs={{0,1},{1,0},{2,3},{3,2},{4,5},{5,4},{6,7},{7,6},{8,9},{9,8},{10,11... | collective-permute-start | bytes 3145736 | tf_op jit(solution)/shard_map/ppermute | solution.py:48
  58.0 1.0 copy-start.5
  59.1 4.3 %collective-permute-start.6 = (f32[128,128]{1,0:T(8,128)S(1)}, f32[128,128]{1,0:T(8,128)S(1)}, u32[]{:S(2)}, u32[]{:S(2)}) collective-permute-start(f32[128,128]{1,0:T(8,128)S(1)} %fusion.9), channel_id=1, source_target_pairs={{0,4},{4,0},{8,12},{12,8},{16,20},{20,16},{24,28},{28,24},{1,5},{5... | collective-permute-start | bytes 196616 | tf_op jit(solution)/shard_map/ppermute | solution.py:36
  63.3 4.3 %collective-permute-start.7 = (f32[128,128]{1,0:T(8,128)S(1)}, f32[128,128]{1,0:T(8,128)S(1)}, u32[]{:S(2)}, u32[]{:S(2)}) collective-permute-start(f32[128,128]{1,0:T(8,128)S(1)} %add.70), channel_id=1, source_target_pairs={{0,8},{4,12},{8,0},{12,4},{16,24},{20,28},{24,16},{28,20},{1,9},{5... | collective-permute-start | bytes 196616 | tf_op jit(solution)/shard_map/ppermute | solution.py:36
  67.7 5.4 %collective-permute-start.8 = (f32[128,128]{1,0:T(8,128)S(1)}, f32[128,128]{1,0:T(8,128)S(1)}, u32[]{:S(2)}, u32[]{:S(2)}) collective-permute-start(f32[128,128]{1,0:T(8,128)S(1)} %add.71), channel_id=1, source_target_pairs={{0,16},{4,20},{8,24},{12,28},{16,0},{20,4},{24,8},{28,12},{1,17},{... | collective-permute-start | bytes 196616 | tf_op jit(solution)/shard_map/ppermute | solution.py:36
  85.2 26.2 %collective-permute-start.9 = (bf16[64,8192]{1,0:T(8,128)(2,1)S(1)}, bf16[64,8192]{1,0:T(8,128)(2,1)S(1)}, u32[]{:S(2)}, u32[]{:S(2)}) collective-permute-start(bf16[64,8192]{1,0:T(8,128)(2,1)S(1)} %convolution_convert_fusion.2), channel_id=1, source_target_pairs={{0,2},{2,0},{1,3},{3,1},{4,6},{6,4},{5,7},{7,5},{8,10},{10,8},{9,1... | collective-permute-start | bytes 3145736 | tf_op jit(solution)/shard_map/ppermute | solution.py:48
  87.3 42.8 %collective-permute-start.14 = (bf16[64,8192]{1,0:T(8,128)(2,1)S(1)}, bf16[64,8192]{1,0:T(8,128)(2,1)}, u32[]{:S(2)}, u32[]{:S(2)}) collective-permute-start(bf16[64,8192]{1,0:T(8,128)(2,1)S(1)} %convolution_convert_fusion), channel_id=1, source_target_pairs={{0,2},{2,0},{1,3},{3,1},{4,6},{6,4},{5,7},{7,5},{8,10},{10,8},{9,1... | collective-permute-start | bytes 3145736 | tf_op jit(solution)/shard_map/ppermute | solution.py:48
  112.2 4.3 %collective-permute-start.10 = (f32[128,128]{1,0:T(8,128)S(1)}, f32[128,128]{1,0:T(8,128)S(1)}, u32[]{:S(2)}, u32[]{:S(2)}) collective-permute-start(f32[128,128]{1,0:T(8,128)S(1)} %fusion.8), channel_id=1, source_target_pairs={{0,4},{4,0},{8,12},{12,8},{16,20},{20,16},{24,28},{28,24},{1,5},{5... | collective-permute-start | bytes 196616 | tf_op jit(solution)/shard_map/ppermute | solution.py:36
  116.6 4.3 %collective-permute-start.11 = (f32[128,128]{1,0:T(8,128)S(1)}, f32[128,128]{1,0:T(8,128)S(1)}, u32[]{:S(2)}, u32[]{:S(2)}) collective-permute-start(f32[128,128]{1,0:T(8,128)S(1)} %add.73), channel_id=1, source_target_pairs={{0,8},{4,12},{8,0},{12,4},{16,24},{20,28},{24,16},{28,20},{1,9},{5... | collective-permute-start | bytes 196616 | tf_op jit(solution)/shard_map/ppermute | solution.py:36
  120.9 10.6 %collective-permute-start.12 = (f32[128,128]{1,0:T(8,128)S(1)}, f32[128,128]{1,0:T(8,128)S(1)}, u32[]{:S(2)}, u32[]{:S(2)}) collective-permute-start(f32[128,128]{1,0:T(8,128)S(1)} %add.74), channel_id=1, source_target_pairs={{0,16},{4,20},{8,24},{12,28},{16,0},{20,4},{24,8},{28,12},{1,17},{... | collective-permute-start | bytes 196616 | tf_op jit(solution)/shard_map/ppermute | solution.py:36

commit v2 on v1

--- a/solution.py
+++ b/solution.py
@@ -27,25 +27,17 @@
     return low, high
 
 
-def total(block, axis):
-    count = lax.axis_size(axis)
-    if count & (count - 1):
-        return lax.psum(block, axis)
+def swapped(block, axis, step):
+    return lax.ppermute(block, axis, [(i, i ^ step) for i in range(lax.axis_size(axis))])
+
+
+def total(block, axis, limit=None):
+    count = limit or lax.axis_size(axis)
     step = 1
     while step < count:
-        block = block + lax.ppermute(block, axis, [(i, i ^ step) for i in range(count)])
+        block = block + swapped(block, axis, step)
         step *= 2
     return block
-
-
-def partner(block, axis, bit):
-    count = lax.axis_size(axis)
-    route = []
-    for low in range(count):
-        high = low | 1 << bit
-        if high != low and high < count:
-            route += [(low, high), (high, low)]
-    return lax.ppermute(block, axis, route)
 
 
 def weigh_kernel(spots, prior_ref, snap_ref, low_ref, high_ref, factor_ref, weighted_ref, gram_ref, bank):
@@ -178,9 +170,7 @@
     lax.fori_loop(0, groups, panel, 0)
 
 
-def compress_kernel(gram_ref, out_ref, left, right, solved):
-    gram = gram_ref[...]
-
+def reduce_gram(gram, left, right, solved):
     product = gram[:RANK]
     for _ in range(SUBSPACE_STEPS):
         image = jnp.dot(product, gram, precision=HIGHEST, preferred_element_type=F32)
@@ -194,22 +184,54 @@
         weights = solved[...].reshape(RANK, TILE)
         product = jnp.dot(weights, gram, precision=HIGHEST, preferred_element_type=F32)
     lengths = jnp.sqrt(jnp.sum(product * product, axis=1, keepdims=True) + 1e-06)
-    out_ref[...] = (solved[...].reshape(RANK, TILE) * lengths).astype(BF16)
-
-
-def compress(gram):
-    order = gram.shape[0]
+    return (solved[...].reshape(RANK, TILE) * lengths).astype(BF16)
+
+
+def inner_of(coefficients, gram):
+    wide = coefficients.astype(F32)
+    image = jnp.dot(wide, gram, precision=HIGHEST, preferred_element_type=F32)
+    return lax.dot_general(image, wide, NT, precision=HIGHEST, preferred_element_type=F32)
+
+
+def first_kernel(gram_ref, out_ref, own_ref, left, right, solved):
+    gram = gram_ref[...]
+    coefficients = reduce_gram(gram, left, right, solved)
+    out_ref[...] = coefficients
+    own_ref[...] = inner_of(coefficients, gram)
+
+
+def merge_kernel(top_ref, upper_ref, out_ref, own_ref, left, right, solved):
+    top = top_ref[...]
+    bottom = jnp.concatenate([top.T[RANK:], upper_ref[...]], axis=1)
+    gram = jnp.concatenate([top, bottom], axis=0)
+    coefficients = reduce_gram(gram, left, right, solved)
+    out_ref[...] = coefficients
+    own_ref[...] = inner_of(coefficients, gram)
+
+
+def compress(kernel, *gram):
     return pl.pallas_call(
-        compress_kernel,
-        out_shape=jax.ShapeDtypeStruct((RANK, order), BF16),
+        kernel,
+        out_shape=(
+            jax.ShapeDtypeStruct((RANK, gram[0].shape[1]), BF16),
+            jax.ShapeDtypeStruct((RANK, RANK), F32),
+        ),
         scratch_shapes=[pltpu.VMEM((RANK // PANEL, PANEL, TILE), F32)] * 3,
         compiler_params=pltpu.CompilerParams(vmem_limit_bytes=16 * 1024 * 1024),
         name="compress",
-    )(gram)
+    )(*gram)
 
 
 def combine(coefficients, rows):
     return jnp.dot(coefficients, rows, preferred_element_type=F32).astype(BF16)
+
+
+def shared_out(rows, width, bit):
+    pieces = [
+        lax.dynamic_slice_in_dim(rows, (2 * pair + bit) * width, width, 1)
+        for pair in range(rows.shape[1] // (2 * width))
+    ]
+    return pieces[0] if len(pieces) == 1 else jnp.concatenate(pieces, axis=1)
 
 
 def ordered(upper_half, own_rows, partner_rows):
@@ -222,20 +244,25 @@
     stacked = jnp.concatenate([prior_basis, snapshots], axis=0)
     low, high = halo(stacked, "space", REACH * BLOCK_DOFS)
     weighted, gram = weigh(prior_basis, snapshots, low, high, mass_factor, neighbours)
-    coefficients = compress(total(gram, "space"))
-    basis, weighted_basis = combine(coefficients, stacked), combine(coefficients, weighted)
+    coefficients, own = compress(first_kernel, total(gram, "space"))
+    members = lax.axis_size("tm")
     member = lax.axis_index("tm")
-    for level_bit in range(lax.axis_size("tm").bit_length() - 1):
-        upper_half = member // (1 << level_bit) % 2 == 1
-        weighted = ordered(upper_half, weighted_basis, partner(weighted_basis, "tm", level_bit))
-        stacked = ordered(upper_half, basis, partner(basis, "tm", level_bit))
-        gram = lax.dot_general(weighted, weighted, NT, preferred_element_type=F32)
-        coefficients = compress(total(gram, "space"))
-        basis, weighted_basis = combine(coefficients, stacked), combine(coefficients, weighted)
-    share_width = basis.shape[1] // lax.axis_size("tm")
-    basis_share = lax.dynamic_slice_in_dim(basis, member * share_width, share_width, 1)
-    weighted_share = lax.dynamic_slice_in_dim(weighted_basis, member * share_width, share_width, 1)
-    return (basis_share, weighted_share)
+    width = stacked.shape[1] // members
+    for level in range(members.bit_length() - 1):
+        step = 1 << level
+        bit = member // step % 2
+        upper_half = bit == 1
+        weighted = combine(coefficients, weighted)
+        sent = swapped(shared_out(weighted, width, 1 - bit), "tm", step)
+        partner_own = swapped(own, "tm", step)
+        weighted = ordered(upper_half, shared_out(weighted, width, bit), sent)
+        stacked = combine(coefficients, stacked)
+        sent = swapped(shared_out(stacked, width, 1 - bit), "tm", step)
+        stacked = ordered(upper_half, shared_out(stacked, width, bit), sent)
+        top = lax.dot_general(weighted[:RANK], weighted, NT, preferred_element_type=F32)
+        top = total(total(top, "tm", 2 * step), "space")
+        coefficients, own = compress(merge_kernel, top, jnp.where(upper_half, own, partner_own))
+    return combine(coefficients, stacked), combine(coefficients, weighted)
 
 
 def solution(mesh):

time: 144 us -> 124 us (0.86)
  waiting for transfers between devices: 55.2 us -> 37.7 us
  other arithmetic: 3.49 us -> 0.83 us
  Pallas kernels: 40.9 us -> 42.9 us
  starting transfers between devices: 30.8 us -> 29.3 us
    ppermute x13 -> x18, waiting for transfers between devices: 51.1 us -> 32.6 us  [swapped(): lax.ppermute(block, axis, [(i, i ^ step) for i in range(lax.axis_size(axi...]
    ppermute x1, waiting for transfers between devices: 1.11 us -> 4.14 us  [halo(): high = lax.ppermute(block[:, :width], axis, backward)]
    select_n x4 -> x2, other arithmetic: 3.32 us -> 0.3 us  [ordered(): lower_part = jnp.where(upper_half, partner_rows, own_rows)]
    pallas_call x3, Pallas kernels: 31.4 us -> 33.4 us  [compress(): pl.pallas_call(kernel, out_shape=(jax.ShapeDtypeStruct((RANK, gram[0].sha...]
    ppermute x1, waiting for transfers between devices: 2.96 us -> 0.99 us  [halo(): low = lax.ppermute(block[:, block.shape[1] - width:], axis, forward)]
    ppermute x13 -> x18, starting transfers between devices: 24 us -> 23.2 us  [swapped(): lax.ppermute(block, axis, [(i, i ^ step) for i in range(lax.axis_size(axi...]
  transfers between devices with their start and end apart: 15 -> 20, of which waited for: 13 -> 17; matrix products, arithmetic and copies ran while one was open for 5% -> 1% of each run, Pallas kernels for 7% -> 9%
where the time goes in v2:
time: 124 us
  Pallas kernels  42.9 us (35%)
  waiting for transfers between devices  37.7 us (30%)
  starting transfers between devices  29.3 us (24%)
  local copies, waits for them, and re-layouts  6.75 us (5%)
  matrix products  5.69 us (5%)
    pallas_call x3, Pallas kernels, compress(): pl.pallas_call(kernel, out_shape=(jax.ShapeDtypeStruct((RANK, gram[0].sha...  33.4 us
    ppermute x18, waiting for transfers between devices, swapped(): lax.ppermute(block, axis, [(i, i ^ step) for i in range(lax.axis_size(axi...  32.6 us
    ppermute x18, starting transfers between devices, swapped(): lax.ppermute(block, axis, [(i, i ^ step) for i in range(lax.axis_size(axi...  23.2 us
    pallas_call x1, Pallas kernels, weigh(): pl.pallas_call(weigh_kernel, out_shape=(jax.ShapeDtypeStruct((columns, wi...  9.48 us
    unnamed x15, local copies, waits for them, and re-layouts  6.05 us
    dot_general x6, matrix products, combine(): return jnp.dot(coefficients, rows, preferred_element_type=F32).astype(BF16)  4.91 us
    ppermute x1, starting transfers between devices, halo(): low = lax.ppermute(block[:, block.shape[1] - width:], axis, forward)  4.88 us
    ppermute x1, waiting for transfers between devices, halo(): high = lax.ppermute(block[:, :width], axis, backward)  4.14 us
  transfers between devices with their start and end apart: 20, of which 17 were waited for; matrix products, arithmetic and copies ran while one was open for 1% of the time, Pallas kernels for 9%

profile of v2, /device:TPU:0, one launch (start us, length us, event | category | flops | bytes accessed | tf_op | source)
XLA Modules:
  0.0 124.2 jit_solution(9418367384710122749)
XLA Ops:
  0.7 1.4 %constant_dynamic-update-slice_fusion.1 = bf16[128,8192]{1,0:T(8,128)(2,1)S(1)} fusion(bf16[64,8192]{1,0:T(8,128)(2,1)} %prior_ref.1), kind=kLoop, calls=%fused_computation.31 | loop fusion | bytes 2097152
  2.4 4.9 %collective-permute-start = (bf16[128,512]{1,0:T(8,128)(2,1)S(1)}, bf16[128,512]{1,0:T(8,128)(2,1)S(1)}, u32[]{:S(2)}, u32[]{:S(2)}) collective-permute-start(bf16[128,512]{1,0:T(8,128)(2,1)S(1)} %get-tuple-element.17), channel_id=1, source_target_pairs={{0,4},{4,8},{8,12},{12,16},{16,20},{20,24},{24,28},{1,5},{5,9},{9,... | collective-permute-start | bytes 393224 | tf_op jit(solution)/shard_map/ppermute | solution.py:25
  10.0 4.1 %collective-permute-done.1.high_ref = bf16[128,512]{1,0:T(8,128)(2,1)S(1)} collective-permute-done((bf16[128,512]{1,0:T(8,128)(2,1)S(1)}, bf16[128,512]{1,0:T(8,128)(2,1)S(1)}, u32[]{:S(2)}, u32[]{:S(2)}) %collective-permute-start.1) | collective-permute-done | bytes 131104 | tf_op jit(solution)/shard_map/ppermute | solution.py:26
  14.1 3.1 %copy-done = bf16[7,64,8192]{2,1,0:T(8,128)(2,1)S(1)} copy-done((bf16[7,64,8192]{2,1,0:T(8,128)(2,1)S(1)}, bf16[7,64,8192]{2,1,0:T(8,128)(2,1)}, u32[]{:S(2)}) %copy-start) | copy-done | bytes 7340056
  17.2 9.5 %weigh.1 = (bf16[128,8192]{1,0:T(8,128)(2,1)S(1)}, f32[128,128]{1,0:T(8,128)S(1)}) custom-call(s32[896]{0:T(1024)S(1)} %reshape.24.spots, bf16[64,8192]{1,0:T(8,128)(2,1)S(1)} %copy-done.1, bf16[64,8192]{1,0:T(8,128)(2,1)S(1)} %copy-done.2, bf16[128,512]{1,0:T(8,128)(2,1)S(1)} %collective-permute-done.low_ref, ...), custom_call_target="tpu_custom_call" | custom-call | tf_op jit(solution)/shard_map/weigh/pallas_call | solution.py:99
  26.7 1.3 %copy-done.3 = bf16[128,8192]{1,0:T(8,128)(2,1)} copy-done((bf16[128,8192]{1,0:T(8,128)(2,1)}, bf16[128,8192]{1,0:T(8,128)(2,1)S(1)}, u32[]{:S(2)}) %copy-start.3) | copy-done | bytes 2097176
  28.1 2.4 %collective-permute-start.2 = (f32[128,128]{1,0:T(8,128)S(1)}, f32[128,128]{1,0:T(8,128)S(1)}, u32[]{:S(2)}, u32[]{:S(2)}) collective-permute-start(f32[128,128]{1,0:T(8,128)S(1)} %get-tuple-element.9), channel_id=1, source_target_pairs={{0,4},{4,0},{8,12},{12,8},{16,20},{20,16},{24,28},{28,24},{1,5},{5... | collective-permute-start | bytes 196616 | tf_op jit(solution)/shard_map/ppermute | solution.py:31
  30.5 2.2 %collective-permute-done.2 = f32[128,128]{1,0:T(8,128)S(1)} collective-permute-done((f32[128,128]{1,0:T(8,128)S(1)}, f32[128,128]{1,0:T(8,128)S(1)}, u32[]{:S(2)}, u32[]{:S(2)}) %collective-permute-start.2) | collective-permute-done | bytes 65568 | tf_op jit(solution)/shard_map/ppermute | solution.py:31
  32.8 1.8 %collective-permute-start.3 = (f32[128,128]{1,0:T(8,128)S(1)}, f32[128,128]{1,0:T(8,128)S(1)}, u32[]{:S(2)}, u32[]{:S(2)}) collective-permute-start(f32[128,128]{1,0:T(8,128)S(1)} %add.105), channel_id=1, source_target_pairs={{0,8},{4,12},{8,0},{12,4},{16,24},{20,28},{24,16},{28,20},{1,9},{5... | collective-permute-start | bytes 196616 | tf_op jit(solution)/shard_map/ppermute | solution.py:31
  34.5 2.6 %collective-permute-done.3 = f32[128,128]{1,0:T(8,128)S(1)} collective-permute-done((f32[128,128]{1,0:T(8,128)S(1)}, f32[128,128]{1,0:T(8,128)S(1)}, u32[]{:S(2)}, u32[]{:S(2)}) %collective-permute-start.3) | collective-permute-done | bytes 65568 | tf_op jit(solution)/shard_map/ppermute | solution.py:31
  37.1 3.4 %collective-permute-start.4 = (f32[128,128]{1,0:T(8,128)S(1)}, f32[128,128]{1,0:T(8,128)S(1)}, u32[]{:S(2)}, u32[]{:S(2)}) collective-permute-start(f32[128,128]{1,0:T(8,128)S(1)} %add.106), channel_id=1, source_target_pairs={{0,16},{4,20},{8,24},{12,28},{16,0},{20,4},{24,8},{28,12},{1,17},{... | collective-permute-start | bytes 196616 | tf_op jit(solution)/shard_map/ppermute | solution.py:31
  40.5 2.2 %collective-permute-done.4 = f32[128,128]{1,0:T(8,128)S(1)} collective-permute-done((f32[128,128]{1,0:T(8,128)S(1)}, f32[128,128]{1,0:T(8,128)S(1)}, u32[]{:S(2)}, u32[]{:S(2)}) %collective-permute-start.4) | collective-permute-done | bytes 65568 | tf_op jit(solution)/shard_map/ppermute | solution.py:31
  42.8 10.9 %compress.3 = (bf16[64,128]{1,0:T(8,128)(2,1)S(1)}, f32[64,64]{1,0:T(8,128)S(1)}) custom-call(f32[128,128]{1,0:T(8,128)S(1)} %add.107.gram_ref), custom_call_target="tpu_custom_call" | custom-call | tf_op jit(solution)/shard_map/compress/pallas_call | solution.py:213
  53.6 2.0 %convolution_convert_fusion = bf16[64,8192]{1,0:T(8,128)(2,1)S(1)} fusion(bf16[64,128]{1,0:T(8,128)(2,1)S(1)} %get-tuple-element.10, bf16[128,8192]{1,0:T(8,128)(2,1)} %copy-done.5), kind=kOutput, calls=%fused_computation | convolution fusion | flops 134742016 | bytes 3162112 | tf_op jit(solution)/shard_map/dot_general | solution.py:226
  56.5 1.9 %collective-permute-done.5 = bf16[64,4096]{1,0:T(8,128)(2,1)S(1)} collective-permute-done((bf16[64,4096]{1,0:T(8,128)(2,1)S(1)}, bf16[64,4096]{1,0:T(8,128)(2,1)S(1)}, u32[]{:S(2)}, u32[]{:S(2)}) %collective-permute-start.5) | collective-permute-done | bytes 524320 | tf_op jit(solution)/shard_map/ppermute | solution.py:31
  60.3 3.0 %collective-permute-start.7 = (f32[64,128]{1,0:T(8,128)S(1)}, f32[64,128]{1,0:T(8,128)S(1)}, u32[]{:S(2)}, u32[]{:S(2)}) collective-permute-start(f32[64,128]{1,0:T(8,128)S(1)} %add.114), channel_id=1, source_target_pairs={{0,4},{4,0},{8,12},{12,8},{16,20},{20,16},{24,28},{28,24},{1,5},{5... | collective-permute-start | bytes 98312 | tf_op jit(solution)/shard_map/ppermute | solution.py:31
  63.4 1.9 %collective-permute-done.7 = f32[64,128]{1,0:T(8,128)S(1)} collective-permute-done((f32[64,128]{1,0:T(8,128)S(1)}, f32[64,128]{1,0:T(8,128)S(1)}, u32[]{:S(2)}, u32[]{:S(2)}) %collective-permute-start.7) | collective-permute-done | bytes 32800 | tf_op jit(solution)/shard_map/ppermute | solution.py:31
  65.9 3.2 %collective-permute-done.8 = f32[64,128]{1,0:T(8,128)S(1)} collective-permute-done((f32[64,128]{1,0:T(8,128)S(1)}, f32[64,128]{1,0:T(8,128)S(1)}, u32[]{:S(2)}, u32[]{:S(2)}) %collective-permute-start.8) | collective-permute-done | bytes 32800 | tf_op jit(solution)/shard_map/ppermute | solution.py:31
  69.2 2.0 %collective-permute-start.9 = (f32[64,128]{1,0:T(8,128)S(1)}, f32[64,128]{1,0:T(8,128)S(1)}, u32[]{:S(2)}, u32[]{:S(2)}) collective-permute-start(f32[64,128]{1,0:T(8,128)S(1)} %add.116), channel_id=1, source_target_pairs={{0,16},{4,20},{8,24},{12,28},{16,0},{20,4},{24,8},{28,12},{1,17},{... | collective-permute-start | bytes 98312 | tf_op jit(solution)/shard_map/ppermute | solution.py:31
  71.2 3.1 %collective-permute-done.9 = f32[64,128]{1,0:T(8,128)S(1)} collective-permute-done((f32[64,128]{1,0:T(8,128)S(1)}, f32[64,128]{1,0:T(8,128)S(1)}, u32[]{:S(2)}, u32[]{:S(2)}) %collective-permute-start.9) | collective-permute-done | bytes 32800 | tf_op jit(solution)/shard_map/ppermute | solution.py:31
  74.4 11.0 %compress.4 = (bf16[64,128]{1,0:T(8,128)(2,1)S(1)}, f32[64,64]{1,0:T(8,128)S(1)}) custom-call(f32[64,128]{1,0:T(8,128)S(1)} %add.117.top_ref, f32[64,64]{1,0:T(8,128)S(1)} %broadcast_select_fusion.9.upper_ref), custom_call_target="tpu_custom_call" | custom-call | tf_op jit(solution)/shard_map/compress/pallas_call | solution.py:213
  85.7 1.6 %collective-permute-start.11 = (bf16[64,2048]{1,0:T(8,128)(2,1)S(1)}, bf16[64,2048]{1,0:T(8,128)(2,1)S(1)}, u32[]{:S(2)}, u32[]{:S(2)}) collective-permute-start(bf16[64,2048]{1,0:T(8,128)(2,1)S(1)} %constant_dynamic-slice_fusion.5), channel_id=1, source_target_pairs={{0,2},{1,3},{2,0},{3,1},{4,6},{5,7},{6,4},{7,5},{8,10},{9,11},{10,... | collective-permute-start | bytes 786440 | tf_op jit(solution)/shard_map/ppermute | solution.py:31
  87.4 4.7 %collective-permute-done.11 = bf16[64,2048]{1,0:T(8,128)(2,1)S(1)} collective-permute-done((bf16[64,2048]{1,0:T(8,128)(2,1)S(1)}, bf16[64,2048]{1,0:T(8,128)(2,1)S(1)}, u32[]{:S(2)}, u32[]{:S(2)}) %collective-permute-start.11) | collective-permute-done | bytes 262176 | tf_op jit(solution)/shard_map/ppermute | solution.py:31
  93.8 1.5 %collective-permute-start.13 = (f32[64,128]{1,0:T(8,128)S(1)}, f32[64,128]{1,0:T(8,128)S(1)}, u32[]{:S(2)}, u32[]{:S(2)}) collective-permute-start(f32[64,128]{1,0:T(8,128)S(1)} %add.120), channel_id=1, source_target_pairs={{0,2},{1,3},{2,0},{3,1},{4,6},{5,7},{6,4},{7,5},{8,10},{9,11},{10,... | collective-permute-start | bytes 98312 | tf_op jit(solution)/shard_map/ppermute | solution.py:31
  95.9 1.8 %collective-permute-done.13 = f32[64,128]{1,0:T(8,128)S(1)} collective-permute-done((f32[64,128]{1,0:T(8,128)S(1)}, f32[64,128]{1,0:T(8,128)S(1)}, u32[]{:S(2)}, u32[]{:S(2)}) %collective-permute-start.13) | collective-permute-done | bytes 32800 | tf_op jit(solution)/shard_map/ppermute | solution.py:31
  97.7 2.0 %collective-permute-start.14 = (f32[64,128]{1,0:T(8,128)S(1)}, f32[64,128]{1,0:T(8,128)S(1)}, u32[]{:S(2)}, u32[]{:S(2)}) collective-permute-start(f32[64,128]{1,0:T(8,128)S(1)} %add.121), channel_id=1, source_target_pairs={{0,4},{4,0},{8,12},{12,8},{16,20},{20,16},{24,28},{28,24},{1,5},{5... | collective-permute-start | bytes 98312 | tf_op jit(solution)/shard_map/ppermute | solution.py:31
  99.7 1.8 %collective-permute-start.17 = (f32[64,64]{1,0:T(8,128)S(1)}, f32[64,64]{1,0:T(8,128)S(1)}, u32[]{:S(2)}, u32[]{:S(2)}) collective-permute-start(f32[64,64]{1,0:T(8,128)S(1)} %get-tuple-element.14), channel_id=1, source_target_pairs={{0,2},{1,3},{2,0},{3,1},{4,6},{5,7},{6,4},{7,5},{8,10},{9,11},{10,... | collective-permute-start | bytes 49160 | tf_op jit(solution)/shard_map/ppermute | solution.py:31
  102.1 2.1 %collective-permute-done.17 = f32[64,64]{1,0:T(8,128)S(1)} collective-permute-done((f32[64,64]{1,0:T(8,128)S(1)}, f32[64,64]{1,0:T(8,128)S(1)}, u32[]{:S(2)}, u32[]{:S(2)}) %collective-permute-start.17) | collective-permute-done | bytes 16416 | tf_op jit(solution)/shard_map/ppermute | solution.py:31
  104.2 1.4 %collective-permute-done.15 = f32[64,128]{1,0:T(8,128)S(1)} collective-permute-done((f32[64,128]{1,0:T(8,128)S(1)}, f32[64,128]{1,0:T(8,128)S(1)}, u32[]{:S(2)}, u32[]{:S(2)}) %collective-permute-start.15) | collective-permute-done | bytes 32800 | tf_op jit(solution)/shard_map/ppermute | solution.py:31
  105.6 1.7 %collective-permute-start.16 = (f32[64,128]{1,0:T(8,128)S(1)}, f32[64,128]{1,0:T(8,128)S(1)}, u32[]{:S(2)}, u32[]{:S(2)}) collective-permute-start(f32[64,128]{1,0:T(8,128)S(1)} %add.123), channel_id=1, source_target_pairs={{0,16},{4,20},{8,24},{12,28},{16,0},{20,4},{24,8},{28,12},{1,17},{... | collective-permute-start | bytes 98312 | tf_op jit(solution)/shard_map/ppermute | solution.py:31
  107.4 3.3 %collective-permute-done.16 = f32[64,128]{1,0:T(8,128)S(1)} collective-permute-done((f32[64,128]{1,0:T(8,128)S(1)}, f32[64,128]{1,0:T(8,128)S(1)}, u32[]{:S(2)}, u32[]{:S(2)}) %collective-permute-start.16) | collective-permute-done | bytes 32800 | tf_op jit(solution)/shard_map/ppermute | solution.py:31
  110.7 11.6 %compress.5 = (bf16[64,128]{1,0:T(8,128)(2,1)S(1)}, f32[64,64]{1,0:T(8,128)}) custom-call(f32[64,128]{1,0:T(8,128)S(1)} %add.124.top_ref, f32[64,64]{1,0:T(8,128)S(1)} %broadcast_select_fusion.8.upper_ref), custom_call_target="tpu_custom_call" | custom-call | tf_op jit(solution)/shard_map/compress/pallas_call | solution.py:213
  (64 shorter events, 11.7 us)
Async XLA Ops:
  0.6 13.5 %copy-start.1 = (bf16[64,8192]{1,0:T(8,128)(2,1)S(1)}, bf16[64,8192]{1,0:T(8,128)(2,1)}, u32[]{:S(2)}) copy-start(bf16[64,8192]{1,0:T(8,128)(2,1)} %prior_ref.1) | copy-start | bytes 3145732
  0.6 1.6 %copy-start.2 = (bf16[64,8192]{1,0:T(8,128)(2,1)S(1)}, bf16[64,8192]{1,0:T(8,128)(2,1)}, u32[]{:S(2)}) copy-start(bf16[64,8192]{1,0:T(8,128)(2,1)} %snap_ref.1) | copy-start | bytes 3145732
  0.6 7.9 %copy-start.6 = (s32[128,7]{0,1:T(8,128)S(1)}, s32[128,7]{0,1:T(8,128)}, u32[]{:S(2)}) copy-start(s32[128,7]{0,1:T(8,128)} %param.7) | copy-start | bytes 10756
  2.3 4.9 %copy-start.5 = (bf16[128,8192]{1,0:T(8,128)(2,1)}, bf16[128,8192]{1,0:T(8,128)(2,1)S(1)}, u32[]{:S(2)}) copy-start(bf16[128,8192]{1,0:T(8,128)(2,1)S(1)} %constant_dynamic-update-slice_fusion) | copy-start | bytes 6291460
  2.4 7.6 %collective-permute-start = (bf16[128,512]{1,0:T(8,128)(2,1)S(1)}, bf16[128,512]{1,0:T(8,128)(2,1)S(1)}, u32[]{:S(2)}, u32[]{:S(2)}) collective-permute-start(bf16[128,512]{1,0:T(8,128)(2,1)S(1)} %get-tuple-element.17), channel_id=1, source_target_pairs={{0,4},{4,8},{8,12},{12,16},{16,20},{20,24},{24,28},{1,5},{5,9},{9,... | collective-permute-start | bytes 393224 | tf_op jit(solution)/shard_map/ppermute | solution.py:25
  7.3 6.9 %collective-permute-start.1 = (bf16[128,512]{1,0:T(8,128)(2,1)S(1)}, bf16[128,512]{1,0:T(8,128)(2,1)S(1)}, u32[]{:S(2)}, u32[]{:S(2)}) collective-permute-start(bf16[128,512]{1,0:T(8,128)(2,1)S(1)} %get-tuple-element.16), channel_id=1, source_target_pairs={{4,0},{8,4},{12,8},{16,12},{20,16},{24,20},{28,24},{5,1},{9,5},{13... | collective-permute-start | bytes 393224 | tf_op jit(solution)/shard_map/ppermute | solution.py:26
  14.1 3.1 %copy-start = (bf16[7,64,8192]{2,1,0:T(8,128)(2,1)S(1)}, bf16[7,64,8192]{2,1,0:T(8,128)(2,1)}, u32[]{:S(2)}) copy-start(bf16[7,64,8192]{2,1,0:T(8,128)(2,1)} %factor_ref.1) | copy-start | bytes 22020100
  26.7 1.3 %copy-start.3 = (bf16[128,8192]{1,0:T(8,128)(2,1)}, bf16[128,8192]{1,0:T(8,128)(2,1)S(1)}, u32[]{:S(2)}) copy-start(bf16[128,8192]{1,0:T(8,128)(2,1)S(1)} %get-tuple-element.11) | copy-start | bytes 6291460
  28.1 27.6 %copy-start.4 = (bf16[128,8192]{1,0:T(8,128)(2,1)S(1)}, bf16[128,8192]{1,0:T(8,128)(2,1)}, u32[]{:S(2)}) copy-start(bf16[128,8192]{1,0:T(8,128)(2,1)} %copy-done.3) | copy-start | bytes 6291460
  28.1 4.7 %collective-permute-start.2 = (f32[128,128]{1,0:T(8,128)S(1)}, f32[128,128]{1,0:T(8,128)S(1)}, u32[]{:S(2)}, u32[]{:S(2)}) collective-permute-start(f32[128,128]{1,0:T(8,128)S(1)} %get-tuple-element.9), channel_id=1, source_target_pairs={{0,4},{4,0},{8,12},{12,8},{16,20},{20,16},{24,28},{28,24},{1,5},{5... | collective-permute-start | bytes 196616 | tf_op jit(solution)/shard_map/ppermute | solution.py:31
  32.8 4.3 %collective-permute-start.3 = (f32[128,128]{1,0:T(8,128)S(1)}, f32[128,128]{1,0:T(8,128)S(1)}, u32[]{:S(2)}, u32[]{:S(2)}) collective-permute-start(f32[128,128]{1,0:T(8,128)S(1)} %add.105), channel_id=1, source_target_pairs={{0,8},{4,12},{8,0},{12,4},{16,24},{20,28},{24,16},{28,20},{1,9},{5... | collective-permute-start | bytes 196616 | tf_op jit(solution)/shard_map/ppermute | solution.py:31
  37.1 5.6 %collective-permute-start.4 = (f32[128,128]{1,0:T(8,128)S(1)}, f32[128,128]{1,0:T(8,128)S(1)}, u32[]{:S(2)}, u32[]{:S(2)}) collective-permute-start(f32[128,128]{1,0:T(8,128)S(1)} %add.106), channel_id=1, source_target_pairs={{0,16},{4,20},{8,24},{12,28},{16,0},{20,4},{24,8},{28,12},{1,17},{... | collective-permute-start | bytes 196616 | tf_op jit(solution)/shard_map/ppermute | solution.py:31
  56.4 2.0 %collective-permute-start.5 = (bf16[64,4096]{1,0:T(8,128)(2,1)S(1)}, bf16[64,4096]{1,0:T(8,128)(2,1)S(1)}, u32[]{:S(2)}, u32[]{:S(2)}) collective-permute-start(bf16[64,4096]{1,0:T(8,128)(2,1)S(1)} %pad_maximum_fusion.3), channel_id=1, source_target_pairs={{0,1},{1,0},{2,3},{3,2},{4,5},{5,4},{6,7},{7,6},{8,9},{9,8},{10,11... | collective-permute-start | bytes 1572872 | tf_op jit(solution)/shard_map/ppermute | solution.py:31
  59.1 1.3 %collective-permute-start.6 = (f32[64,128]{1,0:T(8,128)S(1)}, f32[64,128]{1,0:T(8,128)S(1)}, u32[]{:S(2)}, u32[]{:S(2)}) collective-permute-start(f32[64,128]{1,0:T(8,128)S(1)} %fusion.3), channel_id=1, source_target_pairs={{0,1},{1,0},{2,3},{3,2},{4,5},{5,4},{6,7},{7,6},{8,9},{9,8},{10,11... | collective-permute-start | bytes 98312 | tf_op jit(solution)/shard_map/ppermute | solution.py:31
  60.3 4.9 %collective-permute-start.7 = (f32[64,128]{1,0:T(8,128)S(1)}, f32[64,128]{1,0:T(8,128)S(1)}, u32[]{:S(2)}, u32[]{:S(2)}) collective-permute-start(f32[64,128]{1,0:T(8,128)S(1)} %add.114), channel_id=1, source_target_pairs={{0,4},{4,0},{8,12},{12,8},{16,20},{20,16},{24,28},{28,24},{1,5},{5... | collective-permute-start | bytes 98312 | tf_op jit(solution)/shard_map/ppermute | solution.py:31
  63.4 7.8 %collective-permute-start.10 = (f32[64,64]{1,0:T(8,128)S(1)}, f32[64,64]{1,0:T(8,128)S(1)}, u32[]{:S(2)}, u32[]{:S(2)}) collective-permute-start(f32[64,64]{1,0:T(8,128)S(1)} %get-tuple-element.12), channel_id=1, source_target_pairs={{0,1},{1,0},{2,3},{3,2},{4,5},{5,4},{6,7},{7,6},{8,9},{9,8},{10,11... | collective-permute-start | bytes 49160 | tf_op jit(solution)/shard_map/ppermute | solution.py:31
  65.3 3.9 %collective-permute-start.8 = (f32[64,128]{1,0:T(8,128)S(1)}, f32[64,128]{1,0:T(8,128)S(1)}, u32[]{:S(2)}, u32[]{:S(2)}) collective-permute-start(f32[64,128]{1,0:T(8,128)S(1)} %add.115), channel_id=1, source_target_pairs={{0,8},{4,12},{8,0},{12,4},{16,24},{20,28},{24,16},{28,20},{1,9},{5... | collective-permute-start | bytes 98312 | tf_op jit(solution)/shard_map/ppermute | solution.py:31
  65.9 21.4 %collective-permute-start.18 = (bf16[64,4096]{1,0:T(8,128)(2,1)S(1)}, bf16[64,4096]{1,0:T(8,128)(2,1)S(1)}, u32[]{:S(2)}, u32[]{:S(2)}) collective-permute-start(bf16[64,4096]{1,0:T(8,128)(2,1)S(1)} %pad_maximum_fusion.6), channel_id=1, source_target_pairs={{0,1},{1,0},{2,3},{3,2},{4,5},{5,4},{6,7},{7,6},{8,9},{9,8},{10,11... | collective-permute-start | bytes 1572872 | tf_op jit(solution)/shard_map/ppermute | solution.py:31
  69.2 5.2 %collective-permute-start.9 = (f32[64,128]{1,0:T(8,128)S(1)}, f32[64,128]{1,0:T(8,128)S(1)}, u32[]{:S(2)}, u32[]{:S(2)}) collective-permute-start(f32[64,128]{1,0:T(8,128)S(1)} %add.116), channel_id=1, source_target_pairs={{0,16},{4,20},{8,24},{12,28},{16,0},{20,4},{24,8},{28,12},{1,17},{... | collective-permute-start | bytes 98312 | tf_op jit(solution)/shard_map/ppermute | solution.py:31
  85.7 6.4 %collective-permute-start.11 = (bf16[64,2048]{1,0:T(8,128)(2,1)S(1)}, bf16[64,2048]{1,0:T(8,128)(2,1)S(1)}, u32[]{:S(2)}, u32[]{:S(2)}) collective-permute-start(bf16[64,2048]{1,0:T(8,128)(2,1)S(1)} %constant_dynamic-slice_fusion.5), channel_id=1, source_target_pairs={{0,2},{1,3},{2,0},{3,1},{4,6},{5,7},{6,4},{7,5},{8,10},{9,11},{10,... | collective-permute-start | bytes 786440 | tf_op jit(solution)/shard_map/ppermute | solution.py:31
  92.5 1.3 %collective-permute-start.12 = (f32[64,128]{1,0:T(8,128)S(1)}, f32[64,128]{1,0:T(8,128)S(1)}, u32[]{:S(2)}, u32[]{:S(2)}) collective-permute-start(f32[64,128]{1,0:T(8,128)S(1)} %fusion.7), channel_id=1, source_target_pairs={{0,1},{1,0},{2,3},{3,2},{4,5},{5,4},{6,7},{7,6},{8,9},{9,8},{10,11... | collective-permute-start | bytes 98312 | tf_op jit(solution)/shard_map/ppermute | solution.py:31
  93.8 3.9 %collective-permute-start.13 = (f32[64,128]{1,0:T(8,128)S(1)}, f32[64,128]{1,0:T(8,128)S(1)}, u32[]{:S(2)}, u32[]{:S(2)}) collective-permute-start(f32[64,128]{1,0:T(8,128)S(1)} %add.120), channel_id=1, source_target_pairs={{0,2},{1,3},{2,0},{3,1},{4,6},{5,7},{6,4},{7,5},{8,10},{9,11},{10,... | collective-permute-start | bytes 98312 | tf_op jit(solution)/shard_map/ppermute | solution.py:31
  95.3 12.0 %collective-permute-start.19 = (bf16[64,2048]{1,0:T(8,128)(2,1)S(1)}, bf16[64,2048]{1,0:T(8,128)(2,1)S(1)}, u32[]{:S(2)}, u32[]{:S(2)}) collective-permute-start(bf16[64,2048]{1,0:T(8,128)(2,1)S(1)} %constant_dynamic-slice_fusion), channel_id=1, source_target_pairs={{0,2},{1,3},{2,0},{3,1},{4,6},{5,7},{6,4},{7,5},{8,10},{9,11},{10,... | collective-permute-start | bytes 786440 | tf_op jit(solution)/shard_map/ppermute | solution.py:31
  97.7 3.9 %collective-permute-start.14 = (f32[64,128]{1,0:T(8,128)S(1)}, f32[64,128]{1,0:T(8,128)S(1)}, u32[]{:S(2)}, u32[]{:S(2)}) collective-permute-start(f32[64,128]{1,0:T(8,128)S(1)} %add.121), channel_id=1, source_target_pairs={{0,4},{4,0},{8,12},{12,8},{16,20},{20,16},{24,28},{28,24},{1,5},{5... | collective-permute-start | bytes 98312 | tf_op jit(solution)/shard_map/ppermute | solution.py:31
  99.7 4.5 %collective-permute-start.17 = (f32[64,64]{1,0:T(8,128)S(1)}, f32[64,64]{1,0:T(8,128)S(1)}, u32[]{:S(2)}, u32[]{:S(2)}) collective-permute-start(f32[64,64]{1,0:T(8,128)S(1)} %get-tuple-element.14), channel_id=1, source_target_pairs={{0,2},{1,3},{2,0},{3,1},{4,6},{5,7},{6,4},{7,5},{8,10},{9,11},{10,... | collective-permute-start | bytes 49160 | tf_op jit(solution)/shard_map/ppermute | solution.py:31
  101.6 3.9 %collective-permute-start.15 = (f32[64,128]{1,0:T(8,128)S(1)}, f32[64,128]{1,0:T(8,128)S(1)}, u32[]{:S(2)}, u32[]{:S(2)}) collective-permute-start(f32[64,128]{1,0:T(8,128)S(1)} %add.122), channel_id=1, source_target_pairs={{0,8},{4,12},{8,0},{12,4},{16,24},{20,28},{24,16},{28,20},{1,9},{5... | collective-permute-start | bytes 98312 | tf_op jit(solution)/shard_map/ppermute | solution.py:31
  105.6 5.2 %collective-permute-start.16 = (f32[64,128]{1,0:T(8,128)S(1)}, f32[64,128]{1,0:T(8,128)S(1)}, u32[]{:S(2)}, u32[]{:S(2)}) collective-permute-start(f32[64,128]{1,0:T(8,128)S(1)} %add.123), channel_id=1, source_target_pairs={{0,16},{4,20},{8,24},{12,28},{16,0},{20,4},{24,8},{28,12},{1,17},{... | collective-permute-start | bytes 98312 | tf_op jit(solution)/shard_map/ppermute | solution.py:31

commit v3 on v2

--- a/solution.py
+++ b/solution.py
@@ -27,49 +27,39 @@
     return low, high
 
 
-def swapped(block, axis, step):
-    return lax.ppermute(block, axis, [(i, i ^ step) for i in range(lax.axis_size(axis))])
-
-
-def total(block, axis, limit=None):
-    count = limit or lax.axis_size(axis)
-    step = 1
-    while step < count:
-        block = block + swapped(block, axis, step)
-        step *= 2
+def swapped(block, mask):
+    axes = ("space", "tm")
+    count = lax.axis_size("space") * lax.axis_size("tm")
+    return lax.ppermute(block, axes, [(i, i ^ mask) for i in range(count)])
+
+
+def total(block, bits):
+    for start in range(0, len(bits), 2):
+        first = bits[start]
+        if start + 1 < len(bits):
+            second = bits[start + 1]
+            near, far, both = swapped(block, first), swapped(block, second), swapped(block, first | second)
+            block = (block + near) + (far + both)
+        else:
+            block = block + swapped(block, first)
     return block
 
 
-def weigh_kernel(spots, prior_ref, snap_ref, low_ref, high_ref, factor_ref, weighted_ref, gram_ref, bank):
-    step = pl.program_id(0)
-    rows, width = prior_ref.shape
-    edge = low_ref.shape[1]
+def fill_odd(bank, whole, block, start, stop):
+    bank[:, whole + start + TILE:whole + stop] = bank[:, start + block:stop - block]
+
+
+def weigh_chunk(spots, row, bank, factor_ref):
     neighbours, block, chunk = factor_ref.shape
     columns = bank.shape[0]
-    whole = width + 2 * edge
-
-    @pl.when(step == 0)
-    def _():
-        bank[:, 0:edge] = low_ref[...]
-        bank[:rows, edge:edge + width] = prior_ref[...]
-        bank[rows:, edge:edge + width] = snap_ref[...]
-        bank[:, edge + width:whole] = high_ref[...]
-        bank[:, whole + TILE:2 * whole] = bank[:, block:whole - block]
-        bank[:, whole:whole + TILE] = bank[:, 0:TILE]
-        bank[:, whole + block:whole + TILE] = bank[:, 0:block]
-        bank[:, 2 * whole:2 * whole + TILE] = bank[:, whole - TILE:whole]
-        bank[:, 2 * whole:2 * whole + block] = bank[:, whole - block:whole]
-        gram_ref[...] = jnp.zeros_like(gram_ref)
-
     lower = lax.broadcasted_iota(jnp.int32, (columns, TILE), 1) < block
     pieces = []
     for tile in range(chunk // TILE):
         results = []
         for side in range(2):
-            row = step * (chunk // block) + tile * 2 + side
             parts = []
             for k in range(neighbours):
-                spot = spots[row * neighbours + k]
+                spot = spots[(row + tile * 2 + side) * neighbours + k]
                 parts.append(bank[:, pl.ds(pl.multiple_of(spot * TILE, TILE), TILE)])
             joined = [jnp.where(lower, parts[k], parts[k + 1]) for k in range(0, neighbours - 1, 2)]
             if neighbours % 2:
@@ -79,48 +69,132 @@
         right = factor_ref[:, :, tile * TILE:(tile + 1) * TILE].reshape(neighbours * block, TILE)
         product = jnp.dot(left, right, preferred_element_type=F32)
         pieces.append(jnp.where(lower, product[:columns], product[columns:]).astype(BF16))
-    weighted = jnp.concatenate(pieces, axis=1)
+    return jnp.concatenate(pieces, axis=1)
+
+
+def inside_kernel(edge, spots, prior_ref, snap_ref, factor_ref, weighted_ref, gram_ref, bank):
+    step = pl.program_id(0)
+    rows, width = prior_ref.shape
+    _, block, chunk = factor_ref.shape
+    whole = width + 2 * edge
+
+    @pl.when(step == 0)
+    def _():
+        bank[:rows, edge:edge + width] = prior_ref[...]
+        bank[rows:, edge:edge + width] = snap_ref[...]
+        fill_odd(bank, whole, block, edge, edge + width)
+        gram_ref[...] = jnp.zeros_like(gram_ref)
+
+    weighted = weigh_chunk(spots, (step + 1) * (chunk // block), bank, factor_ref)
     weighted_ref[...] = weighted
     gram_ref[...] += lax.dot_general(weighted, weighted, NT, preferred_element_type=F32)
 
 
-def weigh(prior, snapshots, low, high, factor, neighbours):
+def border_kernel(
+    spots, prior_ref, snap_ref, low_ref, high_ref, factor_ref, part_ref, kept_ref, weighted_ref, gram_ref, bank
+):
+    step = pl.program_id(0)
+    rows, span = prior_ref.shape
+    edge = low_ref.shape[1]
+    _, block, chunk = factor_ref.shape
+    whole = span + edge
+
+    @pl.when(step == 0)
+    def _():
+        bank[:, :edge] = low_ref[...]
+        bank[:rows, edge:whole] = prior_ref[...]
+        bank[rows:, edge:whole] = snap_ref[...]
+        gram_ref[...] = part_ref[...]
+
+    @pl.when(step != 0)
+    def _():
+        bank[:rows, :span] = prior_ref[...]
+        bank[rows:, :span] = snap_ref[...]
+        bank[:, span:whole] = high_ref[...]
+
+    fill_odd(bank, whole, block, 0, whole)
+    bank[:, whole + block:whole + TILE] = bank[:, :block]
+    bank[:, 2 * whole:2 * whole + block] = bank[:, whole - block:whole]
+    weighted = weigh_chunk(spots, step * (chunk // block), bank, factor_ref)
+    weighted_ref[...] = weighted
+    gram_ref[...] += lax.dot_general(weighted, weighted, NT, preferred_element_type=F32)
+
+
+def spots_of(local, tiles):
+    half, odd = local // 2, local % 2
+    side = jnp.arange(local.shape[1], dtype=jnp.int32)[None, :] % 2
+    spots = half + jnp.where(side == 0, odd * (tiles + 1), (1 - odd) * tiles)
+    return spots.reshape(-1).astype(jnp.int32)
+
+
+def weigh(prior, snapshots, factor, neighbours):
     rows, width = prior.shape
     columns = 2 * rows
     count, block, _ = factor.shape
-    edge = low.shape[1]
-    whole = width + 2 * edge
-    local = neighbours - (lax.axis_index("space") * (width // block) - edge // block)
-    half, odd = local // 2, local % 2
-    side = jnp.arange(count, dtype=jnp.int32)[None, :] % 2
-    spots = half + jnp.where(side == 0, odd * (whole // TILE + 1), (1 - odd) * (whole // TILE))
-    chunk = min(width, 1024)
+    edge = REACH * block
+    chunk = 2 * edge
+    span = 2 * chunk
+    chunks = width // chunk
+    low, high = halo(jnp.concatenate([prior, snapshots], axis=0), "space", edge)
+    local = neighbours - (lax.axis_index("space") * (width // block) - REACH)
+    per = chunk // block
+    shift = (width - span + edge) // block
+    near = jnp.concatenate([local[:per], local[-per:] - shift], axis=0)
     full = lambda i, s: (0, 0)
-    return pl.pallas_call(
-        weigh_kernel,
-        out_shape=(
-            jax.ShapeDtypeStruct((columns, width), BF16),
-            jax.ShapeDtypeStruct((columns, columns), F32),
-        ),
+    shapes = (
+        jax.ShapeDtypeStruct((columns, width), BF16),
+        jax.ShapeDtypeStruct((columns, columns), F32),
+    )
+    params = pltpu.CompilerParams(vmem_limit_bytes=56 * 1024 * 1024)
+    weighted, gram = pl.pallas_call(
+        functools.partial(inside_kernel, edge),
+        out_shape=shapes,
         grid_spec=pltpu.PrefetchScalarGridSpec(
             num_scalar_prefetch=1,
-            grid=(width // chunk,),
+            grid=(chunks - 2,),
             in_specs=[
                 pl.BlockSpec((rows, width), full),
                 pl.BlockSpec((rows, width), full),
+                pl.BlockSpec((count, block, chunk), lambda i, s: (0, 0, i + 1)),
+            ],
+            out_specs=(
+                pl.BlockSpec((columns, chunk), lambda i, s: (0, i + 1)),
+                pl.BlockSpec((columns, columns), full),
+            ),
+            scratch_shapes=[pltpu.VMEM((columns, 2 * (width + 2 * edge) + TILE), BF16)],
+        ),
+        compiler_params=params,
+        cost_estimate=pl.CostEstimate(
+            flops=8 * columns * count * block * width, bytes_accessed=2 * factor.size, transcendentals=0
+        ),
+        name="weigh_inside",
+    )(spots_of(local, (width + 2 * edge) // TILE), prior, snapshots, factor)
+    ends = width // span - 1
+    return pl.pallas_call(
+        border_kernel,
+        out_shape=shapes,
+        grid_spec=pltpu.PrefetchScalarGridSpec(
+            num_scalar_prefetch=1,
+            grid=(2,),
+            in_specs=[
+                pl.BlockSpec((rows, span), lambda i, s: (0, i * ends)),
+                pl.BlockSpec((rows, span), lambda i, s: (0, i * ends)),
                 pl.BlockSpec((columns, edge), full),
                 pl.BlockSpec((columns, edge), full),
-                pl.BlockSpec((count, block, chunk), lambda i, s: (0, 0, i)),
+                pl.BlockSpec((count, block, chunk), lambda i, s: (0, 0, i * (chunks - 1))),
+                pl.BlockSpec((columns, columns), full),
+                pl.BlockSpec(memory_space=pl.ANY),
             ],
             out_specs=(
-                pl.BlockSpec((columns, chunk), lambda i, s: (0, i)),
+                pl.BlockSpec((columns, chunk), lambda i, s: (0, i * (chunks - 1))),
                 pl.BlockSpec((columns, columns), full),
             ),
-            scratch_shapes=[pltpu.VMEM((columns, 2 * whole + TILE), BF16)],
+            scratch_shapes=[pltpu.VMEM((columns, 2 * (span + edge) + TILE), BF16)],
         ),
-        compiler_params=pltpu.CompilerParams(vmem_limit_bytes=40 * 1024 * 1024),
-        name="weigh",
-    )(spots.reshape(-1).astype(jnp.int32), prior, snapshots, low, high, factor)
+        input_output_aliases={7: 0},
+        compiler_params=params,
+        name="weigh_border",
+    )(spots_of(near, (span + edge) // TILE), prior, snapshots, low, high, factor, gram, weighted)
 
 
 def lanes_of(group, column):
@@ -242,10 +316,11 @@
 
 def shards(snapshots, prior_basis, mass_factor, neighbours):
     stacked = jnp.concatenate([prior_basis, snapshots], axis=0)
-    low, high = halo(stacked, "space", REACH * BLOCK_DOFS)
-    weighted, gram = weigh(prior_basis, snapshots, low, high, mass_factor, neighbours)
-    coefficients, own = compress(first_kernel, total(gram, "space"))
+    weighted, gram = weigh(prior_basis, snapshots, mass_factor, neighbours)
     members = lax.axis_size("tm")
+    places = members * lax.axis_size("space")
+    across = [1 << i for i in range(members.bit_length() - 1, places.bit_length() - 1)]
+    coefficients, own = compress(first_kernel, total(gram, across))
     member = lax.axis_index("tm")
     width = stacked.shape[1] // members
     for level in range(members.bit_length() - 1):
@@ -253,14 +328,14 @@
         bit = member // step % 2
         upper_half = bit == 1
         weighted = combine(coefficients, weighted)
-        sent = swapped(shared_out(weighted, width, 1 - bit), "tm", step)
-        partner_own = swapped(own, "tm", step)
+        sent = swapped(shared_out(weighted, width, 1 - bit), step)
+        partner_own = swapped(own, step)
         weighted = ordered(upper_half, shared_out(weighted, width, bit), sent)
         stacked = combine(coefficients, stacked)
-        sent = swapped(shared_out(stacked, width, 1 - bit), "tm", step)
+        sent = swapped(shared_out(stacked, width, 1 - bit), step)
         stacked = ordered(upper_half, shared_out(stacked, width, bit), sent)
         top = lax.dot_general(weighted[:RANK], weighted, NT, preferred_element_type=F32)
-        top = total(total(top, "tm", 2 * step), "space")
+        top = total(top, [1 << i for i in range(level + 1)] + across)
         coefficients, own = compress(merge_kernel, top, jnp.where(upper_half, own, partner_own))
     return combine(coefficients, stacked), combine(coefficients, weighted)
 

time: 124 us -> 123 us (level)
  waiting for transfers between devices: 37.7 us -> 26 us
  Pallas kernels: 42.9 us -> 48.9 us
  starting transfers between devices: 29.3 us -> 33 us
  other arithmetic: 0.83 us -> 2.42 us
  local copies, waits for them, and re-layouts: 6.75 us -> 5.18 us
    ppermute x18 -> x23, waiting for transfers between devices: 32.6 us -> 26 us  [swapped(): return lax.ppermute(block, axes, [(i, i ^ mask) for i in range(count)])]
    pallas_call x1 -> x2, Pallas kernels: 9.48 us -> 15.5 us  [the longest x1 10.1 us: weigh(): pl.pallas_call(functools.partial(inside_kernel, edge), out_shape=shapes,...]
    ppermute x1, waiting for transfers between devices: 4.14 us -> 0.01 us  [halo(): high = lax.ppermute(block[:, :width], axis, backward)]
    ppermute x18 -> x23, starting transfers between devices: 23.2 us -> 26.9 us  [swapped(): return lax.ppermute(block, axes, [(i, i ^ mask) for i in range(count)])]
    unnamed x15 -> x13, local copies, waits for them, and re-layouts: 6.05 us -> 3.57 us
    add x13 -> x9, other arithmetic: 0.15 us -> 1.59 us  [the longest x5 0.9 us: total(): block = block + near + (far + both)]
  transfers between devices with their start and end apart: 20 -> 25, of which waited for: 17 -> 15; matrix products, arithmetic and copies ran while one was open for 1% -> 3% of each run, Pallas kernels for 9% -> 17%
where the time goes in v3:
time: 123 us; the launch traced here: 122 us
  Pallas kernels  48.9 us (40%)
  starting transfers between devices  33 us (27%)
  waiting for transfers between devices  26 us (21%)
  matrix products  5.68 us (5%)
  local copies, waits for them, and re-layouts  5.18 us (4%)
  other arithmetic  2.42 us (2%)
    pallas_call x3, Pallas kernels, compress(): pl.pallas_call(kernel, out_shape=(jax.ShapeDtypeStruct((RANK, gram[0].sha...  33.4 us
    ppermute x23, starting transfers between devices, swapped(): return lax.ppermute(block, axes, [(i, i ^ mask) for i in range(count)])  26.9 us
    ppermute x23, waiting for transfers between devices, swapped(): return lax.ppermute(block, axes, [(i, i ^ mask) for i in range(count)])  26 us
    pallas_call x1, Pallas kernels, weigh(): pl.pallas_call(functools.partial(inside_kernel, edge), out_shape=shapes,...  10.1 us
    pallas_call x1, Pallas kernels, weigh(): pl.pallas_call(border_kernel, out_shape=shapes, grid_spec=pltpu.PrefetchS...  5.37 us
    dot_general x6, matrix products, combine(): return jnp.dot(coefficients, rows, preferred_element_type=F32).astype(BF16)  4.91 us
    ppermute x1, starting transfers between devices, halo(): low = lax.ppermute(block[:, block.shape[1] - width:], axis, forward)  4.88 us
    unnamed x13, local copies, waits for them, and re-layouts  3.57 us
  transfers between devices with their start and end apart: 25, of which 15 were waited for; matrix products, arithmetic and copies ran while one was open for 3% of the time, Pallas kernels for 17%

profile of v3, /device:TPU:0, one launch (start us, length us, event | category | flops | bytes accessed | tf_op | source)
XLA Modules:
  0.0 122.1 jit_solution(3999654596161218897)
XLA Ops:
  0.7 1.4 %constant_dynamic-update-slice_fusion.1 = bf16[128,8192]{1,0:T(8,128)(2,1)S(1)} fusion(bf16[64,8192]{1,0:T(8,128)(2,1)} %prior_ref.3), kind=kLoop, calls=%fused_computation.36 | loop fusion | bytes 2097152
  2.3 1.4 %copy-done.1 = bf16[128,8192]{1,0:T(8,128)(2,1)} copy-done((bf16[128,8192]{1,0:T(8,128)(2,1)}, bf16[128,8192]{1,0:T(8,128)(2,1)S(1)}, u32[]{:S(2)}) %copy-start.1) | copy-done | bytes 2097176
  3.6 4.9 %collective-permute-start = (bf16[128,512]{1,0:T(8,128)(2,1)S(1)}, bf16[128,512]{1,0:T(8,128)(2,1)S(1)}, u32[]{:S(2)}, u32[]{:S(2)}) collective-permute-start(bf16[128,512]{1,0:T(8,128)(2,1)S(1)} %get-tuple-element.23), channel_id=1, source_target_pairs={{0,4},{4,8},{8,12},{12,16},{16,20},{20,24},{24,28},{1,5},{5,9},{9,... | collective-permute-start | bytes 393224 | tf_op jit(solution)/shard_map/ppermute | solution.py:25
  8.5 1.3 %collective-permute-start.1 = (bf16[128,512]{1,0:T(8,128)(2,1)S(1)}, bf16[128,512]{1,0:T(8,128)(2,1)S(1)}, u32[]{:S(2)}, u32[]{:S(2)}) collective-permute-start(bf16[128,512]{1,0:T(8,128)(2,1)S(1)} %get-tuple-element.22), channel_id=1, source_target_pairs={{4,0},{8,4},{12,8},{16,12},{20,16},{24,20},{28,24},{5,1},{9,5},{13... | collective-permute-start | bytes 393224 | tf_op jit(solution)/shard_map/ppermute | solution.py:26
  11.3 10.1 %weigh_inside.1 = (bf16[128,8192]{1,0:T(8,128)(2,1)}, f32[128,128]{1,0:T(8,128)}) custom-call(s32[896]{0:T(1024)} %reshape.27.spots, bf16[64,8192]{1,0:T(8,128)(2,1)} %prior_ref.3, bf16[64,8192]{1,0:T(8,128)(2,1)} %snap_ref.3, bf16[7,64,8192]{2,1,0:T(8,128)(2,1)} %factor_ref.3), custom_call_target="tpu_custom_call" | custom-call | flops 3758096384 | bytes 7340032 | tf_op jit(solution)/shard_map/weigh_inside/pallas_call | solution.py:149
  22.7 5.4 %weigh_border.1 = (bf16[128,8192]{1,0:T(8,128)(2,1)}, f32[128,128]{1,0:T(8,128)}) custom-call(s32[224]{0:T(256)} %fusion.13.spots, bf16[64,8192]{1,0:T(8,128)(2,1)} %prior_ref.3, bf16[64,8192]{1,0:T(8,128)(2,1)} %snap_ref.3, bf16[128,512]{1,0:T(8,128)(2,1)} %copy-done.3, bf16[128,512]{1,0:T(8,128)(2,1)} %copy-done.4, ...), custom_call_target="tpu_custom_call", output_to_operand_aliasing={{0}: (7, {})} | custom-call | tf_op jit(solution)/shard_map/weigh_border/pallas_call | solution.py:173
  28.1 2.7 %collective-permute-start.2 = (f32[128,128]{1,0:T(8,128)}, f32[128,128]{1,0:T(8,128)S(1)}, u32[]{:S(2)}, u32[]{:S(2)}) collective-permute-start(f32[128,128]{1,0:T(8,128)} %get-tuple-element.13), channel_id=1, source_target_pairs={{0,4},{1,5},{2,6},{3,7},{4,0},{5,1},{6,2},{7,3},{8,12},{9,13},{10,... | collective-permute-start | bytes 196616 | tf_op jit(solution)/shard_map/ppermute | solution.py:33
  30.8 1.6 %collective-permute-start.3 = (f32[128,128]{1,0:T(8,128)}, f32[128,128]{1,0:T(8,128)S(1)}, u32[]{:S(2)}, u32[]{:S(2)}) collective-permute-start(f32[128,128]{1,0:T(8,128)} %get-tuple-element.13), channel_id=1, source_target_pairs={{0,8},{1,9},{2,10},{3,11},{4,12},{5,13},{6,14},{7,15},{8,0},{9,1},... | collective-permute-start | bytes 196616 | tf_op jit(solution)/shard_map/ppermute | solution.py:33
  33.2 2.5 %collective-permute-done.3 = f32[128,128]{1,0:T(8,128)S(1)} collective-permute-done((f32[128,128]{1,0:T(8,128)}, f32[128,128]{1,0:T(8,128)S(1)}, u32[]{:S(2)}, u32[]{:S(2)}) %collective-permute-start.3) | collective-permute-done | bytes 65568 | tf_op jit(solution)/shard_map/ppermute | solution.py:33
  35.8 2.0 %collective-permute-done.4 = f32[128,128]{1,0:T(8,128)S(1)} collective-permute-done((f32[128,128]{1,0:T(8,128)}, f32[128,128]{1,0:T(8,128)S(1)}, u32[]{:S(2)}, u32[]{:S(2)}) %collective-permute-start.4) | collective-permute-done | bytes 65568 | tf_op jit(solution)/shard_map/ppermute | solution.py:33
  38.6 2.6 %collective-permute-start.5 = (f32[128,128]{1,0:T(8,128)S(1)}, f32[128,128]{1,0:T(8,128)S(1)}, u32[]{:S(2)}, u32[]{:S(2)}) collective-permute-start(f32[128,128]{1,0:T(8,128)S(1)} %add_add_fusion), channel_id=1, source_target_pairs={{0,16},{1,17},{2,18},{3,19},{4,20},{5,21},{6,22},{7,23},{8,24},{9,... | collective-permute-start | bytes 196616 | tf_op jit(solution)/shard_map/ppermute | solution.py:33
  41.3 3.3 %collective-permute-done.5 = f32[128,128]{1,0:T(8,128)S(1)} collective-permute-done((f32[128,128]{1,0:T(8,128)S(1)}, f32[128,128]{1,0:T(8,128)S(1)}, u32[]{:S(2)}, u32[]{:S(2)}) %collective-permute-start.5) | collective-permute-done | bytes 65568 | tf_op jit(solution)/shard_map/ppermute | solution.py:33
  44.6 10.9 %compress.3 = (bf16[64,128]{1,0:T(8,128)(2,1)S(1)}, f32[64,64]{1,0:T(8,128)S(1)}) custom-call(f32[128,128]{1,0:T(8,128)S(1)} %add.143.gram_ref), custom_call_target="tpu_custom_call" | custom-call | tf_op jit(solution)/shard_map/compress/pallas_call | solution.py:287
  55.4 2.0 %convolution_convert_fusion = bf16[64,8192]{1,0:T(8,128)(2,1)S(1)} fusion(bf16[64,128]{1,0:T(8,128)(2,1)S(1)} %get-tuple-element.14, bf16[128,8192]{1,0:T(8,128)(2,1)} %copy-done.1), kind=kOutput, calls=%fused_computation | convolution fusion | flops 134742016 | bytes 3162112 | tf_op jit(solution)/shard_map/dot_general | solution.py:300
  58.8 1.4 %collective-permute-done.6 = bf16[64,4096]{1,0:T(8,128)(2,1)S(1)} collective-permute-done((bf16[64,4096]{1,0:T(8,128)(2,1)S(1)}, bf16[64,4096]{1,0:T(8,128)(2,1)S(1)}, u32[]{:S(2)}, u32[]{:S(2)}) %collective-permute-start.6) | collective-permute-done | bytes 524320 | tf_op jit(solution)/shard_map/ppermute | solution.py:33
  61.1 1.0 collective-permute-start.8
  63.3 1.7 %collective-permute-done.8 = f32[64,128]{1,0:T(8,128)S(1)} collective-permute-done((f32[64,128]{1,0:T(8,128)S(1)}, f32[64,128]{1,0:T(8,128)S(1)}, u32[]{:S(2)}, u32[]{:S(2)}) %collective-permute-start.8) | collective-permute-done | bytes 32800 | tf_op jit(solution)/shard_map/ppermute | solution.py:33
  65.7 2.7 %collective-permute-start.11 = (f32[64,128]{1,0:T(8,128)S(1)}, f32[64,128]{1,0:T(8,128)S(1)}, u32[]{:S(2)}, u32[]{:S(2)}) collective-permute-start(f32[64,128]{1,0:T(8,128)S(1)} %add_add_fusion.4), channel_id=1, source_target_pairs={{0,16},{1,17},{2,18},{3,19},{4,20},{5,21},{6,22},{7,23},{8,24},{9,... | collective-permute-start | bytes 98312 | tf_op jit(solution)/shard_map/ppermute | solution.py:33
  68.4 1.6 %collective-permute-start.12 = (f32[64,128]{1,0:T(8,128)S(1)}, f32[64,128]{1,0:T(8,128)S(1)}, u32[]{:S(2)}, u32[]{:S(2)}) collective-permute-start(f32[64,128]{1,0:T(8,128)S(1)} %add_add_fusion.4), channel_id=1, source_target_pairs={{0,24},{1,25},{2,26},{3,27},{4,28},{5,29},{6,30},{7,31},{8,16},{9,... | collective-permute-start | bytes 98312 | tf_op jit(solution)/shard_map/ppermute | solution.py:33
  70.5 3.6 %collective-permute-done.12 = f32[64,128]{1,0:T(8,128)S(1)} collective-permute-done((f32[64,128]{1,0:T(8,128)S(1)}, f32[64,128]{1,0:T(8,128)S(1)}, u32[]{:S(2)}, u32[]{:S(2)}) %collective-permute-start.12) | collective-permute-done | bytes 32800 | tf_op jit(solution)/shard_map/ppermute | solution.py:33
  74.1 11.0 %compress.4 = (bf16[64,128]{1,0:T(8,128)(2,1)S(1)}, f32[64,64]{1,0:T(8,128)S(1)}) custom-call(f32[64,128]{1,0:T(8,128)S(1)} %add_add_fusion.3.top_ref, f32[64,64]{1,0:T(8,128)S(1)} %broadcast_select_fusion.9.upper_ref), custom_call_target="tpu_custom_call" | custom-call | tf_op jit(solution)/shard_map/compress/pallas_call | solution.py:287
  85.4 1.6 %collective-permute-start.14 = (bf16[64,2048]{1,0:T(8,128)(2,1)S(1)}, bf16[64,2048]{1,0:T(8,128)(2,1)S(1)}, u32[]{:S(2)}, u32[]{:S(2)}) collective-permute-start(bf16[64,2048]{1,0:T(8,128)(2,1)S(1)} %constant_dynamic-slice_fusion.5), channel_id=1, source_target_pairs={{0,2},{1,3},{2,0},{3,1},{4,6},{5,7},{6,4},{7,5},{8,10},{9,11},{10,... | collective-permute-start | bytes 786440 | tf_op jit(solution)/shard_map/ppermute | solution.py:33
  88.1 4.4 %collective-permute-done.14 = bf16[64,2048]{1,0:T(8,128)(2,1)S(1)} collective-permute-done((bf16[64,2048]{1,0:T(8,128)(2,1)S(1)}, bf16[64,2048]{1,0:T(8,128)(2,1)S(1)}, u32[]{:S(2)}, u32[]{:S(2)}) %collective-permute-start.14) | collective-permute-done | bytes 262176 | tf_op jit(solution)/shard_map/ppermute | solution.py:33
  92.9 1.6 %collective-permute-start.16 = (f32[64,128]{1,0:T(8,128)S(1)}, f32[64,128]{1,0:T(8,128)S(1)}, u32[]{:S(2)}, u32[]{:S(2)}) collective-permute-start(f32[64,128]{1,0:T(8,128)S(1)} %fusion.7), channel_id=1, source_target_pairs={{0,2},{1,3},{2,0},{3,1},{4,6},{5,7},{6,4},{7,5},{8,10},{9,11},{10,... | collective-permute-start | bytes 98312 | tf_op jit(solution)/shard_map/ppermute | solution.py:33
  94.8 1.6 %collective-permute-start.24 = (bf16[64,2048]{1,0:T(8,128)(2,1)S(1)}, bf16[64,2048]{1,0:T(8,128)(2,1)S(1)}, u32[]{:S(2)}, u32[]{:S(2)}) collective-permute-start(bf16[64,2048]{1,0:T(8,128)(2,1)S(1)} %constant_dynamic-slice_fusion), channel_id=1, source_target_pairs={{0,2},{1,3},{2,0},{3,1},{4,6},{5,7},{6,4},{7,5},{8,10},{9,11},{10,... | collective-permute-start | bytes 786440 | tf_op jit(solution)/shard_map/ppermute | solution.py:33
  96.9 0.9 collective-permute-done.17
  97.9 1.1 collective-permute-start.18
  99.0 2.4 %collective-permute-start.20 = (f32[64,128]{1,0:T(8,128)S(1)}, f32[64,128]{1,0:T(8,128)S(1)}, u32[]{:S(2)}, u32[]{:S(2)}) collective-permute-start(f32[64,128]{1,0:T(8,128)S(1)} %add_add_fusion.2), channel_id=1, source_target_pairs={{0,12},{1,13},{2,14},{3,15},{4,8},{5,9},{6,10},{7,11},{8,4},{9,5},... | collective-permute-start | bytes 98312 | tf_op jit(solution)/shard_map/ppermute | solution.py:33
  101.8 1.1 collective-permute-done.19
  103.8 2.5 %collective-permute-start.21 = (f32[64,128]{1,0:T(8,128)S(1)}, f32[64,128]{1,0:T(8,128)S(1)}, u32[]{:S(2)}, u32[]{:S(2)}) collective-permute-start(f32[64,128]{1,0:T(8,128)S(1)} %add_add_fusion.1), channel_id=1, source_target_pairs={{0,16},{1,17},{2,18},{3,19},{4,20},{5,21},{6,22},{7,23},{8,24},{9,... | collective-permute-start | bytes 98312 | tf_op jit(solution)/shard_map/ppermute | solution.py:33
  106.4 2.3 %collective-permute-done.21 = f32[64,128]{1,0:T(8,128)S(1)} collective-permute-done((f32[64,128]{1,0:T(8,128)S(1)}, f32[64,128]{1,0:T(8,128)S(1)}, u32[]{:S(2)}, u32[]{:S(2)}) %collective-permute-start.21) | collective-permute-done | bytes 32800 | tf_op jit(solution)/shard_map/ppermute | solution.py:33
  108.7 11.6 %compress.5 = (bf16[64,128]{1,0:T(8,128)(2,1)S(1)}, f32[64,64]{1,0:T(8,128)}) custom-call(f32[64,128]{1,0:T(8,128)S(1)} %add.164.top_ref, f32[64,64]{1,0:T(8,128)S(1)} %broadcast_select_fusion.8.upper_ref), custom_call_target="tpu_custom_call" | custom-call | tf_op jit(solution)/shard_map/compress/pallas_call | solution.py:287
  (75 shorter events, 15.3 us)
Async XLA Ops:
  0.6 1.5 %copy-start.2 = (bf16[64,8192]{1,0:T(8,128)(2,1)S(1)}, bf16[64,8192]{1,0:T(8,128)(2,1)}, u32[]{:S(2)}) copy-start(bf16[64,8192]{1,0:T(8,128)(2,1)} %snap_ref.3) | copy-start | bytes 3145732
  0.6 9.2 %copy-start.5 = (s32[128,7]{0,1:T(8,128)S(1)}, s32[128,7]{0,1:T(8,128)}, u32[]{:S(2)}) copy-start(s32[128,7]{0,1:T(8,128)} %param.7) | copy-start | bytes 10756
  2.2 1.4 %copy-start.1 = (bf16[128,8192]{1,0:T(8,128)(2,1)}, bf16[128,8192]{1,0:T(8,128)(2,1)S(1)}, u32[]{:S(2)}) copy-start(bf16[128,8192]{1,0:T(8,128)(2,1)S(1)} %constant_dynamic-update-slice_fusion) | copy-start | bytes 6291460
  3.6 18.4 %collective-permute-start = (bf16[128,512]{1,0:T(8,128)(2,1)S(1)}, bf16[128,512]{1,0:T(8,128)(2,1)S(1)}, u32[]{:S(2)}, u32[]{:S(2)}) collective-permute-start(bf16[128,512]{1,0:T(8,128)(2,1)S(1)} %get-tuple-element.23), channel_id=1, source_target_pairs={{0,4},{4,8},{8,12},{12,16},{16,20},{20,24},{24,28},{1,5},{5,9},{9,... | collective-permute-start | bytes 393224 | tf_op jit(solution)/shard_map/ppermute | solution.py:25
  8.5 13.5 %collective-permute-start.1 = (bf16[128,512]{1,0:T(8,128)(2,1)S(1)}, bf16[128,512]{1,0:T(8,128)(2,1)S(1)}, u32[]{:S(2)}, u32[]{:S(2)}) collective-permute-start(bf16[128,512]{1,0:T(8,128)(2,1)S(1)} %get-tuple-element.22), channel_id=1, source_target_pairs={{4,0},{8,4},{12,8},{16,12},{20,16},{24,20},{28,24},{5,1},{9,5},{13... | collective-permute-start | bytes 393224 | tf_op jit(solution)/shard_map/ppermute | solution.py:26
  22.0 0.7 copy-start.3
  22.0 0.7 copy-start.4
  28.1 29.4 %copy-start = (bf16[128,8192]{1,0:T(8,128)(2,1)S(1)}, bf16[128,8192]{1,0:T(8,128)(2,1)}, u32[]{:S(2)}) copy-start(bf16[128,8192]{1,0:T(8,128)(2,1)} %get-tuple-element.15) | copy-start | bytes 6291460
  28.1 5.2 %collective-permute-start.2 = (f32[128,128]{1,0:T(8,128)}, f32[128,128]{1,0:T(8,128)S(1)}, u32[]{:S(2)}, u32[]{:S(2)}) collective-permute-start(f32[128,128]{1,0:T(8,128)} %get-tuple-element.13), channel_id=1, source_target_pairs={{0,4},{1,5},{2,6},{3,7},{4,0},{5,1},{6,2},{7,3},{8,12},{9,13},{10,... | collective-permute-start | bytes 196616 | tf_op jit(solution)/shard_map/ppermute | solution.py:33
  30.8 5.0 %collective-permute-start.3 = (f32[128,128]{1,0:T(8,128)}, f32[128,128]{1,0:T(8,128)S(1)}, u32[]{:S(2)}, u32[]{:S(2)}) collective-permute-start(f32[128,128]{1,0:T(8,128)} %get-tuple-element.13), channel_id=1, source_target_pairs={{0,8},{1,9},{2,10},{3,11},{4,12},{5,13},{6,14},{7,15},{8,0},{9,1},... | collective-permute-start | bytes 196616 | tf_op jit(solution)/shard_map/ppermute | solution.py:33
  32.4 5.4 %collective-permute-start.4 = (f32[128,128]{1,0:T(8,128)}, f32[128,128]{1,0:T(8,128)S(1)}, u32[]{:S(2)}, u32[]{:S(2)}) collective-permute-start(f32[128,128]{1,0:T(8,128)} %get-tuple-element.13), channel_id=1, source_target_pairs={{0,12},{1,13},{2,14},{3,15},{4,8},{5,9},{6,10},{7,11},{8,4},{9,5},... | collective-permute-start | bytes 196616 | tf_op jit(solution)/shard_map/ppermute | solution.py:33
  38.6 5.9 %collective-permute-start.5 = (f32[128,128]{1,0:T(8,128)S(1)}, f32[128,128]{1,0:T(8,128)S(1)}, u32[]{:S(2)}, u32[]{:S(2)}) collective-permute-start(f32[128,128]{1,0:T(8,128)S(1)} %add_add_fusion), channel_id=1, source_target_pairs={{0,16},{1,17},{2,18},{3,19},{4,20},{5,21},{6,22},{7,23},{8,24},{9,... | collective-permute-start | bytes 196616 | tf_op jit(solution)/shard_map/ppermute | solution.py:33
  58.2 2.0 %collective-permute-start.6 = (bf16[64,4096]{1,0:T(8,128)(2,1)S(1)}, bf16[64,4096]{1,0:T(8,128)(2,1)S(1)}, u32[]{:S(2)}, u32[]{:S(2)}) collective-permute-start(bf16[64,4096]{1,0:T(8,128)(2,1)S(1)} %pad_maximum_fusion.3), channel_id=1, source_target_pairs={{0,1},{1,0},{2,3},{3,2},{4,5},{5,4},{6,7},{7,6},{8,9},{9,8},{10,11... | collective-permute-start | bytes 1572872 | tf_op jit(solution)/shard_map/ppermute | solution.py:33
  58.3 11.7 %collective-permute-start.13 = (f32[64,64]{1,0:T(8,128)S(1)}, f32[64,64]{1,0:T(8,128)S(1)}, u32[]{:S(2)}, u32[]{:S(2)}) collective-permute-start(f32[64,64]{1,0:T(8,128)S(1)} %get-tuple-element.16), channel_id=1, source_target_pairs={{0,1},{1,0},{2,3},{3,2},{4,5},{5,4},{6,7},{7,6},{8,9},{9,8},{10,11... | collective-permute-start | bytes 49160 | tf_op jit(solution)/shard_map/ppermute | solution.py:33
  60.9 2.5 %collective-permute-start.7 = (f32[64,128]{1,0:T(8,128)S(1)}, f32[64,128]{1,0:T(8,128)S(1)}, u32[]{:S(2)}, u32[]{:S(2)}) collective-permute-start(f32[64,128]{1,0:T(8,128)S(1)} %fusion.3), channel_id=1, source_target_pairs={{0,1},{1,0},{2,3},{3,2},{4,5},{5,4},{6,7},{7,6},{8,9},{9,8},{10,11... | collective-permute-start | bytes 98312 | tf_op jit(solution)/shard_map/ppermute | solution.py:33
  61.1 3.9 %collective-permute-start.8 = (f32[64,128]{1,0:T(8,128)S(1)}, f32[64,128]{1,0:T(8,128)S(1)}, u32[]{:S(2)}, u32[]{:S(2)}) collective-permute-start(f32[64,128]{1,0:T(8,128)S(1)} %fusion.3), channel_id=1, source_target_pairs={{0,4},{1,5},{2,6},{3,7},{4,0},{5,1},{6,2},{7,3},{8,12},{9,13},{10,... | collective-permute-start | bytes 98312 | tf_op jit(solution)/shard_map/ppermute | solution.py:33
  62.1 3.4 %collective-permute-start.9 = (f32[64,128]{1,0:T(8,128)S(1)}, f32[64,128]{1,0:T(8,128)S(1)}, u32[]{:S(2)}, u32[]{:S(2)}) collective-permute-start(f32[64,128]{1,0:T(8,128)S(1)} %fusion.3), channel_id=1, source_target_pairs={{0,5},{1,4},{2,7},{3,6},{4,1},{5,0},{6,3},{7,2},{8,13},{9,12},{10,... | collective-permute-start | bytes 98312 | tf_op jit(solution)/shard_map/ppermute | solution.py:33
  62.8 24.1 %collective-permute-start.23 = (bf16[64,4096]{1,0:T(8,128)(2,1)S(1)}, bf16[64,4096]{1,0:T(8,128)(2,1)S(1)}, u32[]{:S(2)}, u32[]{:S(2)}) collective-permute-start(bf16[64,4096]{1,0:T(8,128)(2,1)S(1)} %pad_maximum_fusion.6), channel_id=1, source_target_pairs={{0,1},{1,0},{2,3},{3,2},{4,5},{5,4},{6,7},{7,6},{8,9},{9,8},{10,11... | collective-permute-start | bytes 1572872 | tf_op jit(solution)/shard_map/ppermute | solution.py:33
  65.5 4.5 %collective-permute-start.10 = (f32[64,128]{1,0:T(8,128)S(1)}, f32[64,128]{1,0:T(8,128)S(1)}, u32[]{:S(2)}, u32[]{:S(2)}) collective-permute-start(f32[64,128]{1,0:T(8,128)S(1)} %add_add_fusion.4), channel_id=1, source_target_pairs={{0,8},{1,9},{2,10},{3,11},{4,12},{5,13},{6,14},{7,15},{8,0},{9,1},... | collective-permute-start | bytes 98312 | tf_op jit(solution)/shard_map/ppermute | solution.py:33
  65.7 4.8 %collective-permute-start.11 = (f32[64,128]{1,0:T(8,128)S(1)}, f32[64,128]{1,0:T(8,128)S(1)}, u32[]{:S(2)}, u32[]{:S(2)}) collective-permute-start(f32[64,128]{1,0:T(8,128)S(1)} %add_add_fusion.4), channel_id=1, source_target_pairs={{0,16},{1,17},{2,18},{3,19},{4,20},{5,21},{6,22},{7,23},{8,24},{9,... | collective-permute-start | bytes 98312 | tf_op jit(solution)/shard_map/ppermute | solution.py:33
  68.4 5.7 %collective-permute-start.12 = (f32[64,128]{1,0:T(8,128)S(1)}, f32[64,128]{1,0:T(8,128)S(1)}, u32[]{:S(2)}, u32[]{:S(2)}) collective-permute-start(f32[64,128]{1,0:T(8,128)S(1)} %add_add_fusion.4), channel_id=1, source_target_pairs={{0,24},{1,25},{2,26},{3,27},{4,28},{5,29},{6,30},{7,31},{8,16},{9,... | collective-permute-start | bytes 98312 | tf_op jit(solution)/shard_map/ppermute | solution.py:33
  85.4 7.0 %collective-permute-start.14 = (bf16[64,2048]{1,0:T(8,128)(2,1)S(1)}, bf16[64,2048]{1,0:T(8,128)(2,1)S(1)}, u32[]{:S(2)}, u32[]{:S(2)}) collective-permute-start(bf16[64,2048]{1,0:T(8,128)(2,1)S(1)} %constant_dynamic-slice_fusion.5), channel_id=1, source_target_pairs={{0,2},{1,3},{2,0},{3,1},{4,6},{5,7},{6,4},{7,5},{8,10},{9,11},{10,... | collective-permute-start | bytes 786440 | tf_op jit(solution)/shard_map/ppermute | solution.py:33
  87.2 14.2 %collective-permute-start.22 = (f32[64,64]{1,0:T(8,128)S(1)}, f32[64,64]{1,0:T(8,128)S(1)}, u32[]{:S(2)}, u32[]{:S(2)}) collective-permute-start(f32[64,64]{1,0:T(8,128)S(1)} %get-tuple-element.18), channel_id=1, source_target_pairs={{0,2},{1,3},{2,0},{3,1},{4,6},{5,7},{6,4},{7,5},{8,10},{9,11},{10,... | collective-permute-start | bytes 49160 | tf_op jit(solution)/shard_map/ppermute | solution.py:33
  92.9 3.5 %collective-permute-start.15 = (f32[64,128]{1,0:T(8,128)S(1)}, f32[64,128]{1,0:T(8,128)S(1)}, u32[]{:S(2)}, u32[]{:S(2)}) collective-permute-start(f32[64,128]{1,0:T(8,128)S(1)} %fusion.7), channel_id=1, source_target_pairs={{0,1},{1,0},{2,3},{3,2},{4,5},{5,4},{6,7},{7,6},{8,9},{9,8},{10,11... | collective-permute-start | bytes 98312 | tf_op jit(solution)/shard_map/ppermute | solution.py:33
  92.9 4.0 %collective-permute-start.16 = (f32[64,128]{1,0:T(8,128)S(1)}, f32[64,128]{1,0:T(8,128)S(1)}, u32[]{:S(2)}, u32[]{:S(2)}) collective-permute-start(f32[64,128]{1,0:T(8,128)S(1)} %fusion.7), channel_id=1, source_target_pairs={{0,2},{1,3},{2,0},{3,1},{4,6},{5,7},{6,4},{7,5},{8,10},{9,11},{10,... | collective-permute-start | bytes 98312 | tf_op jit(solution)/shard_map/ppermute | solution.py:33
  94.5 3.3 %collective-permute-start.17 = (f32[64,128]{1,0:T(8,128)S(1)}, f32[64,128]{1,0:T(8,128)S(1)}, u32[]{:S(2)}, u32[]{:S(2)}) collective-permute-start(f32[64,128]{1,0:T(8,128)S(1)} %fusion.7), channel_id=1, source_target_pairs={{0,3},{1,2},{2,1},{3,0},{4,7},{5,6},{6,5},{7,4},{8,11},{9,10},{10,... | collective-permute-start | bytes 98312 | tf_op jit(solution)/shard_map/ppermute | solution.py:33
  94.8 11.5 %collective-permute-start.24 = (bf16[64,2048]{1,0:T(8,128)(2,1)S(1)}, bf16[64,2048]{1,0:T(8,128)(2,1)S(1)}, u32[]{:S(2)}, u32[]{:S(2)}) collective-permute-start(bf16[64,2048]{1,0:T(8,128)(2,1)S(1)} %constant_dynamic-slice_fusion), channel_id=1, source_target_pairs={{0,2},{1,3},{2,0},{3,1},{4,6},{5,7},{6,4},{7,5},{8,10},{9,11},{10,... | collective-permute-start | bytes 786440 | tf_op jit(solution)/shard_map/ppermute | solution.py:33
  97.9 4.0 %collective-permute-start.18 = (f32[64,128]{1,0:T(8,128)S(1)}, f32[64,128]{1,0:T(8,128)S(1)}, u32[]{:S(2)}, u32[]{:S(2)}) collective-permute-start(f32[64,128]{1,0:T(8,128)S(1)} %add_add_fusion.2), channel_id=1, source_target_pairs={{0,4},{1,5},{2,6},{3,7},{4,0},{5,1},{6,2},{7,3},{8,12},{9,13},{10,... | collective-permute-start | bytes 98312 | tf_op jit(solution)/shard_map/ppermute | solution.py:33
  99.0 3.9 %collective-permute-start.19 = (f32[64,128]{1,0:T(8,128)S(1)}, f32[64,128]{1,0:T(8,128)S(1)}, u32[]{:S(2)}, u32[]{:S(2)}) collective-permute-start(f32[64,128]{1,0:T(8,128)S(1)} %add_add_fusion.2), channel_id=1, source_target_pairs={{0,8},{1,9},{2,10},{3,11},{4,12},{5,13},{6,14},{7,15},{8,0},{9,1},... | collective-permute-start | bytes 98312 | tf_op jit(solution)/shard_map/ppermute | solution.py:33
  99.0 4.8 %collective-permute-start.20 = (f32[64,128]{1,0:T(8,128)S(1)}, f32[64,128]{1,0:T(8,128)S(1)}, u32[]{:S(2)}, u32[]{:S(2)}) collective-permute-start(f32[64,128]{1,0:T(8,128)S(1)} %add_add_fusion.2), channel_id=1, source_target_pairs={{0,12},{1,13},{2,14},{3,15},{4,8},{5,9},{6,10},{7,11},{8,4},{9,5},... | collective-permute-start | bytes 98312 | tf_op jit(solution)/shard_map/ppermute | solution.py:33
  103.8 4.9 %collective-permute-start.21 = (f32[64,128]{1,0:T(8,128)S(1)}, f32[64,128]{1,0:T(8,128)S(1)}, u32[]{:S(2)}, u32[]{:S(2)}) collective-permute-start(f32[64,128]{1,0:T(8,128)S(1)} %add_add_fusion.1), channel_id=1, source_target_pairs={{0,16},{1,17},{2,18},{3,19},{4,20},{5,21},{6,22},{7,23},{8,24},{9,... | collective-permute-start | bytes 98312 | tf_op jit(solution)/shard_map/ppermute | solution.py:33

commit v4 on v3

--- a/solution.py
+++ b/solution.py
@@ -18,12 +18,14 @@
 NT = (((1,), (1,)), ((), ()))
 
 
-def halo(block, axis, width):
+def halo(parts, axis, width):
     count = lax.axis_size(axis)
     forward = [(i, i + 1) for i in range(count - 1)]
     backward = [(target, source) for source, target in forward]
-    low = lax.ppermute(block[:, block.shape[1] - width:], axis, forward)
-    high = lax.ppermute(block[:, :width], axis, backward)
+    last = jnp.concatenate([part[:, part.shape[1] - width:] for part in parts], axis=0)
+    first = jnp.concatenate([part[:, :width] for part in parts], axis=0)
+    low = lax.ppermute(last, axis, forward)
+    high = lax.ppermute(first, axis, backward)
     return low, high
 
 
@@ -49,17 +51,24 @@
     bank[:, whole + start + TILE:whole + stop] = bank[:, start + block:stop - block]
 
 
-def weigh_chunk(spots, row, bank, factor_ref):
+def weigh_chunk(neighbours_ref, row, shift, bank, factor_ref):
     neighbours, block, chunk = factor_ref.shape
     columns = bank.shape[0]
+    tiles = (bank.shape[1] - TILE) // (2 * TILE)
     lower = lax.broadcasted_iota(jnp.int32, (columns, TILE), 1) < block
+
+    def spot_of(k, line):
+        place = neighbours_ref[k, line] - shift
+        odd = place & 1
+        return (place >> 1) + (odd * (tiles + 1) if k % 2 == 0 else (1 - odd) * tiles)
+
     pieces = []
     for tile in range(chunk // TILE):
         results = []
         for side in range(2):
             parts = []
             for k in range(neighbours):
-                spot = spots[(row + tile * 2 + side) * neighbours + k]
+                spot = spot_of(k, row + tile * 2 + side)
                 parts.append(bank[:, pl.ds(pl.multiple_of(spot * TILE, TILE), TILE)])
             joined = [jnp.where(lower, parts[k], parts[k + 1]) for k in range(0, neighbours - 1, 2)]
             if neighbours % 2:
@@ -85,13 +94,14 @@
         fill_odd(bank, whole, block, edge, edge + width)
         gram_ref[...] = jnp.zeros_like(gram_ref)
 
-    weighted = weigh_chunk(spots, (step + 1) * (chunk // block), bank, factor_ref)
+    shift = lax.axis_index("space") * (width // block) - edge // block
+    weighted = weigh_chunk(spots, (step + 1) * (chunk // block), shift, bank, factor_ref)
     weighted_ref[...] = weighted
     gram_ref[...] += lax.dot_general(weighted, weighted, NT, preferred_element_type=F32)
 
 
 def border_kernel(
-    spots, prior_ref, snap_ref, low_ref, high_ref, factor_ref, part_ref, kept_ref, weighted_ref, gram_ref, bank
+    width, spots, prior_ref, snap_ref, low_ref, high_ref, factor_ref, part_ref, kept_ref, weighted_ref, gram_ref, bank
 ):
     step = pl.program_id(0)
     rows, span = prior_ref.shape
@@ -115,16 +125,10 @@
     fill_odd(bank, whole, block, 0, whole)
     bank[:, whole + block:whole + TILE] = bank[:, :block]
     bank[:, 2 * whole:2 * whole + block] = bank[:, whole - block:whole]
-    weighted = weigh_chunk(spots, step * (chunk // block), bank, factor_ref)
+    shift = lax.axis_index("space") * (width // block) - edge // block + step * ((width + 2 * edge - whole) // block)
+    weighted = weigh_chunk(spots, step * ((width - chunk) // block), shift, bank, factor_ref)
     weighted_ref[...] = weighted
     gram_ref[...] += lax.dot_general(weighted, weighted, NT, preferred_element_type=F32)
-
-
-def spots_of(local, tiles):
-    half, odd = local // 2, local % 2
-    side = jnp.arange(local.shape[1], dtype=jnp.int32)[None, :] % 2
-    spots = half + jnp.where(side == 0, odd * (tiles + 1), (1 - odd) * tiles)
-    return spots.reshape(-1).astype(jnp.int32)
 
 
 def weigh(prior, snapshots, factor, neighbours):
@@ -135,11 +139,8 @@
     chunk = 2 * edge
     span = 2 * chunk
     chunks = width // chunk
-    low, high = halo(jnp.concatenate([prior, snapshots], axis=0), "space", edge)
-    local = neighbours - (lax.axis_index("space") * (width // block) - REACH)
-    per = chunk // block
-    shift = (width - span + edge) // block
-    near = jnp.concatenate([local[:per], local[-per:] - shift], axis=0)
+    low, high = halo((prior, snapshots), "space", edge)
+    spots = neighbours.T
     full = lambda i, s: (0, 0)
     shapes = (
         jax.ShapeDtypeStruct((columns, width), BF16),
@@ -168,10 +169,10 @@
             flops=8 * columns * count * block * width, bytes_accessed=2 * factor.size, transcendentals=0
         ),
         name="weigh_inside",
-    )(spots_of(local, (width + 2 * edge) // TILE), prior, snapshots, factor)
+    )(spots, prior, snapshots, factor)
     ends = width // span - 1
     return pl.pallas_call(
-        border_kernel,
+        functools.partial(border_kernel, width),
         out_shape=shapes,
         grid_spec=pltpu.PrefetchScalarGridSpec(
             num_scalar_prefetch=1,
@@ -194,7 +195,7 @@
         input_output_aliases={7: 0},
         compiler_params=params,
         name="weigh_border",
-    )(spots_of(near, (span + edge) // TILE), prior, snapshots, low, high, factor, gram, weighted)
+    )(spots, prior, snapshots, low, high, factor, gram, weighted)
 
 
 def lanes_of(group, column):
@@ -209,9 +210,9 @@
     groups = left.shape[0]
     sub = lax.broadcasted_iota(jnp.int32, (PANEL, TILE), 0)
 
-    def panel(p, _):
+    for p in range(groups):
         pivot, image = left[p], right[p]
-        cols = [lanes_of(pivot, s) for s in range(PANEL)]
+        cols = [lanes_of(pivot, PANEL * p + s) for s in range(PANEL)]
         d = [[row_of(cols[c], r) if r >= c else None for c in range(PANEL)] for r in range(PANEL)]
         rows_a = [row_of(pivot, r) for r in range(PANEL)]
         rows_n = [row_of(image, r) for r in range(PANEL)]
@@ -224,24 +225,21 @@
                     d[r][c] = d[r][c] - m * d[c][s]
                 rows_a[r] = rows_a[r] - m * rows_a[s]
                 rows_n[r] = rows_n[r] - m * rows_n[s]
-        for q in range(groups):
+        for q in range(p + 1, groups):
             fresh_a, fresh_n = left[q], right[q]
-            work = [lanes_of(fresh_a, s) for s in range(PANEL)]
+            work = [lanes_of(fresh_a, PANEL * p + s) for s in range(PANEL)]
             for s in range(PANEL):
                 factor = work[s] * inverse[s]
                 for c in range(s + 1, PANEL):
                     work[c] = work[c] - factor * d[c][s]
                 fresh_a = fresh_a - factor * rows_a[s]
                 fresh_n = fresh_n - factor * rows_n[s]
-            left[q] = pltpu.roll(fresh_a, TILE - PANEL, 1)
+            left[q] = fresh_a
             right[q] = fresh_n
         merged = rows_n[0] * lax.rsqrt(d[0][0])
         for r in range(1, PANEL):
             merged = jnp.where(sub == r, rows_n[r] * lax.rsqrt(d[r][r]), merged)
         solved[p] = merged
-        return 0
-
-    lax.fori_loop(0, groups, panel, 0)
 
 
 def reduce_gram(gram, left, right, solved):
@@ -274,13 +272,13 @@
     own_ref[...] = inner_of(coefficients, gram)
 
 
-def merge_kernel(top_ref, upper_ref, out_ref, own_ref, left, right, solved):
+def merge_kernel(last, top_ref, upper_ref, out_ref, own_ref, left, right, solved):
     top = top_ref[...]
     bottom = jnp.concatenate([top.T[RANK:], upper_ref[...]], axis=1)
     gram = jnp.concatenate([top, bottom], axis=0)
     coefficients = reduce_gram(gram, left, right, solved)
     out_ref[...] = coefficients
-    own_ref[...] = inner_of(coefficients, gram)
+    own_ref[...] = upper_ref[...] if last else inner_of(coefficients, gram)
 
 
 def compress(kernel, *gram):
@@ -300,6 +298,14 @@
     return jnp.dot(coefficients, rows, preferred_element_type=F32).astype(BF16)
 
 
+def combine_two(coefficients, first, second):
+    rows = first.shape[0]
+    return (
+        jnp.dot(coefficients[:, :rows], first, preferred_element_type=F32)
+        + jnp.dot(coefficients[:, rows:], second, preferred_element_type=F32)
+    ).astype(BF16)
+
+
 def shared_out(rows, width, bit):
     pieces = [
         lax.dynamic_slice_in_dim(rows, (2 * pair + bit) * width, width, 1)
@@ -315,14 +321,13 @@
 
 
 def shards(snapshots, prior_basis, mass_factor, neighbours):
-    stacked = jnp.concatenate([prior_basis, snapshots], axis=0)
     weighted, gram = weigh(prior_basis, snapshots, mass_factor, neighbours)
     members = lax.axis_size("tm")
     places = members * lax.axis_size("space")
     across = [1 << i for i in range(members.bit_length() - 1, places.bit_length() - 1)]
     coefficients, own = compress(first_kernel, total(gram, across))
     member = lax.axis_index("tm")
-    width = stacked.shape[1] // members
+    width = snapshots.shape[1] // members
     for level in range(members.bit_length() - 1):
         step = 1 << level
         bit = member // step % 2
@@ -331,12 +336,15 @@
         sent = swapped(shared_out(weighted, width, 1 - bit), step)
         partner_own = swapped(own, step)
         weighted = ordered(upper_half, shared_out(weighted, width, bit), sent)
-        stacked = combine(coefficients, stacked)
+        if level == 0:
+            stacked = combine_two(coefficients, prior_basis, snapshots)
+        else:
+            stacked = combine(coefficients, stacked)
         sent = swapped(shared_out(stacked, width, 1 - bit), step)
         stacked = ordered(upper_half, shared_out(stacked, width, bit), sent)
         top = lax.dot_general(weighted[:RANK], weighted, NT, preferred_element_type=F32)
         top = total(top, [1 << i for i in range(level + 1)] + across)
-        coefficients, own = compress(merge_kernel, top, jnp.where(upper_half, own, partner_own))
+        coefficients, own = compress(functools.partial(merge_kernel, 2 * step == members), top, jnp.where(upper_half, own, partner_own))
     return combine(coefficients, stacked), combine(coefficients, weighted)
 
 

time: 123 us -> 109 us (0.89)
  Pallas kernels: 48.9 us -> 40.2 us
  local copies, waits for them, and re-layouts: 5.18 us -> 2.38 us
  waiting for transfers between devices: 26 us -> 27.5 us
    pallas_call x3, Pallas kernels: 33.4 us -> 24.5 us  [compress(): pl.pallas_call(kernel, out_shape=(jax.ShapeDtypeStruct((RANK, gram[0].sha...]
    unnamed x13 -> x10, local copies, waits for them, and re-layouts: 3.57 us -> 1.15 us
    dot_general x6 -> x5, matrix products: 4.91 us -> 2.88 us  [combine(): return jnp.dot(coefficients, rows, preferred_element_type=F32).astype(BF16)]
    ppermute x23, starting transfers between devices: 26.9 us -> 25 us  [swapped(): return lax.ppermute(block, axes, [(i, i ^ mask) for i in range(count)])]
    ppermute x23, waiting for transfers between devices: 26 us -> 27.5 us  [swapped(): return lax.ppermute(block, axes, [(i, i ^ mask) for i in range(count)])]
where the time goes in v4:
time: 109 us
  Pallas kernels  40.2 us (37%)
  starting transfers between devices  31.8 us (29%)
  waiting for transfers between devices  27.5 us (25%)
  matrix products  4.55 us (4%)
  local copies, waits for them, and re-layouts  2.38 us (2%)
  other arithmetic  1.61 us (1%)
    ppermute x23, waiting for transfers between devices, swapped(): return lax.ppermute(block, axes, [(i, i ^ mask) for i in range(count)])  27.5 us
    ppermute x23, starting transfers between devices, swapped(): return lax.ppermute(block, axes, [(i, i ^ mask) for i in range(count)])  25 us
    pallas_call x3, Pallas kernels, compress(): pl.pallas_call(kernel, out_shape=(jax.ShapeDtypeStruct((RANK, gram[0].sha...  24.5 us
    pallas_call x1, Pallas kernels, weigh(): pl.pallas_call(functools.partial(inside_kernel, edge), out_shape=shapes,...  10.2 us
    pallas_call x1, Pallas kernels, weigh(): pl.pallas_call(functools.partial(border_kernel, width), out_shape=shapes,...  5.55 us
    ppermute x1, starting transfers between devices, halo(): low = lax.ppermute(last, axis, forward)  5.51 us
    dot_general x5, matrix products, combine(): return jnp.dot(coefficients, rows, preferred_element_type=F32).astype(BF16)  2.88 us
  transfers between devices with their start and end apart: 25, of which 15 were waited for; matrix products, arithmetic and copies ran while one was open for 3% of the time, Pallas kernels for 17%

profile of v4, /device:TPU:0, one launch (start us, length us, event | category | flops | bytes accessed | tf_op | source)
XLA Modules:
  0.0 108.9 jit_solution(9872673401366969990)
XLA Ops:
  0.6 1.0 fusion.18
  1.6 1.3 %collective-permute-start.1 = (bf16[128,512]{1,0:T(8,128)(2,1)S(1)}, bf16[128,512]{1,0:T(8,128)(2,1)S(1)}, u32[]{:S(2)}, u32[]{:S(2)}) collective-permute-start(bf16[128,512]{1,0:T(8,128)(2,1)S(1)} %pad_maximum_fusion.11), channel_id=1, source_target_pairs={{4,0},{8,4},{12,8},{16,12},{20,16},{24,20},{28,24},{5,1},{9,5},{13... | collective-permute-start | bytes 393224 | tf_op jit(solution)/shard_map/ppermute | solution.py:28
  2.9 5.5 %collective-permute-start = (bf16[128,512]{1,0:T(8,128)(2,1)S(1)}, bf16[128,512]{1,0:T(8,128)(2,1)S(1)}, u32[]{:S(2)}, u32[]{:S(2)}) collective-permute-start(bf16[128,512]{1,0:T(8,128)(2,1)S(1)} %pad_maximum_fusion.10), channel_id=1, source_target_pairs={{0,4},{4,8},{8,12},{12,16},{16,20},{20,24},{24,28},{1,5},{5,9},{9,... | collective-permute-start | bytes 393224 | tf_op jit(solution)/shard_map/ppermute | solution.py:27
  8.4 10.2 %weigh_inside.1 = (bf16[128,8192]{1,0:T(8,128)(2,1)}, f32[128,128]{1,0:T(8,128)}) custom-call(s32[7,128]{1,0:T(8,128)} %bitcast.11, bf16[64,8192]{1,0:T(8,128)(2,1)} %prior_ref.3, bf16[64,8192]{1,0:T(8,128)(2,1)} %snap_ref.3, bf16[7,64,8192]{2,1,0:T(8,128)(2,1)} %factor_ref.3), custom_call_target="tpu_custom_call" | custom-call | flops 3758096384 | bytes 7340032 | tf_op jit(solution)/shard_map/weigh_inside/pallas_call | solution.py:150
  19.3 5.6 %weigh_border.1 = (bf16[128,8192]{1,0:T(8,128)(2,1)}, f32[128,128]{1,0:T(8,128)}) custom-call(s32[7,128]{1,0:T(8,128)} %bitcast.12, bf16[64,8192]{1,0:T(8,128)(2,1)} %prior_ref.3, bf16[64,8192]{1,0:T(8,128)(2,1)} %snap_ref.3, bf16[128,512]{1,0:T(8,128)(2,1)} %copy-done.4, bf16[128,512]{1,0:T(8,128)(2,1)} %copy-done.3, ...), custom_call_target="tpu_custom_call", output_to_operand_aliasing={{0}: (7, {})} | custom-call | tf_op jit(solution)/shard_map/weigh_border/pallas_call | solution.py:174
  24.9 3.0 %collective-permute-start.2 = (f32[128,128]{1,0:T(8,128)}, f32[128,128]{1,0:T(8,128)S(1)}, u32[]{:S(2)}, u32[]{:S(2)}) collective-permute-start(f32[128,128]{1,0:T(8,128)} %get-tuple-element.13), channel_id=1, source_target_pairs={{0,4},{1,5},{2,6},{3,7},{4,0},{5,1},{6,2},{7,3},{8,12},{9,13},{10,... | collective-permute-start | bytes 196616 | tf_op jit(solution)/shard_map/ppermute | solution.py:35
  27.9 1.5 %collective-permute-start.3 = (f32[128,128]{1,0:T(8,128)}, f32[128,128]{1,0:T(8,128)S(1)}, u32[]{:S(2)}, u32[]{:S(2)}) collective-permute-start(f32[128,128]{1,0:T(8,128)} %get-tuple-element.13), channel_id=1, source_target_pairs={{0,8},{1,9},{2,10},{3,11},{4,12},{5,13},{6,14},{7,15},{8,0},{9,1},... | collective-permute-start | bytes 196616 | tf_op jit(solution)/shard_map/ppermute | solution.py:35
  30.3 2.0 %collective-permute-done.3 = f32[128,128]{1,0:T(8,128)S(1)} collective-permute-done((f32[128,128]{1,0:T(8,128)}, f32[128,128]{1,0:T(8,128)S(1)}, u32[]{:S(2)}, u32[]{:S(2)}) %collective-permute-start.3) | collective-permute-done | bytes 65568 | tf_op jit(solution)/shard_map/ppermute | solution.py:35
  32.4 2.4 %collective-permute-done.4 = f32[128,128]{1,0:T(8,128)S(1)} collective-permute-done((f32[128,128]{1,0:T(8,128)}, f32[128,128]{1,0:T(8,128)S(1)}, u32[]{:S(2)}, u32[]{:S(2)}) %collective-permute-start.4) | collective-permute-done | bytes 65568 | tf_op jit(solution)/shard_map/ppermute | solution.py:35
  35.7 1.1 %collective-permute-start.5 = (f32[128,128]{1,0:T(8,128)S(1)}, f32[128,128]{1,0:T(8,128)S(1)}, u32[]{:S(2)}, u32[]{:S(2)}) collective-permute-start(f32[128,128]{1,0:T(8,128)S(1)} %add_add_fusion), channel_id=1, source_target_pairs={{0,16},{1,17},{2,18},{3,19},{4,20},{5,21},{6,22},{7,23},{8,24},{9,... | collective-permute-start | bytes 196616 | tf_op jit(solution)/shard_map/ppermute | solution.py:35
  36.8 4.7 %collective-permute-done.5 = f32[128,128]{1,0:T(8,128)S(1)} collective-permute-done((f32[128,128]{1,0:T(8,128)S(1)}, f32[128,128]{1,0:T(8,128)S(1)}, u32[]{:S(2)}, u32[]{:S(2)}) %collective-permute-start.5) | collective-permute-done | bytes 65568 | tf_op jit(solution)/shard_map/ppermute | solution.py:35
  41.5 8.0 %compress.3 = (bf16[64,128]{1,0:T(8,128)(2,1)S(1)}, f32[64,64]{1,0:T(8,128)S(1)}) custom-call(f32[128,128]{1,0:T(8,128)S(1)} %add.101.gram_ref), custom_call_target="tpu_custom_call" | custom-call | tf_op jit(solution)/shard_map/compress/pallas_call | solution.py:285
  53.9 1.5 %collective-permute-start.9 = (f32[64,128]{1,0:T(8,128)S(1)}, f32[64,128]{1,0:T(8,128)S(1)}, u32[]{:S(2)}, u32[]{:S(2)}) collective-permute-start(f32[64,128]{1,0:T(8,128)S(1)} %fusion.4), channel_id=1, source_target_pairs={{0,5},{1,4},{2,7},{3,6},{4,1},{5,0},{6,3},{7,2},{8,13},{9,12},{10,... | collective-permute-start | bytes 98312 | tf_op jit(solution)/shard_map/ppermute | solution.py:35
  56.1 1.7 %collective-permute-done.8 = f32[64,128]{1,0:T(8,128)S(1)} collective-permute-done((f32[64,128]{1,0:T(8,128)S(1)}, f32[64,128]{1,0:T(8,128)S(1)}, u32[]{:S(2)}, u32[]{:S(2)}) %collective-permute-start.8) | collective-permute-done | bytes 32800 | tf_op jit(solution)/shard_map/ppermute | solution.py:35
  58.4 2.1 %collective-permute-start.11 = (f32[64,128]{1,0:T(8,128)S(1)}, f32[64,128]{1,0:T(8,128)S(1)}, u32[]{:S(2)}, u32[]{:S(2)}) collective-permute-start(f32[64,128]{1,0:T(8,128)S(1)} %add_add_fusion.4), channel_id=1, source_target_pairs={{0,16},{1,17},{2,18},{3,19},{4,20},{5,21},{6,22},{7,23},{8,24},{9,... | collective-permute-start | bytes 98312 | tf_op jit(solution)/shard_map/ppermute | solution.py:35
  60.5 1.8 %collective-permute-start.12 = (f32[64,128]{1,0:T(8,128)S(1)}, f32[64,128]{1,0:T(8,128)S(1)}, u32[]{:S(2)}, u32[]{:S(2)}) collective-permute-start(f32[64,128]{1,0:T(8,128)S(1)} %add_add_fusion.4), channel_id=1, source_target_pairs={{0,24},{1,25},{2,26},{3,27},{4,28},{5,29},{6,30},{7,31},{8,16},{9,... | collective-permute-start | bytes 98312 | tf_op jit(solution)/shard_map/ppermute | solution.py:35
  62.3 1.5 %collective-permute-done.11 = f32[64,128]{1,0:T(8,128)S(1)} collective-permute-done((f32[64,128]{1,0:T(8,128)S(1)}, f32[64,128]{1,0:T(8,128)S(1)}, u32[]{:S(2)}, u32[]{:S(2)}) %collective-permute-start.11) | collective-permute-done | bytes 32800 | tf_op jit(solution)/shard_map/ppermute | solution.py:35
  63.8 2.4 %collective-permute-done.12 = f32[64,128]{1,0:T(8,128)S(1)} collective-permute-done((f32[64,128]{1,0:T(8,128)S(1)}, f32[64,128]{1,0:T(8,128)S(1)}, u32[]{:S(2)}, u32[]{:S(2)}) %collective-permute-start.12) | collective-permute-done | bytes 32800 | tf_op jit(solution)/shard_map/ppermute | solution.py:35
  66.2 8.3 %compress.4 = (bf16[64,128]{1,0:T(8,128)(2,1)S(1)}, f32[64,64]{1,0:T(8,128)S(1)}) custom-call(f32[64,128]{1,0:T(8,128)S(1)} %add_add_fusion.3.top_ref, f32[64,64]{1,0:T(8,128)S(1)} %broadcast_select_fusion.9.upper_ref), custom_call_target="tpu_custom_call" | custom-call | tf_op jit(solution)/shard_map/compress/pallas_call | solution.py:285
  74.9 1.6 %collective-permute-start.14 = (bf16[64,2048]{1,0:T(8,128)(2,1)S(1)}, bf16[64,2048]{1,0:T(8,128)(2,1)S(1)}, u32[]{:S(2)}, u32[]{:S(2)}) collective-permute-start(bf16[64,2048]{1,0:T(8,128)(2,1)S(1)} %constant_dynamic-slice_fusion.5), channel_id=1, source_target_pairs={{0,2},{1,3},{2,0},{3,1},{4,6},{5,7},{6,4},{7,5},{8,10},{9,11},{10,... | collective-permute-start | bytes 786440 | tf_op jit(solution)/shard_map/ppermute | solution.py:35
  77.5 4.5 %collective-permute-done.14 = bf16[64,2048]{1,0:T(8,128)(2,1)S(1)} collective-permute-done((bf16[64,2048]{1,0:T(8,128)(2,1)S(1)}, bf16[64,2048]{1,0:T(8,128)(2,1)S(1)}, u32[]{:S(2)}, u32[]{:S(2)}) %collective-permute-start.14) | collective-permute-done | bytes 262176 | tf_op jit(solution)/shard_map/ppermute | solution.py:35
  82.6 1.6 %collective-permute-start.16 = (f32[64,128]{1,0:T(8,128)S(1)}, f32[64,128]{1,0:T(8,128)S(1)}, u32[]{:S(2)}, u32[]{:S(2)}) collective-permute-start(f32[64,128]{1,0:T(8,128)S(1)} %fusion.8), channel_id=1, source_target_pairs={{0,2},{1,3},{2,0},{3,1},{4,6},{5,7},{6,4},{7,5},{8,10},{9,11},{10,... | collective-permute-start | bytes 98312 | tf_op jit(solution)/shard_map/ppermute | solution.py:35
  84.5 1.6 %collective-permute-start.24 = (bf16[64,2048]{1,0:T(8,128)(2,1)S(1)}, bf16[64,2048]{1,0:T(8,128)(2,1)S(1)}, u32[]{:S(2)}, u32[]{:S(2)}) collective-permute-start(bf16[64,2048]{1,0:T(8,128)(2,1)S(1)} %constant_dynamic-slice_fusion), channel_id=1, source_target_pairs={{0,2},{1,3},{2,0},{3,1},{4,6},{5,7},{6,4},{7,5},{8,10},{9,11},{10,... | collective-permute-start | bytes 786440 | tf_op jit(solution)/shard_map/ppermute | solution.py:35
  86.5 0.9 collective-permute-done.17
  87.5 1.7 %collective-permute-start.18 = (f32[64,128]{1,0:T(8,128)S(1)}, f32[64,128]{1,0:T(8,128)S(1)}, u32[]{:S(2)}, u32[]{:S(2)}) collective-permute-start(f32[64,128]{1,0:T(8,128)S(1)} %add_add_fusion.2), channel_id=1, source_target_pairs={{0,4},{1,5},{2,6},{3,7},{4,0},{5,1},{6,2},{7,3},{8,12},{9,13},{10,... | collective-permute-start | bytes 98312 | tf_op jit(solution)/shard_map/ppermute | solution.py:35
  89.2 1.9 %collective-permute-start.20 = (f32[64,128]{1,0:T(8,128)S(1)}, f32[64,128]{1,0:T(8,128)S(1)}, u32[]{:S(2)}, u32[]{:S(2)}) collective-permute-start(f32[64,128]{1,0:T(8,128)S(1)} %add_add_fusion.2), channel_id=1, source_target_pairs={{0,12},{1,13},{2,14},{3,15},{4,8},{5,9},{6,10},{7,11},{8,4},{9,5},... | collective-permute-start | bytes 98312 | tf_op jit(solution)/shard_map/ppermute | solution.py:35
  91.5 1.6 %collective-permute-done.19 = f32[64,128]{1,0:T(8,128)S(1)} collective-permute-done((f32[64,128]{1,0:T(8,128)S(1)}, f32[64,128]{1,0:T(8,128)S(1)}, u32[]{:S(2)}, u32[]{:S(2)}) %collective-permute-start.19) | collective-permute-done | bytes 32800 | tf_op jit(solution)/shard_map/ppermute | solution.py:35
  94.0 2.4 %collective-permute-start.21 = (f32[64,128]{1,0:T(8,128)S(1)}, f32[64,128]{1,0:T(8,128)S(1)}, u32[]{:S(2)}, u32[]{:S(2)}) collective-permute-start(f32[64,128]{1,0:T(8,128)S(1)} %add_add_fusion.1), channel_id=1, source_target_pairs={{0,16},{1,17},{2,18},{3,19},{4,20},{5,21},{6,22},{7,23},{8,24},{9,... | collective-permute-start | bytes 98312 | tf_op jit(solution)/shard_map/ppermute | solution.py:35
  96.5 2.3 %collective-permute-done.21 = f32[64,128]{1,0:T(8,128)S(1)} collective-permute-done((f32[64,128]{1,0:T(8,128)S(1)}, f32[64,128]{1,0:T(8,128)S(1)}, u32[]{:S(2)}, u32[]{:S(2)}) %collective-permute-start.21) | collective-permute-done | bytes 32800 | tf_op jit(solution)/shard_map/ppermute | solution.py:35
  98.9 8.1 %compress.5 = (bf16[64,128]{1,0:T(8,128)(2,1)S(1)}, f32[64,64]{1,0:T(8,128)}) custom-call(f32[64,128]{1,0:T(8,128)S(1)} %add.122.top_ref, f32[64,64]{1,0:T(8,128)S(1)} %broadcast_select_fusion.8.upper_ref), custom_call_target="tpu_custom_call" | custom-call | tf_op jit(solution)/shard_map/compress/pallas_call | solution.py:285
  107.0 0.9 convolution_convert_fusion.3
  107.9 0.9 convolution_convert_fusion.4
  (64 shorter events, 12.3 us)
Async XLA Ops:
  1.6 17.0 %collective-permute-start.1 = (bf16[128,512]{1,0:T(8,128)(2,1)S(1)}, bf16[128,512]{1,0:T(8,128)(2,1)S(1)}, u32[]{:S(2)}, u32[]{:S(2)}) collective-permute-start(bf16[128,512]{1,0:T(8,128)(2,1)S(1)} %pad_maximum_fusion.11), channel_id=1, source_target_pairs={{4,0},{8,4},{12,8},{16,12},{20,16},{24,20},{28,24},{5,1},{9,5},{13... | collective-permute-start | bytes 393224 | tf_op jit(solution)/shard_map/ppermute | solution.py:28
  2.9 15.7 %collective-permute-start = (bf16[128,512]{1,0:T(8,128)(2,1)S(1)}, bf16[128,512]{1,0:T(8,128)(2,1)S(1)}, u32[]{:S(2)}, u32[]{:S(2)}) collective-permute-start(bf16[128,512]{1,0:T(8,128)(2,1)S(1)} %pad_maximum_fusion.10), channel_id=1, source_target_pairs={{0,4},{4,8},{8,12},{12,16},{16,20},{20,24},{24,28},{1,5},{5,9},{9,... | collective-permute-start | bytes 393224 | tf_op jit(solution)/shard_map/ppermute | solution.py:27
  18.6 0.7 copy-start.3
  18.6 0.7 copy-start.4
  19.3 30.2 %copy-start.1 = (bf16[64,8192]{1,0:T(8,128)(2,1)S(1)}, bf16[64,8192]{1,0:T(8,128)(2,1)}, u32[]{:S(2)}) copy-start(bf16[64,8192]{1,0:T(8,128)(2,1)} %snap_ref.3) | copy-start | bytes 3145732
  24.9 25.1 %copy-start = (bf16[128,8192]{1,0:T(8,128)(2,1)S(1)}, bf16[128,8192]{1,0:T(8,128)(2,1)}, u32[]{:S(2)}) copy-start(bf16[128,8192]{1,0:T(8,128)(2,1)} %get-tuple-element.15) | copy-start | bytes 6291460
  24.9 5.4 %collective-permute-start.2 = (f32[128,128]{1,0:T(8,128)}, f32[128,128]{1,0:T(8,128)S(1)}, u32[]{:S(2)}, u32[]{:S(2)}) collective-permute-start(f32[128,128]{1,0:T(8,128)} %get-tuple-element.13), channel_id=1, source_target_pairs={{0,4},{1,5},{2,6},{3,7},{4,0},{5,1},{6,2},{7,3},{8,12},{9,13},{10,... | collective-permute-start | bytes 196616 | tf_op jit(solution)/shard_map/ppermute | solution.py:35
  27.9 4.5 %collective-permute-start.3 = (f32[128,128]{1,0:T(8,128)}, f32[128,128]{1,0:T(8,128)S(1)}, u32[]{:S(2)}, u32[]{:S(2)}) collective-permute-start(f32[128,128]{1,0:T(8,128)} %get-tuple-element.13), channel_id=1, source_target_pairs={{0,8},{1,9},{2,10},{3,11},{4,12},{5,13},{6,14},{7,15},{8,0},{9,1},... | collective-permute-start | bytes 196616 | tf_op jit(solution)/shard_map/ppermute | solution.py:35
  29.4 5.4 %collective-permute-start.4 = (f32[128,128]{1,0:T(8,128)}, f32[128,128]{1,0:T(8,128)S(1)}, u32[]{:S(2)}, u32[]{:S(2)}) collective-permute-start(f32[128,128]{1,0:T(8,128)} %get-tuple-element.13), channel_id=1, source_target_pairs={{0,12},{1,13},{2,14},{3,15},{4,8},{5,9},{6,10},{7,11},{8,4},{9,5},... | collective-permute-start | bytes 196616 | tf_op jit(solution)/shard_map/ppermute | solution.py:35
  35.7 5.8 %collective-permute-start.5 = (f32[128,128]{1,0:T(8,128)S(1)}, f32[128,128]{1,0:T(8,128)S(1)}, u32[]{:S(2)}, u32[]{:S(2)}) collective-permute-start(f32[128,128]{1,0:T(8,128)S(1)} %add_add_fusion), channel_id=1, source_target_pairs={{0,16},{1,17},{2,18},{3,19},{4,20},{5,21},{6,22},{7,23},{8,24},{9,... | collective-permute-start | bytes 196616 | tf_op jit(solution)/shard_map/ppermute | solution.py:35
  49.5 12.8 %collective-permute-start.13 = (f32[64,64]{1,0:T(8,128)S(1)}, f32[64,64]{1,0:T(8,128)S(1)}, u32[]{:S(2)}, u32[]{:S(2)}) collective-permute-start(f32[64,64]{1,0:T(8,128)S(1)} %get-tuple-element.16), channel_id=1, source_target_pairs={{0,1},{1,0},{2,3},{3,2},{4,5},{5,4},{6,7},{7,6},{8,9},{9,8},{10,11... | collective-permute-start | bytes 49160 | tf_op jit(solution)/shard_map/ppermute | solution.py:35
  50.5 1.2 %copy-start.2 = (bf16[64,8192]{1,0:T(8,128)(2,1)S(1)}, bf16[64,8192]{1,0:T(8,128)(2,1)}, u32[]{:S(2)}) copy-start(bf16[64,8192]{1,0:T(8,128)(2,1)} %prior_ref.3) | copy-start | bytes 3145732
  50.6 2.1 %collective-permute-start.6 = (bf16[64,4096]{1,0:T(8,128)(2,1)S(1)}, bf16[64,4096]{1,0:T(8,128)(2,1)S(1)}, u32[]{:S(2)}, u32[]{:S(2)}) collective-permute-start(bf16[64,4096]{1,0:T(8,128)(2,1)S(1)} %pad_maximum_fusion.3), channel_id=1, source_target_pairs={{0,1},{1,0},{2,3},{3,2},{4,5},{5,4},{6,7},{7,6},{8,9},{9,8},{10,11... | collective-permute-start | bytes 1572872 | tf_op jit(solution)/shard_map/ppermute | solution.py:35
  53.5 2.7 %collective-permute-start.7 = (f32[64,128]{1,0:T(8,128)S(1)}, f32[64,128]{1,0:T(8,128)S(1)}, u32[]{:S(2)}, u32[]{:S(2)}) collective-permute-start(f32[64,128]{1,0:T(8,128)S(1)} %fusion.4), channel_id=1, source_target_pairs={{0,1},{1,0},{2,3},{3,2},{4,5},{5,4},{6,7},{7,6},{8,9},{9,8},{10,11... | collective-permute-start | bytes 98312 | tf_op jit(solution)/shard_map/ppermute | solution.py:35
  53.9 3.9 %collective-permute-start.8 = (f32[64,128]{1,0:T(8,128)S(1)}, f32[64,128]{1,0:T(8,128)S(1)}, u32[]{:S(2)}, u32[]{:S(2)}) collective-permute-start(f32[64,128]{1,0:T(8,128)S(1)} %fusion.4), channel_id=1, source_target_pairs={{0,4},{1,5},{2,6},{3,7},{4,0},{5,1},{6,2},{7,3},{8,12},{9,13},{10,... | collective-permute-start | bytes 98312 | tf_op jit(solution)/shard_map/ppermute | solution.py:35
  53.9 3.9 %collective-permute-start.9 = (f32[64,128]{1,0:T(8,128)S(1)}, f32[64,128]{1,0:T(8,128)S(1)}, u32[]{:S(2)}, u32[]{:S(2)}) collective-permute-start(f32[64,128]{1,0:T(8,128)S(1)} %fusion.4), channel_id=1, source_target_pairs={{0,5},{1,4},{2,7},{3,6},{4,1},{5,0},{6,3},{7,2},{8,13},{9,12},{10,... | collective-permute-start | bytes 98312 | tf_op jit(solution)/shard_map/ppermute | solution.py:35
  55.4 21.0 %collective-permute-start.23 = (bf16[64,4096]{1,0:T(8,128)(2,1)S(1)}, bf16[64,4096]{1,0:T(8,128)(2,1)S(1)}, u32[]{:S(2)}, u32[]{:S(2)}) collective-permute-start(bf16[64,4096]{1,0:T(8,128)(2,1)S(1)} %pad_maximum_fusion.6), channel_id=1, source_target_pairs={{0,1},{1,0},{2,3},{3,2},{4,5},{5,4},{6,7},{7,6},{8,9},{9,8},{10,11... | collective-permute-start | bytes 1572872 | tf_op jit(solution)/shard_map/ppermute | solution.py:35
  57.8 4.5 %collective-permute-start.10 = (f32[64,128]{1,0:T(8,128)S(1)}, f32[64,128]{1,0:T(8,128)S(1)}, u32[]{:S(2)}, u32[]{:S(2)}) collective-permute-start(f32[64,128]{1,0:T(8,128)S(1)} %add_add_fusion.4), channel_id=1, source_target_pairs={{0,8},{1,9},{2,10},{3,11},{4,12},{5,13},{6,14},{7,15},{8,0},{9,1},... | collective-permute-start | bytes 98312 | tf_op jit(solution)/shard_map/ppermute | solution.py:35
  58.4 5.4 %collective-permute-start.11 = (f32[64,128]{1,0:T(8,128)S(1)}, f32[64,128]{1,0:T(8,128)S(1)}, u32[]{:S(2)}, u32[]{:S(2)}) collective-permute-start(f32[64,128]{1,0:T(8,128)S(1)} %add_add_fusion.4), channel_id=1, source_target_pairs={{0,16},{1,17},{2,18},{3,19},{4,20},{5,21},{6,22},{7,23},{8,24},{9,... | collective-permute-start | bytes 98312 | tf_op jit(solution)/shard_map/ppermute | solution.py:35
  60.5 5.7 %collective-permute-start.12 = (f32[64,128]{1,0:T(8,128)S(1)}, f32[64,128]{1,0:T(8,128)S(1)}, u32[]{:S(2)}, u32[]{:S(2)}) collective-permute-start(f32[64,128]{1,0:T(8,128)S(1)} %add_add_fusion.4), channel_id=1, source_target_pairs={{0,24},{1,25},{2,26},{3,27},{4,28},{5,29},{6,30},{7,31},{8,16},{9,... | collective-permute-start | bytes 98312 | tf_op jit(solution)/shard_map/ppermute | solution.py:35
  74.9 7.2 %collective-permute-start.14 = (bf16[64,2048]{1,0:T(8,128)(2,1)S(1)}, bf16[64,2048]{1,0:T(8,128)(2,1)S(1)}, u32[]{:S(2)}, u32[]{:S(2)}) collective-permute-start(bf16[64,2048]{1,0:T(8,128)(2,1)S(1)} %constant_dynamic-slice_fusion.5), channel_id=1, source_target_pairs={{0,2},{1,3},{2,0},{3,1},{4,6},{5,7},{6,4},{7,5},{8,10},{9,11},{10,... | collective-permute-start | bytes 786440 | tf_op jit(solution)/shard_map/ppermute | solution.py:35
  76.7 14.4 %collective-permute-start.22 = (f32[64,64]{1,0:T(8,128)S(1)}, f32[64,64]{1,0:T(8,128)S(1)}, u32[]{:S(2)}, u32[]{:S(2)}) collective-permute-start(f32[64,64]{1,0:T(8,128)S(1)} %get-tuple-element.18), channel_id=1, source_target_pairs={{0,2},{1,3},{2,0},{3,1},{4,6},{5,7},{6,4},{7,5},{8,10},{9,11},{10,... | collective-permute-start | bytes 49160 | tf_op jit(solution)/shard_map/ppermute | solution.py:35
  82.5 3.5 %collective-permute-start.15 = (f32[64,128]{1,0:T(8,128)S(1)}, f32[64,128]{1,0:T(8,128)S(1)}, u32[]{:S(2)}, u32[]{:S(2)}) collective-permute-start(f32[64,128]{1,0:T(8,128)S(1)} %fusion.8), channel_id=1, source_target_pairs={{0,1},{1,0},{2,3},{3,2},{4,5},{5,4},{6,7},{7,6},{8,9},{9,8},{10,11... | collective-permute-start | bytes 98312 | tf_op jit(solution)/shard_map/ppermute | solution.py:35
  82.6 4.0 %collective-permute-start.16 = (f32[64,128]{1,0:T(8,128)S(1)}, f32[64,128]{1,0:T(8,128)S(1)}, u32[]{:S(2)}, u32[]{:S(2)}) collective-permute-start(f32[64,128]{1,0:T(8,128)S(1)} %fusion.8), channel_id=1, source_target_pairs={{0,2},{1,3},{2,0},{3,1},{4,6},{5,7},{6,4},{7,5},{8,10},{9,11},{10,... | collective-permute-start | bytes 98312 | tf_op jit(solution)/shard_map/ppermute | solution.py:35
  84.1 3.3 %collective-permute-start.17 = (f32[64,128]{1,0:T(8,128)S(1)}, f32[64,128]{1,0:T(8,128)S(1)}, u32[]{:S(2)}, u32[]{:S(2)}) collective-permute-start(f32[64,128]{1,0:T(8,128)S(1)} %fusion.8), channel_id=1, source_target_pairs={{0,3},{1,2},{2,1},{3,0},{4,7},{5,6},{6,5},{7,4},{8,11},{9,10},{10,... | collective-permute-start | bytes 98312 | tf_op jit(solution)/shard_map/ppermute | solution.py:35
  84.5 12.0 %collective-permute-start.24 = (bf16[64,2048]{1,0:T(8,128)(2,1)S(1)}, bf16[64,2048]{1,0:T(8,128)(2,1)S(1)}, u32[]{:S(2)}, u32[]{:S(2)}) collective-permute-start(bf16[64,2048]{1,0:T(8,128)(2,1)S(1)} %constant_dynamic-slice_fusion), channel_id=1, source_target_pairs={{0,2},{1,3},{2,0},{3,1},{4,6},{5,7},{6,4},{7,5},{8,10},{9,11},{10,... | collective-permute-start | bytes 786440 | tf_op jit(solution)/shard_map/ppermute | solution.py:35
  87.5 4.0 %collective-permute-start.18 = (f32[64,128]{1,0:T(8,128)S(1)}, f32[64,128]{1,0:T(8,128)S(1)}, u32[]{:S(2)}, u32[]{:S(2)}) collective-permute-start(f32[64,128]{1,0:T(8,128)S(1)} %add_add_fusion.2), channel_id=1, source_target_pairs={{0,4},{1,5},{2,6},{3,7},{4,0},{5,1},{6,2},{7,3},{8,12},{9,13},{10,... | collective-permute-start | bytes 98312 | tf_op jit(solution)/shard_map/ppermute | solution.py:35
  89.2 3.9 %collective-permute-start.19 = (f32[64,128]{1,0:T(8,128)S(1)}, f32[64,128]{1,0:T(8,128)S(1)}, u32[]{:S(2)}, u32[]{:S(2)}) collective-permute-start(f32[64,128]{1,0:T(8,128)S(1)} %add_add_fusion.2), channel_id=1, source_target_pairs={{0,8},{1,9},{2,10},{3,11},{4,12},{5,13},{6,14},{7,15},{8,0},{9,1},... | collective-permute-start | bytes 98312 | tf_op jit(solution)/shard_map/ppermute | solution.py:35
  89.2 4.8 %collective-permute-start.20 = (f32[64,128]{1,0:T(8,128)S(1)}, f32[64,128]{1,0:T(8,128)S(1)}, u32[]{:S(2)}, u32[]{:S(2)}) collective-permute-start(f32[64,128]{1,0:T(8,128)S(1)} %add_add_fusion.2), channel_id=1, source_target_pairs={{0,12},{1,13},{2,14},{3,15},{4,8},{5,9},{6,10},{7,11},{8,4},{9,5},... | collective-permute-start | bytes 98312 | tf_op jit(solution)/shard_map/ppermute | solution.py:35
  94.0 4.9 %collective-permute-start.21 = (f32[64,128]{1,0:T(8,128)S(1)}, f32[64,128]{1,0:T(8,128)S(1)}, u32[]{:S(2)}, u32[]{:S(2)}) collective-permute-start(f32[64,128]{1,0:T(8,128)S(1)} %add_add_fusion.1), channel_id=1, source_target_pairs={{0,16},{1,17},{2,18},{3,19},{4,20},{5,21},{6,22},{7,23},{8,24},{9,... | collective-permute-start | bytes 98312 | tf_op jit(solution)/shard_map/ppermute | solution.py:35

commit v5 on v4

--- a/solution.py
+++ b/solution.py
@@ -146,7 +146,7 @@
         jax.ShapeDtypeStruct((columns, width), BF16),
         jax.ShapeDtypeStruct((columns, columns), F32),
     )
-    params = pltpu.CompilerParams(vmem_limit_bytes=56 * 1024 * 1024)
+    params = pltpu.CompilerParams(vmem_limit_bytes=24 * 1024 * 1024)
     weighted, gram = pl.pallas_call(
         functools.partial(inside_kernel, edge),
         out_shape=shapes,
@@ -298,14 +298,6 @@
     return jnp.dot(coefficients, rows, preferred_element_type=F32).astype(BF16)
 
 
-def combine_two(coefficients, first, second):
-    rows = first.shape[0]
-    return (
-        jnp.dot(coefficients[:, :rows], first, preferred_element_type=F32)
-        + jnp.dot(coefficients[:, rows:], second, preferred_element_type=F32)
-    ).astype(BF16)
-
-
 def shared_out(rows, width, bit):
     pieces = [
         lax.dynamic_slice_in_dim(rows, (2 * pair + bit) * width, width, 1)
@@ -314,6 +306,10 @@
     return pieces[0] if len(pieces) == 1 else jnp.concatenate(pieces, axis=1)
 
 
+def joined(parts, width, bit):
+    return jnp.concatenate([shared_out(part, width, bit) for part in parts], axis=0)
+
+
 def ordered(upper_half, own_rows, partner_rows):
     lower_part = jnp.where(upper_half, partner_rows, own_rows)
     upper_part = jnp.where(upper_half, own_rows, partner_rows)
@@ -325,26 +321,35 @@
     members = lax.axis_size("tm")
     places = members * lax.axis_size("space")
     across = [1 << i for i in range(members.bit_length() - 1, places.bit_length() - 1)]
-    coefficients, own = compress(first_kernel, total(gram, across))
     member = lax.axis_index("tm")
     width = snapshots.shape[1] // members
+    stacked = (prior_basis, snapshots)
     for level in range(members.bit_length() - 1):
         step = 1 << level
         bit = member // step % 2
         upper_half = bit == 1
-        weighted = combine(coefficients, weighted)
-        sent = swapped(shared_out(weighted, width, 1 - bit), step)
+        partner_weighted = swapped(shared_out(weighted, width, 1 - bit), step)
+        own_weighted = shared_out(weighted, width, bit)
+        if level == 0:
+            partner_stacked = swapped(joined(stacked, width, 1 - bit), step)
+            own_stacked = joined(stacked, width, bit)
+            coefficients, own = compress(first_kernel, total(gram, across))
+        else:
+            partner_stacked = swapped(shared_out(stacked, width, 1 - bit), step)
+            own_stacked = shared_out(stacked, width, bit)
+            coefficients, own = compress(functools.partial(merge_kernel, False), top, upper)
+        partner_coefficients = swapped(coefficients, step)
         partner_own = swapped(own, step)
-        weighted = ordered(upper_half, shared_out(weighted, width, bit), sent)
-        if level == 0:
-            stacked = combine_two(coefficients, prior_basis, snapshots)
-        else:
-            stacked = combine(coefficients, stacked)
-        sent = swapped(shared_out(stacked, width, 1 - bit), step)
-        stacked = ordered(upper_half, shared_out(stacked, width, bit), sent)
+        weighted = ordered(
+            upper_half, combine(coefficients, own_weighted), combine(partner_coefficients, partner_weighted)
+        )
         top = lax.dot_general(weighted[:RANK], weighted, NT, preferred_element_type=F32)
         top = total(top, [1 << i for i in range(level + 1)] + across)
-        coefficients, own = compress(functools.partial(merge_kernel, 2 * step == members), top, jnp.where(upper_half, own, partner_own))
+        upper = jnp.where(upper_half, own, partner_own)
+        stacked = ordered(
+            upper_half, combine(coefficients, own_stacked), combine(partner_coefficients, partner_stacked)
+        )
+    coefficients, _ = compress(functools.partial(merge_kernel, True), top, upper)
     return combine(coefficients, stacked), combine(coefficients, weighted)
 
 

time: 109 us -> 113 us (1.037)
  local copies, waits for them, and re-layouts: 2.38 us -> 9.24 us
  Pallas kernels: 40.2 us -> 35.6 us
  starting transfers between devices: 31.8 us -> 33.3 us
    dynamic_slice x4 -> x2, local copies, waits for them, and re-layouts: 0.27 us -> 3.79 us  [shared_out(): lax.dynamic_slice_in_dim(rows, (2 * pair + bit) * width, width, 1)]
    unnamed x10 -> x20, local copies, waits for them, and re-layouts: 1.15 us -> 4.49 us
    pallas_call x1, Pallas kernels: 10.2 us -> 7.51 us  [weigh(): pl.pallas_call(functools.partial(inside_kernel, edge), out_shape=shapes,...]
    ppermute x23 -> x25, starting transfers between devices: 25 us -> 27.2 us  [swapped(): return lax.ppermute(block, axes, [(i, i ^ mask) for i in range(count)])]
    pallas_call x1, Pallas kernels: 5.55 us -> 3.63 us  [weigh(): pl.pallas_call(functools.partial(border_kernel, width), out_shape=shapes,...]
    dot_general x5 -> x10, matrix products: 2.88 us -> 3.92 us  [combine(): return jnp.dot(coefficients, rows, preferred_element_type=F32).astype(BF16)]
    ppermute x23 -> x25, waiting for transfers between devices: 27.5 us -> 27.3 us  [swapped(): return lax.ppermute(block, axes, [(i, i ^ mask) for i in range(count)])]
  transfers between devices with their start and end apart: 25 -> 27, of which waited for: 15 -> 17; matrix products, arithmetic and copies ran while one was open for 3% -> 6% of each run, Pallas kernels for 17% -> 24%
where the time goes in v5:
time: 113 us
  Pallas kernels  35.6 us (32%)
  starting transfers between devices  33.3 us (29%)
  waiting for transfers between devices  27.3 us (24%)
  local copies, waits for them, and re-layouts  9.24 us (8%)
  matrix products  4.69 us (4%)
  other arithmetic  1.34 us (1%)
    ppermute x25, waiting for transfers between devices, swapped(): return lax.ppermute(block, axes, [(i, i ^ mask) for i in range(count)])  27.3 us
    ppermute x25, starting transfers between devices, swapped(): return lax.ppermute(block, axes, [(i, i ^ mask) for i in range(count)])  27.2 us
    pallas_call x3, Pallas kernels, compress(): pl.pallas_call(kernel, out_shape=(jax.ShapeDtypeStruct((RANK, gram[0].sha...  24.5 us
    pallas_call x1, Pallas kernels, weigh(): pl.pallas_call(functools.partial(inside_kernel, edge), out_shape=shapes,...  7.51 us
    ppermute x1, starting transfers between devices, halo(): low = lax.ppermute(last, axis, forward)  4.88 us
    unnamed x20, local copies, waits for them, and re-layouts  4.49 us
    dot_general x10, matrix products, combine(): return jnp.dot(coefficients, rows, preferred_element_type=F32).astype(BF16)  3.92 us
    dynamic_slice x2, local copies, waits for them, and re-layouts, shared_out(): lax.dynamic_slice_in_dim(rows, (2 * pair + bit) * width, width, 1)  3.79 us
  transfers between devices with their start and end apart: 27, of which 17 were waited for; matrix products, arithmetic and copies ran while one was open for 6% of the time, Pallas kernels for 24%

profile of v5, /device:TPU:0, one launch (start us, length us, event | category | flops | bytes accessed | tf_op | source)
XLA Modules:
  0.0 112.5 jit_solution(11464897704764087543)
XLA Ops:
  1.6 4.9 %collective-permute-start = (bf16[128,512]{1,0:T(8,128)(2,1)S(1)}, bf16[128,512]{1,0:T(8,128)(2,1)S(1)}, u32[]{:S(2)}, u32[]{:S(2)}) collective-permute-start(bf16[128,512]{1,0:T(8,128)(2,1)S(1)} %pad_maximum_fusion.6), channel_id=1, source_target_pairs={{0,4},{4,8},{8,12},{12,16},{16,20},{20,24},{24,28},{1,5},{5,9},{9,... | collective-permute-start | bytes 393224 | tf_op jit(solution)/shard_map/ppermute | solution.py:27
  6.5 1.3 %collective-permute-start.1 = (bf16[128,512]{1,0:T(8,128)(2,1)S(1)}, bf16[128,512]{1,0:T(8,128)(2,1)S(1)}, u32[]{:S(2)}, u32[]{:S(2)}) collective-permute-start(bf16[128,512]{1,0:T(8,128)(2,1)S(1)} %pad_maximum_fusion.7), channel_id=1, source_target_pairs={{4,0},{8,4},{12,8},{16,12},{20,16},{24,20},{28,24},{5,1},{9,5},{13... | collective-permute-start | bytes 393224 | tf_op jit(solution)/shard_map/ppermute | solution.py:28
  7.8 2.6 %constant_dynamic-slice_fusion.1 = (bf16[64,2048]{1,0:T(8,128)(2,1)}, bf16[64,2048]{1,0:T(8,128)(2,1)S(1)}, bf16[64,2048]{1,0:T(8,128)(2,1)S(1)}, bf16[64,2048]{...) fusion(bf16[64,8192]{1,0:T(8,128)(2,1)} %snap_ref.3, ...), kind=kLoop, calls=%fused_computation.60 | loop fusion | bytes 4194320 | tf_op jit(solution)/shard_map/dynamic_slice | solution.py:303
  12.0 3.1 %copy-done = bf16[7,64,8192]{2,1,0:T(8,128)(2,1)S(1)} copy-done((bf16[7,64,8192]{2,1,0:T(8,128)(2,1)S(1)}, bf16[7,64,8192]{2,1,0:T(8,128)(2,1)}, u32[]{:S(2)}) %copy-start) | copy-done | bytes 7340056
  15.1 7.5 %weigh_inside.1 = (bf16[128,8192]{1,0:T(8,128)(2,1)S(1)}, f32[128,128]{1,0:T(8,128)S(1)}) custom-call(s32[7,128]{1,0:T(8,128)S(1)} %bitcast.17, bf16[64,8192]{1,0:T(8,128)(2,1)S(1)} %copy-done.1, bf16[64,8192]{1,0:T(8,128)(2,1)S(1)} %copy-done.2, bf16[7,64,8192]{2,1,0:T(8,128)(2,1)S(1)} %copy-done), custom_call_target="tpu_custom_call" | custom-call | flops 3758096384 | bytes 7340032 | tf_op jit(solution)/shard_map/weigh_inside/pallas_call | solution.py:150
  22.6 3.6 %weigh_border.1 = (bf16[128,8192]{1,0:T(8,128)(2,1)S(1)}, f32[128,128]{1,0:T(8,128)S(1)}) custom-call(s32[7,128]{1,0:T(8,128)S(1)} %bitcast.18, bf16[64,8192]{1,0:T(8,128)(2,1)S(1)} %copy-done.1, bf16[64,8192]{1,0:T(8,128)(2,1)S(1)} %copy-done.2, bf16[128,512]{1,0:T(8,128)(2,1)S(1)} %collective-permute-done.low_ref, ...), custom_call_target="tpu_custom_call", output_to_operand_aliasing={{0}: (7, {})} | custom-call | tf_op jit(solution)/shard_map/weigh_border/pallas_call | solution.py:174
  26.3 1.2 %constant_dynamic-slice_fusion.9 = (bf16[128,2048]{1,0:T(8,128)(2,1)}, bf16[128,2048]{1,0:T(8,128)(2,1)}, bf16[128,2048]{1,0:T(8,128)(2,1)S(1)}, bf16[128,2048]{1,0:T(8,128)(2,1)S(1)}) fusion(bf16[128,8192]{1,0:T(8,128)(2,1)S(1)} %get-tuple-element.15, s32[]{:T(128)S(6)} %select_n.105, s32[]{:T(128)S(6)} %select_n.106, s32[]{:T(128)S(6)} %select_n.104, ...), kind=kLoop, calls=%fused_computation.69 | loop fusion | bytes 4194320 | tf_op jit(solution)/shard_map/dynamic_slice | solution.py:303
  27.5 1.1 pad_maximum_fusion.2
  28.5 3.6 %collective-permute-start.3 = (f32[128,128]{1,0:T(8,128)S(1)}, f32[128,128]{1,0:T(8,128)S(1)}, u32[]{:S(2)}, u32[]{:S(2)}) collective-permute-start(f32[128,128]{1,0:T(8,128)S(1)} %get-tuple-element.13), channel_id=1, source_target_pairs={{0,8},{1,9},{2,10},{3,11},{4,12},{5,13},{6,14},{7,15},{8,0},{9,1},... | collective-permute-start | bytes 196616 | tf_op jit(solution)/shard_map/ppermute | solution.py:35
  33.6 1.3 %collective-permute-done.3 = f32[128,128]{1,0:T(8,128)S(1)} collective-permute-done((f32[128,128]{1,0:T(8,128)S(1)}, f32[128,128]{1,0:T(8,128)S(1)}, u32[]{:S(2)}, u32[]{:S(2)}) %collective-permute-start.3) | collective-permute-done | bytes 65568 | tf_op jit(solution)/shard_map/ppermute | solution.py:35
  34.9 2.5 %collective-permute-done.4 = f32[128,128]{1,0:T(8,128)S(1)} collective-permute-done((f32[128,128]{1,0:T(8,128)S(1)}, f32[128,128]{1,0:T(8,128)S(1)}, u32[]{:S(2)}, u32[]{:S(2)}) %collective-permute-start.4) | collective-permute-done | bytes 65568 | tf_op jit(solution)/shard_map/ppermute | solution.py:35
  38.0 2.7 %collective-permute-start.5 = (f32[128,128]{1,0:T(8,128)S(1)}, f32[128,128]{1,0:T(8,128)S(1)}, u32[]{:S(2)}, u32[]{:S(2)}) collective-permute-start(f32[128,128]{1,0:T(8,128)S(1)} %add_add_fusion), channel_id=1, source_target_pairs={{0,16},{1,17},{2,18},{3,19},{4,20},{5,21},{6,22},{7,23},{8,24},{9,... | collective-permute-start | bytes 196616 | tf_op jit(solution)/shard_map/ppermute | solution.py:35
  40.7 3.6 %collective-permute-done.5 = f32[128,128]{1,0:T(8,128)S(1)} collective-permute-done((f32[128,128]{1,0:T(8,128)S(1)}, f32[128,128]{1,0:T(8,128)S(1)}, u32[]{:S(2)}, u32[]{:S(2)}) %collective-permute-start.5) | collective-permute-done | bytes 65568 | tf_op jit(solution)/shard_map/ppermute | solution.py:35
  44.3 8.0 %compress.3 = (bf16[64,128]{1,0:T(8,128)(2,1)S(1)}, f32[64,64]{1,0:T(8,128)S(1)}) custom-call(f32[128,128]{1,0:T(8,128)S(1)} %add.104.gram_ref), custom_call_target="tpu_custom_call" | custom-call | tf_op jit(solution)/shard_map/compress/pallas_call | solution.py:285
  55.2 1.5 %collective-permute-start.9 = (f32[64,128]{1,0:T(8,128)S(1)}, f32[64,128]{1,0:T(8,128)S(1)}, u32[]{:S(2)}, u32[]{:S(2)}) collective-permute-start(f32[64,128]{1,0:T(8,128)S(1)} %fusion), channel_id=1, source_target_pairs={{0,4},{1,5},{2,6},{3,7},{4,0},{5,1},{6,2},{7,3},{8,12},{9,13},{10,... | collective-permute-start | bytes 98312 | tf_op jit(solution)/shard_map/ppermute | solution.py:35
  57.4 1.6 %collective-permute-start.16 = (bf16[128,2048]{1,0:T(8,128)(2,1)S(1)}, bf16[128,2048]{1,0:T(8,128)(2,1)S(1)}, u32[]{:S(2)}, u32[]{:S(2)}) collective-permute-start(bf16[128,2048]{1,0:T(8,128)(2,1)S(1)} %fusion.14), channel_id=1, source_target_pairs={{0,2},{1,3},{2,0},{3,1},{4,6},{5,7},{6,4},{7,5},{8,10},{9,11},{10,... | collective-permute-start | bytes 1572872 | tf_op jit(solution)/shard_map/ppermute | solution.py:35
  60.1 1.5 %collective-permute-start.12 = (f32[64,128]{1,0:T(8,128)S(1)}, f32[64,128]{1,0:T(8,128)S(1)}, u32[]{:S(2)}, u32[]{:S(2)}) collective-permute-start(f32[64,128]{1,0:T(8,128)S(1)} %add_add_fusion.4), channel_id=1, source_target_pairs={{0,16},{1,17},{2,18},{3,19},{4,20},{5,21},{6,22},{7,23},{8,24},{9,... | collective-permute-start | bytes 98312 | tf_op jit(solution)/shard_map/ppermute | solution.py:35
  61.6 1.9 %collective-permute-start.13 = (f32[64,128]{1,0:T(8,128)S(1)}, f32[64,128]{1,0:T(8,128)S(1)}, u32[]{:S(2)}, u32[]{:S(2)}) collective-permute-start(f32[64,128]{1,0:T(8,128)S(1)} %add_add_fusion.4), channel_id=1, source_target_pairs={{0,24},{1,25},{2,26},{3,27},{4,28},{5,29},{6,30},{7,31},{8,16},{9,... | collective-permute-start | bytes 98312 | tf_op jit(solution)/shard_map/ppermute | solution.py:35
  64.4 1.1 %collective-permute-done.12 = f32[64,128]{1,0:T(8,128)S(1)} collective-permute-done((f32[64,128]{1,0:T(8,128)S(1)}, f32[64,128]{1,0:T(8,128)S(1)}, u32[]{:S(2)}, u32[]{:S(2)}) %collective-permute-start.12) | collective-permute-done | bytes 32800 | tf_op jit(solution)/shard_map/ppermute | solution.py:35
  65.5 2.1 %collective-permute-done.13 = f32[64,128]{1,0:T(8,128)S(1)} collective-permute-done((f32[64,128]{1,0:T(8,128)S(1)}, f32[64,128]{1,0:T(8,128)S(1)}, u32[]{:S(2)}, u32[]{:S(2)}) %collective-permute-start.13) | collective-permute-done | bytes 32800 | tf_op jit(solution)/shard_map/ppermute | solution.py:35
  67.7 8.3 %compress.4 = (bf16[64,128]{1,0:T(8,128)(2,1)S(1)}, f32[64,64]{1,0:T(8,128)S(1)}) custom-call(f32[64,128]{1,0:T(8,128)S(1)} %add_add_fusion.3.top_ref, f32[64,64]{1,0:T(8,128)S(1)} %broadcast_select_fusion.9.upper_ref), custom_call_target="tpu_custom_call" | custom-call | tf_op jit(solution)/shard_map/compress/pallas_call | solution.py:285
  76.0 1.5 %collective-permute-start.15 = (bf16[64,128]{1,0:T(8,128)(2,1)S(1)}, bf16[64,128]{1,0:T(8,128)(2,1)S(1)}, u32[]{:S(2)}, u32[]{:S(2)}) collective-permute-start(bf16[64,128]{1,0:T(8,128)(2,1)S(1)} %get-tuple-element.17), channel_id=1, source_target_pairs={{0,2},{1,3},{2,0},{3,1},{4,6},{5,7},{6,4},{7,5},{8,10},{9,11},{10,... | collective-permute-start | bytes 49160 | tf_op jit(solution)/shard_map/ppermute | solution.py:35
  78.2 1.7 %collective-permute-done.15 = bf16[64,128]{1,0:T(8,128)(2,1)S(1)} collective-permute-done((bf16[64,128]{1,0:T(8,128)(2,1)S(1)}, bf16[64,128]{1,0:T(8,128)(2,1)S(1)}, u32[]{:S(2)}, u32[]{:S(2)}) %collective-permute-start.15) | collective-permute-done | bytes 16416 | tf_op jit(solution)/shard_map/ppermute | solution.py:35
  80.7 1.7 %collective-permute-start.18 = (f32[64,128]{1,0:T(8,128)S(1)}, f32[64,128]{1,0:T(8,128)S(1)}, u32[]{:S(2)}, u32[]{:S(2)}) collective-permute-start(f32[64,128]{1,0:T(8,128)S(1)} %fusion.20), channel_id=1, source_target_pairs={{0,2},{1,3},{2,0},{3,1},{4,6},{5,7},{6,4},{7,5},{8,10},{9,11},{10,... | collective-permute-start | bytes 98312 | tf_op jit(solution)/shard_map/ppermute | solution.py:35
  83.1 1.7 %collective-permute-start.24 = (f32[64,64]{1,0:T(8,128)S(1)}, f32[64,64]{1,0:T(8,128)S(1)}, u32[]{:S(2)}, u32[]{:S(2)}) collective-permute-start(f32[64,64]{1,0:T(8,128)S(1)} %get-tuple-element.18), channel_id=1, source_target_pairs={{0,2},{1,3},{2,0},{3,1},{4,6},{5,7},{6,4},{7,5},{8,10},{9,11},{10,... | collective-permute-start | bytes 49160 | tf_op jit(solution)/shard_map/ppermute | solution.py:35
  84.8 7.0 %collective-permute-done.18 = f32[64,128]{1,0:T(8,128)S(1)} collective-permute-done((f32[64,128]{1,0:T(8,128)S(1)}, f32[64,128]{1,0:T(8,128)S(1)}, u32[]{:S(2)}, u32[]{:S(2)}) %collective-permute-start.18) | collective-permute-done | bytes 32800 | tf_op jit(solution)/shard_map/ppermute | solution.py:35
  92.4 1.3 %collective-permute-start.22 = (f32[64,128]{1,0:T(8,128)S(1)}, f32[64,128]{1,0:T(8,128)S(1)}, u32[]{:S(2)}, u32[]{:S(2)}) collective-permute-start(f32[64,128]{1,0:T(8,128)S(1)} %add_add_fusion.2), channel_id=1, source_target_pairs={{0,12},{1,13},{2,14},{3,15},{4,8},{5,9},{6,10},{7,11},{8,4},{9,5},... | collective-permute-start | bytes 98312 | tf_op jit(solution)/shard_map/ppermute | solution.py:35
  93.7 1.6 %collective-permute-start.20 = (f32[64,128]{1,0:T(8,128)S(1)}, f32[64,128]{1,0:T(8,128)S(1)}, u32[]{:S(2)}, u32[]{:S(2)}) collective-permute-start(f32[64,128]{1,0:T(8,128)S(1)} %add_add_fusion.2), channel_id=1, source_target_pairs={{0,4},{1,5},{2,6},{3,7},{4,0},{5,1},{6,2},{7,3},{8,12},{9,13},{10,... | collective-permute-start | bytes 98312 | tf_op jit(solution)/shard_map/ppermute | solution.py:35
  95.8 1.5 %collective-permute-done.22 = f32[64,128]{1,0:T(8,128)S(1)} collective-permute-done((f32[64,128]{1,0:T(8,128)S(1)}, f32[64,128]{1,0:T(8,128)S(1)}, u32[]{:S(2)}, u32[]{:S(2)}) %collective-permute-start.22) | collective-permute-done | bytes 32800 | tf_op jit(solution)/shard_map/ppermute | solution.py:35
  97.7 1.7 %collective-permute-start.23 = (f32[64,128]{1,0:T(8,128)S(1)}, f32[64,128]{1,0:T(8,128)S(1)}, u32[]{:S(2)}, u32[]{:S(2)}) collective-permute-start(f32[64,128]{1,0:T(8,128)S(1)} %add_add_fusion.1), channel_id=1, source_target_pairs={{0,16},{1,17},{2,18},{3,19},{4,20},{5,21},{6,22},{7,23},{8,24},{9,... | collective-permute-start | bytes 98312 | tf_op jit(solution)/shard_map/ppermute | solution.py:35
  99.6 3.0 %collective-permute-done.23 = f32[64,128]{1,0:T(8,128)S(1)} collective-permute-done((f32[64,128]{1,0:T(8,128)S(1)}, f32[64,128]{1,0:T(8,128)S(1)}, u32[]{:S(2)}, u32[]{:S(2)}) %collective-permute-start.23) | collective-permute-done | bytes 32800 | tf_op jit(solution)/shard_map/ppermute | solution.py:35
  102.5 8.1 %compress.5 = (bf16[64,128]{1,0:T(8,128)(2,1)S(1)}, f32[64,64]{1,0:T(8,128)}) custom-call(f32[64,128]{1,0:T(8,128)S(1)} %add.125.top_ref, f32[64,64]{1,0:T(8,128)S(1)} %broadcast_select_fusion.8.upper_ref), custom_call_target="tpu_custom_call" | custom-call | tf_op jit(solution)/shard_map/compress/pallas_call | solution.py:285
  (77 shorter events, 15.9 us)
Async XLA Ops:
  1.6 21.0 %collective-permute-start = (bf16[128,512]{1,0:T(8,128)(2,1)S(1)}, bf16[128,512]{1,0:T(8,128)(2,1)S(1)}, u32[]{:S(2)}, u32[]{:S(2)}) collective-permute-start(bf16[128,512]{1,0:T(8,128)(2,1)S(1)} %pad_maximum_fusion.6), channel_id=1, source_target_pairs={{0,4},{4,8},{8,12},{12,16},{16,20},{20,24},{24,28},{1,5},{5,9},{9,... | collective-permute-start | bytes 393224 | tf_op jit(solution)/shard_map/ppermute | solution.py:27
  6.5 16.1 %collective-permute-start.1 = (bf16[128,512]{1,0:T(8,128)(2,1)S(1)}, bf16[128,512]{1,0:T(8,128)(2,1)S(1)}, u32[]{:S(2)}, u32[]{:S(2)}) collective-permute-start(bf16[128,512]{1,0:T(8,128)(2,1)S(1)} %pad_maximum_fusion.7), channel_id=1, source_target_pairs={{4,0},{8,4},{12,8},{16,12},{20,16},{24,20},{28,24},{5,1},{9,5},{13... | collective-permute-start | bytes 393224 | tf_op jit(solution)/shard_map/ppermute | solution.py:28
  10.5 43.2 %collective-permute-start.25 = (bf16[128,4096]{1,0:T(8,128)(2,1)S(1)}, bf16[128,4096]{1,0:T(8,128)(2,1)S(1)}, u32[]{:S(2)}, u32[]{:S(2)}) collective-permute-start(bf16[128,4096]{1,0:T(8,128)(2,1)S(1)} %maximum_maximum_fusion), channel_id=1, source_target_pairs={{0,1},{1,0},{2,3},{3,2},{4,5},{5,4},{6,7},{7,6},{8,9},{9,8},{10,11... | collective-permute-start | bytes 3145736 | tf_op jit(solution)/shard_map/ppermute | solution.py:35
  12.0 3.1 %copy-start = (bf16[7,64,8192]{2,1,0:T(8,128)(2,1)S(1)}, bf16[7,64,8192]{2,1,0:T(8,128)(2,1)}, u32[]{:S(2)}) copy-start(bf16[7,64,8192]{2,1,0:T(8,128)(2,1)} %factor_ref.3) | copy-start | bytes 22020100
  28.5 25.5 %collective-permute-start.7 = (bf16[128,4096]{1,0:T(8,128)(2,1)}, bf16[128,4096]{1,0:T(8,128)(2,1)S(1)}, u32[]{:S(2)}, u32[]{:S(2)}) collective-permute-start(bf16[128,4096]{1,0:T(8,128)(2,1)} %pad_maximum_fusion.2), channel_id=1, source_target_pairs={{0,1},{1,0},{2,3},{3,2},{4,5},{5,4},{6,7},{7,6},{8,9},{9,8},{10,11... | collective-permute-start | bytes 3145736 | tf_op jit(solution)/shard_map/ppermute | solution.py:35
  28.5 6.4 %collective-permute-start.3 = (f32[128,128]{1,0:T(8,128)S(1)}, f32[128,128]{1,0:T(8,128)S(1)}, u32[]{:S(2)}, u32[]{:S(2)}) collective-permute-start(f32[128,128]{1,0:T(8,128)S(1)} %get-tuple-element.13), channel_id=1, source_target_pairs={{0,8},{1,9},{2,10},{3,11},{4,12},{5,13},{6,14},{7,15},{8,0},{9,1},... | collective-permute-start | bytes 196616 | tf_op jit(solution)/shard_map/ppermute | solution.py:35
  32.1 5.2 %collective-permute-start.4 = (f32[128,128]{1,0:T(8,128)S(1)}, f32[128,128]{1,0:T(8,128)S(1)}, u32[]{:S(2)}, u32[]{:S(2)}) collective-permute-start(f32[128,128]{1,0:T(8,128)S(1)} %get-tuple-element.13), channel_id=1, source_target_pairs={{0,12},{1,13},{2,14},{3,15},{4,8},{5,9},{6,10},{7,11},{8,4},{9,5},... | collective-permute-start | bytes 196616 | tf_op jit(solution)/shard_map/ppermute | solution.py:35
  32.7 5.3 %collective-permute-start.2 = (f32[128,128]{1,0:T(8,128)S(1)}, f32[128,128]{1,0:T(8,128)S(1)}, u32[]{:S(2)}, u32[]{:S(2)}) collective-permute-start(f32[128,128]{1,0:T(8,128)S(1)} %get-tuple-element.13), channel_id=1, source_target_pairs={{0,4},{1,5},{2,6},{3,7},{4,0},{5,1},{6,2},{7,3},{8,12},{9,13},{10,... | collective-permute-start | bytes 196616 | tf_op jit(solution)/shard_map/ppermute | solution.py:35
  38.0 6.3 %collective-permute-start.5 = (f32[128,128]{1,0:T(8,128)S(1)}, f32[128,128]{1,0:T(8,128)S(1)}, u32[]{:S(2)}, u32[]{:S(2)}) collective-permute-start(f32[128,128]{1,0:T(8,128)S(1)} %add_add_fusion), channel_id=1, source_target_pairs={{0,16},{1,17},{2,18},{3,19},{4,20},{5,21},{6,22},{7,23},{8,24},{9,... | collective-permute-start | bytes 196616 | tf_op jit(solution)/shard_map/ppermute | solution.py:35
  52.3 1.2 %collective-permute-start.14 = (f32[64,64]{1,0:T(8,128)S(1)}, f32[64,64]{1,0:T(8,128)S(1)}, u32[]{:S(2)}, u32[]{:S(2)}) collective-permute-start(f32[64,64]{1,0:T(8,128)S(1)} %get-tuple-element.16), channel_id=1, source_target_pairs={{0,1},{1,0},{2,3},{3,2},{4,5},{5,4},{6,7},{7,6},{8,9},{9,8},{10,11... | collective-permute-start | bytes 49160 | tf_op jit(solution)/shard_map/ppermute | solution.py:35
  52.4 1.3 %collective-permute-start.6 = (bf16[64,128]{1,0:T(8,128)(2,1)S(1)}, bf16[64,128]{1,0:T(8,128)(2,1)S(1)}, u32[]{:S(2)}, u32[]{:S(2)}) collective-permute-start(bf16[64,128]{1,0:T(8,128)(2,1)S(1)} %get-tuple-element.14), channel_id=1, source_target_pairs={{0,1},{1,0},{2,3},{3,2},{4,5},{5,4},{6,7},{7,6},{8,9},{9,8},{10,11... | collective-permute-start | bytes 49160 | tf_op jit(solution)/shard_map/ppermute | solution.py:35
  54.6 9.4 %copy-start.6 = (bf16[64,2048]{1,0:T(8,128)(2,1)S(1)}, bf16[64,2048]{1,0:T(8,128)(2,1)}, u32[]{:S(2)}) copy-start(bf16[64,2048]{1,0:T(8,128)(2,1)} %get-tuple-element.30) | copy-start | bytes 786436
  54.7 9.4 %copy-start.7 = (bf16[64,2048]{1,0:T(8,128)(2,1)S(1)}, bf16[64,2048]{1,0:T(8,128)(2,1)}, u32[]{:S(2)}) copy-start(bf16[64,2048]{1,0:T(8,128)(2,1)} %get-tuple-element.33) | copy-start | bytes 786436
  54.7 9.4 %copy-start.8 = (bf16[64,2048]{1,0:T(8,128)(2,1)S(1)}, bf16[64,2048]{1,0:T(8,128)(2,1)}, u32[]{:S(2)}) copy-start(bf16[64,2048]{1,0:T(8,128)(2,1)} %get-tuple-element.46) | copy-start | bytes 786436
  54.7 9.4 %copy-start.9 = (bf16[64,2048]{1,0:T(8,128)(2,1)S(1)}, bf16[64,2048]{1,0:T(8,128)(2,1)}, u32[]{:S(2)}) copy-start(bf16[64,2048]{1,0:T(8,128)(2,1)} %get-tuple-element.49) | copy-start | bytes 786436
  55.2 4.0 %collective-permute-start.9 = (f32[64,128]{1,0:T(8,128)S(1)}, f32[64,128]{1,0:T(8,128)S(1)}, u32[]{:S(2)}, u32[]{:S(2)}) collective-permute-start(f32[64,128]{1,0:T(8,128)S(1)} %fusion), channel_id=1, source_target_pairs={{0,4},{1,5},{2,6},{3,7},{4,0},{5,1},{6,2},{7,3},{8,12},{9,13},{10,... | collective-permute-start | bytes 98312 | tf_op jit(solution)/shard_map/ppermute | solution.py:35
  56.6 3.4 %collective-permute-start.10 = (f32[64,128]{1,0:T(8,128)S(1)}, f32[64,128]{1,0:T(8,128)S(1)}, u32[]{:S(2)}, u32[]{:S(2)}) collective-permute-start(f32[64,128]{1,0:T(8,128)S(1)} %fusion), channel_id=1, source_target_pairs={{0,5},{1,4},{2,7},{3,6},{4,1},{5,0},{6,3},{7,2},{8,13},{9,12},{10,... | collective-permute-start | bytes 98312 | tf_op jit(solution)/shard_map/ppermute | solution.py:35
  56.9 3.2 %collective-permute-start.8 = (f32[64,128]{1,0:T(8,128)S(1)}, f32[64,128]{1,0:T(8,128)S(1)}, u32[]{:S(2)}, u32[]{:S(2)}) collective-permute-start(f32[64,128]{1,0:T(8,128)S(1)} %fusion), channel_id=1, source_target_pairs={{0,1},{1,0},{2,3},{3,2},{4,5},{5,4},{6,7},{7,6},{8,9},{9,8},{10,11... | collective-permute-start | bytes 98312 | tf_op jit(solution)/shard_map/ppermute | solution.py:35
  57.4 22.5 %collective-permute-start.16 = (bf16[128,2048]{1,0:T(8,128)(2,1)S(1)}, bf16[128,2048]{1,0:T(8,128)(2,1)S(1)}, u32[]{:S(2)}, u32[]{:S(2)}) collective-permute-start(bf16[128,2048]{1,0:T(8,128)(2,1)S(1)} %fusion.14), channel_id=1, source_target_pairs={{0,2},{1,3},{2,0},{3,1},{4,6},{5,7},{6,4},{7,5},{8,10},{9,11},{10,... | collective-permute-start | bytes 1572872 | tf_op jit(solution)/shard_map/ppermute | solution.py:35
  60.1 5.4 %collective-permute-start.12 = (f32[64,128]{1,0:T(8,128)S(1)}, f32[64,128]{1,0:T(8,128)S(1)}, u32[]{:S(2)}, u32[]{:S(2)}) collective-permute-start(f32[64,128]{1,0:T(8,128)S(1)} %add_add_fusion.4), channel_id=1, source_target_pairs={{0,16},{1,17},{2,18},{3,19},{4,20},{5,21},{6,22},{7,23},{8,24},{9,... | collective-permute-start | bytes 98312 | tf_op jit(solution)/shard_map/ppermute | solution.py:35
  61.6 6.0 %collective-permute-start.13 = (f32[64,128]{1,0:T(8,128)S(1)}, f32[64,128]{1,0:T(8,128)S(1)}, u32[]{:S(2)}, u32[]{:S(2)}) collective-permute-start(f32[64,128]{1,0:T(8,128)S(1)} %add_add_fusion.4), channel_id=1, source_target_pairs={{0,24},{1,25},{2,26},{3,27},{4,28},{5,29},{6,30},{7,31},{8,16},{9,... | collective-permute-start | bytes 98312 | tf_op jit(solution)/shard_map/ppermute | solution.py:35
  63.6 4.2 %collective-permute-start.11 = (f32[64,128]{1,0:T(8,128)S(1)}, f32[64,128]{1,0:T(8,128)S(1)}, u32[]{:S(2)}, u32[]{:S(2)}) collective-permute-start(f32[64,128]{1,0:T(8,128)S(1)} %add_add_fusion.4), channel_id=1, source_target_pairs={{0,8},{1,9},{2,10},{3,11},{4,12},{5,13},{6,14},{7,15},{8,0},{9,1},... | collective-permute-start | bytes 98312 | tf_op jit(solution)/shard_map/ppermute | solution.py:35
  76.0 3.9 %collective-permute-start.15 = (bf16[64,128]{1,0:T(8,128)(2,1)S(1)}, bf16[64,128]{1,0:T(8,128)(2,1)S(1)}, u32[]{:S(2)}, u32[]{:S(2)}) collective-permute-start(bf16[64,128]{1,0:T(8,128)(2,1)S(1)} %get-tuple-element.17), channel_id=1, source_target_pairs={{0,2},{1,3},{2,0},{3,1},{4,6},{5,7},{6,4},{7,5},{8,10},{9,11},{10,... | collective-permute-start | bytes 49160 | tf_op jit(solution)/shard_map/ppermute | solution.py:35
  77.6 21.8 %collective-permute-start.26 = (bf16[128,2048]{1,0:T(8,128)(2,1)S(1)}, bf16[128,2048]{1,0:T(8,128)(2,1)S(1)}, u32[]{:S(2)}, u32[]{:S(2)}) collective-permute-start(bf16[128,2048]{1,0:T(8,128)(2,1)S(1)} %fusion.13), channel_id=1, source_target_pairs={{0,2},{1,3},{2,0},{3,1},{4,6},{5,7},{6,4},{7,5},{8,10},{9,11},{10,... | collective-permute-start | bytes 1572872 | tf_op jit(solution)/shard_map/ppermute | solution.py:35
  80.7 11.1 %collective-permute-start.18 = (f32[64,128]{1,0:T(8,128)S(1)}, f32[64,128]{1,0:T(8,128)S(1)}, u32[]{:S(2)}, u32[]{:S(2)}) collective-permute-start(f32[64,128]{1,0:T(8,128)S(1)} %fusion.20), channel_id=1, source_target_pairs={{0,2},{1,3},{2,0},{3,1},{4,6},{5,7},{6,4},{7,5},{8,10},{9,11},{10,... | collective-permute-start | bytes 98312 | tf_op jit(solution)/shard_map/ppermute | solution.py:35
  82.4 9.4 %collective-permute-start.19 = (f32[64,128]{1,0:T(8,128)S(1)}, f32[64,128]{1,0:T(8,128)S(1)}, u32[]{:S(2)}, u32[]{:S(2)}) collective-permute-start(f32[64,128]{1,0:T(8,128)S(1)} %fusion.20), channel_id=1, source_target_pairs={{0,3},{1,2},{2,1},{3,0},{4,7},{5,6},{6,5},{7,4},{8,11},{9,10},{10,... | collective-permute-start | bytes 98312 | tf_op jit(solution)/shard_map/ppermute | solution.py:35
  82.4 9.4 %collective-permute-start.17 = (f32[64,128]{1,0:T(8,128)S(1)}, f32[64,128]{1,0:T(8,128)S(1)}, u32[]{:S(2)}, u32[]{:S(2)}) collective-permute-start(f32[64,128]{1,0:T(8,128)S(1)} %fusion.20), channel_id=1, source_target_pairs={{0,1},{1,0},{2,3},{3,2},{4,5},{5,4},{6,7},{7,6},{8,9},{9,8},{10,11... | collective-permute-start | bytes 98312 | tf_op jit(solution)/shard_map/ppermute | solution.py:35
  83.1 12.2 %collective-permute-start.24 = (f32[64,64]{1,0:T(8,128)S(1)}, f32[64,64]{1,0:T(8,128)S(1)}, u32[]{:S(2)}, u32[]{:S(2)}) collective-permute-start(f32[64,64]{1,0:T(8,128)S(1)} %get-tuple-element.18), channel_id=1, source_target_pairs={{0,2},{1,3},{2,0},{3,1},{4,6},{5,7},{6,4},{7,5},{8,10},{9,11},{10,... | collective-permute-start | bytes 49160 | tf_op jit(solution)/shard_map/ppermute | solution.py:35
  91.8 4.0 %collective-permute-start.21 = (f32[64,128]{1,0:T(8,128)S(1)}, f32[64,128]{1,0:T(8,128)S(1)}, u32[]{:S(2)}, u32[]{:S(2)}) collective-permute-start(f32[64,128]{1,0:T(8,128)S(1)} %add_add_fusion.2), channel_id=1, source_target_pairs={{0,8},{1,9},{2,10},{3,11},{4,12},{5,13},{6,14},{7,15},{8,0},{9,1},... | collective-permute-start | bytes 98312 | tf_op jit(solution)/shard_map/ppermute | solution.py:35
  92.4 4.8 %collective-permute-start.22 = (f32[64,128]{1,0:T(8,128)S(1)}, f32[64,128]{1,0:T(8,128)S(1)}, u32[]{:S(2)}, u32[]{:S(2)}) collective-permute-start(f32[64,128]{1,0:T(8,128)S(1)} %add_add_fusion.2), channel_id=1, source_target_pairs={{0,12},{1,13},{2,14},{3,15},{4,8},{5,9},{6,10},{7,11},{8,4},{9,5},... | collective-permute-start | bytes 98312 | tf_op jit(solution)/shard_map/ppermute | solution.py:35
  93.7 3.9 %collective-permute-start.20 = (f32[64,128]{1,0:T(8,128)S(1)}, f32[64,128]{1,0:T(8,128)S(1)}, u32[]{:S(2)}, u32[]{:S(2)}) collective-permute-start(f32[64,128]{1,0:T(8,128)S(1)} %add_add_fusion.2), channel_id=1, source_target_pairs={{0,4},{1,5},{2,6},{3,7},{4,0},{5,1},{6,2},{7,3},{8,12},{9,13},{10,... | collective-permute-start | bytes 98312 | tf_op jit(solution)/shard_map/ppermute | solution.py:35
  97.7 4.9 %collective-permute-start.23 = (f32[64,128]{1,0:T(8,128)S(1)}, f32[64,128]{1,0:T(8,128)S(1)}, u32[]{:S(2)}, u32[]{:S(2)}) collective-permute-start(f32[64,128]{1,0:T(8,128)S(1)} %add_add_fusion.1), channel_id=1, source_target_pairs={{0,16},{1,17},{2,18},{3,19},{4,20},{5,21},{6,22},{7,23},{8,24},{9,... | collective-permute-start | bytes 98312 | tf_op jit(solution)/shard_map/ppermute | solution.py:35
  (5 other events, 8.2 us)

commit v6 on v4

--- a/solution.py
+++ b/solution.py
@@ -81,36 +81,48 @@
     return jnp.concatenate(pieces, axis=1)
 
 
-def inside_kernel(edge, spots, prior_ref, snap_ref, factor_ref, weighted_ref, gram_ref, bank):
+def fetch(factor_ref, start, fetched, arrived, step):
+    chunk = fetched.shape[3]
+    piece = factor_ref.at[:, :, pl.ds(pl.multiple_of(start, TILE), chunk)]
+    return pltpu.make_async_copy(piece, fetched.at[step], arrived.at[step])
+
+
+def inside_kernel(edge, spots, prior_ref, snap_ref, factor_ref, weighted_ref, gram_ref, bank, fetched, arrived):
     step = pl.program_id(0)
     rows, width = prior_ref.shape
-    _, block, chunk = factor_ref.shape
+    steps, _, block, chunk = fetched.shape
     whole = width + 2 * edge
 
     @pl.when(step == 0)
     def _():
+        for i in range(steps):
+            fetch(factor_ref, (i + 1) * chunk, fetched, arrived, i).start()
         bank[:rows, edge:edge + width] = prior_ref[...]
         bank[rows:, edge:edge + width] = snap_ref[...]
         fill_odd(bank, whole, block, edge, edge + width)
         gram_ref[...] = jnp.zeros_like(gram_ref)
 
     shift = lax.axis_index("space") * (width // block) - edge // block
-    weighted = weigh_chunk(spots, (step + 1) * (chunk // block), shift, bank, factor_ref)
+    fetch(factor_ref, (step + 1) * chunk, fetched, arrived, step).wait()
+    weighted = weigh_chunk(spots, (step + 1) * (chunk // block), shift, bank, fetched.at[step])
     weighted_ref[...] = weighted
     gram_ref[...] += lax.dot_general(weighted, weighted, NT, preferred_element_type=F32)
 
 
 def border_kernel(
-    width, spots, prior_ref, snap_ref, low_ref, high_ref, factor_ref, part_ref, kept_ref, weighted_ref, gram_ref, bank
+    width, spots, prior_ref, snap_ref, low_ref, high_ref, factor_ref, part_ref, kept_ref, weighted_ref, gram_ref, bank,
+    fetched, arrived,
 ):
     step = pl.program_id(0)
     rows, span = prior_ref.shape
     edge = low_ref.shape[1]
-    _, block, chunk = factor_ref.shape
+    steps, _, block, chunk = fetched.shape
     whole = span + edge
 
     @pl.when(step == 0)
     def _():
+        for i in range(steps):
+            fetch(factor_ref, i * (width - chunk), fetched, arrived, i).start()
         bank[:, :edge] = low_ref[...]
         bank[:rows, edge:whole] = prior_ref[...]
         bank[rows:, edge:whole] = snap_ref[...]
@@ -126,7 +138,8 @@
     bank[:, whole + block:whole + TILE] = bank[:, :block]
     bank[:, 2 * whole:2 * whole + block] = bank[:, whole - block:whole]
     shift = lax.axis_index("space") * (width // block) - edge // block + step * ((width + 2 * edge - whole) // block)
-    weighted = weigh_chunk(spots, step * ((width - chunk) // block), shift, bank, factor_ref)
+    fetch(factor_ref, step * (width - chunk), fetched, arrived, step).wait()
+    weighted = weigh_chunk(spots, step * ((width - chunk) // block), shift, bank, fetched.at[step])
     weighted_ref[...] = weighted
     gram_ref[...] += lax.dot_general(weighted, weighted, NT, preferred_element_type=F32)
 
@@ -142,6 +155,9 @@
     low, high = halo((prior, snapshots), "space", edge)
     spots = neighbours.T
     full = lambda i, s: (0, 0)
+    fetching = lambda steps: [
+        pltpu.VMEM((steps, count, block, chunk), BF16), pltpu.SemaphoreType.DMA((steps,))
+    ]
     shapes = (
         jax.ShapeDtypeStruct((columns, width), BF16),
         jax.ShapeDtypeStruct((columns, columns), F32),
@@ -156,13 +172,13 @@
             in_specs=[
                 pl.BlockSpec((rows, width), full),
                 pl.BlockSpec((rows, width), full),
-                pl.BlockSpec((count, block, chunk), lambda i, s: (0, 0, i + 1)),
+                pl.BlockSpec(memory_space=pl.ANY),
             ],
             out_specs=(
                 pl.BlockSpec((columns, chunk), lambda i, s: (0, i + 1)),
                 pl.BlockSpec((columns, columns), full),
             ),
-            scratch_shapes=[pltpu.VMEM((columns, 2 * (width + 2 * edge) + TILE), BF16)],
+            scratch_shapes=[pltpu.VMEM((columns, 2 * (width + 2 * edge) + TILE), BF16)] + fetching(chunks - 2),
         ),
         compiler_params=params,
         cost_estimate=pl.CostEstimate(
@@ -182,7 +198,7 @@
                 pl.BlockSpec((rows, span), lambda i, s: (0, i * ends)),
                 pl.BlockSpec((columns, edge), full),
                 pl.BlockSpec((columns, edge), full),
-                pl.BlockSpec((count, block, chunk), lambda i, s: (0, 0, i * (chunks - 1))),
+                pl.BlockSpec(memory_space=pl.ANY),
                 pl.BlockSpec((columns, columns), full),
                 pl.BlockSpec(memory_space=pl.ANY),
             ],
@@ -190,7 +206,7 @@
                 pl.BlockSpec((columns, chunk), lambda i, s: (0, i * (chunks - 1))),
                 pl.BlockSpec((columns, columns), full),
             ),
-            scratch_shapes=[pltpu.VMEM((columns, 2 * (span + edge) + TILE), BF16)],
+            scratch_shapes=[pltpu.VMEM((columns, 2 * (span + edge) + TILE), BF16)] + fetching(2),
         ),
         input_output_aliases={7: 0},
         compiler_params=params,
@@ -325,26 +341,37 @@
     members = lax.axis_size("tm")
     places = members * lax.axis_size("space")
     across = [1 << i for i in range(members.bit_length() - 1, places.bit_length() - 1)]
-    coefficients, own = compress(first_kernel, total(gram, across))
     member = lax.axis_index("tm")
     width = snapshots.shape[1] // members
+    partner_weighted = None
+    coefficients, own = compress(first_kernel, total(gram, across))
     for level in range(members.bit_length() - 1):
         step = 1 << level
         bit = member // step % 2
         upper_half = bit == 1
-        weighted = combine(coefficients, weighted)
-        sent = swapped(shared_out(weighted, width, 1 - bit), step)
         partner_own = swapped(own, step)
-        weighted = ordered(upper_half, shared_out(weighted, width, bit), sent)
+        if partner_weighted is None:
+            weighted = combine(coefficients, weighted)
+            partner_weighted = swapped(shared_out(weighted, width, 1 - bit), step)
+            own_weighted = shared_out(weighted, width, bit)
+        else:
+            partner_weighted = combine(swapped(coefficients, step), partner_weighted)
+            own_weighted = combine(coefficients, shared_out(weighted, width, bit))
+        weighted = ordered(upper_half, own_weighted, partner_weighted)
         if level == 0:
             stacked = combine_two(coefficients, prior_basis, snapshots)
         else:
             stacked = combine(coefficients, stacked)
-        sent = swapped(shared_out(stacked, width, 1 - bit), step)
-        stacked = ordered(upper_half, shared_out(stacked, width, bit), sent)
+        partner_stacked = swapped(shared_out(stacked, width, 1 - bit), step)
+        stacked = ordered(upper_half, shared_out(stacked, width, bit), partner_stacked)
         top = lax.dot_general(weighted[:RANK], weighted, NT, preferred_element_type=F32)
+        last = 2 * step == members
+        if not last:
+            next_bit = member // (2 * step) % 2
+            partner_weighted = swapped(shared_out(weighted, width, 1 - next_bit), 2 * step)
         top = total(top, [1 << i for i in range(level + 1)] + across)
-        coefficients, own = compress(functools.partial(merge_kernel, 2 * step == members), top, jnp.where(upper_half, own, partner_own))
+        upper = jnp.where(upper_half, own, partner_own)
+        coefficients, own = compress(functools.partial(merge_kernel, last), top, upper)
     return combine(coefficients, stacked), combine(coefficients, weighted)
 
 

time: 109 us -> 107 us (0.982)
  waiting for transfers between devices: 27.5 us -> 24.6 us
    ppermute x23 -> x24, waiting for transfers between devices: 27.5 us -> 24.6 us  [swapped(): return lax.ppermute(block, axes, [(i, i ^ mask) for i in range(count)])]
    ppermute x23 -> x24, starting transfers between devices: 25 us -> 25.3 us  [swapped(): return lax.ppermute(block, axes, [(i, i ^ mask) for i in range(count)])]
    dot_general x5 -> x6, matrix products: 2.88 us -> 3.02 us  [combine(): return jnp.dot(coefficients, rows, preferred_element_type=F32).astype(BF16)]
  transfers between devices with their start and end apart: 25 -> 26, of which waited for: 15 -> 13; matrix products, arithmetic and copies ran while one was open for 3% -> 4% of each run, Pallas kernels for 17% -> 17%
where the time goes in v6:
time: 107 us
  Pallas kernels  40.8 us (38%)
  starting transfers between devices  32.1 us (30%)
  waiting for transfers between devices  24.6 us (23%)
  matrix products  4.68 us (4%)
  local copies, waits for them, and re-layouts  2.35 us (2%)
  other arithmetic  1.58 us (1%)
    ppermute x24, starting transfers between devices, swapped(): return lax.ppermute(block, axes, [(i, i ^ mask) for i in range(count)])  25.3 us
    ppermute x24, waiting for transfers between devices, swapped(): return lax.ppermute(block, axes, [(i, i ^ mask) for i in range(count)])  24.6 us
    pallas_call x3, Pallas kernels, compress(): pl.pallas_call(kernel, out_shape=(jax.ShapeDtypeStruct((RANK, gram[0].sha...  24.5 us
    pallas_call x1, Pallas kernels, weigh(): pl.pallas_call(functools.partial(inside_kernel, edge), out_shape=shapes,...  10.2 us
    pallas_call x1, Pallas kernels, weigh(): pl.pallas_call(functools.partial(border_kernel, width), out_shape=shapes,...  6.15 us
    ppermute x1, starting transfers between devices, halo(): low = lax.ppermute(last, axis, forward)  5.51 us
    dot_general x6, matrix products, combine(): return jnp.dot(coefficients, rows, preferred_element_type=F32).astype(BF16)  3.02 us
  transfers between devices with their start and end apart: 26, of which 13 were waited for; matrix products, arithmetic and copies ran while one was open for 4% of the time, Pallas kernels for 17%

profile of v6, /device:TPU:0, one launch (start us, length us, event | category | flops | bytes accessed | tf_op | source)
XLA Modules:
  0.0 107.0 jit_solution(14940430985848003455)
XLA Ops:
  0.6 1.0 fusion.22
  1.6 1.3 %collective-permute-start.1 = (bf16[128,512]{1,0:T(8,128)(2,1)S(1)}, bf16[128,512]{1,0:T(8,128)(2,1)S(1)}, u32[]{:S(2)}, u32[]{:S(2)}) collective-permute-start(bf16[128,512]{1,0:T(8,128)(2,1)S(1)} %pad_maximum_fusion.10), channel_id=1, source_target_pairs={{4,0},{8,4},{12,8},{16,12},{20,16},{24,20},{28,24},{5,1},{9,5},{13... | collective-permute-start | bytes 393224 | tf_op jit(solution)/shard_map/ppermute | solution.py:28
  2.9 5.5 %collective-permute-start = (bf16[128,512]{1,0:T(8,128)(2,1)S(1)}, bf16[128,512]{1,0:T(8,128)(2,1)S(1)}, u32[]{:S(2)}, u32[]{:S(2)}) collective-permute-start(bf16[128,512]{1,0:T(8,128)(2,1)S(1)} %pad_maximum_fusion.9), channel_id=1, source_target_pairs={{0,4},{4,8},{8,12},{12,16},{16,20},{20,24},{24,28},{1,5},{5,9},{9,... | collective-permute-start | bytes 393224 | tf_op jit(solution)/shard_map/ppermute | solution.py:27
  8.4 10.2 %weigh_inside.1 = (bf16[128,8192]{1,0:T(8,128)(2,1)}, f32[128,128]{1,0:T(8,128)}) custom-call(s32[7,128]{1,0:T(8,128)} %bitcast.13, bf16[64,8192]{1,0:T(8,128)(2,1)} %prior_ref.3, bf16[64,8192]{1,0:T(8,128)(2,1)} %snap_ref.3, bf16[7,64,8192]{2,1,0:T(8,128)(2,1)} %factor_ref.3), custom_call_target="tpu_custom_call" | custom-call | flops 3758096384 | bytes 7340032 | tf_op jit(solution)/shard_map/weigh_inside/pallas_call | solution.py:166
  19.3 6.1 %weigh_border.1 = (bf16[128,8192]{1,0:T(8,128)(2,1)}, f32[128,128]{1,0:T(8,128)}) custom-call(s32[7,128]{1,0:T(8,128)} %bitcast.14, bf16[64,8192]{1,0:T(8,128)(2,1)} %prior_ref.3, bf16[64,8192]{1,0:T(8,128)(2,1)} %snap_ref.3, bf16[128,512]{1,0:T(8,128)(2,1)} %copy-done.4, bf16[128,512]{1,0:T(8,128)(2,1)} %copy-done.3, ...), custom_call_target="tpu_custom_call", output_to_operand_aliasing={{0}: (7, {})} | custom-call | tf_op jit(solution)/shard_map/weigh_border/pallas_call | solution.py:190
  25.5 3.0 %collective-permute-start.2 = (f32[128,128]{1,0:T(8,128)}, f32[128,128]{1,0:T(8,128)S(1)}, u32[]{:S(2)}, u32[]{:S(2)}) collective-permute-start(f32[128,128]{1,0:T(8,128)} %get-tuple-element.13), channel_id=1, source_target_pairs={{0,4},{1,5},{2,6},{3,7},{4,0},{5,1},{6,2},{7,3},{8,12},{9,13},{10,... | collective-permute-start | bytes 196616 | tf_op jit(solution)/shard_map/ppermute | solution.py:35
  28.5 1.6 %collective-permute-start.3 = (f32[128,128]{1,0:T(8,128)}, f32[128,128]{1,0:T(8,128)S(1)}, u32[]{:S(2)}, u32[]{:S(2)}) collective-permute-start(f32[128,128]{1,0:T(8,128)} %get-tuple-element.13), channel_id=1, source_target_pairs={{0,8},{1,9},{2,10},{3,11},{4,12},{5,13},{6,14},{7,15},{8,0},{9,1},... | collective-permute-start | bytes 196616 | tf_op jit(solution)/shard_map/ppermute | solution.py:35
  30.9 2.0 %collective-permute-done.3 = f32[128,128]{1,0:T(8,128)S(1)} collective-permute-done((f32[128,128]{1,0:T(8,128)}, f32[128,128]{1,0:T(8,128)S(1)}, u32[]{:S(2)}, u32[]{:S(2)}) %collective-permute-start.3) | collective-permute-done | bytes 65568 | tf_op jit(solution)/shard_map/ppermute | solution.py:35
  32.9 2.5 %collective-permute-done.4 = f32[128,128]{1,0:T(8,128)S(1)} collective-permute-done((f32[128,128]{1,0:T(8,128)}, f32[128,128]{1,0:T(8,128)S(1)}, u32[]{:S(2)}, u32[]{:S(2)}) %collective-permute-start.4) | collective-permute-done | bytes 65568 | tf_op jit(solution)/shard_map/ppermute | solution.py:35
  36.3 1.1 collective-permute-start.5
  37.4 4.7 %collective-permute-done.5 = f32[128,128]{1,0:T(8,128)S(1)} collective-permute-done((f32[128,128]{1,0:T(8,128)S(1)}, f32[128,128]{1,0:T(8,128)S(1)}, u32[]{:S(2)}, u32[]{:S(2)}) %collective-permute-start.5) | collective-permute-done | bytes 65568 | tf_op jit(solution)/shard_map/ppermute | solution.py:35
  42.1 8.0 %compress.3 = (bf16[64,128]{1,0:T(8,128)(2,1)S(1)}, f32[64,64]{1,0:T(8,128)S(1)}) custom-call(f32[128,128]{1,0:T(8,128)S(1)} %add.102.gram_ref), custom_call_target="tpu_custom_call" | custom-call | tf_op jit(solution)/shard_map/compress/pallas_call | solution.py:301
  54.5 1.6 %collective-permute-start.9 = (f32[64,128]{1,0:T(8,128)S(1)}, f32[64,128]{1,0:T(8,128)S(1)}, u32[]{:S(2)}, u32[]{:S(2)}) collective-permute-start(f32[64,128]{1,0:T(8,128)S(1)} %fusion.1), channel_id=1, source_target_pairs={{0,5},{1,4},{2,7},{3,6},{4,1},{5,0},{6,3},{7,2},{8,13},{9,12},{10,... | collective-permute-start | bytes 98312 | tf_op jit(solution)/shard_map/ppermute | solution.py:35
  56.2 1.5 %collective-permute-start.15 = (bf16[128,2048]{1,0:T(8,128)(2,1)S(1)}, bf16[128,2048]{1,0:T(8,128)(2,1)S(1)}, u32[]{:S(2)}, u32[]{:S(2)}) collective-permute-start(bf16[128,2048]{1,0:T(8,128)(2,1)S(1)} %fusion.5), channel_id=1, source_target_pairs={{0,2},{1,3},{2,0},{3,1},{4,6},{5,7},{6,4},{7,5},{8,10},{9,11},{10,... | collective-permute-start | bytes 1572872 | tf_op jit(solution)/shard_map/ppermute | solution.py:35
  59.0 2.1 %collective-permute-start.11 = (f32[64,128]{1,0:T(8,128)S(1)}, f32[64,128]{1,0:T(8,128)S(1)}, u32[]{:S(2)}, u32[]{:S(2)}) collective-permute-start(f32[64,128]{1,0:T(8,128)S(1)} %add_add_fusion.4), channel_id=1, source_target_pairs={{0,16},{1,17},{2,18},{3,19},{4,20},{5,21},{6,22},{7,23},{8,24},{9,... | collective-permute-start | bytes 98312 | tf_op jit(solution)/shard_map/ppermute | solution.py:35
  61.1 1.8 %collective-permute-start.12 = (f32[64,128]{1,0:T(8,128)S(1)}, f32[64,128]{1,0:T(8,128)S(1)}, u32[]{:S(2)}, u32[]{:S(2)}) collective-permute-start(f32[64,128]{1,0:T(8,128)S(1)} %add_add_fusion.4), channel_id=1, source_target_pairs={{0,24},{1,25},{2,26},{3,27},{4,28},{5,29},{6,30},{7,31},{8,16},{9,... | collective-permute-start | bytes 98312 | tf_op jit(solution)/shard_map/ppermute | solution.py:35
  63.1 1.3 %collective-permute-done.11 = f32[64,128]{1,0:T(8,128)S(1)} collective-permute-done((f32[64,128]{1,0:T(8,128)S(1)}, f32[64,128]{1,0:T(8,128)S(1)}, u32[]{:S(2)}, u32[]{:S(2)}) %collective-permute-start.11) | collective-permute-done | bytes 32800 | tf_op jit(solution)/shard_map/ppermute | solution.py:35
  64.4 2.4 %collective-permute-done.12 = f32[64,128]{1,0:T(8,128)S(1)} collective-permute-done((f32[64,128]{1,0:T(8,128)S(1)}, f32[64,128]{1,0:T(8,128)S(1)}, u32[]{:S(2)}, u32[]{:S(2)}) %collective-permute-start.12) | collective-permute-done | bytes 32800 | tf_op jit(solution)/shard_map/ppermute | solution.py:35
  66.8 8.3 %compress.4 = (bf16[64,128]{1,0:T(8,128)(2,1)S(1)}, f32[64,64]{1,0:T(8,128)S(1)}) custom-call(f32[64,128]{1,0:T(8,128)S(1)} %add_add_fusion.3.top_ref, f32[64,64]{1,0:T(8,128)S(1)} %broadcast_select_fusion.9.upper_ref), custom_call_target="tpu_custom_call" | custom-call | tf_op jit(solution)/shard_map/compress/pallas_call | solution.py:301
  75.2 1.5 %collective-permute-start.23 = (f32[64,64]{1,0:T(8,128)S(1)}, f32[64,64]{1,0:T(8,128)S(1)}, u32[]{:S(2)}, u32[]{:S(2)}) collective-permute-start(f32[64,64]{1,0:T(8,128)S(1)} %get-tuple-element.18), channel_id=1, source_target_pairs={{0,2},{1,3},{2,0},{3,1},{4,6},{5,7},{6,4},{7,5},{8,10},{9,11},{10,... | collective-permute-start | bytes 49160 | tf_op jit(solution)/shard_map/ppermute | solution.py:35
  77.5 2.9 %collective-permute-done.14 = bf16[64,128]{1,0:T(8,128)(2,1)S(1)} collective-permute-done((bf16[64,128]{1,0:T(8,128)(2,1)S(1)}, bf16[64,128]{1,0:T(8,128)(2,1)S(1)}, u32[]{:S(2)}, u32[]{:S(2)}) %collective-permute-start.14) | collective-permute-done | bytes 16416 | tf_op jit(solution)/shard_map/ppermute | solution.py:35
  81.9 1.3 %collective-permute-start.18 = (f32[64,128]{1,0:T(8,128)S(1)}, f32[64,128]{1,0:T(8,128)S(1)}, u32[]{:S(2)}, u32[]{:S(2)}) collective-permute-start(f32[64,128]{1,0:T(8,128)S(1)} %fusion.11), channel_id=1, source_target_pairs={{0,3},{1,2},{2,1},{3,0},{4,7},{5,6},{6,5},{7,4},{8,11},{9,10},{10,... | collective-permute-start | bytes 98312 | tf_op jit(solution)/shard_map/ppermute | solution.py:35
  83.7 1.8 %collective-permute-done.17 = f32[64,128]{1,0:T(8,128)S(1)} collective-permute-done((f32[64,128]{1,0:T(8,128)S(1)}, f32[64,128]{1,0:T(8,128)S(1)}, u32[]{:S(2)}, u32[]{:S(2)}) %collective-permute-start.17) | collective-permute-done | bytes 32800 | tf_op jit(solution)/shard_map/ppermute | solution.py:35
  85.6 1.7 %collective-permute-start.19 = (f32[64,128]{1,0:T(8,128)S(1)}, f32[64,128]{1,0:T(8,128)S(1)}, u32[]{:S(2)}, u32[]{:S(2)}) collective-permute-start(f32[64,128]{1,0:T(8,128)S(1)} %add_add_fusion.2), channel_id=1, source_target_pairs={{0,4},{1,5},{2,6},{3,7},{4,0},{5,1},{6,2},{7,3},{8,12},{9,13},{10,... | collective-permute-start | bytes 98312 | tf_op jit(solution)/shard_map/ppermute | solution.py:35
  87.3 1.8 %collective-permute-start.21 = (f32[64,128]{1,0:T(8,128)S(1)}, f32[64,128]{1,0:T(8,128)S(1)}, u32[]{:S(2)}, u32[]{:S(2)}) collective-permute-start(f32[64,128]{1,0:T(8,128)S(1)} %add_add_fusion.2), channel_id=1, source_target_pairs={{0,12},{1,13},{2,14},{3,15},{4,8},{5,9},{6,10},{7,11},{8,4},{9,5},... | collective-permute-start | bytes 98312 | tf_op jit(solution)/shard_map/ppermute | solution.py:35
  89.5 1.6 %collective-permute-done.20 = f32[64,128]{1,0:T(8,128)S(1)} collective-permute-done((f32[64,128]{1,0:T(8,128)S(1)}, f32[64,128]{1,0:T(8,128)S(1)}, u32[]{:S(2)}, u32[]{:S(2)}) %collective-permute-start.20) | collective-permute-done | bytes 32800 | tf_op jit(solution)/shard_map/ppermute | solution.py:35
  91.2 0.9 collective-permute-done.21
  92.1 2.4 %collective-permute-start.22 = (f32[64,128]{1,0:T(8,128)S(1)}, f32[64,128]{1,0:T(8,128)S(1)}, u32[]{:S(2)}, u32[]{:S(2)}) collective-permute-start(f32[64,128]{1,0:T(8,128)S(1)} %add_add_fusion.1), channel_id=1, source_target_pairs={{0,16},{1,17},{2,18},{3,19},{4,20},{5,21},{6,22},{7,23},{8,24},{9,... | collective-permute-start | bytes 98312 | tf_op jit(solution)/shard_map/ppermute | solution.py:35
  94.6 2.3 %collective-permute-done.22 = f32[64,128]{1,0:T(8,128)S(1)} collective-permute-done((f32[64,128]{1,0:T(8,128)S(1)}, f32[64,128]{1,0:T(8,128)S(1)}, u32[]{:S(2)}, u32[]{:S(2)}) %collective-permute-start.22) | collective-permute-done | bytes 32800 | tf_op jit(solution)/shard_map/ppermute | solution.py:35
  97.0 8.1 %compress.5 = (bf16[64,128]{1,0:T(8,128)(2,1)S(1)}, f32[64,64]{1,0:T(8,128)}) custom-call(f32[64,128]{1,0:T(8,128)S(1)} %add.123.top_ref, f32[64,64]{1,0:T(8,128)S(1)} %broadcast_select_fusion.8.upper_ref), custom_call_target="tpu_custom_call" | custom-call | tf_op jit(solution)/shard_map/compress/pallas_call | solution.py:301
  105.1 0.9 convolution_convert_fusion.2
  106.0 0.9 convolution_convert_fusion.3
  (66 shorter events, 11.7 us)
Async XLA Ops:
  1.6 17.0 %collective-permute-start.1 = (bf16[128,512]{1,0:T(8,128)(2,1)S(1)}, bf16[128,512]{1,0:T(8,128)(2,1)S(1)}, u32[]{:S(2)}, u32[]{:S(2)}) collective-permute-start(bf16[128,512]{1,0:T(8,128)(2,1)S(1)} %pad_maximum_fusion.10), channel_id=1, source_target_pairs={{4,0},{8,4},{12,8},{16,12},{20,16},{24,20},{28,24},{5,1},{9,5},{13... | collective-permute-start | bytes 393224 | tf_op jit(solution)/shard_map/ppermute | solution.py:28
  2.9 15.7 %collective-permute-start = (bf16[128,512]{1,0:T(8,128)(2,1)S(1)}, bf16[128,512]{1,0:T(8,128)(2,1)S(1)}, u32[]{:S(2)}, u32[]{:S(2)}) collective-permute-start(bf16[128,512]{1,0:T(8,128)(2,1)S(1)} %pad_maximum_fusion.9), channel_id=1, source_target_pairs={{0,4},{4,8},{8,12},{12,16},{16,20},{20,24},{24,28},{1,5},{5,9},{9,... | collective-permute-start | bytes 393224 | tf_op jit(solution)/shard_map/ppermute | solution.py:27
  18.6 0.7 copy-start.3
  18.6 0.7 copy-start.4
  19.3 30.8 %copy-start.1 = (bf16[64,8192]{1,0:T(8,128)(2,1)S(1)}, bf16[64,8192]{1,0:T(8,128)(2,1)}, u32[]{:S(2)}) copy-start(bf16[64,8192]{1,0:T(8,128)(2,1)} %snap_ref.3) | copy-start | bytes 3145732
  25.5 25.1 %copy-start = (bf16[128,8192]{1,0:T(8,128)(2,1)S(1)}, bf16[128,8192]{1,0:T(8,128)(2,1)}, u32[]{:S(2)}) copy-start(bf16[128,8192]{1,0:T(8,128)(2,1)} %get-tuple-element.15) | copy-start | bytes 6291460
  25.5 5.4 %collective-permute-start.2 = (f32[128,128]{1,0:T(8,128)}, f32[128,128]{1,0:T(8,128)S(1)}, u32[]{:S(2)}, u32[]{:S(2)}) collective-permute-start(f32[128,128]{1,0:T(8,128)} %get-tuple-element.13), channel_id=1, source_target_pairs={{0,4},{1,5},{2,6},{3,7},{4,0},{5,1},{6,2},{7,3},{8,12},{9,13},{10,... | collective-permute-start | bytes 196616 | tf_op jit(solution)/shard_map/ppermute | solution.py:35
  28.5 4.5 %collective-permute-start.3 = (f32[128,128]{1,0:T(8,128)}, f32[128,128]{1,0:T(8,128)S(1)}, u32[]{:S(2)}, u32[]{:S(2)}) collective-permute-start(f32[128,128]{1,0:T(8,128)} %get-tuple-element.13), channel_id=1, source_target_pairs={{0,8},{1,9},{2,10},{3,11},{4,12},{5,13},{6,14},{7,15},{8,0},{9,1},... | collective-permute-start | bytes 196616 | tf_op jit(solution)/shard_map/ppermute | solution.py:35
  30.1 5.4 %collective-permute-start.4 = (f32[128,128]{1,0:T(8,128)}, f32[128,128]{1,0:T(8,128)S(1)}, u32[]{:S(2)}, u32[]{:S(2)}) collective-permute-start(f32[128,128]{1,0:T(8,128)} %get-tuple-element.13), channel_id=1, source_target_pairs={{0,12},{1,13},{2,14},{3,15},{4,8},{5,9},{6,10},{7,11},{8,4},{9,5},... | collective-permute-start | bytes 196616 | tf_op jit(solution)/shard_map/ppermute | solution.py:35
  36.3 5.8 %collective-permute-start.5 = (f32[128,128]{1,0:T(8,128)S(1)}, f32[128,128]{1,0:T(8,128)S(1)}, u32[]{:S(2)}, u32[]{:S(2)}) collective-permute-start(f32[128,128]{1,0:T(8,128)S(1)} %add_add_fusion), channel_id=1, source_target_pairs={{0,16},{1,17},{2,18},{3,19},{4,20},{5,21},{6,22},{7,23},{8,24},{9,... | collective-permute-start | bytes 196616 | tf_op jit(solution)/shard_map/ppermute | solution.py:35
  50.1 3.4 %collective-permute-start.13 = (f32[64,64]{1,0:T(8,128)S(1)}, f32[64,64]{1,0:T(8,128)S(1)}, u32[]{:S(2)}, u32[]{:S(2)}) collective-permute-start(f32[64,64]{1,0:T(8,128)S(1)} %get-tuple-element.16), channel_id=1, source_target_pairs={{0,1},{1,0},{2,3},{3,2},{4,5},{5,4},{6,7},{7,6},{8,9},{9,8},{10,11... | collective-permute-start | bytes 49160 | tf_op jit(solution)/shard_map/ppermute | solution.py:35
  51.1 1.2 %copy-start.2 = (bf16[64,8192]{1,0:T(8,128)(2,1)S(1)}, bf16[64,8192]{1,0:T(8,128)(2,1)}, u32[]{:S(2)}) copy-start(bf16[64,8192]{1,0:T(8,128)(2,1)} %prior_ref.3) | copy-start | bytes 3145732
  51.2 2.2 %collective-permute-start.6 = (bf16[64,4096]{1,0:T(8,128)(2,1)S(1)}, bf16[64,4096]{1,0:T(8,128)(2,1)S(1)}, u32[]{:S(2)}, u32[]{:S(2)}) collective-permute-start(bf16[64,4096]{1,0:T(8,128)(2,1)S(1)} %pad_maximum_fusion.2), channel_id=1, source_target_pairs={{0,1},{1,0},{2,3},{3,2},{4,5},{5,4},{6,7},{7,6},{8,9},{9,8},{10,11... | collective-permute-start | bytes 1572872 | tf_op jit(solution)/shard_map/ppermute | solution.py:35
  52.9 10.0 %collective-permute-start.24 = (bf16[64,4096]{1,0:T(8,128)(2,1)S(1)}, bf16[64,4096]{1,0:T(8,128)(2,1)S(1)}, u32[]{:S(2)}, u32[]{:S(2)}) collective-permute-start(bf16[64,4096]{1,0:T(8,128)(2,1)S(1)} %pad_maximum_fusion.5), channel_id=1, source_target_pairs={{0,1},{1,0},{2,3},{3,2},{4,5},{5,4},{6,7},{7,6},{8,9},{9,8},{10,11... | collective-permute-start | bytes 1572872 | tf_op jit(solution)/shard_map/ppermute | solution.py:35
  54.2 3.5 %collective-permute-start.7 = (f32[64,128]{1,0:T(8,128)S(1)}, f32[64,128]{1,0:T(8,128)S(1)}, u32[]{:S(2)}, u32[]{:S(2)}) collective-permute-start(f32[64,128]{1,0:T(8,128)S(1)} %fusion.1), channel_id=1, source_target_pairs={{0,1},{1,0},{2,3},{3,2},{4,5},{5,4},{6,7},{7,6},{8,9},{9,8},{10,11... | collective-permute-start | bytes 98312 | tf_op jit(solution)/shard_map/ppermute | solution.py:35
  54.5 3.9 %collective-permute-start.8 = (f32[64,128]{1,0:T(8,128)S(1)}, f32[64,128]{1,0:T(8,128)S(1)}, u32[]{:S(2)}, u32[]{:S(2)}) collective-permute-start(f32[64,128]{1,0:T(8,128)S(1)} %fusion.1), channel_id=1, source_target_pairs={{0,4},{1,5},{2,6},{3,7},{4,0},{5,1},{6,2},{7,3},{8,12},{9,13},{10,... | collective-permute-start | bytes 98312 | tf_op jit(solution)/shard_map/ppermute | solution.py:35
  54.5 3.9 %collective-permute-start.9 = (f32[64,128]{1,0:T(8,128)S(1)}, f32[64,128]{1,0:T(8,128)S(1)}, u32[]{:S(2)}, u32[]{:S(2)}) collective-permute-start(f32[64,128]{1,0:T(8,128)S(1)} %fusion.1), channel_id=1, source_target_pairs={{0,5},{1,4},{2,7},{3,6},{4,1},{5,0},{6,3},{7,2},{8,13},{9,12},{10,... | collective-permute-start | bytes 98312 | tf_op jit(solution)/shard_map/ppermute | solution.py:35
  56.2 24.2 %collective-permute-start.15 = (bf16[128,2048]{1,0:T(8,128)(2,1)S(1)}, bf16[128,2048]{1,0:T(8,128)(2,1)S(1)}, u32[]{:S(2)}, u32[]{:S(2)}) collective-permute-start(bf16[128,2048]{1,0:T(8,128)(2,1)S(1)} %fusion.5), channel_id=1, source_target_pairs={{0,2},{1,3},{2,0},{3,1},{4,6},{5,7},{6,4},{7,5},{8,10},{9,11},{10,... | collective-permute-start | bytes 1572872 | tf_op jit(solution)/shard_map/ppermute | solution.py:35
  58.5 4.7 %collective-permute-start.10 = (f32[64,128]{1,0:T(8,128)S(1)}, f32[64,128]{1,0:T(8,128)S(1)}, u32[]{:S(2)}, u32[]{:S(2)}) collective-permute-start(f32[64,128]{1,0:T(8,128)S(1)} %add_add_fusion.4), channel_id=1, source_target_pairs={{0,8},{1,9},{2,10},{3,11},{4,12},{5,13},{6,14},{7,15},{8,0},{9,1},... | collective-permute-start | bytes 98312 | tf_op jit(solution)/shard_map/ppermute | solution.py:35
  59.0 5.4 %collective-permute-start.11 = (f32[64,128]{1,0:T(8,128)S(1)}, f32[64,128]{1,0:T(8,128)S(1)}, u32[]{:S(2)}, u32[]{:S(2)}) collective-permute-start(f32[64,128]{1,0:T(8,128)S(1)} %add_add_fusion.4), channel_id=1, source_target_pairs={{0,16},{1,17},{2,18},{3,19},{4,20},{5,21},{6,22},{7,23},{8,24},{9,... | collective-permute-start | bytes 98312 | tf_op jit(solution)/shard_map/ppermute | solution.py:35
  61.1 5.7 %collective-permute-start.12 = (f32[64,128]{1,0:T(8,128)S(1)}, f32[64,128]{1,0:T(8,128)S(1)}, u32[]{:S(2)}, u32[]{:S(2)}) collective-permute-start(f32[64,128]{1,0:T(8,128)S(1)} %add_add_fusion.4), channel_id=1, source_target_pairs={{0,24},{1,25},{2,26},{3,27},{4,28},{5,29},{6,30},{7,31},{8,16},{9,... | collective-permute-start | bytes 98312 | tf_op jit(solution)/shard_map/ppermute | solution.py:35
  75.2 14.0 %collective-permute-start.23 = (f32[64,64]{1,0:T(8,128)S(1)}, f32[64,64]{1,0:T(8,128)S(1)}, u32[]{:S(2)}, u32[]{:S(2)}) collective-permute-start(f32[64,64]{1,0:T(8,128)S(1)} %get-tuple-element.18), channel_id=1, source_target_pairs={{0,2},{1,3},{2,0},{3,1},{4,6},{5,7},{6,4},{7,5},{8,10},{9,11},{10,... | collective-permute-start | bytes 49160 | tf_op jit(solution)/shard_map/ppermute | solution.py:35
  76.7 3.7 %collective-permute-start.14 = (bf16[64,128]{1,0:T(8,128)(2,1)S(1)}, bf16[64,128]{1,0:T(8,128)(2,1)S(1)}, u32[]{:S(2)}, u32[]{:S(2)}) collective-permute-start(bf16[64,128]{1,0:T(8,128)(2,1)S(1)} %get-tuple-element.17), channel_id=1, source_target_pairs={{0,2},{1,3},{2,0},{3,1},{4,6},{5,7},{6,4},{7,5},{8,10},{9,11},{10,... | collective-permute-start | bytes 49160 | tf_op jit(solution)/shard_map/ppermute | solution.py:35
  81.2 2.6 %collective-permute-start.16 = (f32[64,128]{1,0:T(8,128)S(1)}, f32[64,128]{1,0:T(8,128)S(1)}, u32[]{:S(2)}, u32[]{:S(2)}) collective-permute-start(f32[64,128]{1,0:T(8,128)S(1)} %fusion.11), channel_id=1, source_target_pairs={{0,1},{1,0},{2,3},{3,2},{4,5},{5,4},{6,7},{7,6},{8,9},{9,8},{10,11... | collective-permute-start | bytes 98312 | tf_op jit(solution)/shard_map/ppermute | solution.py:35
  81.3 4.3 %collective-permute-start.17 = (f32[64,128]{1,0:T(8,128)S(1)}, f32[64,128]{1,0:T(8,128)S(1)}, u32[]{:S(2)}, u32[]{:S(2)}) collective-permute-start(f32[64,128]{1,0:T(8,128)S(1)} %fusion.11), channel_id=1, source_target_pairs={{0,2},{1,3},{2,0},{3,1},{4,6},{5,7},{6,4},{7,5},{8,10},{9,11},{10,... | collective-permute-start | bytes 98312 | tf_op jit(solution)/shard_map/ppermute | solution.py:35
  81.9 3.7 %collective-permute-start.18 = (f32[64,128]{1,0:T(8,128)S(1)}, f32[64,128]{1,0:T(8,128)S(1)}, u32[]{:S(2)}, u32[]{:S(2)}) collective-permute-start(f32[64,128]{1,0:T(8,128)S(1)} %fusion.11), channel_id=1, source_target_pairs={{0,3},{1,2},{2,1},{3,0},{4,7},{5,6},{6,5},{7,4},{8,11},{9,10},{10,... | collective-permute-start | bytes 98312 | tf_op jit(solution)/shard_map/ppermute | solution.py:35
  83.2 11.4 %collective-permute-start.25 = (bf16[64,2048]{1,0:T(8,128)(2,1)S(1)}, bf16[64,2048]{1,0:T(8,128)(2,1)S(1)}, u32[]{:S(2)}, u32[]{:S(2)}) collective-permute-start(bf16[64,2048]{1,0:T(8,128)(2,1)S(1)} %constant_dynamic-slice_fusion), channel_id=1, source_target_pairs={{0,2},{1,3},{2,0},{3,1},{4,6},{5,7},{6,4},{7,5},{8,10},{9,11},{10,... | collective-permute-start | bytes 786440 | tf_op jit(solution)/shard_map/ppermute | solution.py:35
  85.6 4.0 %collective-permute-start.19 = (f32[64,128]{1,0:T(8,128)S(1)}, f32[64,128]{1,0:T(8,128)S(1)}, u32[]{:S(2)}, u32[]{:S(2)}) collective-permute-start(f32[64,128]{1,0:T(8,128)S(1)} %add_add_fusion.2), channel_id=1, source_target_pairs={{0,4},{1,5},{2,6},{3,7},{4,0},{5,1},{6,2},{7,3},{8,12},{9,13},{10,... | collective-permute-start | bytes 98312 | tf_op jit(solution)/shard_map/ppermute | solution.py:35
  87.3 3.9 %collective-permute-start.20 = (f32[64,128]{1,0:T(8,128)S(1)}, f32[64,128]{1,0:T(8,128)S(1)}, u32[]{:S(2)}, u32[]{:S(2)}) collective-permute-start(f32[64,128]{1,0:T(8,128)S(1)} %add_add_fusion.2), channel_id=1, source_target_pairs={{0,8},{1,9},{2,10},{3,11},{4,12},{5,13},{6,14},{7,15},{8,0},{9,1},... | collective-permute-start | bytes 98312 | tf_op jit(solution)/shard_map/ppermute | solution.py:35
  87.3 4.8 %collective-permute-start.21 = (f32[64,128]{1,0:T(8,128)S(1)}, f32[64,128]{1,0:T(8,128)S(1)}, u32[]{:S(2)}, u32[]{:S(2)}) collective-permute-start(f32[64,128]{1,0:T(8,128)S(1)} %add_add_fusion.2), channel_id=1, source_target_pairs={{0,12},{1,13},{2,14},{3,15},{4,8},{5,9},{6,10},{7,11},{8,4},{9,5},... | collective-permute-start | bytes 98312 | tf_op jit(solution)/shard_map/ppermute | solution.py:35
  92.1 4.9 %collective-permute-start.22 = (f32[64,128]{1,0:T(8,128)S(1)}, f32[64,128]{1,0:T(8,128)S(1)}, u32[]{:S(2)}, u32[]{:S(2)}) collective-permute-start(f32[64,128]{1,0:T(8,128)S(1)} %add_add_fusion.1), channel_id=1, source_target_pairs={{0,16},{1,17},{2,18},{3,19},{4,20},{5,21},{6,22},{7,23},{8,24},{9,... | collective-permute-start | bytes 98312 | tf_op jit(solution)/shard_map/ppermute | solution.py:35

commit v7 on v6

--- a/solution.py
+++ b/solution.py
@@ -35,10 +35,10 @@
     return lax.ppermute(block, axes, [(i, i ^ mask) for i in range(count)])
 
 
-def total(block, bits):
-    for start in range(0, len(bits), 2):
+def total(block, bits, stage):
+    for start in range(0, len(bits), stage):
         first = bits[start]
-        if start + 1 < len(bits):
+        if stage == 2 and start + 1 < len(bits):
             second = bits[start + 1]
             near, far, both = swapped(block, first), swapped(block, second), swapped(block, first | second)
             block = (block + near) + (far + both)
@@ -109,24 +109,40 @@
     gram_ref[...] += lax.dot_general(weighted, weighted, NT, preferred_element_type=F32)
 
 
+def packed(gram):
+    half = gram.shape[0] // 2
+    quarter = half // 2
+    corner = gram[half:, half:]
+    return jnp.concatenate([gram[:half], jnp.concatenate([corner[:quarter], corner[quarter:]], axis=1)], axis=0)
+
+
+def unpacked(blocks):
+    half = blocks.shape[1] // 2
+    top, pair = blocks[:half], blocks[half:]
+    corner = jnp.concatenate([pair[:, :half], pair[:, half:]], axis=0)
+    return whole_of(top, corner)
+
+
+def whole_of(top, corner):
+    half = top.shape[0]
+    return jnp.concatenate([top, jnp.concatenate([top.T[half:], corner], axis=1)], axis=0)
+
+
 def border_kernel(
-    width, spots, prior_ref, snap_ref, low_ref, high_ref, factor_ref, part_ref, kept_ref, weighted_ref, gram_ref, bank,
-    fetched, arrived,
+    width, spots, prior_ref, snap_ref, low_ref, high_ref, factor_ref, part_ref, kept_ref, weighted_ref, packed_ref, bank, gram
 ):
     step = pl.program_id(0)
     rows, span = prior_ref.shape
     edge = low_ref.shape[1]
-    steps, _, block, chunk = fetched.shape
+    _, block, chunk = factor_ref.shape
     whole = span + edge
 
     @pl.when(step == 0)
     def _():
-        for i in range(steps):
-            fetch(factor_ref, i * (width - chunk), fetched, arrived, i).start()
         bank[:, :edge] = low_ref[...]
         bank[:rows, edge:whole] = prior_ref[...]
         bank[rows:, edge:whole] = snap_ref[...]
-        gram_ref[...] = part_ref[...]
+        gram[...] = part_ref[...]
 
     @pl.when(step != 0)
     def _():
@@ -138,10 +154,13 @@
     bank[:, whole + block:whole + TILE] = bank[:, :block]
     bank[:, 2 * whole:2 * whole + block] = bank[:, whole - block:whole]
     shift = lax.axis_index("space") * (width // block) - edge // block + step * ((width + 2 * edge - whole) // block)
-    fetch(factor_ref, step * (width - chunk), fetched, arrived, step).wait()
-    weighted = weigh_chunk(spots, step * ((width - chunk) // block), shift, bank, fetched.at[step])
+    weighted = weigh_chunk(spots, step * ((width - chunk) // block), shift, bank, factor_ref)
     weighted_ref[...] = weighted
-    gram_ref[...] += lax.dot_general(weighted, weighted, NT, preferred_element_type=F32)
+    gram[...] += lax.dot_general(weighted, weighted, NT, preferred_element_type=F32)
+
+    @pl.when(step == pl.num_programs(0) - 1)
+    def _():
+        packed_ref[...] = packed(gram[...])
 
 
 def weigh(prior, snapshots, factor, neighbours):
@@ -189,7 +208,7 @@
     ends = width // span - 1
     return pl.pallas_call(
         functools.partial(border_kernel, width),
-        out_shape=shapes,
+        out_shape=(shapes[0], jax.ShapeDtypeStruct((columns * 3 // 4, columns), F32)),
         grid_spec=pltpu.PrefetchScalarGridSpec(
             num_scalar_prefetch=1,
             grid=(2,),
@@ -198,15 +217,18 @@
                 pl.BlockSpec((rows, span), lambda i, s: (0, i * ends)),
                 pl.BlockSpec((columns, edge), full),
                 pl.BlockSpec((columns, edge), full),
-                pl.BlockSpec(memory_space=pl.ANY),
+                pl.BlockSpec((count, block, chunk), lambda i, s: (0, 0, i * (chunks - 1))),
                 pl.BlockSpec((columns, columns), full),
                 pl.BlockSpec(memory_space=pl.ANY),
             ],
             out_specs=(
                 pl.BlockSpec((columns, chunk), lambda i, s: (0, i * (chunks - 1))),
-                pl.BlockSpec((columns, columns), full),
+                pl.BlockSpec((columns * 3 // 4, columns), full),
             ),
-            scratch_shapes=[pltpu.VMEM((columns, 2 * (span + edge) + TILE), BF16)] + fetching(2),
+            scratch_shapes=[
+                pltpu.VMEM((columns, 2 * (span + edge) + TILE), BF16),
+                pltpu.VMEM((columns, columns), F32),
+            ],
         ),
         input_output_aliases={7: 0},
         compiler_params=params,
@@ -281,33 +303,34 @@
     return lax.dot_general(image, wide, NT, precision=HIGHEST, preferred_element_type=F32)
 
 
-def first_kernel(gram_ref, out_ref, own_ref, left, right, solved):
-    gram = gram_ref[...]
+def first_kernel(blocks_ref, out_ref, own_ref, left, right, solved):
+    gram = unpacked(blocks_ref[...])
     coefficients = reduce_gram(gram, left, right, solved)
     out_ref[...] = coefficients
     own_ref[...] = inner_of(coefficients, gram)
 
 
-def merge_kernel(last, top_ref, upper_ref, out_ref, own_ref, left, right, solved):
-    top = top_ref[...]
-    bottom = jnp.concatenate([top.T[RANK:], upper_ref[...]], axis=1)
-    gram = jnp.concatenate([top, bottom], axis=0)
+def merge_kernel(top_ref, upper_ref, out_ref, own_ref, left, right, solved):
+    gram = whole_of(top_ref[...], upper_ref[...])
     coefficients = reduce_gram(gram, left, right, solved)
     out_ref[...] = coefficients
-    own_ref[...] = upper_ref[...] if last else inner_of(coefficients, gram)
-
-
-def compress(kernel, *gram):
+    own_ref[...] = inner_of(coefficients, gram)
+
+
+def last_kernel(top_ref, upper_ref, stacked_ref, weighted_ref, basis_ref, merged_ref, left, right, solved):
+    coefficients = reduce_gram(whole_of(top_ref[...], upper_ref[...]), left, right, solved)
+    basis_ref[...] = combine(coefficients, stacked_ref[...])
+    merged_ref[...] = combine(coefficients, weighted_ref[...])
+
+
+def compress(kernel, outs, *operands):
     return pl.pallas_call(
         kernel,
-        out_shape=(
-            jax.ShapeDtypeStruct((RANK, gram[0].shape[1]), BF16),
-            jax.ShapeDtypeStruct((RANK, RANK), F32),
-        ),
+        out_shape=outs,
         scratch_shapes=[pltpu.VMEM((RANK // PANEL, PANEL, TILE), F32)] * 3,
         compiler_params=pltpu.CompilerParams(vmem_limit_bytes=16 * 1024 * 1024),
         name="compress",
-    )(*gram)
+    )(*operands)
 
 
 def combine(coefficients, rows):
@@ -344,7 +367,8 @@
     member = lax.axis_index("tm")
     width = snapshots.shape[1] // members
     partner_weighted = None
-    coefficients, own = compress(first_kernel, total(gram, across))
+    reduced = (jax.ShapeDtypeStruct((RANK, 2 * RANK), BF16), jax.ShapeDtypeStruct((RANK, RANK), F32))
+    coefficients, own = compress(first_kernel, reduced, total(gram, across, 1))
     for level in range(members.bit_length() - 1):
         step = 1 << level
         bit = member // step % 2
@@ -369,10 +393,12 @@
         if not last:
             next_bit = member // (2 * step) % 2
             partner_weighted = swapped(shared_out(weighted, width, 1 - next_bit), 2 * step)
-        top = total(top, [1 << i for i in range(level + 1)] + across)
+        top = total(top, [1 << i for i in range(level + 1)] + across, 2)
         upper = jnp.where(upper_half, own, partner_own)
-        coefficients, own = compress(functools.partial(merge_kernel, last), top, upper)
-    return combine(coefficients, stacked), combine(coefficients, weighted)
+        if not last:
+            coefficients, own = compress(merge_kernel, reduced, top, upper)
+    share = jax.ShapeDtypeStruct((RANK, width), BF16)
+    return compress(last_kernel, (share, share), top, upper, stacked, weighted)
 
 
 def solution(mesh):

time: 107 us -> 106 us (level)
  starting transfers between devices: 32.1 us -> 35.2 us
  waiting for transfers between devices: 24.6 us -> 21.9 us
  matrix products: 4.68 us -> 2.85 us
    ppermute x24 -> x23, starting transfers between devices: 25.3 us -> 29 us  [swapped(): return lax.ppermute(block, axes, [(i, i ^ mask) for i in range(count)])]
    ppermute x24 -> x23, waiting for transfers between devices: 24.6 us -> 21.9 us  [swapped(): return lax.ppermute(block, axes, [(i, i ^ mask) for i in range(count)])]
    dot_general x6 -> x4, matrix products: 3.02 us -> 1.17 us  [combine(): return jnp.dot(coefficients, rows, preferred_element_type=F32).astype(BF16)]
  transfers between devices with their start and end apart: 26 -> 25, of which waited for: 13 -> 14; matrix products, arithmetic and copies ran while one was open for 4% -> 3% of each run, Pallas kernels for 17% -> 17%
where the time goes in v7:
time: 106 us
  Pallas kernels  41.2 us (39%)
  starting transfers between devices  35.2 us (33%)
  waiting for transfers between devices  21.9 us (21%)
  matrix products  2.85 us (3%)
  local copies, waits for them, and re-layouts  2.37 us (2%)
  other arithmetic  1.61 us (2%)
    ppermute x23, starting transfers between devices, swapped(): return lax.ppermute(block, axes, [(i, i ^ mask) for i in range(count)])  29 us
    pallas_call x3, Pallas kernels, compress(): pl.pallas_call(kernel, out_shape=outs, scratch_shapes=[pltpu.VMEM((RANK /...  25.3 us
    ppermute x23, waiting for transfers between devices, swapped(): return lax.ppermute(block, axes, [(i, i ^ mask) for i in range(count)])  21.9 us
    pallas_call x1, Pallas kernels, weigh(): pl.pallas_call(functools.partial(inside_kernel, edge), out_shape=shapes,...  10.2 us
    pallas_call x1, Pallas kernels, weigh(): pl.pallas_call(functools.partial(border_kernel, width), out_shape=(shapes...  5.75 us
    ppermute x1, starting transfers between devices, halo(): low = lax.ppermute(last, axis, forward)  4.88 us
  transfers between devices with their start and end apart: 25, of which 14 were waited for; matrix products, arithmetic and copies ran while one was open for 3% of the time, Pallas kernels for 17%

profile of v7, /device:TPU:0, one launch (start us, length us, event | category | flops | bytes accessed | tf_op | source)
XLA Modules:
  0.0 106.1 jit_solution(13974180656967175776)
XLA Ops:
  0.6 1.0 fusion.16
  1.6 4.9 %collective-permute-start = (bf16[128,512]{1,0:T(8,128)(2,1)S(1)}, bf16[128,512]{1,0:T(8,128)(2,1)S(1)}, u32[]{:S(2)}, u32[]{:S(2)}) collective-permute-start(bf16[128,512]{1,0:T(8,128)(2,1)S(1)} %pad_maximum_fusion.8), channel_id=1, source_target_pairs={{0,4},{4,8},{8,12},{12,16},{16,20},{20,24},{24,28},{1,5},{5,9},{9,... | collective-permute-start | bytes 393224 | tf_op jit(solution)/shard_map/ppermute | solution.py:27
  6.5 1.3 %collective-permute-start.1 = (bf16[128,512]{1,0:T(8,128)(2,1)S(1)}, bf16[128,512]{1,0:T(8,128)(2,1)S(1)}, u32[]{:S(2)}, u32[]{:S(2)}) collective-permute-start(bf16[128,512]{1,0:T(8,128)(2,1)S(1)} %pad_maximum_fusion.9), channel_id=1, source_target_pairs={{4,0},{8,4},{12,8},{16,12},{20,16},{24,20},{28,24},{5,1},{9,5},{13... | collective-permute-start | bytes 393224 | tf_op jit(solution)/shard_map/ppermute | solution.py:28
  7.8 10.2 %weigh_inside.1 = (bf16[128,8192]{1,0:T(8,128)(2,1)}, f32[128,128]{1,0:T(8,128)}) custom-call(s32[7,128]{1,0:T(8,128)} %bitcast.11, bf16[64,8192]{1,0:T(8,128)(2,1)} %prior_ref.3, bf16[64,8192]{1,0:T(8,128)(2,1)} %snap_ref.3, bf16[7,64,8192]{2,1,0:T(8,128)(2,1)} %factor_ref.3), custom_call_target="tpu_custom_call" | custom-call | flops 3758096384 | bytes 7340032 | tf_op jit(solution)/shard_map/weigh_inside/pallas_call | solution.py:185
  18.7 5.8 %weigh_border.1 = (bf16[128,8192]{1,0:T(8,128)(2,1)}, f32[96,128]{1,0:T(8,128)}) custom-call(s32[7,128]{1,0:T(8,128)} %bitcast.12, bf16[64,8192]{1,0:T(8,128)(2,1)} %prior_ref.3, bf16[64,8192]{1,0:T(8,128)(2,1)} %snap_ref.3, bf16[128,512]{1,0:T(8,128)(2,1)} %copy-done.3, bf16[128,512]{1,0:T(8,128)(2,1)} %copy-done.4, ...), custom_call_target="tpu_custom_call", output_to_operand_aliasing={{0}: (7, {})} | custom-call | tf_op jit(solution)/shard_map/weigh_border/pallas_call | solution.py:209
  24.5 2.7 %collective-permute-start.2 = (f32[96,128]{1,0:T(8,128)}, f32[96,128]{1,0:T(8,128)S(1)}, u32[]{:S(2)}, u32[]{:S(2)}) collective-permute-start(f32[96,128]{1,0:T(8,128)} %get-tuple-element.12), channel_id=1, source_target_pairs={{0,4},{1,5},{2,6},{3,7},{4,0},{5,1},{6,2},{7,3},{8,12},{9,13},{10,... | collective-permute-start | bytes 147464 | tf_op jit(solution)/shard_map/ppermute | solution.py:35
  27.2 2.3 %collective-permute-done.2 = f32[96,128]{1,0:T(8,128)S(1)} collective-permute-done((f32[96,128]{1,0:T(8,128)}, f32[96,128]{1,0:T(8,128)S(1)}, u32[]{:S(2)}, u32[]{:S(2)}) %collective-permute-start.2) | collective-permute-done | bytes 49184 | tf_op jit(solution)/shard_map/ppermute | solution.py:35
  29.5 0.8 add.96
  30.3 3.0 %collective-permute-start.3 = (f32[96,128]{1,0:T(8,128)S(1)}, f32[96,128]{1,0:T(8,128)S(1)}, u32[]{:S(2)}, u32[]{:S(2)}) collective-permute-start(f32[96,128]{1,0:T(8,128)S(1)} %add.96), channel_id=1, source_target_pairs={{0,8},{1,9},{2,10},{3,11},{4,12},{5,13},{6,14},{7,15},{8,0},{9,1},... | collective-permute-start | bytes 147464 | tf_op jit(solution)/shard_map/ppermute | solution.py:35
  33.2 2.1 %collective-permute-done.3 = f32[96,128]{1,0:T(8,128)S(1)} collective-permute-done((f32[96,128]{1,0:T(8,128)S(1)}, f32[96,128]{1,0:T(8,128)S(1)}, u32[]{:S(2)}, u32[]{:S(2)}) %collective-permute-start.3) | collective-permute-done | bytes 49184 | tf_op jit(solution)/shard_map/ppermute | solution.py:35
  35.3 3.6 %collective-permute-start.4 = (f32[96,128]{1,0:T(8,128)S(1)}, f32[96,128]{1,0:T(8,128)S(1)}, u32[]{:S(2)}, u32[]{:S(2)}) collective-permute-start(f32[96,128]{1,0:T(8,128)S(1)} %add.97), channel_id=1, source_target_pairs={{0,16},{1,17},{2,18},{3,19},{4,20},{5,21},{6,22},{7,23},{8,24},{9,... | collective-permute-start | bytes 147464 | tf_op jit(solution)/shard_map/ppermute | solution.py:35
  38.9 2.1 %collective-permute-done.4 = f32[96,128]{1,0:T(8,128)S(1)} collective-permute-done((f32[96,128]{1,0:T(8,128)S(1)}, f32[96,128]{1,0:T(8,128)S(1)}, u32[]{:S(2)}, u32[]{:S(2)}) %collective-permute-start.4) | collective-permute-done | bytes 49184 | tf_op jit(solution)/shard_map/ppermute | solution.py:35
  41.0 8.2 %compress.3 = (bf16[64,128]{1,0:T(8,128)(2,1)S(1)}, f32[64,64]{1,0:T(8,128)S(1)}) custom-call(f32[96,128]{1,0:T(8,128)S(1)} %add.98.blocks_ref), custom_call_target="tpu_custom_call" | custom-call | tf_op jit(solution)/shard_map/compress/pallas_call | solution.py:327
  53.7 1.0 collective-permute-start.8
  55.3 1.6 %collective-permute-start.14 = (bf16[128,2048]{1,0:T(8,128)(2,1)S(1)}, bf16[128,2048]{1,0:T(8,128)(2,1)S(1)}, u32[]{:S(2)}, u32[]{:S(2)}) collective-permute-start(bf16[128,2048]{1,0:T(8,128)(2,1)S(1)} %fusion.5), channel_id=1, source_target_pairs={{0,2},{1,3},{2,0},{3,1},{4,6},{5,7},{6,4},{7,5},{8,10},{9,11},{10,... | collective-permute-start | bytes 1572872 | tf_op jit(solution)/shard_map/ppermute | solution.py:35
  57.4 3.1 %collective-permute-start.10 = (f32[64,128]{1,0:T(8,128)S(1)}, f32[64,128]{1,0:T(8,128)S(1)}, u32[]{:S(2)}, u32[]{:S(2)}) collective-permute-start(f32[64,128]{1,0:T(8,128)S(1)} %add_add_fusion.3), channel_id=1, source_target_pairs={{0,16},{1,17},{2,18},{3,19},{4,20},{5,21},{6,22},{7,23},{8,24},{9,... | collective-permute-start | bytes 98312 | tf_op jit(solution)/shard_map/ppermute | solution.py:35
  60.5 1.1 collective-permute-start.11
  62.4 3.8 %collective-permute-done.11 = f32[64,128]{1,0:T(8,128)S(1)} collective-permute-done((f32[64,128]{1,0:T(8,128)S(1)}, f32[64,128]{1,0:T(8,128)S(1)}, u32[]{:S(2)}, u32[]{:S(2)}) %collective-permute-start.11) | collective-permute-done | bytes 32800 | tf_op jit(solution)/shard_map/ppermute | solution.py:35
  66.2 8.3 %compress.4 = (bf16[64,128]{1,0:T(8,128)(2,1)S(1)}, f32[64,64]{1,0:T(8,128)S(1)}) custom-call(f32[64,128]{1,0:T(8,128)S(1)} %add_add_fusion.2.top_ref, f32[64,64]{1,0:T(8,128)S(1)} %broadcast_select_fusion.9.upper_ref), custom_call_target="tpu_custom_call" | custom-call | tf_op jit(solution)/shard_map/compress/pallas_call | solution.py:327
  74.5 1.5 %collective-permute-start.13 = (bf16[64,128]{1,0:T(8,128)(2,1)S(1)}, bf16[64,128]{1,0:T(8,128)(2,1)S(1)}, u32[]{:S(2)}, u32[]{:S(2)}) collective-permute-start(bf16[64,128]{1,0:T(8,128)(2,1)S(1)} %get-tuple-element.16), channel_id=1, source_target_pairs={{0,2},{1,3},{2,0},{3,1},{4,6},{5,7},{6,4},{7,5},{8,10},{9,11},{10,... | collective-permute-start | bytes 49160 | tf_op jit(solution)/shard_map/ppermute | solution.py:35
  76.9 1.6 %collective-permute-start.24 = (bf16[64,2048]{1,0:T(8,128)(2,1)S(1)}, bf16[64,2048]{1,0:T(8,128)(2,1)S(1)}, u32[]{:S(2)}, u32[]{:S(2)}) collective-permute-start(bf16[64,2048]{1,0:T(8,128)(2,1)S(1)} %constant_dynamic-slice_fusion), channel_id=1, source_target_pairs={{0,2},{1,3},{2,0},{3,1},{4,6},{5,7},{6,4},{7,5},{8,10},{9,11},{10,... | collective-permute-start | bytes 786440 | tf_op jit(solution)/shard_map/ppermute | solution.py:35
  78.5 1.9 %collective-permute-done.22 = f32[64,64]{1,0:T(8,128)S(1)} collective-permute-done((f32[64,64]{1,0:T(8,128)S(1)}, f32[64,64]{1,0:T(8,128)S(1)}, u32[]{:S(2)}, u32[]{:S(2)}) %collective-permute-start.22) | collective-permute-done | bytes 16416 | tf_op jit(solution)/shard_map/ppermute | solution.py:35
  81.7 1.7 %collective-permute-start.15 = (f32[64,128]{1,0:T(8,128)S(1)}, f32[64,128]{1,0:T(8,128)S(1)}, u32[]{:S(2)}, u32[]{:S(2)}) collective-permute-start(f32[64,128]{1,0:T(8,128)S(1)} %fusion.15), channel_id=1, source_target_pairs={{0,1},{1,0},{2,3},{3,2},{4,5},{5,4},{6,7},{7,6},{8,9},{9,8},{10,11... | collective-permute-start | bytes 98312 | tf_op jit(solution)/shard_map/ppermute | solution.py:35
  83.4 0.8 collective-permute-done.24
  84.4 1.0 collective-permute-done.16
  85.5 2.8 %collective-permute-start.20 = (f32[64,128]{1,0:T(8,128)S(1)}, f32[64,128]{1,0:T(8,128)S(1)}, u32[]{:S(2)}, u32[]{:S(2)}) collective-permute-start(f32[64,128]{1,0:T(8,128)S(1)} %add_add_fusion.1), channel_id=1, source_target_pairs={{0,12},{1,13},{2,14},{3,15},{4,8},{5,9},{6,10},{7,11},{8,4},{9,5},... | collective-permute-start | bytes 98312 | tf_op jit(solution)/shard_map/ppermute | solution.py:35
  88.3 0.7 collective-permute-start.18
  89.7 0.8 collective-permute-done.20
  90.5 1.7 %collective-permute-done.18 = f32[64,128]{1,0:T(8,128)S(1)} collective-permute-done((f32[64,128]{1,0:T(8,128)S(1)}, f32[64,128]{1,0:T(8,128)S(1)}, u32[]{:S(2)}, u32[]{:S(2)}) %collective-permute-start.18) | collective-permute-done | bytes 32800 | tf_op jit(solution)/shard_map/ppermute | solution.py:35
  92.2 1.3 %collective-permute-start.21 = (f32[64,128]{1,0:T(8,128)S(1)}, f32[64,128]{1,0:T(8,128)S(1)}, u32[]{:S(2)}, u32[]{:S(2)}) collective-permute-start(f32[64,128]{1,0:T(8,128)S(1)} %add_add_fusion), channel_id=1, source_target_pairs={{0,16},{1,17},{2,18},{3,19},{4,20},{5,21},{6,22},{7,23},{8,24},{9,... | collective-permute-start | bytes 98312 | tf_op jit(solution)/shard_map/ppermute | solution.py:35
  93.5 3.8 %collective-permute-done.21 = f32[64,128]{1,0:T(8,128)S(1)} collective-permute-done((f32[64,128]{1,0:T(8,128)S(1)}, f32[64,128]{1,0:T(8,128)S(1)}, u32[]{:S(2)}, u32[]{:S(2)}) %collective-permute-start.21) | collective-permute-done | bytes 32800 | tf_op jit(solution)/shard_map/ppermute | solution.py:35
  97.3 8.8 %compress.5 = (bf16[64,2048]{1,0:T(8,128)(2,1)}, bf16[64,2048]{1,0:T(8,128)(2,1)}) custom-call(f32[64,128]{1,0:T(8,128)S(1)} %add.119.top_ref, f32[64,64]{1,0:T(8,128)S(1)} %broadcast_select_fusion.8.upper_ref, bf16[128,2048]{1,0:T(8,128)(2,1)S(1)} %pad_maximum_fusion.7.stacked_ref, bf16[128,2048]{1,0:T(8,128)(2,1)S(1)} %pad_maximum_fusion.4.weighted_ref), custom_call_target="tpu_custom_call" | custom-call | tf_op jit(solution)/shard_map/compress/pallas_call | solution.py:327
  (65 shorter events, 10.2 us)
Async XLA Ops:
  1.6 16.4 %collective-permute-start = (bf16[128,512]{1,0:T(8,128)(2,1)S(1)}, bf16[128,512]{1,0:T(8,128)(2,1)S(1)}, u32[]{:S(2)}, u32[]{:S(2)}) collective-permute-start(bf16[128,512]{1,0:T(8,128)(2,1)S(1)} %pad_maximum_fusion.8), channel_id=1, source_target_pairs={{0,4},{4,8},{8,12},{12,16},{16,20},{20,24},{24,28},{1,5},{5,9},{9,... | collective-permute-start | bytes 393224 | tf_op jit(solution)/shard_map/ppermute | solution.py:27
  6.5 11.5 %collective-permute-start.1 = (bf16[128,512]{1,0:T(8,128)(2,1)S(1)}, bf16[128,512]{1,0:T(8,128)(2,1)S(1)}, u32[]{:S(2)}, u32[]{:S(2)}) collective-permute-start(bf16[128,512]{1,0:T(8,128)(2,1)S(1)} %pad_maximum_fusion.9), channel_id=1, source_target_pairs={{4,0},{8,4},{12,8},{16,12},{20,16},{24,20},{28,24},{5,1},{9,5},{13... | collective-permute-start | bytes 393224 | tf_op jit(solution)/shard_map/ppermute | solution.py:28
  18.0 0.7 copy-start.3
  18.0 0.7 copy-start.4
  18.7 30.5 %copy-start.1 = (bf16[64,8192]{1,0:T(8,128)(2,1)S(1)}, bf16[64,8192]{1,0:T(8,128)(2,1)}, u32[]{:S(2)}) copy-start(bf16[64,8192]{1,0:T(8,128)(2,1)} %snap_ref.3) | copy-start | bytes 3145732
  24.5 25.2 %copy-start = (bf16[128,8192]{1,0:T(8,128)(2,1)S(1)}, bf16[128,8192]{1,0:T(8,128)(2,1)}, u32[]{:S(2)}) copy-start(bf16[128,8192]{1,0:T(8,128)(2,1)} %get-tuple-element.14) | copy-start | bytes 6291460
  24.5 5.0 %collective-permute-start.2 = (f32[96,128]{1,0:T(8,128)}, f32[96,128]{1,0:T(8,128)S(1)}, u32[]{:S(2)}, u32[]{:S(2)}) collective-permute-start(f32[96,128]{1,0:T(8,128)} %get-tuple-element.12), channel_id=1, source_target_pairs={{0,4},{1,5},{2,6},{3,7},{4,0},{5,1},{6,2},{7,3},{8,12},{9,13},{10,... | collective-permute-start | bytes 147464 | tf_op jit(solution)/shard_map/ppermute | solution.py:35
  30.3 5.0 %collective-permute-start.3 = (f32[96,128]{1,0:T(8,128)S(1)}, f32[96,128]{1,0:T(8,128)S(1)}, u32[]{:S(2)}, u32[]{:S(2)}) collective-permute-start(f32[96,128]{1,0:T(8,128)S(1)} %add.96), channel_id=1, source_target_pairs={{0,8},{1,9},{2,10},{3,11},{4,12},{5,13},{6,14},{7,15},{8,0},{9,1},... | collective-permute-start | bytes 147464 | tf_op jit(solution)/shard_map/ppermute | solution.py:35
  35.3 5.7 %collective-permute-start.4 = (f32[96,128]{1,0:T(8,128)S(1)}, f32[96,128]{1,0:T(8,128)S(1)}, u32[]{:S(2)}, u32[]{:S(2)}) collective-permute-start(f32[96,128]{1,0:T(8,128)S(1)} %add.97), channel_id=1, source_target_pairs={{0,16},{1,17},{2,18},{3,19},{4,20},{5,21},{6,22},{7,23},{8,24},{9,... | collective-permute-start | bytes 147464 | tf_op jit(solution)/shard_map/ppermute | solution.py:35
  50.1 1.2 %copy-start.2 = (bf16[64,8192]{1,0:T(8,128)(2,1)S(1)}, bf16[64,8192]{1,0:T(8,128)(2,1)}, u32[]{:S(2)}) copy-start(bf16[64,8192]{1,0:T(8,128)(2,1)} %prior_ref.3) | copy-start | bytes 3145732
  50.3 2.0 %collective-permute-start.5 = (bf16[64,4096]{1,0:T(8,128)(2,1)S(1)}, bf16[64,4096]{1,0:T(8,128)(2,1)S(1)}, u32[]{:S(2)}, u32[]{:S(2)}) collective-permute-start(bf16[64,4096]{1,0:T(8,128)(2,1)S(1)} %pad_maximum_fusion.2), channel_id=1, source_target_pairs={{0,1},{1,0},{2,3},{3,2},{4,5},{5,4},{6,7},{7,6},{8,9},{9,8},{10,11... | collective-permute-start | bytes 1572872 | tf_op jit(solution)/shard_map/ppermute | solution.py:35
  50.4 1.9 %collective-permute-start.12 = (f32[64,64]{1,0:T(8,128)S(1)}, f32[64,64]{1,0:T(8,128)S(1)}, u32[]{:S(2)}, u32[]{:S(2)}) collective-permute-start(f32[64,64]{1,0:T(8,128)S(1)} %get-tuple-element.15), channel_id=1, source_target_pairs={{0,1},{1,0},{2,3},{3,2},{4,5},{5,4},{6,7},{7,6},{8,9},{9,8},{10,11... | collective-permute-start | bytes 49160 | tf_op jit(solution)/shard_map/ppermute | solution.py:35
  51.9 10.1 %collective-permute-start.23 = (bf16[64,4096]{1,0:T(8,128)(2,1)S(1)}, bf16[64,4096]{1,0:T(8,128)(2,1)S(1)}, u32[]{:S(2)}, u32[]{:S(2)}) collective-permute-start(bf16[64,4096]{1,0:T(8,128)(2,1)S(1)} %pad_maximum_fusion.5), channel_id=1, source_target_pairs={{0,1},{1,0},{2,3},{3,2},{4,5},{5,4},{6,7},{7,6},{8,9},{9,8},{10,11... | collective-permute-start | bytes 1572872 | tf_op jit(solution)/shard_map/ppermute | solution.py:35
  53.0 4.3 %collective-permute-start.7 = (f32[64,128]{1,0:T(8,128)S(1)}, f32[64,128]{1,0:T(8,128)S(1)}, u32[]{:S(2)}, u32[]{:S(2)}) collective-permute-start(f32[64,128]{1,0:T(8,128)S(1)} %fusion.1), channel_id=1, source_target_pairs={{0,4},{1,5},{2,6},{3,7},{4,0},{5,1},{6,2},{7,3},{8,12},{9,13},{10,... | collective-permute-start | bytes 98312 | tf_op jit(solution)/shard_map/ppermute | solution.py:35
  53.7 3.7 %collective-permute-start.8 = (f32[64,128]{1,0:T(8,128)S(1)}, f32[64,128]{1,0:T(8,128)S(1)}, u32[]{:S(2)}, u32[]{:S(2)}) collective-permute-start(f32[64,128]{1,0:T(8,128)S(1)} %fusion.1), channel_id=1, source_target_pairs={{0,5},{1,4},{2,7},{3,6},{4,1},{5,0},{6,3},{7,2},{8,13},{9,12},{10,... | collective-permute-start | bytes 98312 | tf_op jit(solution)/shard_map/ppermute | solution.py:35
  54.7 2.7 %collective-permute-start.6 = (f32[64,128]{1,0:T(8,128)S(1)}, f32[64,128]{1,0:T(8,128)S(1)}, u32[]{:S(2)}, u32[]{:S(2)}) collective-permute-start(f32[64,128]{1,0:T(8,128)S(1)} %fusion.1), channel_id=1, source_target_pairs={{0,1},{1,0},{2,3},{3,2},{4,5},{5,4},{6,7},{7,6},{8,9},{9,8},{10,11... | collective-permute-start | bytes 98312 | tf_op jit(solution)/shard_map/ppermute | solution.py:35
  55.3 25.1 %collective-permute-start.14 = (bf16[128,2048]{1,0:T(8,128)(2,1)S(1)}, bf16[128,2048]{1,0:T(8,128)(2,1)S(1)}, u32[]{:S(2)}, u32[]{:S(2)}) collective-permute-start(bf16[128,2048]{1,0:T(8,128)(2,1)S(1)} %fusion.5), channel_id=1, source_target_pairs={{0,2},{1,3},{2,0},{3,1},{4,6},{5,7},{6,4},{7,5},{8,10},{9,11},{10,... | collective-permute-start | bytes 1572872 | tf_op jit(solution)/shard_map/ppermute | solution.py:35
  57.4 5.0 %collective-permute-start.10 = (f32[64,128]{1,0:T(8,128)S(1)}, f32[64,128]{1,0:T(8,128)S(1)}, u32[]{:S(2)}, u32[]{:S(2)}) collective-permute-start(f32[64,128]{1,0:T(8,128)S(1)} %add_add_fusion.3), channel_id=1, source_target_pairs={{0,16},{1,17},{2,18},{3,19},{4,20},{5,21},{6,22},{7,23},{8,24},{9,... | collective-permute-start | bytes 98312 | tf_op jit(solution)/shard_map/ppermute | solution.py:35
  60.5 5.7 %collective-permute-start.11 = (f32[64,128]{1,0:T(8,128)S(1)}, f32[64,128]{1,0:T(8,128)S(1)}, u32[]{:S(2)}, u32[]{:S(2)}) collective-permute-start(f32[64,128]{1,0:T(8,128)S(1)} %add_add_fusion.3), channel_id=1, source_target_pairs={{0,24},{1,25},{2,26},{3,27},{4,28},{5,29},{6,30},{7,31},{8,16},{9,... | collective-permute-start | bytes 98312 | tf_op jit(solution)/shard_map/ppermute | solution.py:35
  61.5 4.7 %collective-permute-start.9 = (f32[64,128]{1,0:T(8,128)S(1)}, f32[64,128]{1,0:T(8,128)S(1)}, u32[]{:S(2)}, u32[]{:S(2)}) collective-permute-start(f32[64,128]{1,0:T(8,128)S(1)} %add_add_fusion.3), channel_id=1, source_target_pairs={{0,8},{1,9},{2,10},{3,11},{4,12},{5,13},{6,14},{7,15},{8,0},{9,1},... | collective-permute-start | bytes 98312 | tf_op jit(solution)/shard_map/ppermute | solution.py:35
  74.5 5.9 %collective-permute-start.13 = (bf16[64,128]{1,0:T(8,128)(2,1)S(1)}, bf16[64,128]{1,0:T(8,128)(2,1)S(1)}, u32[]{:S(2)}, u32[]{:S(2)}) collective-permute-start(bf16[64,128]{1,0:T(8,128)(2,1)S(1)} %get-tuple-element.16), channel_id=1, source_target_pairs={{0,2},{1,3},{2,0},{3,1},{4,6},{5,7},{6,4},{7,5},{8,10},{9,11},{10,... | collective-permute-start | bytes 49160 | tf_op jit(solution)/shard_map/ppermute | solution.py:35
  76.1 4.3 %collective-permute-start.22 = (f32[64,64]{1,0:T(8,128)S(1)}, f32[64,64]{1,0:T(8,128)S(1)}, u32[]{:S(2)}, u32[]{:S(2)}) collective-permute-start(f32[64,64]{1,0:T(8,128)S(1)} %get-tuple-element.17), channel_id=1, source_target_pairs={{0,2},{1,3},{2,0},{3,1},{4,6},{5,7},{6,4},{7,5},{8,10},{9,11},{10,... | collective-permute-start | bytes 49160 | tf_op jit(solution)/shard_map/ppermute | solution.py:35
  76.9 7.3 %collective-permute-start.24 = (bf16[64,2048]{1,0:T(8,128)(2,1)S(1)}, bf16[64,2048]{1,0:T(8,128)(2,1)S(1)}, u32[]{:S(2)}, u32[]{:S(2)}) collective-permute-start(bf16[64,2048]{1,0:T(8,128)(2,1)S(1)} %constant_dynamic-slice_fusion), channel_id=1, source_target_pairs={{0,2},{1,3},{2,0},{3,1},{4,6},{5,7},{6,4},{7,5},{8,10},{9,11},{10,... | collective-permute-start | bytes 786440 | tf_op jit(solution)/shard_map/ppermute | solution.py:35
  81.2 4.2 %collective-permute-start.16 = (f32[64,128]{1,0:T(8,128)S(1)}, f32[64,128]{1,0:T(8,128)S(1)}, u32[]{:S(2)}, u32[]{:S(2)}) collective-permute-start(f32[64,128]{1,0:T(8,128)S(1)} %fusion.15), channel_id=1, source_target_pairs={{0,2},{1,3},{2,0},{3,1},{4,6},{5,7},{6,4},{7,5},{8,10},{9,11},{10,... | collective-permute-start | bytes 98312 | tf_op jit(solution)/shard_map/ppermute | solution.py:35
  81.7 3.7 %collective-permute-start.17 = (f32[64,128]{1,0:T(8,128)S(1)}, f32[64,128]{1,0:T(8,128)S(1)}, u32[]{:S(2)}, u32[]{:S(2)}) collective-permute-start(f32[64,128]{1,0:T(8,128)S(1)} %fusion.15), channel_id=1, source_target_pairs={{0,3},{1,2},{2,1},{3,0},{4,7},{5,6},{6,5},{7,4},{8,11},{9,10},{10,... | collective-permute-start | bytes 98312 | tf_op jit(solution)/shard_map/ppermute | solution.py:35
  81.7 3.7 %collective-permute-start.15 = (f32[64,128]{1,0:T(8,128)S(1)}, f32[64,128]{1,0:T(8,128)S(1)}, u32[]{:S(2)}, u32[]{:S(2)}) collective-permute-start(f32[64,128]{1,0:T(8,128)S(1)} %fusion.15), channel_id=1, source_target_pairs={{0,1},{1,0},{2,3},{3,2},{4,5},{5,4},{6,7},{7,6},{8,9},{9,8},{10,11... | collective-permute-start | bytes 98312 | tf_op jit(solution)/shard_map/ppermute | solution.py:35
  85.4 4.3 %collective-permute-start.19 = (f32[64,128]{1,0:T(8,128)S(1)}, f32[64,128]{1,0:T(8,128)S(1)}, u32[]{:S(2)}, u32[]{:S(2)}) collective-permute-start(f32[64,128]{1,0:T(8,128)S(1)} %add_add_fusion.1), channel_id=1, source_target_pairs={{0,8},{1,9},{2,10},{3,11},{4,12},{5,13},{6,14},{7,15},{8,0},{9,1},... | collective-permute-start | bytes 98312 | tf_op jit(solution)/shard_map/ppermute | solution.py:35
  85.5 5.0 %collective-permute-start.20 = (f32[64,128]{1,0:T(8,128)S(1)}, f32[64,128]{1,0:T(8,128)S(1)}, u32[]{:S(2)}, u32[]{:S(2)}) collective-permute-start(f32[64,128]{1,0:T(8,128)S(1)} %add_add_fusion.1), channel_id=1, source_target_pairs={{0,12},{1,13},{2,14},{3,15},{4,8},{5,9},{6,10},{7,11},{8,4},{9,5},... | collective-permute-start | bytes 98312 | tf_op jit(solution)/shard_map/ppermute | solution.py:35
  88.3 3.9 %collective-permute-start.18 = (f32[64,128]{1,0:T(8,128)S(1)}, f32[64,128]{1,0:T(8,128)S(1)}, u32[]{:S(2)}, u32[]{:S(2)}) collective-permute-start(f32[64,128]{1,0:T(8,128)S(1)} %add_add_fusion.1), channel_id=1, source_target_pairs={{0,4},{1,5},{2,6},{3,7},{4,0},{5,1},{6,2},{7,3},{8,12},{9,13},{10,... | collective-permute-start | bytes 98312 | tf_op jit(solution)/shard_map/ppermute | solution.py:35
  92.2 5.1 %collective-permute-start.21 = (f32[64,128]{1,0:T(8,128)S(1)}, f32[64,128]{1,0:T(8,128)S(1)}, u32[]{:S(2)}, u32[]{:S(2)}) collective-permute-start(f32[64,128]{1,0:T(8,128)S(1)} %add_add_fusion), channel_id=1, source_target_pairs={{0,16},{1,17},{2,18},{3,19},{4,20},{5,21},{6,22},{7,23},{8,24},{9,... | collective-permute-start | bytes 98312 | tf_op jit(solution)/shard_map/ppermute | solution.py:35

commit v8 on v7

--- a/solution.py
+++ b/solution.py
@@ -81,30 +81,21 @@
     return jnp.concatenate(pieces, axis=1)
 
 
-def fetch(factor_ref, start, fetched, arrived, step):
-    chunk = fetched.shape[3]
-    piece = factor_ref.at[:, :, pl.ds(pl.multiple_of(start, TILE), chunk)]
-    return pltpu.make_async_copy(piece, fetched.at[step], arrived.at[step])
-
-
-def inside_kernel(edge, spots, prior_ref, snap_ref, factor_ref, weighted_ref, gram_ref, bank, fetched, arrived):
+def inside_kernel(edge, spots, prior_ref, snap_ref, factor_ref, weighted_ref, gram_ref, bank):
     step = pl.program_id(0)
     rows, width = prior_ref.shape
-    steps, _, block, chunk = fetched.shape
+    _, block, chunk = factor_ref.shape
     whole = width + 2 * edge
 
     @pl.when(step == 0)
     def _():
-        for i in range(steps):
-            fetch(factor_ref, (i + 1) * chunk, fetched, arrived, i).start()
         bank[:rows, edge:edge + width] = prior_ref[...]
         bank[rows:, edge:edge + width] = snap_ref[...]
         fill_odd(bank, whole, block, edge, edge + width)
         gram_ref[...] = jnp.zeros_like(gram_ref)
 
     shift = lax.axis_index("space") * (width // block) - edge // block
-    fetch(factor_ref, (step + 1) * chunk, fetched, arrived, step).wait()
-    weighted = weigh_chunk(spots, (step + 1) * (chunk // block), shift, bank, fetched.at[step])
+    weighted = weigh_chunk(spots, (step + 1) * (chunk // block), shift, bank, factor_ref)
     weighted_ref[...] = weighted
     gram_ref[...] += lax.dot_general(weighted, weighted, NT, preferred_element_type=F32)
 
@@ -174,14 +165,11 @@
     low, high = halo((prior, snapshots), "space", edge)
     spots = neighbours.T
     full = lambda i, s: (0, 0)
-    fetching = lambda steps: [
-        pltpu.VMEM((steps, count, block, chunk), BF16), pltpu.SemaphoreType.DMA((steps,))
-    ]
     shapes = (
         jax.ShapeDtypeStruct((columns, width), BF16),
         jax.ShapeDtypeStruct((columns, columns), F32),
     )
-    params = pltpu.CompilerParams(vmem_limit_bytes=56 * 1024 * 1024)
+    params = pltpu.CompilerParams(vmem_limit_bytes=24 * 1024 * 1024)
     weighted, gram = pl.pallas_call(
         functools.partial(inside_kernel, edge),
         out_shape=shapes,
@@ -191,13 +179,13 @@
             in_specs=[
                 pl.BlockSpec((rows, width), full),
                 pl.BlockSpec((rows, width), full),
-                pl.BlockSpec(memory_space=pl.ANY),
+                pl.BlockSpec((count, block, chunk), lambda i, s: (0, 0, i + 1)),
             ],
             out_specs=(
                 pl.BlockSpec((columns, chunk), lambda i, s: (0, i + 1)),
                 pl.BlockSpec((columns, columns), full),
             ),
-            scratch_shapes=[pltpu.VMEM((columns, 2 * (width + 2 * edge) + TILE), BF16)] + fetching(chunks - 2),
+            scratch_shapes=[pltpu.VMEM((columns, 2 * (width + 2 * edge) + TILE), BF16)],
         ),
         compiler_params=params,
         cost_estimate=pl.CostEstimate(
@@ -373,7 +361,6 @@
         step = 1 << level
         bit = member // step % 2
         upper_half = bit == 1
-        partner_own = swapped(own, step)
         if partner_weighted is None:
             weighted = combine(coefficients, weighted)
             partner_weighted = swapped(shared_out(weighted, width, 1 - bit), step)
@@ -382,18 +369,22 @@
             partner_weighted = combine(swapped(coefficients, step), partner_weighted)
             own_weighted = combine(coefficients, shared_out(weighted, width, bit))
         weighted = ordered(upper_half, own_weighted, partner_weighted)
+        top = lax.dot_general(weighted[:RANK], weighted, NT, preferred_element_type=F32)
+        last = 2 * step == members
+        if not last:
+            next_bit = member // (2 * step) % 2
+            partner_weighted = swapped(shared_out(weighted, width, 1 - next_bit), 2 * step)
+        bits = [1 << i for i in range(level + 1)] + across
+        top = total(top, bits[:2], 2)
+        coefficients, own, top = lax.optimization_barrier((coefficients, own, top))
+        partner_own = swapped(own, step)
         if level == 0:
             stacked = combine_two(coefficients, prior_basis, snapshots)
         else:
             stacked = combine(coefficients, stacked)
         partner_stacked = swapped(shared_out(stacked, width, 1 - bit), step)
         stacked = ordered(upper_half, shared_out(stacked, width, bit), partner_stacked)
-        top = lax.dot_general(weighted[:RANK], weighted, NT, preferred_element_type=F32)
-        last = 2 * step == members
-        if not last:
-            next_bit = member // (2 * step) % 2
-            partner_weighted = swapped(shared_out(weighted, width, 1 - next_bit), 2 * step)
-        top = total(top, [1 << i for i in range(level + 1)] + across, 2)
+        top = total(top, bits[2:], 2)
         upper = jnp.where(upper_half, own, partner_own)
         if not last:
             coefficients, own = compress(merge_kernel, reduced, top, upper)

time: 106 us -> 105 us (level)
  local copies, waits for them, and re-layouts: 2.37 us -> 7.44 us
  Pallas kernels: 41.2 us -> 36.6 us
    unnamed x10 -> x12, local copies, waits for them, and re-layouts: 1.16 us -> 6.25 us
    pallas_call x1, Pallas kernels: 10.2 us -> 7.5 us  [weigh(): pl.pallas_call(functools.partial(inside_kernel, edge), out_shape=shapes,...]
    pallas_call x1, Pallas kernels: 5.75 us -> 3.75 us  [weigh(): pl.pallas_call(functools.partial(border_kernel, width), out_shape=(shapes...]
  transfers between devices with their start and end apart: 25 -> 25, of which waited for: 14 -> 13; matrix products, arithmetic and copies ran while one was open for 3% -> 2% of each run, Pallas kernels for 17% -> 15%
where the time goes in v8:
time: 105 us
  Pallas kernels  36.6 us (35%)
  starting transfers between devices  34.7 us (33%)
  waiting for transfers between devices  21.7 us (21%)
  local copies, waits for them, and re-layouts  7.44 us (7%)
  matrix products  2.85 us (3%)
    ppermute x23, starting transfers between devices, swapped(): return lax.ppermute(block, axes, [(i, i ^ mask) for i in range(count)])  28.5 us
    pallas_call x3, Pallas kernels, compress(): pl.pallas_call(kernel, out_shape=outs, scratch_shapes=[pltpu.VMEM((RANK /...  25.3 us
    ppermute x23, waiting for transfers between devices, swapped(): return lax.ppermute(block, axes, [(i, i ^ mask) for i in range(count)])  21.7 us
    pallas_call x1, Pallas kernels, weigh(): pl.pallas_call(functools.partial(inside_kernel, edge), out_shape=shapes,...  7.5 us
    unnamed x12, local copies, waits for them, and re-layouts  6.25 us
    ppermute x1, starting transfers between devices, halo(): low = lax.ppermute(last, axis, forward)  4.88 us
    pallas_call x1, Pallas kernels, weigh(): pl.pallas_call(functools.partial(border_kernel, width), out_shape=(shapes...  3.75 us
  transfers between devices with their start and end apart: 25, of which 13 were waited for; matrix products, arithmetic and copies ran while one was open for 2% of the time, Pallas kernels for 15%

profile of v8, /device:TPU:0, one launch (start us, length us, event | category | flops | bytes accessed | tf_op | source)
XLA Modules:
  0.0 105.0 jit_solution(11235987283634937331)
XLA Ops:
  0.6 1.0 fusion.16
  1.6 4.9 %collective-permute-start = (bf16[128,512]{1,0:T(8,128)(2,1)S(1)}, bf16[128,512]{1,0:T(8,128)(2,1)S(1)}, u32[]{:S(2)}, u32[]{:S(2)}) collective-permute-start(bf16[128,512]{1,0:T(8,128)(2,1)S(1)} %pad_maximum_fusion.8), channel_id=1, source_target_pairs={{0,4},{4,8},{8,12},{12,16},{16,20},{20,24},{24,28},{1,5},{5,9},{9,... | collective-permute-start | bytes 393224 | tf_op jit(solution)/shard_map/ppermute | solution.py:27
  6.5 1.3 %collective-permute-start.1 = (bf16[128,512]{1,0:T(8,128)(2,1)S(1)}, bf16[128,512]{1,0:T(8,128)(2,1)S(1)}, u32[]{:S(2)}, u32[]{:S(2)}) collective-permute-start(bf16[128,512]{1,0:T(8,128)(2,1)S(1)} %pad_maximum_fusion.9), channel_id=1, source_target_pairs={{4,0},{8,4},{12,8},{16,12},{20,16},{24,20},{28,24},{5,1},{9,5},{13... | collective-permute-start | bytes 393224 | tf_op jit(solution)/shard_map/ppermute | solution.py:28
  7.8 3.1 %copy-done = bf16[7,64,8192]{2,1,0:T(8,128)(2,1)S(1)} copy-done((bf16[7,64,8192]{2,1,0:T(8,128)(2,1)S(1)}, bf16[7,64,8192]{2,1,0:T(8,128)(2,1)}, u32[]{:S(2)}) %copy-start) | copy-done | bytes 7340056
  10.9 1.2 %copy-done.1 = bf16[64,8192]{1,0:T(8,128)(2,1)S(1)} copy-done((bf16[64,8192]{1,0:T(8,128)(2,1)S(1)}, bf16[64,8192]{1,0:T(8,128)(2,1)}, u32[]{:S(2)}) %copy-start.1) | copy-done | bytes 1048600
  12.2 1.2 %copy-done.3 = bf16[64,8192]{1,0:T(8,128)(2,1)S(1)} copy-done((bf16[64,8192]{1,0:T(8,128)(2,1)S(1)}, bf16[64,8192]{1,0:T(8,128)(2,1)}, u32[]{:S(2)}) %copy-start.3) | copy-done | bytes 1048600
  14.1 7.5 %weigh_inside.1 = (bf16[128,8192]{1,0:T(8,128)(2,1)S(1)}, f32[128,128]{1,0:T(8,128)S(1)}) custom-call(s32[7,128]{1,0:T(8,128)S(1)} %bitcast.11, bf16[64,8192]{1,0:T(8,128)(2,1)S(1)} %copy-done.1, bf16[64,8192]{1,0:T(8,128)(2,1)S(1)} %copy-done.3, bf16[7,64,8192]{2,1,0:T(8,128)(2,1)S(1)} %copy-done), custom_call_target="tpu_custom_call" | custom-call | flops 3758096384 | bytes 7340032 | tf_op jit(solution)/shard_map/weigh_inside/pallas_call | solution.py:173
  21.6 3.7 %weigh_border.1 = (bf16[128,8192]{1,0:T(8,128)(2,1)S(1)}, f32[96,128]{1,0:T(8,128)S(1)}) custom-call(s32[7,128]{1,0:T(8,128)S(1)} %bitcast.12, bf16[64,8192]{1,0:T(8,128)(2,1)S(1)} %copy-done.1, bf16[64,8192]{1,0:T(8,128)(2,1)S(1)} %copy-done.3, bf16[128,512]{1,0:T(8,128)(2,1)S(1)} %collective-permute-done.low_ref, ...), custom_call_target="tpu_custom_call", output_to_operand_aliasing={{0}: (7, {})} | custom-call | tf_op jit(solution)/shard_map/weigh_border/pallas_call | solution.py:197
  25.4 2.7 %collective-permute-start.2 = (f32[96,128]{1,0:T(8,128)S(1)}, f32[96,128]{1,0:T(8,128)S(1)}, u32[]{:S(2)}, u32[]{:S(2)}) collective-permute-start(f32[96,128]{1,0:T(8,128)S(1)} %get-tuple-element.18), channel_id=1, source_target_pairs={{0,4},{1,5},{2,6},{3,7},{4,0},{5,1},{6,2},{7,3},{8,12},{9,13},{10,... | collective-permute-start | bytes 147464 | tf_op jit(solution)/shard_map/ppermute | solution.py:35
  28.1 2.1 %collective-permute-done.2 = f32[96,128]{1,0:T(8,128)S(1)} collective-permute-done((f32[96,128]{1,0:T(8,128)S(1)}, f32[96,128]{1,0:T(8,128)S(1)}, u32[]{:S(2)}, u32[]{:S(2)}) %collective-permute-start.2) | collective-permute-done | bytes 49184 | tf_op jit(solution)/shard_map/ppermute | solution.py:35
  30.1 3.0 %collective-permute-start.3 = (f32[96,128]{1,0:T(8,128)S(1)}, f32[96,128]{1,0:T(8,128)S(1)}, u32[]{:S(2)}, u32[]{:S(2)}) collective-permute-start(f32[96,128]{1,0:T(8,128)S(1)} %add.94), channel_id=1, source_target_pairs={{0,8},{1,9},{2,10},{3,11},{4,12},{5,13},{6,14},{7,15},{8,0},{9,1},... | collective-permute-start | bytes 147464 | tf_op jit(solution)/shard_map/ppermute | solution.py:35
  33.2 2.1 %collective-permute-done.3 = f32[96,128]{1,0:T(8,128)S(1)} collective-permute-done((f32[96,128]{1,0:T(8,128)S(1)}, f32[96,128]{1,0:T(8,128)S(1)}, u32[]{:S(2)}, u32[]{:S(2)}) %collective-permute-start.3) | collective-permute-done | bytes 49184 | tf_op jit(solution)/shard_map/ppermute | solution.py:35
  35.2 3.6 %collective-permute-start.4 = (f32[96,128]{1,0:T(8,128)S(1)}, f32[96,128]{1,0:T(8,128)S(1)}, u32[]{:S(2)}, u32[]{:S(2)}) collective-permute-start(f32[96,128]{1,0:T(8,128)S(1)} %add.95), channel_id=1, source_target_pairs={{0,16},{1,17},{2,18},{3,19},{4,20},{5,21},{6,22},{7,23},{8,24},{9,... | collective-permute-start | bytes 147464 | tf_op jit(solution)/shard_map/ppermute | solution.py:35
  38.8 2.1 %collective-permute-done.4 = f32[96,128]{1,0:T(8,128)S(1)} collective-permute-done((f32[96,128]{1,0:T(8,128)S(1)}, f32[96,128]{1,0:T(8,128)S(1)}, u32[]{:S(2)}, u32[]{:S(2)}) %collective-permute-start.4) | collective-permute-done | bytes 49184 | tf_op jit(solution)/shard_map/ppermute | solution.py:35
  40.9 8.2 %compress.3 = (bf16[64,128]{1,0:T(8,128)(2,1)S(1)}, f32[64,64]{1,0:T(8,128)S(1)}) custom-call(f32[96,128]{1,0:T(8,128)S(1)} %add.96.blocks_ref), custom_call_target="tpu_custom_call" | custom-call | tf_op jit(solution)/shard_map/compress/pallas_call | solution.py:315
  49.8 1.8 %collective-permute-done.5 = bf16[64,4096]{1,0:T(8,128)(2,1)S(1)} collective-permute-done((bf16[64,4096]{1,0:T(8,128)(2,1)S(1)}, bf16[64,4096]{1,0:T(8,128)(2,1)S(1)}, u32[]{:S(2)}, u32[]{:S(2)}) %collective-permute-start.5) | collective-permute-done | bytes 524320 | tf_op jit(solution)/shard_map/ppermute | solution.py:35
  53.0 0.9 collective-permute-start.8
  54.6 1.5 %collective-permute-start.14 = (bf16[128,2048]{1,0:T(8,128)(2,1)S(1)}, bf16[128,2048]{1,0:T(8,128)(2,1)S(1)}, u32[]{:S(2)}, u32[]{:S(2)}) collective-permute-start(bf16[128,2048]{1,0:T(8,128)(2,1)S(1)} %fusion.5), channel_id=1, source_target_pairs={{0,2},{1,3},{2,0},{3,1},{4,6},{5,7},{6,4},{7,5},{8,10},{9,11},{10,... | collective-permute-start | bytes 1572872 | tf_op jit(solution)/shard_map/ppermute | solution.py:35
  56.8 3.1 %collective-permute-start.10 = (f32[64,128]{1,0:T(8,128)S(1)}, f32[64,128]{1,0:T(8,128)S(1)}, u32[]{:S(2)}, u32[]{:S(2)}) collective-permute-start(f32[64,128]{1,0:T(8,128)S(1)} %add_add_fusion.3), channel_id=1, source_target_pairs={{0,16},{1,17},{2,18},{3,19},{4,20},{5,21},{6,22},{7,23},{8,24},{9,... | collective-permute-start | bytes 98312 | tf_op jit(solution)/shard_map/ppermute | solution.py:35
  59.8 1.1 %collective-permute-start.11 = (f32[64,128]{1,0:T(8,128)S(1)}, f32[64,128]{1,0:T(8,128)S(1)}, u32[]{:S(2)}, u32[]{:S(2)}) collective-permute-start(f32[64,128]{1,0:T(8,128)S(1)} %add_add_fusion.3), channel_id=1, source_target_pairs={{0,24},{1,25},{2,26},{3,27},{4,28},{5,29},{6,30},{7,31},{8,16},{9,... | collective-permute-start | bytes 98312 | tf_op jit(solution)/shard_map/ppermute | solution.py:35
  62.6 2.9 %collective-permute-done.11 = f32[64,128]{1,0:T(8,128)S(1)} collective-permute-done((f32[64,128]{1,0:T(8,128)S(1)}, f32[64,128]{1,0:T(8,128)S(1)}, u32[]{:S(2)}, u32[]{:S(2)}) %collective-permute-start.11) | collective-permute-done | bytes 32800 | tf_op jit(solution)/shard_map/ppermute | solution.py:35
  65.6 8.3 %compress.4 = (bf16[64,128]{1,0:T(8,128)(2,1)S(1)}, f32[64,64]{1,0:T(8,128)S(1)}) custom-call(f32[64,128]{1,0:T(8,128)S(1)} %add_add_fusion.2.top_ref, f32[64,64]{1,0:T(8,128)S(1)} %broadcast_select_fusion.9.upper_ref), custom_call_target="tpu_custom_call" | custom-call | tf_op jit(solution)/shard_map/compress/pallas_call | solution.py:315
  73.9 1.5 %collective-permute-start.13 = (bf16[64,128]{1,0:T(8,128)(2,1)S(1)}, bf16[64,128]{1,0:T(8,128)(2,1)S(1)}, u32[]{:S(2)}, u32[]{:S(2)}) collective-permute-start(bf16[64,128]{1,0:T(8,128)(2,1)S(1)} %get-tuple-element.28), channel_id=1, source_target_pairs={{0,2},{1,3},{2,0},{3,1},{4,6},{5,7},{6,4},{7,5},{8,10},{9,11},{10,... | collective-permute-start | bytes 49160 | tf_op jit(solution)/shard_map/ppermute | solution.py:35
  75.5 2.1 %collective-permute-done.13 = bf16[64,128]{1,0:T(8,128)(2,1)S(1)} collective-permute-done((bf16[64,128]{1,0:T(8,128)(2,1)S(1)}, bf16[64,128]{1,0:T(8,128)(2,1)S(1)}, u32[]{:S(2)}, u32[]{:S(2)}) %collective-permute-start.13) | collective-permute-done | bytes 16416 | tf_op jit(solution)/shard_map/ppermute | solution.py:35
  78.4 1.6 %collective-permute-start.16 = (f32[64,128]{1,0:T(8,128)S(1)}, f32[64,128]{1,0:T(8,128)S(1)}, u32[]{:S(2)}, u32[]{:S(2)}) collective-permute-start(f32[64,128]{1,0:T(8,128)S(1)} %fusion.15), channel_id=1, source_target_pairs={{0,2},{1,3},{2,0},{3,1},{4,6},{5,7},{6,4},{7,5},{8,10},{9,11},{10,... | collective-permute-start | bytes 98312 | tf_op jit(solution)/shard_map/ppermute | solution.py:35
  80.7 1.7 %collective-permute-done.16 = f32[64,128]{1,0:T(8,128)S(1)} collective-permute-done((f32[64,128]{1,0:T(8,128)S(1)}, f32[64,128]{1,0:T(8,128)S(1)}, u32[]{:S(2)}, u32[]{:S(2)}) %collective-permute-start.16) | collective-permute-done | bytes 32800 | tf_op jit(solution)/shard_map/ppermute | solution.py:35
  82.4 0.9 collective-permute-done.17
  83.4 2.8 %collective-permute-start.20 = (f32[64,128]{1,0:T(8,128)S(1)}, f32[64,128]{1,0:T(8,128)S(1)}, u32[]{:S(2)}, u32[]{:S(2)}) collective-permute-start(f32[64,128]{1,0:T(8,128)S(1)} %add_add_fusion.1), channel_id=1, source_target_pairs={{0,12},{1,13},{2,14},{3,15},{4,8},{5,9},{6,10},{7,11},{8,4},{9,5},... | collective-permute-start | bytes 98312 | tf_op jit(solution)/shard_map/ppermute | solution.py:35
  88.3 1.2 %collective-permute-start.24 = (bf16[64,2048]{1,0:T(8,128)(2,1)S(1)}, bf16[64,2048]{1,0:T(8,128)(2,1)S(1)}, u32[]{:S(2)}, u32[]{:S(2)}) collective-permute-start(bf16[64,2048]{1,0:T(8,128)(2,1)S(1)} %constant_dynamic-slice_fusion), channel_id=1, source_target_pairs={{0,2},{1,3},{2,0},{3,1},{4,6},{5,7},{6,4},{7,5},{8,10},{9,11},{10,... | collective-permute-start | bytes 786440 | tf_op jit(solution)/shard_map/ppermute | solution.py:35
  90.2 1.3 %collective-permute-start.21 = (f32[64,128]{1,0:T(8,128)S(1)}, f32[64,128]{1,0:T(8,128)S(1)}, u32[]{:S(2)}, u32[]{:S(2)}) collective-permute-start(f32[64,128]{1,0:T(8,128)S(1)} %add_add_fusion), channel_id=1, source_target_pairs={{0,16},{1,17},{2,18},{3,19},{4,20},{5,21},{6,22},{7,23},{8,24},{9,... | collective-permute-start | bytes 98312 | tf_op jit(solution)/shard_map/ppermute | solution.py:35
  91.4 3.8 %collective-permute-done.21 = f32[64,128]{1,0:T(8,128)S(1)} collective-permute-done((f32[64,128]{1,0:T(8,128)S(1)}, f32[64,128]{1,0:T(8,128)S(1)}, u32[]{:S(2)}, u32[]{:S(2)}) %collective-permute-start.21) | collective-permute-done | bytes 32800 | tf_op jit(solution)/shard_map/ppermute | solution.py:35
  96.2 8.8 %compress.5 = (bf16[64,2048]{1,0:T(8,128)(2,1)}, bf16[64,2048]{1,0:T(8,128)(2,1)}) custom-call(f32[64,128]{1,0:T(8,128)S(1)} %add.119.top_ref, f32[64,64]{1,0:T(8,128)S(1)} %broadcast_select_fusion.8.upper_ref, bf16[128,2048]{1,0:T(8,128)(2,1)S(1)} %pad_maximum_fusion.7.stacked_ref, bf16[128,2048]{1,0:T(8,128)(2,1)S(1)} %pad_maximum_fusion.4.weighted_ref), custom_call_target="tpu_custom_call" | custom-call | tf_op jit(solution)/shard_map/compress/pallas_call | solution.py:315
  (67 shorter events, 10.9 us)
Async XLA Ops:
  1.6 20.0 %collective-permute-start = (bf16[128,512]{1,0:T(8,128)(2,1)S(1)}, bf16[128,512]{1,0:T(8,128)(2,1)S(1)}, u32[]{:S(2)}, u32[]{:S(2)}) collective-permute-start(bf16[128,512]{1,0:T(8,128)(2,1)S(1)} %pad_maximum_fusion.8), channel_id=1, source_target_pairs={{0,4},{4,8},{8,12},{12,16},{16,20},{20,24},{24,28},{1,5},{5,9},{9,... | collective-permute-start | bytes 393224 | tf_op jit(solution)/shard_map/ppermute | solution.py:27
  6.5 15.1 %collective-permute-start.1 = (bf16[128,512]{1,0:T(8,128)(2,1)S(1)}, bf16[128,512]{1,0:T(8,128)(2,1)S(1)}, u32[]{:S(2)}, u32[]{:S(2)}) collective-permute-start(bf16[128,512]{1,0:T(8,128)(2,1)S(1)} %pad_maximum_fusion.9), channel_id=1, source_target_pairs={{4,0},{8,4},{12,8},{16,12},{20,16},{24,20},{28,24},{5,1},{9,5},{13... | collective-permute-start | bytes 393224 | tf_op jit(solution)/shard_map/ppermute | solution.py:28
  7.8 3.1 %copy-start = (bf16[7,64,8192]{2,1,0:T(8,128)(2,1)S(1)}, bf16[7,64,8192]{2,1,0:T(8,128)(2,1)}, u32[]{:S(2)}) copy-start(bf16[7,64,8192]{2,1,0:T(8,128)(2,1)} %factor_ref.3) | copy-start | bytes 22020100
  10.9 1.2 %copy-start.1 = (bf16[64,8192]{1,0:T(8,128)(2,1)S(1)}, bf16[64,8192]{1,0:T(8,128)(2,1)}, u32[]{:S(2)}) copy-start(bf16[64,8192]{1,0:T(8,128)(2,1)} %prior_ref.3) | copy-start | bytes 3145732
  12.2 1.2 %copy-start.3 = (bf16[64,8192]{1,0:T(8,128)(2,1)S(1)}, bf16[64,8192]{1,0:T(8,128)(2,1)}, u32[]{:S(2)}) copy-start(bf16[64,8192]{1,0:T(8,128)(2,1)} %snap_ref.3) | copy-start | bytes 3145732
  13.4 0.7 copy-start.5
  25.4 4.8 %collective-permute-start.2 = (f32[96,128]{1,0:T(8,128)S(1)}, f32[96,128]{1,0:T(8,128)S(1)}, u32[]{:S(2)}, u32[]{:S(2)}) collective-permute-start(f32[96,128]{1,0:T(8,128)S(1)} %get-tuple-element.18), channel_id=1, source_target_pairs={{0,4},{1,5},{2,6},{3,7},{4,0},{5,1},{6,2},{7,3},{8,12},{9,13},{10,... | collective-permute-start | bytes 147464 | tf_op jit(solution)/shard_map/ppermute | solution.py:35
  30.1 5.1 %collective-permute-start.3 = (f32[96,128]{1,0:T(8,128)S(1)}, f32[96,128]{1,0:T(8,128)S(1)}, u32[]{:S(2)}, u32[]{:S(2)}) collective-permute-start(f32[96,128]{1,0:T(8,128)S(1)} %add.94), channel_id=1, source_target_pairs={{0,8},{1,9},{2,10},{3,11},{4,12},{5,13},{6,14},{7,15},{8,0},{9,1},... | collective-permute-start | bytes 147464 | tf_op jit(solution)/shard_map/ppermute | solution.py:35
  35.2 5.7 %collective-permute-start.4 = (f32[96,128]{1,0:T(8,128)S(1)}, f32[96,128]{1,0:T(8,128)S(1)}, u32[]{:S(2)}, u32[]{:S(2)}) collective-permute-start(f32[96,128]{1,0:T(8,128)S(1)} %add.95), channel_id=1, source_target_pairs={{0,16},{1,17},{2,18},{3,19},{4,20},{5,21},{6,22},{7,23},{8,24},{9,... | collective-permute-start | bytes 147464 | tf_op jit(solution)/shard_map/ppermute | solution.py:35
  49.7 2.0 %collective-permute-start.5 = (bf16[64,4096]{1,0:T(8,128)(2,1)S(1)}, bf16[64,4096]{1,0:T(8,128)(2,1)S(1)}, u32[]{:S(2)}, u32[]{:S(2)}) collective-permute-start(bf16[64,4096]{1,0:T(8,128)(2,1)S(1)} %pad_maximum_fusion.2), channel_id=1, source_target_pairs={{0,1},{1,0},{2,3},{3,2},{4,5},{5,4},{6,7},{7,6},{8,9},{9,8},{10,11... | collective-permute-start | bytes 1572872 | tf_op jit(solution)/shard_map/ppermute | solution.py:35
  51.9 9.5 %copy-start.2 = (bf16[64,8192]{1,0:T(8,128)(2,1)S(1)}, bf16[64,8192]{1,0:T(8,128)(2,1)}, u32[]{:S(2)}) copy-start(bf16[64,8192]{1,0:T(8,128)(2,1)} %prior_ref.3) | copy-start | bytes 3145732
  52.4 9.4 %copy-start.4 = (bf16[64,8192]{1,0:T(8,128)(2,1)S(1)}, bf16[64,8192]{1,0:T(8,128)(2,1)}, u32[]{:S(2)}) copy-start(bf16[64,8192]{1,0:T(8,128)(2,1)} %snap_ref.3) | copy-start | bytes 3145732
  52.4 4.3 %collective-permute-start.7 = (f32[64,128]{1,0:T(8,128)S(1)}, f32[64,128]{1,0:T(8,128)S(1)}, u32[]{:S(2)}, u32[]{:S(2)}) collective-permute-start(f32[64,128]{1,0:T(8,128)S(1)} %fusion.1), channel_id=1, source_target_pairs={{0,4},{1,5},{2,6},{3,7},{4,0},{5,1},{6,2},{7,3},{8,12},{9,13},{10,... | collective-permute-start | bytes 98312 | tf_op jit(solution)/shard_map/ppermute | solution.py:35
  53.0 3.7 %collective-permute-start.8 = (f32[64,128]{1,0:T(8,128)S(1)}, f32[64,128]{1,0:T(8,128)S(1)}, u32[]{:S(2)}, u32[]{:S(2)}) collective-permute-start(f32[64,128]{1,0:T(8,128)S(1)} %fusion.1), channel_id=1, source_target_pairs={{0,5},{1,4},{2,7},{3,6},{4,1},{5,0},{6,3},{7,2},{8,13},{9,12},{10,... | collective-permute-start | bytes 98312 | tf_op jit(solution)/shard_map/ppermute | solution.py:35
  53.9 2.8 %collective-permute-start.6 = (f32[64,128]{1,0:T(8,128)S(1)}, f32[64,128]{1,0:T(8,128)S(1)}, u32[]{:S(2)}, u32[]{:S(2)}) collective-permute-start(f32[64,128]{1,0:T(8,128)S(1)} %fusion.1), channel_id=1, source_target_pairs={{0,1},{1,0},{2,3},{3,2},{4,5},{5,4},{6,7},{7,6},{8,9},{9,8},{10,11... | collective-permute-start | bytes 98312 | tf_op jit(solution)/shard_map/ppermute | solution.py:35
  54.6 23.0 %collective-permute-start.14 = (bf16[128,2048]{1,0:T(8,128)(2,1)S(1)}, bf16[128,2048]{1,0:T(8,128)(2,1)S(1)}, u32[]{:S(2)}, u32[]{:S(2)}) collective-permute-start(bf16[128,2048]{1,0:T(8,128)(2,1)S(1)} %fusion.5), channel_id=1, source_target_pairs={{0,2},{1,3},{2,0},{3,1},{4,6},{5,7},{6,4},{7,5},{8,10},{9,11},{10,... | collective-permute-start | bytes 1572872 | tf_op jit(solution)/shard_map/ppermute | solution.py:35
  56.8 5.9 %collective-permute-start.10 = (f32[64,128]{1,0:T(8,128)S(1)}, f32[64,128]{1,0:T(8,128)S(1)}, u32[]{:S(2)}, u32[]{:S(2)}) collective-permute-start(f32[64,128]{1,0:T(8,128)S(1)} %add_add_fusion.3), channel_id=1, source_target_pairs={{0,16},{1,17},{2,18},{3,19},{4,20},{5,21},{6,22},{7,23},{8,24},{9,... | collective-permute-start | bytes 98312 | tf_op jit(solution)/shard_map/ppermute | solution.py:35
  59.8 5.7 %collective-permute-start.11 = (f32[64,128]{1,0:T(8,128)S(1)}, f32[64,128]{1,0:T(8,128)S(1)}, u32[]{:S(2)}, u32[]{:S(2)}) collective-permute-start(f32[64,128]{1,0:T(8,128)S(1)} %add_add_fusion.3), channel_id=1, source_target_pairs={{0,24},{1,25},{2,26},{3,27},{4,28},{5,29},{6,30},{7,31},{8,16},{9,... | collective-permute-start | bytes 98312 | tf_op jit(solution)/shard_map/ppermute | solution.py:35
  60.9 4.6 %collective-permute-start.9 = (f32[64,128]{1,0:T(8,128)S(1)}, f32[64,128]{1,0:T(8,128)S(1)}, u32[]{:S(2)}, u32[]{:S(2)}) collective-permute-start(f32[64,128]{1,0:T(8,128)S(1)} %add_add_fusion.3), channel_id=1, source_target_pairs={{0,8},{1,9},{2,10},{3,11},{4,12},{5,13},{6,14},{7,15},{8,0},{9,1},... | collective-permute-start | bytes 98312 | tf_op jit(solution)/shard_map/ppermute | solution.py:35
  61.4 1.2 %collective-permute-start.12 = (f32[64,64]{1,0:T(8,128)S(1)}, f32[64,64]{1,0:T(8,128)S(1)}, u32[]{:S(2)}, u32[]{:S(2)}) collective-permute-start(f32[64,64]{1,0:T(8,128)S(1)} %get-tuple-element.23), channel_id=1, source_target_pairs={{0,1},{1,0},{2,3},{3,2},{4,5},{5,4},{6,7},{7,6},{8,9},{9,8},{10,11... | collective-permute-start | bytes 49160 | tf_op jit(solution)/shard_map/ppermute | solution.py:35
  73.9 3.8 %collective-permute-start.13 = (bf16[64,128]{1,0:T(8,128)(2,1)S(1)}, bf16[64,128]{1,0:T(8,128)(2,1)S(1)}, u32[]{:S(2)}, u32[]{:S(2)}) collective-permute-start(bf16[64,128]{1,0:T(8,128)(2,1)S(1)} %get-tuple-element.28), channel_id=1, source_target_pairs={{0,2},{1,3},{2,0},{3,1},{4,6},{5,7},{6,4},{7,5},{8,10},{9,11},{10,... | collective-permute-start | bytes 49160 | tf_op jit(solution)/shard_map/ppermute | solution.py:35
  75.4 12.3 %collective-permute-start.23 = (bf16[64,4096]{1,0:T(8,128)(2,1)S(1)}, bf16[64,4096]{1,0:T(8,128)(2,1)S(1)}, u32[]{:S(2)}, u32[]{:S(2)}) collective-permute-start(bf16[64,4096]{1,0:T(8,128)(2,1)S(1)} %pad_maximum_fusion.5), channel_id=1, source_target_pairs={{0,1},{1,0},{2,3},{3,2},{4,5},{5,4},{6,7},{7,6},{8,9},{9,8},{10,11... | collective-permute-start | bytes 1572872 | tf_op jit(solution)/shard_map/ppermute | solution.py:35
  78.4 4.0 %collective-permute-start.16 = (f32[64,128]{1,0:T(8,128)S(1)}, f32[64,128]{1,0:T(8,128)S(1)}, u32[]{:S(2)}, u32[]{:S(2)}) collective-permute-start(f32[64,128]{1,0:T(8,128)S(1)} %fusion.15), channel_id=1, source_target_pairs={{0,2},{1,3},{2,0},{3,1},{4,6},{5,7},{6,4},{7,5},{8,10},{9,11},{10,... | collective-permute-start | bytes 98312 | tf_op jit(solution)/shard_map/ppermute | solution.py:35
  80.0 3.3 %collective-permute-start.17 = (f32[64,128]{1,0:T(8,128)S(1)}, f32[64,128]{1,0:T(8,128)S(1)}, u32[]{:S(2)}, u32[]{:S(2)}) collective-permute-start(f32[64,128]{1,0:T(8,128)S(1)} %fusion.15), channel_id=1, source_target_pairs={{0,3},{1,2},{2,1},{3,0},{4,7},{5,6},{6,5},{7,4},{8,11},{9,10},{10,... | collective-permute-start | bytes 98312 | tf_op jit(solution)/shard_map/ppermute | solution.py:35
  80.0 3.3 %collective-permute-start.15 = (f32[64,128]{1,0:T(8,128)S(1)}, f32[64,128]{1,0:T(8,128)S(1)}, u32[]{:S(2)}, u32[]{:S(2)}) collective-permute-start(f32[64,128]{1,0:T(8,128)S(1)} %fusion.15), channel_id=1, source_target_pairs={{0,1},{1,0},{2,3},{3,2},{4,5},{5,4},{6,7},{7,6},{8,9},{9,8},{10,11... | collective-permute-start | bytes 98312 | tf_op jit(solution)/shard_map/ppermute | solution.py:35
  83.3 6.2 %collective-permute-start.19 = (f32[64,128]{1,0:T(8,128)S(1)}, f32[64,128]{1,0:T(8,128)S(1)}, u32[]{:S(2)}, u32[]{:S(2)}) collective-permute-start(f32[64,128]{1,0:T(8,128)S(1)} %add_add_fusion.1), channel_id=1, source_target_pairs={{0,8},{1,9},{2,10},{3,11},{4,12},{5,13},{6,14},{7,15},{8,0},{9,1},... | collective-permute-start | bytes 98312 | tf_op jit(solution)/shard_map/ppermute | solution.py:35
  83.4 6.1 %collective-permute-start.20 = (f32[64,128]{1,0:T(8,128)S(1)}, f32[64,128]{1,0:T(8,128)S(1)}, u32[]{:S(2)}, u32[]{:S(2)}) collective-permute-start(f32[64,128]{1,0:T(8,128)S(1)} %add_add_fusion.1), channel_id=1, source_target_pairs={{0,12},{1,13},{2,14},{3,15},{4,8},{5,9},{6,10},{7,11},{8,4},{9,5},... | collective-permute-start | bytes 98312 | tf_op jit(solution)/shard_map/ppermute | solution.py:35
  86.2 3.9 %collective-permute-start.18 = (f32[64,128]{1,0:T(8,128)S(1)}, f32[64,128]{1,0:T(8,128)S(1)}, u32[]{:S(2)}, u32[]{:S(2)}) collective-permute-start(f32[64,128]{1,0:T(8,128)S(1)} %add_add_fusion.1), channel_id=1, source_target_pairs={{0,4},{1,5},{2,6},{3,7},{4,0},{5,1},{6,2},{7,3},{8,12},{9,13},{10,... | collective-permute-start | bytes 98312 | tf_op jit(solution)/shard_map/ppermute | solution.py:35
  86.9 4.5 %collective-permute-start.22 = (f32[64,64]{1,0:T(8,128)S(1)}, f32[64,64]{1,0:T(8,128)S(1)}, u32[]{:S(2)}, u32[]{:S(2)}) collective-permute-start(f32[64,64]{1,0:T(8,128)S(1)} %get-tuple-element.27), channel_id=1, source_target_pairs={{0,2},{1,3},{2,0},{3,1},{4,6},{5,7},{6,4},{7,5},{8,10},{9,11},{10,... | collective-permute-start | bytes 49160 | tf_op jit(solution)/shard_map/ppermute | solution.py:35
  88.3 7.7 %collective-permute-start.24 = (bf16[64,2048]{1,0:T(8,128)(2,1)S(1)}, bf16[64,2048]{1,0:T(8,128)(2,1)S(1)}, u32[]{:S(2)}, u32[]{:S(2)}) collective-permute-start(bf16[64,2048]{1,0:T(8,128)(2,1)S(1)} %constant_dynamic-slice_fusion), channel_id=1, source_target_pairs={{0,2},{1,3},{2,0},{3,1},{4,6},{5,7},{6,4},{7,5},{8,10},{9,11},{10,... | collective-permute-start | bytes 786440 | tf_op jit(solution)/shard_map/ppermute | solution.py:35
  90.2 5.1 %collective-permute-start.21 = (f32[64,128]{1,0:T(8,128)S(1)}, f32[64,128]{1,0:T(8,128)S(1)}, u32[]{:S(2)}, u32[]{:S(2)}) collective-permute-start(f32[64,128]{1,0:T(8,128)S(1)} %add_add_fusion), channel_id=1, source_target_pairs={{0,16},{1,17},{2,18},{3,19},{4,20},{5,21},{6,22},{7,23},{8,24},{9,... | collective-permute-start | bytes 98312 | tf_op jit(solution)/shard_map/ppermute | solution.py:35

commit v9 on v8

--- a/solution.py
+++ b/solution.py
@@ -371,12 +371,12 @@
         weighted = ordered(upper_half, own_weighted, partner_weighted)
         top = lax.dot_general(weighted[:RANK], weighted, NT, preferred_element_type=F32)
         last = 2 * step == members
+        bits = [1 << i for i in range(level + 1)] + across
+        top = total(top, bits[:2], 2)
+        coefficients, own, weighted, top = lax.optimization_barrier((coefficients, own, weighted, top))
         if not last:
             next_bit = member // (2 * step) % 2
             partner_weighted = swapped(shared_out(weighted, width, 1 - next_bit), 2 * step)
-        bits = [1 << i for i in range(level + 1)] + across
-        top = total(top, bits[:2], 2)
-        coefficients, own, top = lax.optimization_barrier((coefficients, own, top))
         partner_own = swapped(own, step)
         if level == 0:
             stacked = combine_two(coefficients, prior_basis, snapshots)

time: 105 us -> 105 us (level)
  no operation moved by 1% of the time
where the time goes in v9:
time: 105 us
  Pallas kernels  36.6 us (35%)
  starting transfers between devices  35.1 us (33%)
  waiting for transfers between devices  20.8 us (20%)
  local copies, waits for them, and re-layouts  7.48 us (7%)
  matrix products  2.84 us (3%)
    ppermute x23, starting transfers between devices, swapped(): return lax.ppermute(block, axes, [(i, i ^ mask) for i in range(count)])  28.9 us
    pallas_call x3, Pallas kernels, compress(): pl.pallas_call(kernel, out_shape=outs, scratch_shapes=[pltpu.VMEM((RANK /...  25.3 us
    ppermute x23, waiting for transfers between devices, swapped(): return lax.ppermute(block, axes, [(i, i ^ mask) for i in range(count)])  20.8 us
    pallas_call x1, Pallas kernels, weigh(): pl.pallas_call(functools.partial(inside_kernel, edge), out_shape=shapes,...  7.53 us
    unnamed x12, local copies, waits for them, and re-layouts  6.25 us
    ppermute x1, starting transfers between devices, halo(): low = lax.ppermute(last, axis, forward)  4.88 us
    pallas_call x1, Pallas kernels, weigh(): pl.pallas_call(functools.partial(border_kernel, width), out_shape=(shapes...  3.74 us
  transfers between devices with their start and end apart: 25, of which 13 were waited for; matrix products, arithmetic and copies ran while one was open for 2% of the time, Pallas kernels for 15%

profile of v9, /device:TPU:0, one launch (start us, length us, event | category | flops | bytes accessed | tf_op | source)
XLA Modules:
  0.0 104.5 jit_solution(2587699449242998226)
XLA Ops:
  0.6 1.0 fusion.12
  1.6 4.9 %collective-permute-start = (bf16[128,512]{1,0:T(8,128)(2,1)S(1)}, bf16[128,512]{1,0:T(8,128)(2,1)S(1)}, u32[]{:S(2)}, u32[]{:S(2)}) collective-permute-start(bf16[128,512]{1,0:T(8,128)(2,1)S(1)} %pad_maximum_fusion.7), channel_id=1, source_target_pairs={{0,4},{4,8},{8,12},{12,16},{16,20},{20,24},{24,28},{1,5},{5,9},{9,... | collective-permute-start | bytes 393224 | tf_op jit(solution)/shard_map/ppermute | solution.py:27
  6.5 1.3 %collective-permute-start.1 = (bf16[128,512]{1,0:T(8,128)(2,1)S(1)}, bf16[128,512]{1,0:T(8,128)(2,1)S(1)}, u32[]{:S(2)}, u32[]{:S(2)}) collective-permute-start(bf16[128,512]{1,0:T(8,128)(2,1)S(1)} %pad_maximum_fusion.8), channel_id=1, source_target_pairs={{4,0},{8,4},{12,8},{16,12},{20,16},{24,20},{28,24},{5,1},{9,5},{13... | collective-permute-start | bytes 393224 | tf_op jit(solution)/shard_map/ppermute | solution.py:28
  7.8 3.1 %copy-done = bf16[7,64,8192]{2,1,0:T(8,128)(2,1)S(1)} copy-done((bf16[7,64,8192]{2,1,0:T(8,128)(2,1)S(1)}, bf16[7,64,8192]{2,1,0:T(8,128)(2,1)}, u32[]{:S(2)}) %copy-start) | copy-done | bytes 7340056
  10.9 1.2 %copy-done.1 = bf16[64,8192]{1,0:T(8,128)(2,1)S(1)} copy-done((bf16[64,8192]{1,0:T(8,128)(2,1)S(1)}, bf16[64,8192]{1,0:T(8,128)(2,1)}, u32[]{:S(2)}) %copy-start.1) | copy-done | bytes 1048600
  12.2 1.2 %copy-done.3 = bf16[64,8192]{1,0:T(8,128)(2,1)S(1)} copy-done((bf16[64,8192]{1,0:T(8,128)(2,1)S(1)}, bf16[64,8192]{1,0:T(8,128)(2,1)}, u32[]{:S(2)}) %copy-start.3) | copy-done | bytes 1048600
  14.1 7.5 %weigh_inside.1 = (bf16[128,8192]{1,0:T(8,128)(2,1)S(1)}, f32[128,128]{1,0:T(8,128)S(1)}) custom-call(s32[7,128]{1,0:T(8,128)S(1)} %bitcast.11, bf16[64,8192]{1,0:T(8,128)(2,1)S(1)} %copy-done.1, bf16[64,8192]{1,0:T(8,128)(2,1)S(1)} %copy-done.3, bf16[7,64,8192]{2,1,0:T(8,128)(2,1)S(1)} %copy-done), custom_call_target="tpu_custom_call" | custom-call | flops 3758096384 | bytes 7340032 | tf_op jit(solution)/shard_map/weigh_inside/pallas_call | solution.py:173
  21.6 3.7 %weigh_border.1 = (bf16[128,8192]{1,0:T(8,128)(2,1)S(1)}, f32[96,128]{1,0:T(8,128)S(1)}) custom-call(s32[7,128]{1,0:T(8,128)S(1)} %bitcast.12, bf16[64,8192]{1,0:T(8,128)(2,1)S(1)} %copy-done.1, bf16[64,8192]{1,0:T(8,128)(2,1)S(1)} %copy-done.3, bf16[128,512]{1,0:T(8,128)(2,1)S(1)} %collective-permute-done.low_ref, ...), custom_call_target="tpu_custom_call", output_to_operand_aliasing={{0}: (7, {})} | custom-call | tf_op jit(solution)/shard_map/weigh_border/pallas_call | solution.py:197
  25.4 2.7 %collective-permute-start.2 = (f32[96,128]{1,0:T(8,128)S(1)}, f32[96,128]{1,0:T(8,128)S(1)}, u32[]{:S(2)}, u32[]{:S(2)}) collective-permute-start(f32[96,128]{1,0:T(8,128)S(1)} %get-tuple-element.20), channel_id=1, source_target_pairs={{0,4},{1,5},{2,6},{3,7},{4,0},{5,1},{6,2},{7,3},{8,12},{9,13},{10,... | collective-permute-start | bytes 147464 | tf_op jit(solution)/shard_map/ppermute | solution.py:35
  28.1 2.1 %collective-permute-done.2 = f32[96,128]{1,0:T(8,128)S(1)} collective-permute-done((f32[96,128]{1,0:T(8,128)S(1)}, f32[96,128]{1,0:T(8,128)S(1)}, u32[]{:S(2)}, u32[]{:S(2)}) %collective-permute-start.2) | collective-permute-done | bytes 49184 | tf_op jit(solution)/shard_map/ppermute | solution.py:35
  30.2 3.0 %collective-permute-start.3 = (f32[96,128]{1,0:T(8,128)S(1)}, f32[96,128]{1,0:T(8,128)S(1)}, u32[]{:S(2)}, u32[]{:S(2)}) collective-permute-start(f32[96,128]{1,0:T(8,128)S(1)} %add.94), channel_id=1, source_target_pairs={{0,8},{1,9},{2,10},{3,11},{4,12},{5,13},{6,14},{7,15},{8,0},{9,1},... | collective-permute-start | bytes 147464 | tf_op jit(solution)/shard_map/ppermute | solution.py:35
  33.2 2.1 %collective-permute-done.3 = f32[96,128]{1,0:T(8,128)S(1)} collective-permute-done((f32[96,128]{1,0:T(8,128)S(1)}, f32[96,128]{1,0:T(8,128)S(1)}, u32[]{:S(2)}, u32[]{:S(2)}) %collective-permute-start.3) | collective-permute-done | bytes 49184 | tf_op jit(solution)/shard_map/ppermute | solution.py:35
  35.3 3.5 %collective-permute-start.4 = (f32[96,128]{1,0:T(8,128)S(1)}, f32[96,128]{1,0:T(8,128)S(1)}, u32[]{:S(2)}, u32[]{:S(2)}) collective-permute-start(f32[96,128]{1,0:T(8,128)S(1)} %add.95), channel_id=1, source_target_pairs={{0,16},{1,17},{2,18},{3,19},{4,20},{5,21},{6,22},{7,23},{8,24},{9,... | collective-permute-start | bytes 147464 | tf_op jit(solution)/shard_map/ppermute | solution.py:35
  38.8 2.1 %collective-permute-done.4 = f32[96,128]{1,0:T(8,128)S(1)} collective-permute-done((f32[96,128]{1,0:T(8,128)S(1)}, f32[96,128]{1,0:T(8,128)S(1)}, u32[]{:S(2)}, u32[]{:S(2)}) %collective-permute-start.4) | collective-permute-done | bytes 49184 | tf_op jit(solution)/shard_map/ppermute | solution.py:35
  40.8 8.2 %compress.3 = (bf16[64,128]{1,0:T(8,128)(2,1)S(1)}, f32[64,64]{1,0:T(8,128)S(1)}) custom-call(f32[96,128]{1,0:T(8,128)S(1)} %add.96.blocks_ref), custom_call_target="tpu_custom_call" | custom-call | tf_op jit(solution)/shard_map/compress/pallas_call | solution.py:315
  49.8 1.8 %collective-permute-done.5 = bf16[64,4096]{1,0:T(8,128)(2,1)S(1)} collective-permute-done((bf16[64,4096]{1,0:T(8,128)(2,1)S(1)}, bf16[64,4096]{1,0:T(8,128)(2,1)S(1)}, u32[]{:S(2)}, u32[]{:S(2)}) %collective-permute-start.5) | collective-permute-done | bytes 524320 | tf_op jit(solution)/shard_map/ppermute | solution.py:35
  54.6 1.9 %collective-permute-done.7 = f32[64,128]{1,0:T(8,128)S(1)} collective-permute-done((f32[64,128]{1,0:T(8,128)S(1)}, f32[64,128]{1,0:T(8,128)S(1)}, u32[]{:S(2)}, u32[]{:S(2)}) %collective-permute-start.7) | collective-permute-done | bytes 32800 | tf_op jit(solution)/shard_map/ppermute | solution.py:35
  56.8 3.1 %collective-permute-start.10 = (f32[64,128]{1,0:T(8,128)S(1)}, f32[64,128]{1,0:T(8,128)S(1)}, u32[]{:S(2)}, u32[]{:S(2)}) collective-permute-start(f32[64,128]{1,0:T(8,128)S(1)} %add_add_fusion.3), channel_id=1, source_target_pairs={{0,16},{1,17},{2,18},{3,19},{4,20},{5,21},{6,22},{7,23},{8,24},{9,... | collective-permute-start | bytes 98312 | tf_op jit(solution)/shard_map/ppermute | solution.py:35
  59.9 1.0 collective-permute-start.11
  61.4 1.6 %collective-permute-start.14 = (bf16[128,2048]{1,0:T(8,128)(2,1)S(1)}, bf16[128,2048]{1,0:T(8,128)(2,1)S(1)}, u32[]{:S(2)}, u32[]{:S(2)}) collective-permute-start(bf16[128,2048]{1,0:T(8,128)(2,1)S(1)} %constant_dynamic-slice_fusion.5), channel_id=1, source_target_pairs={{0,2},{1,3},{2,0},{3,1},{4,6},{5,7},{6,4},{7,5},{8,10},{9,11},{10,... | collective-permute-start | bytes 1572872 | tf_op jit(solution)/shard_map/ppermute | solution.py:35
  64.4 1.2 %collective-permute-done.11 = f32[64,128]{1,0:T(8,128)S(1)} collective-permute-done((f32[64,128]{1,0:T(8,128)S(1)}, f32[64,128]{1,0:T(8,128)S(1)}, u32[]{:S(2)}, u32[]{:S(2)}) %collective-permute-start.11) | collective-permute-done | bytes 32800 | tf_op jit(solution)/shard_map/ppermute | solution.py:35
  65.6 8.3 %compress.4 = (bf16[64,128]{1,0:T(8,128)(2,1)S(1)}, f32[64,64]{1,0:T(8,128)S(1)}) custom-call(f32[64,128]{1,0:T(8,128)S(1)} %add_add_fusion.2.top_ref, f32[64,64]{1,0:T(8,128)S(1)} %broadcast_select_fusion.9.upper_ref), custom_call_target="tpu_custom_call" | custom-call | tf_op jit(solution)/shard_map/compress/pallas_call | solution.py:315
  73.9 1.5 %collective-permute-start.13 = (bf16[64,128]{1,0:T(8,128)(2,1)S(1)}, bf16[64,128]{1,0:T(8,128)(2,1)S(1)}, u32[]{:S(2)}, u32[]{:S(2)}) collective-permute-start(bf16[64,128]{1,0:T(8,128)(2,1)S(1)} %get-tuple-element.31), channel_id=1, source_target_pairs={{0,2},{1,3},{2,0},{3,1},{4,6},{5,7},{6,4},{7,5},{8,10},{9,11},{10,... | collective-permute-start | bytes 49160 | tf_op jit(solution)/shard_map/ppermute | solution.py:35
  75.6 2.0 %collective-permute-done.13 = bf16[64,128]{1,0:T(8,128)(2,1)S(1)} collective-permute-done((bf16[64,128]{1,0:T(8,128)(2,1)S(1)}, bf16[64,128]{1,0:T(8,128)(2,1)S(1)}, u32[]{:S(2)}, u32[]{:S(2)}) %collective-permute-start.13) | collective-permute-done | bytes 16416 | tf_op jit(solution)/shard_map/ppermute | solution.py:35
  78.2 1.5 %collective-permute-start.16 = (f32[64,128]{1,0:T(8,128)S(1)}, f32[64,128]{1,0:T(8,128)S(1)}, u32[]{:S(2)}, u32[]{:S(2)}) collective-permute-start(f32[64,128]{1,0:T(8,128)S(1)} %fusion.10), channel_id=1, source_target_pairs={{0,2},{1,3},{2,0},{3,1},{4,6},{5,7},{6,4},{7,5},{8,10},{9,11},{10,... | collective-permute-start | bytes 98312 | tf_op jit(solution)/shard_map/ppermute | solution.py:35
  80.7 1.5 %collective-permute-done.16 = f32[64,128]{1,0:T(8,128)S(1)} collective-permute-done((f32[64,128]{1,0:T(8,128)S(1)}, f32[64,128]{1,0:T(8,128)S(1)}, u32[]{:S(2)}, u32[]{:S(2)}) %collective-permute-start.16) | collective-permute-done | bytes 32800 | tf_op jit(solution)/shard_map/ppermute | solution.py:35
  82.2 0.9 collective-permute-done.17
  83.3 2.6 %collective-permute-start.20 = (f32[64,128]{1,0:T(8,128)S(1)}, f32[64,128]{1,0:T(8,128)S(1)}, u32[]{:S(2)}, u32[]{:S(2)}) collective-permute-start(f32[64,128]{1,0:T(8,128)S(1)} %add_add_fusion.1), channel_id=1, source_target_pairs={{0,12},{1,13},{2,14},{3,15},{4,8},{5,9},{6,10},{7,11},{8,4},{9,5},... | collective-permute-start | bytes 98312 | tf_op jit(solution)/shard_map/ppermute | solution.py:35
  87.9 1.2 %collective-permute-start.24 = (bf16[64,2048]{1,0:T(8,128)(2,1)S(1)}, bf16[64,2048]{1,0:T(8,128)(2,1)S(1)}, u32[]{:S(2)}, u32[]{:S(2)}) collective-permute-start(bf16[64,2048]{1,0:T(8,128)(2,1)S(1)} %constant_dynamic-slice_fusion), channel_id=1, source_target_pairs={{0,2},{1,3},{2,0},{3,1},{4,6},{5,7},{6,4},{7,5},{8,10},{9,11},{10,... | collective-permute-start | bytes 786440 | tf_op jit(solution)/shard_map/ppermute | solution.py:35
  89.9 1.5 %collective-permute-start.21 = (f32[64,128]{1,0:T(8,128)S(1)}, f32[64,128]{1,0:T(8,128)S(1)}, u32[]{:S(2)}, u32[]{:S(2)}) collective-permute-start(f32[64,128]{1,0:T(8,128)S(1)} %add_add_fusion), channel_id=1, source_target_pairs={{0,16},{1,17},{2,18},{3,19},{4,20},{5,21},{6,22},{7,23},{8,24},{9,... | collective-permute-start | bytes 98312 | tf_op jit(solution)/shard_map/ppermute | solution.py:35
  91.4 3.6 %collective-permute-done.21 = f32[64,128]{1,0:T(8,128)S(1)} collective-permute-done((f32[64,128]{1,0:T(8,128)S(1)}, f32[64,128]{1,0:T(8,128)S(1)}, u32[]{:S(2)}, u32[]{:S(2)}) %collective-permute-start.21) | collective-permute-done | bytes 32800 | tf_op jit(solution)/shard_map/ppermute | solution.py:35
  95.7 8.8 %compress.5 = (bf16[64,2048]{1,0:T(8,128)(2,1)}, bf16[64,2048]{1,0:T(8,128)(2,1)}) custom-call(f32[64,128]{1,0:T(8,128)S(1)} %add.119.top_ref, f32[64,64]{1,0:T(8,128)S(1)} %broadcast_select_fusion.8.upper_ref, bf16[128,2048]{1,0:T(8,128)(2,1)S(1)} %pad_maximum_fusion.6.stacked_ref, bf16[128,2048]{1,0:T(8,128)(2,1)S(1)} %pad_maximum_fusion.3.weighted_ref), custom_call_target="tpu_custom_call" | custom-call | tf_op jit(solution)/shard_map/compress/pallas_call | solution.py:315
  (68 shorter events, 11.7 us)
Async XLA Ops:
  1.6 20.0 %collective-permute-start = (bf16[128,512]{1,0:T(8,128)(2,1)S(1)}, bf16[128,512]{1,0:T(8,128)(2,1)S(1)}, u32[]{:S(2)}, u32[]{:S(2)}) collective-permute-start(bf16[128,512]{1,0:T(8,128)(2,1)S(1)} %pad_maximum_fusion.7), channel_id=1, source_target_pairs={{0,4},{4,8},{8,12},{12,16},{16,20},{20,24},{24,28},{1,5},{5,9},{9,... | collective-permute-start | bytes 393224 | tf_op jit(solution)/shard_map/ppermute | solution.py:27
  6.5 15.1 %collective-permute-start.1 = (bf16[128,512]{1,0:T(8,128)(2,1)S(1)}, bf16[128,512]{1,0:T(8,128)(2,1)S(1)}, u32[]{:S(2)}, u32[]{:S(2)}) collective-permute-start(bf16[128,512]{1,0:T(8,128)(2,1)S(1)} %pad_maximum_fusion.8), channel_id=1, source_target_pairs={{4,0},{8,4},{12,8},{16,12},{20,16},{24,20},{28,24},{5,1},{9,5},{13... | collective-permute-start | bytes 393224 | tf_op jit(solution)/shard_map/ppermute | solution.py:28
  7.8 3.1 %copy-start = (bf16[7,64,8192]{2,1,0:T(8,128)(2,1)S(1)}, bf16[7,64,8192]{2,1,0:T(8,128)(2,1)}, u32[]{:S(2)}) copy-start(bf16[7,64,8192]{2,1,0:T(8,128)(2,1)} %factor_ref.3) | copy-start | bytes 22020100
  10.9 1.2 %copy-start.1 = (bf16[64,8192]{1,0:T(8,128)(2,1)S(1)}, bf16[64,8192]{1,0:T(8,128)(2,1)}, u32[]{:S(2)}) copy-start(bf16[64,8192]{1,0:T(8,128)(2,1)} %prior_ref.3) | copy-start | bytes 3145732
  12.2 1.2 %copy-start.3 = (bf16[64,8192]{1,0:T(8,128)(2,1)S(1)}, bf16[64,8192]{1,0:T(8,128)(2,1)}, u32[]{:S(2)}) copy-start(bf16[64,8192]{1,0:T(8,128)(2,1)} %snap_ref.3) | copy-start | bytes 3145732
  13.4 0.7 copy-start.5
  25.4 4.8 %collective-permute-start.2 = (f32[96,128]{1,0:T(8,128)S(1)}, f32[96,128]{1,0:T(8,128)S(1)}, u32[]{:S(2)}, u32[]{:S(2)}) collective-permute-start(f32[96,128]{1,0:T(8,128)S(1)} %get-tuple-element.20), channel_id=1, source_target_pairs={{0,4},{1,5},{2,6},{3,7},{4,0},{5,1},{6,2},{7,3},{8,12},{9,13},{10,... | collective-permute-start | bytes 147464 | tf_op jit(solution)/shard_map/ppermute | solution.py:35
  30.2 5.1 %collective-permute-start.3 = (f32[96,128]{1,0:T(8,128)S(1)}, f32[96,128]{1,0:T(8,128)S(1)}, u32[]{:S(2)}, u32[]{:S(2)}) collective-permute-start(f32[96,128]{1,0:T(8,128)S(1)} %add.94), channel_id=1, source_target_pairs={{0,8},{1,9},{2,10},{3,11},{4,12},{5,13},{6,14},{7,15},{8,0},{9,1},... | collective-permute-start | bytes 147464 | tf_op jit(solution)/shard_map/ppermute | solution.py:35
  35.3 5.6 %collective-permute-start.4 = (f32[96,128]{1,0:T(8,128)S(1)}, f32[96,128]{1,0:T(8,128)S(1)}, u32[]{:S(2)}, u32[]{:S(2)}) collective-permute-start(f32[96,128]{1,0:T(8,128)S(1)} %add.95), channel_id=1, source_target_pairs={{0,16},{1,17},{2,18},{3,19},{4,20},{5,21},{6,22},{7,23},{8,24},{9,... | collective-permute-start | bytes 147464 | tf_op jit(solution)/shard_map/ppermute | solution.py:35
  49.6 2.0 %collective-permute-start.5 = (bf16[64,4096]{1,0:T(8,128)(2,1)S(1)}, bf16[64,4096]{1,0:T(8,128)(2,1)S(1)}, u32[]{:S(2)}, u32[]{:S(2)}) collective-permute-start(bf16[64,4096]{1,0:T(8,128)(2,1)S(1)} %pad_maximum_fusion.1), channel_id=1, source_target_pairs={{0,1},{1,0},{2,3},{3,2},{4,5},{5,4},{6,7},{7,6},{8,9},{9,8},{10,11... | collective-permute-start | bytes 1572872 | tf_op jit(solution)/shard_map/ppermute | solution.py:35
  52.3 10.7 %copy-start.2 = (bf16[64,8192]{1,0:T(8,128)(2,1)S(1)}, bf16[64,8192]{1,0:T(8,128)(2,1)}, u32[]{:S(2)}) copy-start(bf16[64,8192]{1,0:T(8,128)(2,1)} %prior_ref.3) | copy-start | bytes 3145732
  52.3 4.2 %collective-permute-start.7 = (f32[64,128]{1,0:T(8,128)S(1)}, f32[64,128]{1,0:T(8,128)S(1)}, u32[]{:S(2)}, u32[]{:S(2)}) collective-permute-start(f32[64,128]{1,0:T(8,128)S(1)} %fusion.11), channel_id=1, source_target_pairs={{0,4},{1,5},{2,6},{3,7},{4,0},{5,1},{6,2},{7,3},{8,12},{9,13},{10,... | collective-permute-start | bytes 98312 | tf_op jit(solution)/shard_map/ppermute | solution.py:35
  53.0 3.7 %collective-permute-start.8 = (f32[64,128]{1,0:T(8,128)S(1)}, f32[64,128]{1,0:T(8,128)S(1)}, u32[]{:S(2)}, u32[]{:S(2)}) collective-permute-start(f32[64,128]{1,0:T(8,128)S(1)} %fusion.11), channel_id=1, source_target_pairs={{0,5},{1,4},{2,7},{3,6},{4,1},{5,0},{6,3},{7,2},{8,13},{9,12},{10,... | collective-permute-start | bytes 98312 | tf_op jit(solution)/shard_map/ppermute | solution.py:35
  53.9 2.9 %collective-permute-start.6 = (f32[64,128]{1,0:T(8,128)S(1)}, f32[64,128]{1,0:T(8,128)S(1)}, u32[]{:S(2)}, u32[]{:S(2)}) collective-permute-start(f32[64,128]{1,0:T(8,128)S(1)} %fusion.11), channel_id=1, source_target_pairs={{0,1},{1,0},{2,3},{3,2},{4,5},{5,4},{6,7},{7,6},{8,9},{9,8},{10,11... | collective-permute-start | bytes 98312 | tf_op jit(solution)/shard_map/ppermute | solution.py:35
  56.8 6.7 %copy-start.4 = (bf16[64,8192]{1,0:T(8,128)(2,1)S(1)}, bf16[64,8192]{1,0:T(8,128)(2,1)}, u32[]{:S(2)}) copy-start(bf16[64,8192]{1,0:T(8,128)(2,1)} %snap_ref.3) | copy-start | bytes 3145732
  56.8 7.6 %collective-permute-start.10 = (f32[64,128]{1,0:T(8,128)S(1)}, f32[64,128]{1,0:T(8,128)S(1)}, u32[]{:S(2)}, u32[]{:S(2)}) collective-permute-start(f32[64,128]{1,0:T(8,128)S(1)} %add_add_fusion.3), channel_id=1, source_target_pairs={{0,16},{1,17},{2,18},{3,19},{4,20},{5,21},{6,22},{7,23},{8,24},{9,... | collective-permute-start | bytes 98312 | tf_op jit(solution)/shard_map/ppermute | solution.py:35
  59.9 5.7 %collective-permute-start.11 = (f32[64,128]{1,0:T(8,128)S(1)}, f32[64,128]{1,0:T(8,128)S(1)}, u32[]{:S(2)}, u32[]{:S(2)}) collective-permute-start(f32[64,128]{1,0:T(8,128)S(1)} %add_add_fusion.3), channel_id=1, source_target_pairs={{0,24},{1,25},{2,26},{3,27},{4,28},{5,29},{6,30},{7,31},{8,16},{9,... | collective-permute-start | bytes 98312 | tf_op jit(solution)/shard_map/ppermute | solution.py:35
  60.9 4.7 %collective-permute-start.9 = (f32[64,128]{1,0:T(8,128)S(1)}, f32[64,128]{1,0:T(8,128)S(1)}, u32[]{:S(2)}, u32[]{:S(2)}) collective-permute-start(f32[64,128]{1,0:T(8,128)S(1)} %add_add_fusion.3), channel_id=1, source_target_pairs={{0,8},{1,9},{2,10},{3,11},{4,12},{5,13},{6,14},{7,15},{8,0},{9,1},... | collective-permute-start | bytes 98312 | tf_op jit(solution)/shard_map/ppermute | solution.py:35
  61.4 2.7 %collective-permute-start.12 = (f32[64,64]{1,0:T(8,128)S(1)}, f32[64,64]{1,0:T(8,128)S(1)}, u32[]{:S(2)}, u32[]{:S(2)}) collective-permute-start(f32[64,64]{1,0:T(8,128)S(1)} %get-tuple-element.25), channel_id=1, source_target_pairs={{0,1},{1,0},{2,3},{3,2},{4,5},{5,4},{6,7},{7,6},{8,9},{9,8},{10,11... | collective-permute-start | bytes 49160 | tf_op jit(solution)/shard_map/ppermute | solution.py:35
  61.4 16.2 %collective-permute-start.14 = (bf16[128,2048]{1,0:T(8,128)(2,1)S(1)}, bf16[128,2048]{1,0:T(8,128)(2,1)S(1)}, u32[]{:S(2)}, u32[]{:S(2)}) collective-permute-start(bf16[128,2048]{1,0:T(8,128)(2,1)S(1)} %constant_dynamic-slice_fusion.5), channel_id=1, source_target_pairs={{0,2},{1,3},{2,0},{3,1},{4,6},{5,7},{6,4},{7,5},{8,10},{9,11},{10,... | collective-permute-start | bytes 1572872 | tf_op jit(solution)/shard_map/ppermute | solution.py:35
  64.0 16.4 %collective-permute-start.23 = (bf16[64,4096]{1,0:T(8,128)(2,1)S(1)}, bf16[64,4096]{1,0:T(8,128)(2,1)S(1)}, u32[]{:S(2)}, u32[]{:S(2)}) collective-permute-start(bf16[64,4096]{1,0:T(8,128)(2,1)S(1)} %pad_maximum_fusion.4), channel_id=1, source_target_pairs={{0,1},{1,0},{2,3},{3,2},{4,5},{5,4},{6,7},{7,6},{8,9},{9,8},{10,11... | collective-permute-start | bytes 1572872 | tf_op jit(solution)/shard_map/ppermute | solution.py:35
  73.9 3.8 %collective-permute-start.13 = (bf16[64,128]{1,0:T(8,128)(2,1)S(1)}, bf16[64,128]{1,0:T(8,128)(2,1)S(1)}, u32[]{:S(2)}, u32[]{:S(2)}) collective-permute-start(bf16[64,128]{1,0:T(8,128)(2,1)S(1)} %get-tuple-element.31), channel_id=1, source_target_pairs={{0,2},{1,3},{2,0},{3,1},{4,6},{5,7},{6,4},{7,5},{8,10},{9,11},{10,... | collective-permute-start | bytes 49160 | tf_op jit(solution)/shard_map/ppermute | solution.py:35
  78.2 4.0 %collective-permute-start.16 = (f32[64,128]{1,0:T(8,128)S(1)}, f32[64,128]{1,0:T(8,128)S(1)}, u32[]{:S(2)}, u32[]{:S(2)}) collective-permute-start(f32[64,128]{1,0:T(8,128)S(1)} %fusion.10), channel_id=1, source_target_pairs={{0,2},{1,3},{2,0},{3,1},{4,6},{5,7},{6,4},{7,5},{8,10},{9,11},{10,... | collective-permute-start | bytes 98312 | tf_op jit(solution)/shard_map/ppermute | solution.py:35
  79.8 3.3 %collective-permute-start.17 = (f32[64,128]{1,0:T(8,128)S(1)}, f32[64,128]{1,0:T(8,128)S(1)}, u32[]{:S(2)}, u32[]{:S(2)}) collective-permute-start(f32[64,128]{1,0:T(8,128)S(1)} %fusion.10), channel_id=1, source_target_pairs={{0,3},{1,2},{2,1},{3,0},{4,7},{5,6},{6,5},{7,4},{8,11},{9,10},{10,... | collective-permute-start | bytes 98312 | tf_op jit(solution)/shard_map/ppermute | solution.py:35
  79.8 3.3 %collective-permute-start.15 = (f32[64,128]{1,0:T(8,128)S(1)}, f32[64,128]{1,0:T(8,128)S(1)}, u32[]{:S(2)}, u32[]{:S(2)}) collective-permute-start(f32[64,128]{1,0:T(8,128)S(1)} %fusion.10), channel_id=1, source_target_pairs={{0,1},{1,0},{2,3},{3,2},{4,5},{5,4},{6,7},{7,6},{8,9},{9,8},{10,11... | collective-permute-start | bytes 98312 | tf_op jit(solution)/shard_map/ppermute | solution.py:35
  83.1 6.0 %collective-permute-start.19 = (f32[64,128]{1,0:T(8,128)S(1)}, f32[64,128]{1,0:T(8,128)S(1)}, u32[]{:S(2)}, u32[]{:S(2)}) collective-permute-start(f32[64,128]{1,0:T(8,128)S(1)} %add_add_fusion.1), channel_id=1, source_target_pairs={{0,8},{1,9},{2,10},{3,11},{4,12},{5,13},{6,14},{7,15},{8,0},{9,1},... | collective-permute-start | bytes 98312 | tf_op jit(solution)/shard_map/ppermute | solution.py:35
  83.3 5.8 %collective-permute-start.20 = (f32[64,128]{1,0:T(8,128)S(1)}, f32[64,128]{1,0:T(8,128)S(1)}, u32[]{:S(2)}, u32[]{:S(2)}) collective-permute-start(f32[64,128]{1,0:T(8,128)S(1)} %add_add_fusion.1), channel_id=1, source_target_pairs={{0,12},{1,13},{2,14},{3,15},{4,8},{5,9},{6,10},{7,11},{8,4},{9,5},... | collective-permute-start | bytes 98312 | tf_op jit(solution)/shard_map/ppermute | solution.py:35
  86.0 3.9 %collective-permute-start.18 = (f32[64,128]{1,0:T(8,128)S(1)}, f32[64,128]{1,0:T(8,128)S(1)}, u32[]{:S(2)}, u32[]{:S(2)}) collective-permute-start(f32[64,128]{1,0:T(8,128)S(1)} %add_add_fusion.1), channel_id=1, source_target_pairs={{0,4},{1,5},{2,6},{3,7},{4,0},{5,1},{6,2},{7,3},{8,12},{9,13},{10,... | collective-permute-start | bytes 98312 | tf_op jit(solution)/shard_map/ppermute | solution.py:35
  86.7 4.8 %collective-permute-start.22 = (f32[64,64]{1,0:T(8,128)S(1)}, f32[64,64]{1,0:T(8,128)S(1)}, u32[]{:S(2)}, u32[]{:S(2)}) collective-permute-start(f32[64,64]{1,0:T(8,128)S(1)} %get-tuple-element.30), channel_id=1, source_target_pairs={{0,2},{1,3},{2,0},{3,1},{4,6},{5,7},{6,4},{7,5},{8,10},{9,11},{10,... | collective-permute-start | bytes 49160 | tf_op jit(solution)/shard_map/ppermute | solution.py:35
  87.9 7.7 %collective-permute-start.24 = (bf16[64,2048]{1,0:T(8,128)(2,1)S(1)}, bf16[64,2048]{1,0:T(8,128)(2,1)S(1)}, u32[]{:S(2)}, u32[]{:S(2)}) collective-permute-start(bf16[64,2048]{1,0:T(8,128)(2,1)S(1)} %constant_dynamic-slice_fusion), channel_id=1, source_target_pairs={{0,2},{1,3},{2,0},{3,1},{4,6},{5,7},{6,4},{7,5},{8,10},{9,11},{10,... | collective-permute-start | bytes 786440 | tf_op jit(solution)/shard_map/ppermute | solution.py:35
  89.9 5.2 %collective-permute-start.21 = (f32[64,128]{1,0:T(8,128)S(1)}, f32[64,128]{1,0:T(8,128)S(1)}, u32[]{:S(2)}, u32[]{:S(2)}) collective-permute-start(f32[64,128]{1,0:T(8,128)S(1)} %add_add_fusion), channel_id=1, source_target_pairs={{0,16},{1,17},{2,18},{3,19},{4,20},{5,21},{6,22},{7,23},{8,24},{9,... | collective-permute-start | bytes 98312 | tf_op jit(solution)/shard_map/ppermute | solution.py:35

commit v10 on v8

--- a/solution.py
+++ b/solution.py
@@ -356,7 +356,7 @@
     width = snapshots.shape[1] // members
     partner_weighted = None
     reduced = (jax.ShapeDtypeStruct((RANK, 2 * RANK), BF16), jax.ShapeDtypeStruct((RANK, RANK), F32))
-    coefficients, own = compress(first_kernel, reduced, total(gram, across, 1))
+    coefficients, own = compress(first_kernel, reduced, total(gram, across, 2))
     for level in range(members.bit_length() - 1):
         step = 1 << level
         bit = member // step % 2

time: 105 us -> 104 us (level)
  starting transfers between devices: 34.7 us -> 32.8 us
    ppermute x23 -> x24, starting transfers between devices: 28.5 us -> 26.6 us  [swapped(): return lax.ppermute(block, axes, [(i, i ^ mask) for i in range(count)])]
    ppermute x23 -> x24, waiting for transfers between devices: 21.7 us -> 21.9 us  [swapped(): return lax.ppermute(block, axes, [(i, i ^ mask) for i in range(count)])]
  transfers between devices with their start and end apart: 25 -> 26, of which waited for: 13 -> 14; matrix products, arithmetic and copies ran while one was open for 2% -> 2% of each run, Pallas kernels for 15% -> 15%
where the time goes in v10:
time: 104 us; the launch traced here: 103 us
  Pallas kernels  36.6 us (35%)
  starting transfers between devices  32.8 us (32%)
  waiting for transfers between devices  22 us (21%)
  local copies, waits for them, and re-layouts  7.44 us (7%)
  matrix products  2.86 us (3%)
    ppermute x24, starting transfers between devices, swapped(): return lax.ppermute(block, axes, [(i, i ^ mask) for i in range(count)])  26.6 us
    pallas_call x3, Pallas kernels, compress(): pl.pallas_call(kernel, out_shape=outs, scratch_shapes=[pltpu.VMEM((RANK /...  25.3 us
    ppermute x24, waiting for transfers between devices, swapped(): return lax.ppermute(block, axes, [(i, i ^ mask) for i in range(count)])  21.9 us
    pallas_call x1, Pallas kernels, weigh(): pl.pallas_call(functools.partial(inside_kernel, edge), out_shape=shapes,...  7.52 us
    unnamed x12, local copies, waits for them, and re-layouts  6.25 us
    ppermute x1, starting transfers between devices, halo(): low = lax.ppermute(last, axis, forward)  4.88 us
    pallas_call x1, Pallas kernels, weigh(): pl.pallas_call(functools.partial(border_kernel, width), out_shape=(shapes...  3.76 us
  transfers between devices with their start and end apart: 26, of which 14 were waited for; matrix products, arithmetic and copies ran while one was open for 2% of the time, Pallas kernels for 15%

profile of v10, /device:TPU:0, one launch (start us, length us, event | category | flops | bytes accessed | tf_op | source)
XLA Modules:
  0.0 103.4 jit_solution(5450613913734003888)
XLA Ops:
  1.6 4.9 %collective-permute-start = (bf16[128,512]{1,0:T(8,128)(2,1)S(1)}, bf16[128,512]{1,0:T(8,128)(2,1)S(1)}, u32[]{:S(2)}, u32[]{:S(2)}) collective-permute-start(bf16[128,512]{1,0:T(8,128)(2,1)S(1)} %pad_maximum_fusion.8), channel_id=1, source_target_pairs={{0,4},{4,8},{8,12},{12,16},{16,20},{20,24},{24,28},{1,5},{5,9},{9,... | collective-permute-start | bytes 393224 | tf_op jit(solution)/shard_map/ppermute | solution.py:27
  6.5 1.3 %collective-permute-start.1 = (bf16[128,512]{1,0:T(8,128)(2,1)S(1)}, bf16[128,512]{1,0:T(8,128)(2,1)S(1)}, u32[]{:S(2)}, u32[]{:S(2)}) collective-permute-start(bf16[128,512]{1,0:T(8,128)(2,1)S(1)} %pad_maximum_fusion.9), channel_id=1, source_target_pairs={{4,0},{8,4},{12,8},{16,12},{20,16},{24,20},{28,24},{5,1},{9,5},{13... | collective-permute-start | bytes 393224 | tf_op jit(solution)/shard_map/ppermute | solution.py:28
  7.8 3.1 %copy-done = bf16[7,64,8192]{2,1,0:T(8,128)(2,1)S(1)} copy-done((bf16[7,64,8192]{2,1,0:T(8,128)(2,1)S(1)}, bf16[7,64,8192]{2,1,0:T(8,128)(2,1)}, u32[]{:S(2)}) %copy-start) | copy-done | bytes 7340056
  10.9 1.2 %copy-done.1 = bf16[64,8192]{1,0:T(8,128)(2,1)S(1)} copy-done((bf16[64,8192]{1,0:T(8,128)(2,1)S(1)}, bf16[64,8192]{1,0:T(8,128)(2,1)}, u32[]{:S(2)}) %copy-start.1) | copy-done | bytes 1048600
  12.2 1.2 %copy-done.3 = bf16[64,8192]{1,0:T(8,128)(2,1)S(1)} copy-done((bf16[64,8192]{1,0:T(8,128)(2,1)S(1)}, bf16[64,8192]{1,0:T(8,128)(2,1)}, u32[]{:S(2)}) %copy-start.3) | copy-done | bytes 1048600
  14.1 7.5 %weigh_inside.1 = (bf16[128,8192]{1,0:T(8,128)(2,1)S(1)}, f32[128,128]{1,0:T(8,128)S(1)}) custom-call(s32[7,128]{1,0:T(8,128)S(1)} %bitcast.11, bf16[64,8192]{1,0:T(8,128)(2,1)S(1)} %copy-done.1, bf16[64,8192]{1,0:T(8,128)(2,1)S(1)} %copy-done.3, bf16[7,64,8192]{2,1,0:T(8,128)(2,1)S(1)} %copy-done), custom_call_target="tpu_custom_call" | custom-call | flops 3758096384 | bytes 7340032 | tf_op jit(solution)/shard_map/weigh_inside/pallas_call | solution.py:173
  21.6 3.8 %weigh_border.1 = (bf16[128,8192]{1,0:T(8,128)(2,1)S(1)}, f32[96,128]{1,0:T(8,128)S(1)}) custom-call(s32[7,128]{1,0:T(8,128)S(1)} %bitcast.12, bf16[64,8192]{1,0:T(8,128)(2,1)S(1)} %copy-done.1, bf16[64,8192]{1,0:T(8,128)(2,1)S(1)} %copy-done.3, bf16[128,512]{1,0:T(8,128)(2,1)S(1)} %collective-permute-done.low_ref, ...), custom_call_target="tpu_custom_call", output_to_operand_aliasing={{0}: (7, {})} | custom-call | tf_op jit(solution)/shard_map/weigh_border/pallas_call | solution.py:197
  25.4 3.7 %collective-permute-start.3 = (f32[96,128]{1,0:T(8,128)S(1)}, f32[96,128]{1,0:T(8,128)S(1)}, u32[]{:S(2)}, u32[]{:S(2)}) collective-permute-start(f32[96,128]{1,0:T(8,128)S(1)} %get-tuple-element.18), channel_id=1, source_target_pairs={{0,8},{1,9},{2,10},{3,11},{4,12},{5,13},{6,14},{7,15},{8,0},{9,1},... | collective-permute-start | bytes 147464 | tf_op jit(solution)/shard_map/ppermute | solution.py:35
  29.6 1.0 collective-permute-start.2
  30.6 1.0 collective-permute-done.3
  31.6 2.6 %collective-permute-done.4 = f32[96,128]{1,0:T(8,128)S(1)} collective-permute-done((f32[96,128]{1,0:T(8,128)S(1)}, f32[96,128]{1,0:T(8,128)S(1)}, u32[]{:S(2)}, u32[]{:S(2)}) %collective-permute-start.4) | collective-permute-done | bytes 49184 | tf_op jit(solution)/shard_map/ppermute | solution.py:35
  34.2 2.6 %collective-permute-start.5 = (f32[96,128]{1,0:T(8,128)S(1)}, f32[96,128]{1,0:T(8,128)S(1)}, u32[]{:S(2)}, u32[]{:S(2)}) collective-permute-start(f32[96,128]{1,0:T(8,128)S(1)} %add_add_fusion), channel_id=1, source_target_pairs={{0,16},{1,17},{2,18},{3,19},{4,20},{5,21},{6,22},{7,23},{8,24},{9,... | collective-permute-start | bytes 147464 | tf_op jit(solution)/shard_map/ppermute | solution.py:35
  36.8 3.0 %collective-permute-done.5 = f32[96,128]{1,0:T(8,128)S(1)} collective-permute-done((f32[96,128]{1,0:T(8,128)S(1)}, f32[96,128]{1,0:T(8,128)S(1)}, u32[]{:S(2)}, u32[]{:S(2)}) %collective-permute-start.5) | collective-permute-done | bytes 49184 | tf_op jit(solution)/shard_map/ppermute | solution.py:35
  39.8 8.2 %compress.3 = (bf16[64,128]{1,0:T(8,128)(2,1)S(1)}, f32[64,64]{1,0:T(8,128)S(1)}) custom-call(f32[96,128]{1,0:T(8,128)S(1)} %add.100.blocks_ref), custom_call_target="tpu_custom_call" | custom-call | tf_op jit(solution)/shard_map/compress/pallas_call | solution.py:315
  48.7 1.8 %collective-permute-done.6 = bf16[64,4096]{1,0:T(8,128)(2,1)S(1)} collective-permute-done((bf16[64,4096]{1,0:T(8,128)(2,1)S(1)}, bf16[64,4096]{1,0:T(8,128)(2,1)S(1)}, u32[]{:S(2)}, u32[]{:S(2)}) %collective-permute-start.6) | collective-permute-done | bytes 524320 | tf_op jit(solution)/shard_map/ppermute | solution.py:35
  51.8 1.1 %collective-permute-start.9 = (f32[64,128]{1,0:T(8,128)S(1)}, f32[64,128]{1,0:T(8,128)S(1)}, u32[]{:S(2)}, u32[]{:S(2)}) collective-permute-start(f32[64,128]{1,0:T(8,128)S(1)} %fusion.1), channel_id=1, source_target_pairs={{0,5},{1,4},{2,7},{3,6},{4,1},{5,0},{6,3},{7,2},{8,13},{9,12},{10,... | collective-permute-start | bytes 98312 | tf_op jit(solution)/shard_map/ppermute | solution.py:35
  53.5 1.0 collective-permute-start.15
  55.5 2.8 %collective-permute-start.11 = (f32[64,128]{1,0:T(8,128)S(1)}, f32[64,128]{1,0:T(8,128)S(1)}, u32[]{:S(2)}, u32[]{:S(2)}) collective-permute-start(f32[64,128]{1,0:T(8,128)S(1)} %add_add_fusion.4), channel_id=1, source_target_pairs={{0,16},{1,17},{2,18},{3,19},{4,20},{5,21},{6,22},{7,23},{8,24},{9,... | collective-permute-start | bytes 98312 | tf_op jit(solution)/shard_map/ppermute | solution.py:35
  58.2 1.4 %collective-permute-start.12 = (f32[64,128]{1,0:T(8,128)S(1)}, f32[64,128]{1,0:T(8,128)S(1)}, u32[]{:S(2)}, u32[]{:S(2)}) collective-permute-start(f32[64,128]{1,0:T(8,128)S(1)} %add_add_fusion.4), channel_id=1, source_target_pairs={{0,24},{1,25},{2,26},{3,27},{4,28},{5,29},{6,30},{7,31},{8,16},{9,... | collective-permute-start | bytes 98312 | tf_op jit(solution)/shard_map/ppermute | solution.py:35
  61.3 2.6 %collective-permute-done.12 = f32[64,128]{1,0:T(8,128)S(1)} collective-permute-done((f32[64,128]{1,0:T(8,128)S(1)}, f32[64,128]{1,0:T(8,128)S(1)}, u32[]{:S(2)}, u32[]{:S(2)}) %collective-permute-start.12) | collective-permute-done | bytes 32800 | tf_op jit(solution)/shard_map/ppermute | solution.py:35
  64.0 8.3 %compress.4 = (bf16[64,128]{1,0:T(8,128)(2,1)S(1)}, f32[64,64]{1,0:T(8,128)S(1)}) custom-call(f32[64,128]{1,0:T(8,128)S(1)} %add_add_fusion.3.top_ref, f32[64,64]{1,0:T(8,128)S(1)} %broadcast_select_fusion.9.upper_ref), custom_call_target="tpu_custom_call" | custom-call | tf_op jit(solution)/shard_map/compress/pallas_call | solution.py:315
  72.3 1.5 %collective-permute-start.14 = (bf16[64,128]{1,0:T(8,128)(2,1)S(1)}, bf16[64,128]{1,0:T(8,128)(2,1)S(1)}, u32[]{:S(2)}, u32[]{:S(2)}) collective-permute-start(bf16[64,128]{1,0:T(8,128)(2,1)S(1)} %get-tuple-element.28), channel_id=1, source_target_pairs={{0,2},{1,3},{2,0},{3,1},{4,6},{5,7},{6,4},{7,5},{8,10},{9,11},{10,... | collective-permute-start | bytes 49160 | tf_op jit(solution)/shard_map/ppermute | solution.py:35
  73.9 2.1 %collective-permute-done.14 = bf16[64,128]{1,0:T(8,128)(2,1)S(1)} collective-permute-done((bf16[64,128]{1,0:T(8,128)(2,1)S(1)}, bf16[64,128]{1,0:T(8,128)(2,1)S(1)}, u32[]{:S(2)}, u32[]{:S(2)}) %collective-permute-start.14) | collective-permute-done | bytes 16416 | tf_op jit(solution)/shard_map/ppermute | solution.py:35
  76.8 1.5 %collective-permute-start.17 = (f32[64,128]{1,0:T(8,128)S(1)}, f32[64,128]{1,0:T(8,128)S(1)}, u32[]{:S(2)}, u32[]{:S(2)}) collective-permute-start(f32[64,128]{1,0:T(8,128)S(1)} %fusion.15), channel_id=1, source_target_pairs={{0,2},{1,3},{2,0},{3,1},{4,6},{5,7},{6,4},{7,5},{8,10},{9,11},{10,... | collective-permute-start | bytes 98312 | tf_op jit(solution)/shard_map/ppermute | solution.py:35
  79.1 1.7 %collective-permute-done.17 = f32[64,128]{1,0:T(8,128)S(1)} collective-permute-done((f32[64,128]{1,0:T(8,128)S(1)}, f32[64,128]{1,0:T(8,128)S(1)}, u32[]{:S(2)}, u32[]{:S(2)}) %collective-permute-start.17) | collective-permute-done | bytes 32800 | tf_op jit(solution)/shard_map/ppermute | solution.py:35
  81.9 2.4 %collective-permute-start.21 = (f32[64,128]{1,0:T(8,128)S(1)}, f32[64,128]{1,0:T(8,128)S(1)}, u32[]{:S(2)}, u32[]{:S(2)}) collective-permute-start(f32[64,128]{1,0:T(8,128)S(1)} %add_add_fusion.2), channel_id=1, source_target_pairs={{0,12},{1,13},{2,14},{3,15},{4,8},{5,9},{6,10},{7,11},{8,4},{9,5},... | collective-permute-start | bytes 98312 | tf_op jit(solution)/shard_map/ppermute | solution.py:35
  84.3 1.0 collective-permute-start.19
  86.7 1.2 %collective-permute-start.25 = (bf16[64,2048]{1,0:T(8,128)(2,1)S(1)}, bf16[64,2048]{1,0:T(8,128)(2,1)S(1)}, u32[]{:S(2)}, u32[]{:S(2)}) collective-permute-start(bf16[64,2048]{1,0:T(8,128)(2,1)S(1)} %constant_dynamic-slice_fusion), channel_id=1, source_target_pairs={{0,2},{1,3},{2,0},{3,1},{4,6},{5,7},{6,4},{7,5},{8,10},{9,11},{10,... | collective-permute-start | bytes 786440 | tf_op jit(solution)/shard_map/ppermute | solution.py:35
  88.2 1.4 %collective-permute-start.22 = (f32[64,128]{1,0:T(8,128)S(1)}, f32[64,128]{1,0:T(8,128)S(1)}, u32[]{:S(2)}, u32[]{:S(2)}) collective-permute-start(f32[64,128]{1,0:T(8,128)S(1)} %add_add_fusion.1), channel_id=1, source_target_pairs={{0,16},{1,17},{2,18},{3,19},{4,20},{5,21},{6,22},{7,23},{8,24},{9,... | collective-permute-start | bytes 98312 | tf_op jit(solution)/shard_map/ppermute | solution.py:35
  89.6 3.7 %collective-permute-done.22 = f32[64,128]{1,0:T(8,128)S(1)} collective-permute-done((f32[64,128]{1,0:T(8,128)S(1)}, f32[64,128]{1,0:T(8,128)S(1)}, u32[]{:S(2)}, u32[]{:S(2)}) %collective-permute-start.22) | collective-permute-done | bytes 32800 | tf_op jit(solution)/shard_map/ppermute | solution.py:35
  93.3 1.1 %collective-permute-done.25 = bf16[64,2048]{1,0:T(8,128)(2,1)S(1)} collective-permute-done((bf16[64,2048]{1,0:T(8,128)(2,1)S(1)}, bf16[64,2048]{1,0:T(8,128)(2,1)S(1)}, u32[]{:S(2)}, u32[]{:S(2)}) %collective-permute-start.25) | collective-permute-done | bytes 262176 | tf_op jit(solution)/shard_map/ppermute | solution.py:35
  94.6 8.8 %compress.5 = (bf16[64,2048]{1,0:T(8,128)(2,1)}, bf16[64,2048]{1,0:T(8,128)(2,1)}) custom-call(f32[64,128]{1,0:T(8,128)S(1)} %add.123.top_ref, f32[64,64]{1,0:T(8,128)S(1)} %broadcast_select_fusion.8.upper_ref, bf16[128,2048]{1,0:T(8,128)(2,1)S(1)} %pad_maximum_fusion.7.stacked_ref, bf16[128,2048]{1,0:T(8,128)(2,1)S(1)} %pad_maximum_fusion.4.weighted_ref), custom_call_target="tpu_custom_call" | custom-call | tf_op jit(solution)/shard_map/compress/pallas_call | solution.py:315
  (68 shorter events, 11.9 us)
Async XLA Ops:
  1.6 20.0 %collective-permute-start = (bf16[128,512]{1,0:T(8,128)(2,1)S(1)}, bf16[128,512]{1,0:T(8,128)(2,1)S(1)}, u32[]{:S(2)}, u32[]{:S(2)}) collective-permute-start(bf16[128,512]{1,0:T(8,128)(2,1)S(1)} %pad_maximum_fusion.8), channel_id=1, source_target_pairs={{0,4},{4,8},{8,12},{12,16},{16,20},{20,24},{24,28},{1,5},{5,9},{9,... | collective-permute-start | bytes 393224 | tf_op jit(solution)/shard_map/ppermute | solution.py:27
  6.5 15.1 %collective-permute-start.1 = (bf16[128,512]{1,0:T(8,128)(2,1)S(1)}, bf16[128,512]{1,0:T(8,128)(2,1)S(1)}, u32[]{:S(2)}, u32[]{:S(2)}) collective-permute-start(bf16[128,512]{1,0:T(8,128)(2,1)S(1)} %pad_maximum_fusion.9), channel_id=1, source_target_pairs={{4,0},{8,4},{12,8},{16,12},{20,16},{24,20},{28,24},{5,1},{9,5},{13... | collective-permute-start | bytes 393224 | tf_op jit(solution)/shard_map/ppermute | solution.py:28
  7.8 3.1 %copy-start = (bf16[7,64,8192]{2,1,0:T(8,128)(2,1)S(1)}, bf16[7,64,8192]{2,1,0:T(8,128)(2,1)}, u32[]{:S(2)}) copy-start(bf16[7,64,8192]{2,1,0:T(8,128)(2,1)} %factor_ref.3) | copy-start | bytes 22020100
  10.9 1.2 %copy-start.1 = (bf16[64,8192]{1,0:T(8,128)(2,1)S(1)}, bf16[64,8192]{1,0:T(8,128)(2,1)}, u32[]{:S(2)}) copy-start(bf16[64,8192]{1,0:T(8,128)(2,1)} %prior_ref.3) | copy-start | bytes 3145732
  12.2 1.2 %copy-start.3 = (bf16[64,8192]{1,0:T(8,128)(2,1)S(1)}, bf16[64,8192]{1,0:T(8,128)(2,1)}, u32[]{:S(2)}) copy-start(bf16[64,8192]{1,0:T(8,128)(2,1)} %snap_ref.3) | copy-start | bytes 3145732
  13.4 0.7 copy-start.5
  25.4 6.2 %collective-permute-start.3 = (f32[96,128]{1,0:T(8,128)S(1)}, f32[96,128]{1,0:T(8,128)S(1)}, u32[]{:S(2)}, u32[]{:S(2)}) collective-permute-start(f32[96,128]{1,0:T(8,128)S(1)} %get-tuple-element.18), channel_id=1, source_target_pairs={{0,8},{1,9},{2,10},{3,11},{4,12},{5,13},{6,14},{7,15},{8,0},{9,1},... | collective-permute-start | bytes 147464 | tf_op jit(solution)/shard_map/ppermute | solution.py:35
  29.0 5.1 %collective-permute-start.4 = (f32[96,128]{1,0:T(8,128)S(1)}, f32[96,128]{1,0:T(8,128)S(1)}, u32[]{:S(2)}, u32[]{:S(2)}) collective-permute-start(f32[96,128]{1,0:T(8,128)S(1)} %get-tuple-element.18), channel_id=1, source_target_pairs={{0,12},{1,13},{2,14},{3,15},{4,8},{5,9},{6,10},{7,11},{8,4},{9,5},... | collective-permute-start | bytes 147464 | tf_op jit(solution)/shard_map/ppermute | solution.py:35
  29.6 4.6 %collective-permute-start.2 = (f32[96,128]{1,0:T(8,128)S(1)}, f32[96,128]{1,0:T(8,128)S(1)}, u32[]{:S(2)}, u32[]{:S(2)}) collective-permute-start(f32[96,128]{1,0:T(8,128)S(1)} %get-tuple-element.18), channel_id=1, source_target_pairs={{0,4},{1,5},{2,6},{3,7},{4,0},{5,1},{6,2},{7,3},{8,12},{9,13},{10,... | collective-permute-start | bytes 147464 | tf_op jit(solution)/shard_map/ppermute | solution.py:35
  34.2 5.6 %collective-permute-start.5 = (f32[96,128]{1,0:T(8,128)S(1)}, f32[96,128]{1,0:T(8,128)S(1)}, u32[]{:S(2)}, u32[]{:S(2)}) collective-permute-start(f32[96,128]{1,0:T(8,128)S(1)} %add_add_fusion), channel_id=1, source_target_pairs={{0,16},{1,17},{2,18},{3,19},{4,20},{5,21},{6,22},{7,23},{8,24},{9,... | collective-permute-start | bytes 147464 | tf_op jit(solution)/shard_map/ppermute | solution.py:35
  48.6 2.0 %collective-permute-start.6 = (bf16[64,4096]{1,0:T(8,128)(2,1)S(1)}, bf16[64,4096]{1,0:T(8,128)(2,1)S(1)}, u32[]{:S(2)}, u32[]{:S(2)}) collective-permute-start(bf16[64,4096]{1,0:T(8,128)(2,1)S(1)} %pad_maximum_fusion.2), channel_id=1, source_target_pairs={{0,1},{1,0},{2,3},{3,2},{4,5},{5,4},{6,7},{7,6},{8,9},{9,8},{10,11... | collective-permute-start | bytes 1572872 | tf_op jit(solution)/shard_map/ppermute | solution.py:35
  50.8 9.3 %copy-start.2 = (bf16[64,8192]{1,0:T(8,128)(2,1)S(1)}, bf16[64,8192]{1,0:T(8,128)(2,1)}, u32[]{:S(2)}) copy-start(bf16[64,8192]{1,0:T(8,128)(2,1)} %prior_ref.3) | copy-start | bytes 3145732
  51.3 9.2 %copy-start.4 = (bf16[64,8192]{1,0:T(8,128)(2,1)S(1)}, bf16[64,8192]{1,0:T(8,128)(2,1)}, u32[]{:S(2)}) copy-start(bf16[64,8192]{1,0:T(8,128)(2,1)} %snap_ref.3) | copy-start | bytes 3145732
  51.3 4.2 %collective-permute-start.8 = (f32[64,128]{1,0:T(8,128)S(1)}, f32[64,128]{1,0:T(8,128)S(1)}, u32[]{:S(2)}, u32[]{:S(2)}) collective-permute-start(f32[64,128]{1,0:T(8,128)S(1)} %fusion.1), channel_id=1, source_target_pairs={{0,4},{1,5},{2,6},{3,7},{4,0},{5,1},{6,2},{7,3},{8,12},{9,13},{10,... | collective-permute-start | bytes 98312 | tf_op jit(solution)/shard_map/ppermute | solution.py:35
  51.8 3.7 %collective-permute-start.9 = (f32[64,128]{1,0:T(8,128)S(1)}, f32[64,128]{1,0:T(8,128)S(1)}, u32[]{:S(2)}, u32[]{:S(2)}) collective-permute-start(f32[64,128]{1,0:T(8,128)S(1)} %fusion.1), channel_id=1, source_target_pairs={{0,5},{1,4},{2,7},{3,6},{4,1},{5,0},{6,3},{7,2},{8,13},{9,12},{10,... | collective-permute-start | bytes 98312 | tf_op jit(solution)/shard_map/ppermute | solution.py:35
  52.8 2.6 %collective-permute-start.7 = (f32[64,128]{1,0:T(8,128)S(1)}, f32[64,128]{1,0:T(8,128)S(1)}, u32[]{:S(2)}, u32[]{:S(2)}) collective-permute-start(f32[64,128]{1,0:T(8,128)S(1)} %fusion.1), channel_id=1, source_target_pairs={{0,1},{1,0},{2,3},{3,2},{4,5},{5,4},{6,7},{7,6},{8,9},{9,8},{10,11... | collective-permute-start | bytes 98312 | tf_op jit(solution)/shard_map/ppermute | solution.py:35
  53.5 22.5 %collective-permute-start.15 = (bf16[128,2048]{1,0:T(8,128)(2,1)S(1)}, bf16[128,2048]{1,0:T(8,128)(2,1)S(1)}, u32[]{:S(2)}, u32[]{:S(2)}) collective-permute-start(bf16[128,2048]{1,0:T(8,128)(2,1)S(1)} %fusion.5), channel_id=1, source_target_pairs={{0,2},{1,3},{2,0},{3,1},{4,6},{5,7},{6,4},{7,5},{8,10},{9,11},{10,... | collective-permute-start | bytes 1572872 | tf_op jit(solution)/shard_map/ppermute | solution.py:35
  55.5 5.8 %collective-permute-start.11 = (f32[64,128]{1,0:T(8,128)S(1)}, f32[64,128]{1,0:T(8,128)S(1)}, u32[]{:S(2)}, u32[]{:S(2)}) collective-permute-start(f32[64,128]{1,0:T(8,128)S(1)} %add_add_fusion.4), channel_id=1, source_target_pairs={{0,16},{1,17},{2,18},{3,19},{4,20},{5,21},{6,22},{7,23},{8,24},{9,... | collective-permute-start | bytes 98312 | tf_op jit(solution)/shard_map/ppermute | solution.py:35
  58.2 5.7 %collective-permute-start.12 = (f32[64,128]{1,0:T(8,128)S(1)}, f32[64,128]{1,0:T(8,128)S(1)}, u32[]{:S(2)}, u32[]{:S(2)}) collective-permute-start(f32[64,128]{1,0:T(8,128)S(1)} %add_add_fusion.4), channel_id=1, source_target_pairs={{0,24},{1,25},{2,26},{3,27},{4,28},{5,29},{6,30},{7,31},{8,16},{9,... | collective-permute-start | bytes 98312 | tf_op jit(solution)/shard_map/ppermute | solution.py:35
  59.6 4.3 %collective-permute-start.10 = (f32[64,128]{1,0:T(8,128)S(1)}, f32[64,128]{1,0:T(8,128)S(1)}, u32[]{:S(2)}, u32[]{:S(2)}) collective-permute-start(f32[64,128]{1,0:T(8,128)S(1)} %add_add_fusion.4), channel_id=1, source_target_pairs={{0,8},{1,9},{2,10},{3,11},{4,12},{5,13},{6,14},{7,15},{8,0},{9,1},... | collective-permute-start | bytes 98312 | tf_op jit(solution)/shard_map/ppermute | solution.py:35
  60.1 1.2 %collective-permute-start.13 = (f32[64,64]{1,0:T(8,128)S(1)}, f32[64,64]{1,0:T(8,128)S(1)}, u32[]{:S(2)}, u32[]{:S(2)}) collective-permute-start(f32[64,64]{1,0:T(8,128)S(1)} %get-tuple-element.23), channel_id=1, source_target_pairs={{0,1},{1,0},{2,3},{3,2},{4,5},{5,4},{6,7},{7,6},{8,9},{9,8},{10,11... | collective-permute-start | bytes 49160 | tf_op jit(solution)/shard_map/ppermute | solution.py:35
  72.3 3.8 %collective-permute-start.14 = (bf16[64,128]{1,0:T(8,128)(2,1)S(1)}, bf16[64,128]{1,0:T(8,128)(2,1)S(1)}, u32[]{:S(2)}, u32[]{:S(2)}) collective-permute-start(bf16[64,128]{1,0:T(8,128)(2,1)S(1)} %get-tuple-element.28), channel_id=1, source_target_pairs={{0,2},{1,3},{2,0},{3,1},{4,6},{5,7},{6,4},{7,5},{8,10},{9,11},{10,... | collective-permute-start | bytes 49160 | tf_op jit(solution)/shard_map/ppermute | solution.py:35
  73.8 12.4 %collective-permute-start.24 = (bf16[64,4096]{1,0:T(8,128)(2,1)S(1)}, bf16[64,4096]{1,0:T(8,128)(2,1)S(1)}, u32[]{:S(2)}, u32[]{:S(2)}) collective-permute-start(bf16[64,4096]{1,0:T(8,128)(2,1)S(1)} %pad_maximum_fusion.5), channel_id=1, source_target_pairs={{0,1},{1,0},{2,3},{3,2},{4,5},{5,4},{6,7},{7,6},{8,9},{9,8},{10,11... | collective-permute-start | bytes 1572872 | tf_op jit(solution)/shard_map/ppermute | solution.py:35
  76.8 4.0 %collective-permute-start.17 = (f32[64,128]{1,0:T(8,128)S(1)}, f32[64,128]{1,0:T(8,128)S(1)}, u32[]{:S(2)}, u32[]{:S(2)}) collective-permute-start(f32[64,128]{1,0:T(8,128)S(1)} %fusion.15), channel_id=1, source_target_pairs={{0,2},{1,3},{2,0},{3,1},{4,6},{5,7},{6,4},{7,5},{8,10},{9,11},{10,... | collective-permute-start | bytes 98312 | tf_op jit(solution)/shard_map/ppermute | solution.py:35
  78.4 3.3 %collective-permute-start.18 = (f32[64,128]{1,0:T(8,128)S(1)}, f32[64,128]{1,0:T(8,128)S(1)}, u32[]{:S(2)}, u32[]{:S(2)}) collective-permute-start(f32[64,128]{1,0:T(8,128)S(1)} %fusion.15), channel_id=1, source_target_pairs={{0,3},{1,2},{2,1},{3,0},{4,7},{5,6},{6,5},{7,4},{8,11},{9,10},{10,... | collective-permute-start | bytes 98312 | tf_op jit(solution)/shard_map/ppermute | solution.py:35
  78.4 3.3 %collective-permute-start.16 = (f32[64,128]{1,0:T(8,128)S(1)}, f32[64,128]{1,0:T(8,128)S(1)}, u32[]{:S(2)}, u32[]{:S(2)}) collective-permute-start(f32[64,128]{1,0:T(8,128)S(1)} %fusion.15), channel_id=1, source_target_pairs={{0,1},{1,0},{2,3},{3,2},{4,5},{5,4},{6,7},{7,6},{8,9},{9,8},{10,11... | collective-permute-start | bytes 98312 | tf_op jit(solution)/shard_map/ppermute | solution.py:35
  81.7 6.2 %collective-permute-start.20 = (f32[64,128]{1,0:T(8,128)S(1)}, f32[64,128]{1,0:T(8,128)S(1)}, u32[]{:S(2)}, u32[]{:S(2)}) collective-permute-start(f32[64,128]{1,0:T(8,128)S(1)} %add_add_fusion.2), channel_id=1, source_target_pairs={{0,8},{1,9},{2,10},{3,11},{4,12},{5,13},{6,14},{7,15},{8,0},{9,1},... | collective-permute-start | bytes 98312 | tf_op jit(solution)/shard_map/ppermute | solution.py:35
  81.9 6.1 %collective-permute-start.21 = (f32[64,128]{1,0:T(8,128)S(1)}, f32[64,128]{1,0:T(8,128)S(1)}, u32[]{:S(2)}, u32[]{:S(2)}) collective-permute-start(f32[64,128]{1,0:T(8,128)S(1)} %add_add_fusion.2), channel_id=1, source_target_pairs={{0,12},{1,13},{2,14},{3,15},{4,8},{5,9},{6,10},{7,11},{8,4},{9,5},... | collective-permute-start | bytes 98312 | tf_op jit(solution)/shard_map/ppermute | solution.py:35
  84.3 3.9 %collective-permute-start.19 = (f32[64,128]{1,0:T(8,128)S(1)}, f32[64,128]{1,0:T(8,128)S(1)}, u32[]{:S(2)}, u32[]{:S(2)}) collective-permute-start(f32[64,128]{1,0:T(8,128)S(1)} %add_add_fusion.2), channel_id=1, source_target_pairs={{0,4},{1,5},{2,6},{3,7},{4,0},{5,1},{6,2},{7,3},{8,12},{9,13},{10,... | collective-permute-start | bytes 98312 | tf_op jit(solution)/shard_map/ppermute | solution.py:35
  85.3 4.3 %collective-permute-start.23 = (f32[64,64]{1,0:T(8,128)S(1)}, f32[64,64]{1,0:T(8,128)S(1)}, u32[]{:S(2)}, u32[]{:S(2)}) collective-permute-start(f32[64,64]{1,0:T(8,128)S(1)} %get-tuple-element.27), channel_id=1, source_target_pairs={{0,2},{1,3},{2,0},{3,1},{4,6},{5,7},{6,4},{7,5},{8,10},{9,11},{10,... | collective-permute-start | bytes 49160 | tf_op jit(solution)/shard_map/ppermute | solution.py:35
  86.7 7.7 %collective-permute-start.25 = (bf16[64,2048]{1,0:T(8,128)(2,1)S(1)}, bf16[64,2048]{1,0:T(8,128)(2,1)S(1)}, u32[]{:S(2)}, u32[]{:S(2)}) collective-permute-start(bf16[64,2048]{1,0:T(8,128)(2,1)S(1)} %constant_dynamic-slice_fusion), channel_id=1, source_target_pairs={{0,2},{1,3},{2,0},{3,1},{4,6},{5,7},{6,4},{7,5},{8,10},{9,11},{10,... | collective-permute-start | bytes 786440 | tf_op jit(solution)/shard_map/ppermute | solution.py:35
  88.2 5.1 %collective-permute-start.22 = (f32[64,128]{1,0:T(8,128)S(1)}, f32[64,128]{1,0:T(8,128)S(1)}, u32[]{:S(2)}, u32[]{:S(2)}) collective-permute-start(f32[64,128]{1,0:T(8,128)S(1)} %add_add_fusion.1), channel_id=1, source_target_pairs={{0,16},{1,17},{2,18},{3,19},{4,20},{5,21},{6,22},{7,23},{8,24},{9,... | collective-permute-start | bytes 98312 | tf_op jit(solution)/shard_map/ppermute | solution.py:35
